TPU v7x, 256 devices: a whole 4x4x8 slice. The times are simulated.
256 devices in a mesh: segment: 8 (over y_lo, x), az: 32 (over y_hi, z, core).
Axes of the slice: x: 4, y: 4 (y_hi: 2, y_lo: 2; y = y_hi * 2 + y_lo), z: 8, core: 2. Of those that a mesh axis runs over, the one named last changes fastest.
Arguments:
- stored_inputs: bfloat16 [4, 8, 3, 2048, 512], P(None, 'segment', None, 'az'), may hold values from -6 to 6
- filter_weights: bfloat16 [8, 3, 3, 512, 512], P('segment'), may hold values from -0.09375 to 0.09375
- pending_slopes: bfloat16 [8, 3, 2048, 512], P('segment', None, 'az'), may hold values from -6 to 6
- topmost_slopes: bfloat16 [3, 3, 2048, 512], P(None, None, 'az'), may hold values from -6 to 6
Outputs:
- sent: bfloat16 [4, 8, 3, 2048, 512], P(None, 'segment', None, 'az')
- weight_grads: bfloat16 [8, 3, 3, 512, 512], P('segment', None, None, 'az')
All inputs are finite; a program needn't handle non-finite values.
Results may differ from a plain program's by a relative error of at most 0.022.
Values may be sent and summed in bfloat16 or wider, within the bound.
No kernel may reach another device: no remote copies, remote signals or barrier semaphores. Data moves between devices by JAX's collectives and lax.ppermute only.
A program may use at most 128 MiB of HBM per device.

v0:
```python
import math

import jax
import jax.numpy as jnp
from jax import lax
from jax.experimental import pallas as pl
from jax.experimental.pallas import tpu as pltpu
from jax.sharding import PartitionSpec as P

BF = jnp.bfloat16
F32 = jnp.float32
ROWS, WIDTH, CH, STEPS = 3, 64, 512, 4
WIDE = WIDTH + 8
QUARTER = CH // 4


def az_route(move):
    route = []
    for i in range(32):
        h, z, c = move(i // 16, (i // 2) % 8, i % 2)
        route.append((i, (h % 2) * 16 + (z % 8) * 2 + c % 2))
    return route


RIGHT = [(i, (i + 1) % 32) for i in range(32)]
LEFT = [(i, (i - 1) % 32) for i in range(32)]
CORE = az_route(lambda h, z, c: (h, z, c + 1))
PAIR = az_route(lambda h, z, c: (h, z ^ 1, c))
DIAG = az_route(lambda h, z, c: (h, z ^ 1, c + 1))
FAR = az_route(lambda h, z, c: (h + 1, z, c))
UP = az_route(lambda h, z, c: (h, z + 2, c))
DOWN = az_route(lambda h, z, c: (h, z - 2, c))


def send(block, route):
    return lax.ppermute(block, "az", route)


def relay(block):
    count = lax.axis_size("segment")
    return lax.ppermute(block, "segment", [(i, i - 1) for i in range(1, count)])


def params(mib=48):
    return pltpu.CompilerParams(vmem_limit_bytes=mib * 1024 * 1024)


def cost(flops, size):
    return pl.CostEstimate(flops=int(flops), bytes_accessed=int(size), transcendentals=0)


VMEM = pl.BlockSpec(memory_space=pltpu.VMEM)
SMEM = pl.BlockSpec(memory_space=pltpu.SMEM)


def block(shape, *index):
    return pl.BlockSpec(shape, lambda *_: index)


def pack_kernel(x_right, p_right, t_right, x_left, p_left, t_left, right_ref, left_ref):
    for refs, first, out in (((x_right, p_right, t_right), 8, right_ref), ((x_left, p_left, t_left), 0, left_ref)):
        xs, ps, ts = refs
        for r in range(ROWS):
            planes = [xs[t, r] for t in range(STEPS)] + [ps[r]] + [ts[t, r] for t in range(STEPS - 1)]
            for n, plane in enumerate(planes):
                out[n * ROWS + r] = plane.astype(F32)[first : first + 8].astype(BF)


def pack_edges(x, pending, top):
    def specs(edge):
        return [
            block((STEPS, ROWS, 16, CH), 0, 0, edge, 0),
            block((ROWS, 16, CH), 0, edge, 0),
            block((STEPS - 1, ROWS, 16, CH), 0, 0, edge, 0),
        ]

    shape = jax.ShapeDtypeStruct((24, 8, CH), BF)
    return pl.pallas_call(
        pack_kernel,
        grid=(1,),
        out_shape=(shape, shape),
        in_specs=specs(3) + specs(0),
        out_specs=(block((24, 8, CH), 0, 0, 0),) * 2,
        compiler_params=params(),
        cost_estimate=cost(0, 1 << 20),
    )(x, pending, top, x, pending, top)


def first_four(high, low):
    pick = lax.broadcasted_iota(jnp.int32, high.shape, 0) < 4
    return jnp.where(pick, high, low)


def widen(own, high, low):
    return jnp.concatenate([own.astype(F32), first_four(high.astype(F32), low.astype(F32))], axis=0)


def factor_kernel(x_ref, low_ref, high_ref, w_ref, out_ref):
    wide = WIDTH + 16
    planes = [
        jnp.concatenate(
            [x_ref[0, r].astype(F32), high_ref[r].astype(F32), low_ref[r].astype(F32)], axis=0
        )
        for r in range(ROWS)
    ]
    field = jnp.concatenate(planes, axis=0).astype(BF)
    sums = []
    for b in range(3):
        up = jnp.dot(field[: 2 * wide], w_ref[b], preferred_element_type=F32)
        mid = jnp.dot(field, w_ref[3 + b], preferred_element_type=F32)
        down = jnp.dot(field[wide:], w_ref[6 + b], preferred_element_type=F32)
        rows = []
        for r in range(ROWS):
            value = mid[r * wide : (r + 1) * wide]
            if r > 0:
                value = value + up[(r - 1) * wide : r * wide]
            if r < 2:
                value = value + down[r * wide : (r + 1) * wide]
            rows.append(value)
        sums.append(rows)
    for r in range(ROWS):
        preact = pltpu.roll(sums[0][r], 1, 0) + sums[1][r] + pltpu.roll(sums[2][r], wide - 1, 0)
        gate = jax.nn.sigmoid(preact)
        value = gate * (1.0 + preact * (1.0 - gate))
        out_ref[0, r, :WIDTH] = value[:WIDTH]
        out_ref[0, r, WIDTH:] = first_four(value[WIDTH : WIDTH + 8], value[WIDTH + 8 :])


def slope_factors(x, low, high, weights, first, count):
    return pl.pallas_call(
        factor_kernel,
        grid=(count,),
        out_shape=jax.ShapeDtypeStruct((count, ROWS, WIDE, CH), F32),
        in_specs=[
            pl.BlockSpec((1, ROWS, WIDTH, CH), lambda n: (first + n, 0, 0, 0)),
            pl.BlockSpec((ROWS, 8, CH), lambda n: (first + n, 0, 0)),
            pl.BlockSpec((ROWS, 8, CH), lambda n: (first + n, 0, 0)),
            pl.BlockSpec((9, CH, CH), lambda n: (0, 0, 0)),
        ],
        out_specs=pl.BlockSpec((1, ROWS, WIDE, CH), lambda n: (n, 0, 0, 0)),
        compiler_params=params(),
        cost_estimate=cost(count * 1.2e9, 5e6),
    )(x, low, high, weights)


def back_kernel(first, *refs):
    if first:
        own_ref, low_ref, high_ref, factor_ref, w_ref, sent_ref, grad_ref = refs
    else:
        flag_ref, own_ref, low_ref, high_ref, relay_ref, factor_ref, w_ref, sent_ref, grad_ref = refs
    slopes = []
    for r in range(ROWS):
        own = own_ref[r] if first else own_ref[0, r]
        slope = widen(own, high_ref[r], low_ref[r])
        if not first:
            slope = jnp.where(flag_ref[0] == 1, slope, relay_ref[r].astype(F32))
        slopes.append(slope)
    grads = []
    for r in range(ROWS):
        grad = slopes[r] * factor_ref[0, r]
        grad_ref[r] = grad[:WIDTH].astype(BF)
        grads.append(grad)
    field = jnp.concatenate(grads, axis=0).astype(BF)
    above = jnp.concatenate(grads[1:], axis=0).astype(BF)
    below = jnp.concatenate(grads[:2], axis=0).astype(BF)
    turned = (((1,), (1,)), ((), ()))
    sums = []
    for b in range(3):
        up = lax.dot_general(above, w_ref[b], turned, preferred_element_type=F32)
        mid = lax.dot_general(field, w_ref[3 + b], turned, preferred_element_type=F32)
        down = lax.dot_general(below, w_ref[6 + b], turned, preferred_element_type=F32)
        rows = []
        for r in range(ROWS):
            value = mid[r * WIDE : (r + 1) * WIDE]
            if r < 2:
                value = value + up[r * WIDE : (r + 1) * WIDE]
            if r > 0:
                value = value + down[(r - 1) * WIDE : r * WIDE]
            rows.append(value)
        sums.append(rows)
    for r in range(ROWS):
        value = pltpu.roll(sums[0][r], WIDE - 1, 0) + sums[1][r] + pltpu.roll(sums[2][r], 1, 0)
        sent_ref[r] = (slopes[r] + value).astype(BF)


def back_step(own, low, high, factors, weights, t, flag=None, arrived=None):
    first = t == 0
    edge = block((ROWS, 8, CH), 4 + t, 0, 0)
    operands = [own, low, high]
    if first:
        specs = [block((ROWS, WIDTH, CH), 0, 0, 0), edge, edge]
    else:
        specs = [SMEM, block((1, ROWS, WIDTH, CH), t - 1, 0, 0, 0), edge, edge]
        specs += [block((ROWS, WIDE, CH), 0, 0, 0)]
        operands = [flag, *operands, arrived]
    specs += [block((1, ROWS, WIDE, CH), max(t - 1, 0), 0, 0, 0), block((9, CH, CH), 0, 0, 0)]
    return pl.pallas_call(
        lambda *refs: back_kernel(first, *refs),
        grid=(1,),
        out_shape=(
            jax.ShapeDtypeStruct((ROWS, WIDE, CH), BF),
            jax.ShapeDtypeStruct((ROWS, WIDTH, CH), BF),
        ),
        in_specs=specs,
        out_specs=(block((ROWS, WIDE, CH), 0, 0, 0), block((ROWS, WIDTH, CH), 0, 0, 0)),
        compiler_params=params(),
        cost_estimate=cost(1.1e9, 6e6),
    )(*operands, factors, weights)


def spread_kernel(place_ref, x_ref, low_ref, high_ref, out0, out1, out2, out3, order_ref):
    @pl.when(pl.program_id(0) == 0)
    def _():
        h, j, q = place_ref[0], place_ref[1], place_ref[2]
        lane = lax.broadcasted_iota(jnp.int32, (8, CH), 1)
        slot, rest = lane // QUARTER, lane % QUARTER
        quarter = jnp.bitwise_xor(slot, q)
        half = jnp.bitwise_xor(rest // 64, h)
        turn = jnp.bitwise_and(rest // 16 + j, 3)
        source = (half * 4 + turn) * 64 + quarter * 16 + rest % 16
        row = lax.broadcasted_iota(jnp.int32, (CH, CH), 0)
        order_ref[...] = jnp.where(row == source[:1], 1.0, 0.0).astype(BF)

    planes = [widen(x_ref[0, r], high_ref[r], low_ref[r]) for r in range(ROWS)]
    field = jnp.concatenate(planes, axis=0).astype(BF)
    value = jnp.dot(field, order_ref[...], preferred_element_type=F32)
    for n, out in enumerate((out0, out1, out2, out3)):
        for r in range(ROWS):
            out[0, r] = value[r * WIDE : (r + 1) * WIDE, n * QUARTER : (n + 1) * QUARTER].astype(BF)


def spread(place, x, low, high):
    shape = jax.ShapeDtypeStruct((STEPS, ROWS, WIDE, QUARTER), BF)
    return pl.pallas_call(
        spread_kernel,
        grid=(STEPS,),
        out_shape=(shape,) * 4,
        in_specs=[
            SMEM,
            pl.BlockSpec((1, ROWS, WIDTH, CH), lambda n: (n, 0, 0, 0)),
            pl.BlockSpec((ROWS, 8, CH), lambda n: (n, 0, 0)),
            pl.BlockSpec((ROWS, 8, CH), lambda n: (n, 0, 0)),
        ],
        out_specs=(pl.BlockSpec((1, ROWS, WIDE, QUARTER), lambda n: (n, 0, 0, 0)),) * 4,
        scratch_shapes=[pltpu.VMEM((CH, CH), BF)],
        compiler_params=params(),
        cost_estimate=cost(4.5e8, 2e6),
    )(place, x, low, high)


def weight_kernel(more, last, *refs):
    xs, gs = refs[:4], refs[4:8]
    out_ref = refs[-1]
    left, right = [], []
    for r in range(ROWS):
        taps = [[], [], []]
        for x_ref in xs:
            plane = x_ref[0, r].astype(F32)
            for b, shift in enumerate((1, 0, WIDE - 1)):
                moved = pltpu.roll(plane, shift, 0) if shift else plane
                taps[b].append(moved[:WIDTH])
        left.append(
            jnp.concatenate([jnp.concatenate(parts, axis=0).astype(BF) for parts in taps], axis=1)
        )
        right.append(jnp.concatenate([g[r] for g in gs], axis=0))
    for a in range(3):
        ls = left[: 2 + (a > 0)] if a < 2 else left[1:]
        rs = right[1:] if a == 0 else (right if a == 1 else right[:2])
        value = lax.dot_general(
            jnp.concatenate(ls, axis=0),
            jnp.concatenate(rs, axis=0),
            (((0,), (0,)), ((), ())),
            preferred_element_type=F32,
        )
        for b in range(3):
            part = value[b * QUARTER : (b + 1) * QUARTER]
            if more:
                part = part + refs[8][a * 3 + b]
            out_ref[a * 3 + b] = part.astype(BF) if last else part


def weight_step(xs, gs, t, total):
    more, last = t > 0, t == STEPS - 1
    whole = block((9, QUARTER, CH), 0, 0, 0)
    operands = [*xs, *gs] + ([total] if more else [])
    return pl.pallas_call(
        lambda *refs: weight_kernel(more, last, *refs),
        grid=(1,),
        out_shape=jax.ShapeDtypeStruct((9, QUARTER, CH), BF if last else F32),
        in_specs=[block((1, ROWS, WIDE, QUARTER), t, 0, 0, 0)] * 4
        + [block((ROWS, WIDTH, CH), 0, 0, 0)] * 4
        + ([whole] if more else []),
        out_specs=whole,
        compiler_params=params(),
        cost_estimate=cost(9e8, 6e6),
    )(*operands)


def add(left, right):
    return (left.astype(F32) + right.astype(F32)).astype(BF)


def fold_far(part):
    return add(send(part[:, 1], FAR), part[:, 0])


def fold_ring(part):
    half = part.shape[-1] // 2
    ups, downs = part[..., :half], part[..., half:]
    up, down = ups[:, 3], downs[:, 1]
    for s in range(3):
        up = add(send(up, UP), ups[:, 2 - s])
        down = add(send(down, DOWN), downs[:, (s + 2) % 4])
    return jnp.concatenate([up, down], axis=-1)


def body(stored_inputs, filter_weights, pending_slopes, topmost_slopes):
    x = stored_inputs[:, 0]
    pending = pending_slopes[0]
    top = topmost_slopes
    weights = filter_weights[0].reshape(9, CH, CH)
    az = lax.axis_index("az")
    place = jnp.stack([az // 16, (az // 4) % 4, az % 4]).astype(jnp.int32)
    last = lax.axis_index("segment") == lax.axis_size("segment") - 1
    flag = last.astype(jnp.int32).reshape(1)
    scale = 1.0 / math.sqrt(STEPS * ROWS * WIDTH * lax.axis_size("az"))

    right_edge, left_edge = pack_edges(x, pending, top)
    low = send(right_edge, RIGHT)
    high = send(left_edge, LEFT)

    factors = slope_factors(x, low, high, weights, 0, 1)
    sent, own = back_step(pending, low, high, factors, weights, 0)
    arrived = relay(sent)
    emitted = [sent[:, :WIDTH]]
    factors = slope_factors(x, low, high, weights, 1, 3)

    spreads = spread(place, x, low, high)
    xs = [spreads[0], send(spreads[1], CORE), send(spreads[2], PAIR), send(spreads[3], DIAG)]

    total = None
    for t in range(STEPS):
        from_core = send(own, CORE)
        from_pair = send(own, PAIR)
        from_diag = send(from_pair, CORE)
        total = weight_step(xs, (own, from_core, from_pair, from_diag), t, total)
        if t + 1 < STEPS:
            sent, own = back_step(top, low, high, factors, weights, t + 1, flag, arrived)
            emitted.append(sent[:, :WIDTH])
            if t + 2 < STEPS:
                arrived = relay(sent)

    cut = CH // 2
    part = total.reshape(9, 2, 4, 16, CH)
    first = fold_ring(fold_far(part[..., :cut]))
    second = part[..., cut:].transpose(0, 2, 1, 3, 4).reshape(9, 4, 32, cut)
    second = fold_far(fold_ring(second).reshape(9, 2, 16, cut))
    summed = jnp.concatenate([first, second], axis=-1).astype(F32)
    weight_grads = (summed * scale).astype(BF).reshape(1, 3, 3, 16, CH)
    return (jnp.stack(emitted)[:, None], weight_grads)


def solution(mesh):
    return jax.shard_map(
        body,
        mesh=mesh,
        in_specs=(
            P(None, "segment", None, "az", None),
            P("segment", None, None, None, None),
            P("segment", None, "az", None),
            P(None, None, "az", None),
        ),
        out_specs=(P(None, "segment", None, "az", None), P("segment", None, None, "az", None)),
        check_vma=False,
    )
```

profile of v0, /device:TPU:6, one launch (start us, length us, event | category | flops | bytes accessed | tf_op | source)
XLA Modules:
  0.0 130.0 jit_solution(13468306589840909818)
XLA Ops:
  0.6 1.1 copy-done.1
  1.7 1.1 copy-done.5
  2.8 0.9 copy-done.7
  3.9 8.0 %collective-permute-start.1 = (bf16[24,8,512]{2,1,0:T(8,128)(2,1)S(1)}, bf16[24,8,512]{2,1,0:T(8,128)(2,1)S(1)}, u32[]{:S(2)}, u32[]{:S(2)}) collective-permute-start(bf16[24,8,512]{2,1,0:T(8,128)(2,1)S(1)} %get-tuple-element.17), channel_id=1, source_target_pairs={{0,31},{1,0},{2,1},{3,2},{4,3},{5,4},{6,5},{7,6},{8,7},{9,8},{10,9... | collective-permute-start | bytes 589832 | tf_op jit(solution)/shard_map/ppermute | solution.py:36
  12.0 3.2 %collective-permute-done.low_ref.refs_1_.refs_2_ = bf16[24,8,512]{2,1,0:T(8,128)(2,1)S(1)} collective-permute-done((bf16[24,8,512]{2,1,0:T(8,128)(2,1)S(1)}, bf16[24,8,512]{2,1,0:T(8,128)(2,1)S(1)}, u32[]{:S(2)}, u32[]{:S(2)}) %collective-permute-start) | collective-permute-done | bytes 196640 | tf_op jit(solution)/shard_map/ppermute | solution.py:36
  15.2 3.6 %shard_map.60.refs_3_ = f32[1,3,72,512]{3,2,1,0:T(8,128)S(1)} custom-call(bf16[4,3,64,512]{3,2,1,0:T(8,128)(2,1)S(1)} %bitcast.147, bf16[24,8,512]{2,1,0:T(8,128)(2,1)S(1)} %collective-permute-done.low_ref.refs_1_.refs_2_, bf16[24,8,512]{2,1,0:T(8,128)(2,1)S(1)} %collective-permute-done.1.high_ref.refs_2_.refs_3_, bf16[9,512,512]{2,1,0:T(8,128)(2,1)} %bitcast.139), custom_call_target="tpu_custom_call" | custom-call | flops 1200000000 | bytes 5000000 | tf_op jit(solution)/shard_map/pallas_call | solution.py:130
  18.9 1.7 %shard_map.61 = (bf16[3,72,512]{2,1,0:T(8,128)(2,1)S(1)}, bf16[3,64,512]{2,1,0:T(8,128)(2,1)S(1)}) custom-call(bf16[3,64,512]{2,1,0:T(8,128)(2,1)S(1)} %bitcast.155, bf16[24,8,512]{2,1,0:T(8,128)(2,1)S(1)} %collective-permute-done.low_ref.refs_1_.refs_2_, bf16[24,8,512]{2,1,0:T(8,128)(2,1)S(1)} %collective-permute-done.1.high_ref.refs_2_.refs_3_, ...), custom_call_target="tpu_custom_call" | custom-call | flops 1100000000 | bytes 6000000 | tf_op jit(solution)/shard_map/pallas_call | solution.py:197
  20.8 2.7 %collective-permute-start.2 = (bf16[3,72,512]{2,1,0:T(8,128)(2,1)S(1)}, bf16[3,72,512]{2,1,0:T(8,128)(2,1)S(1)}, u32[]{:S(2)}, u32[]{:S(2)}) collective-permute-start(bf16[3,72,512]{2,1,0:T(8,128)(2,1)S(1)} %get-tuple-element.18), channel_id=1, source_target_pairs={{32,0},{64,32},{96,64},{128,96},{160,128},{192,160},{224,192},{33,... | collective-permute-start | bytes 663560 | tf_op jit(solution)/shard_map/ppermute | solution.py:41
  23.5 1.9 %shard_map.66 = (bf16[4,3,72,128]{3,2,1,0:T(8,128)(2,1)S(1)}, bf16[4,3,72,128]{3,2,1,0:T(8,128)(2,1)S(1)}, bf16[4,3,72,128]{3,2,1,0:T(8,128)(2,1)S(1)}, bf16[4,3,72,128]{3,2,1,0:T(8,128)(2,1)S(1)}) custom-call(s32[3]{0:T(128)S(1)} %pad_add_fusion.place_ref, bf16[4,3,64,512]{3,2,1,0:T(8,128)(2,1)S(1)} %bitcast.148, ...), custom_call_target="tpu_custom_call" | custom-call | flops 450000000 | bytes 2000000 | tf_op jit(solution)/shard_map/pallas_call | solution.py:234
  25.7 5.7 %shard_map.62.refs_5_ = f32[3,3,72,512]{3,2,1,0:T(8,128)S(1)} custom-call(bf16[4,3,64,512]{3,2,1,0:T(8,128)(2,1)S(1)} %bitcast.149, bf16[24,8,512]{2,1,0:T(8,128)(2,1)S(1)} %collective-permute-done.low_ref.refs_1_.refs_2_, bf16[24,8,512]{2,1,0:T(8,128)(2,1)S(1)} %collective-permute-done.1.high_ref.refs_2_.refs_3_, bf16[9,512,512]{2,1,0:T(8,128)(2,1)} %bitcast.140), custom_call_target="tpu_custom_call" | custom-call | flops 3600000000 | bytes 5000000 | tf_op jit(solution)/shard_map/pallas_call | solution.py:130
  31.5 1.2 collective-permute-done.2.refs_4_
  32.6 4.0 %shard_map.63 = (bf16[3,72,512]{2,1,0:T(8,128)(2,1)S(1)}, bf16[3,64,512]{2,1,0:T(8,128)(2,1)S(1)}) custom-call(s32[1]{0:T(128)} %bitcast.4.refs_0_, bf16[3,3,64,512]{3,2,1,0:T(8,128)(2,1)S(1)} %copy-done.2, bf16[24,8,512]{2,1,0:T(8,128)(2,1)S(1)} %collective-permute-done.low_ref.refs_1_.refs_2_, ...), custom_call_target="tpu_custom_call" | custom-call | flops 1100000000 | bytes 6000000 | tf_op jit(solution)/shard_map/pallas_call | solution.py:197
  36.6 1.9 %collective-permute-start.3 = (bf16[3,72,512]{2,1,0:T(8,128)(2,1)S(1)}, bf16[3,72,512]{2,1,0:T(8,128)(2,1)S(1)}, u32[]{:S(2)}, u32[]{:S(2)}) collective-permute-start(bf16[3,72,512]{2,1,0:T(8,128)(2,1)S(1)} %get-tuple-element.19), channel_id=1, source_target_pairs={{32,0},{64,32},{96,64},{128,96},{160,128},{192,160},{224,192},{33,... | collective-permute-start | bytes 663560 | tf_op jit(solution)/shard_map/ppermute | solution.py:41
  38.6 2.0 %collective-permute-start.6 = (bf16[4,3,72,128]{3,2,1,0:T(8,128)(2,1)S(1)}, bf16[4,3,72,128]{3,2,1,0:T(8,128)(2,1)S(1)}, u32[]{:S(2)}, u32[]{:S(2)}) collective-permute-start(bf16[4,3,72,128]{3,2,1,0:T(8,128)(2,1)S(1)} %get-tuple-element.24), channel_id=1, source_target_pairs={{0,2},{1,3},{2,0},{3,1},{4,6},{5,7},{6,4},{7,5},{8,10},{9,11},{10,... | collective-permute-start | bytes 663560 | tf_op jit(solution)/shard_map/ppermute | solution.py:36
  40.6 7.1 %collective-permute-done.3.refs_4_ = bf16[3,72,512]{2,1,0:T(8,128)(2,1)S(1)} collective-permute-done((bf16[3,72,512]{2,1,0:T(8,128)(2,1)S(1)}, bf16[3,72,512]{2,1,0:T(8,128)(2,1)S(1)}, u32[]{:S(2)}, u32[]{:S(2)}) %collective-permute-start.3) | collective-permute-done | bytes 221216 | tf_op jit(solution)/shard_map/ppermute | solution.py:41
  47.7 4.0 %shard_map.64 = (bf16[3,72,512]{2,1,0:T(8,128)(2,1)S(1)}, bf16[3,64,512]{2,1,0:T(8,128)(2,1)S(1)}) custom-call(s32[1]{0:T(128)} %bitcast.4.refs_0_, bf16[3,3,64,512]{3,2,1,0:T(8,128)(2,1)S(1)} %copy-done.2, bf16[24,8,512]{2,1,0:T(8,128)(2,1)S(1)} %collective-permute-done.low_ref.refs_1_.refs_2_, ...), custom_call_target="tpu_custom_call" | custom-call | flops 1100000000 | bytes 6000000 | tf_op jit(solution)/shard_map/pallas_call | solution.py:197
  51.7 2.0 %collective-permute-start.15 = (bf16[3,64,512]{2,1,0:T(8,128)(2,1)S(1)}, bf16[3,64,512]{2,1,0:T(8,128)(2,1)S(1)}, u32[]{:S(2)}, u32[]{:S(2)}) collective-permute-start(bf16[3,64,512]{2,1,0:T(8,128)(2,1)S(1)} %get-tuple-element.28.refs_4_), channel_id=1, source_target_pairs={{0,2},{1,3},{2,0},{3,1},{4,6},{5,7},{6,4},{7,5},{8,10},{9,11},{10,... | collective-permute-start | bytes 589832 | tf_op jit(solution)/shard_map/ppermute | solution.py:36
  53.7 1.9 %collective-permute-start.4 = (bf16[3,72,512]{2,1,0:T(8,128)(2,1)S(1)}, bf16[3,72,512]{2,1,0:T(8,128)(2,1)S(1)}, u32[]{:S(2)}, u32[]{:S(2)}) collective-permute-start(bf16[3,72,512]{2,1,0:T(8,128)(2,1)S(1)} %get-tuple-element.20), channel_id=1, source_target_pairs={{32,0},{64,32},{96,64},{128,96},{160,128},{192,160},{224,192},{33,... | collective-permute-start | bytes 663560 | tf_op jit(solution)/shard_map/ppermute | solution.py:41
  56.0 0.9 shard_map.67.refs_8_
  56.9 1.4 %copy-done.4 = f32[9,128,512]{2,1,0:T(8,128)} copy-done((f32[9,128,512]{2,1,0:T(8,128)}, f32[9,128,512]{2,1,0:T(8,128)S(1)}, u32[]{:S(2)}) %copy-start.4) | copy-done | bytes 2359320
  58.3 1.0 collective-permute-done.15.refs_6_
  59.3 1.7 %collective-permute-start.12 = (bf16[3,64,512]{2,1,0:T(8,128)(2,1)S(1)}, bf16[3,64,512]{2,1,0:T(8,128)(2,1)S(1)}, u32[]{:S(2)}, u32[]{:S(2)}) collective-permute-start(bf16[3,64,512]{2,1,0:T(8,128)(2,1)S(1)} %get-tuple-element.27.refs_4_), channel_id=1, source_target_pairs={{0,2},{1,3},{2,0},{3,1},{4,6},{5,7},{6,4},{7,5},{8,10},{9,11},{10,... | collective-permute-start | bytes 589832 | tf_op jit(solution)/shard_map/ppermute | solution.py:36
  61.0 4.2 %collective-permute-done.4.refs_4_ = bf16[3,72,512]{2,1,0:T(8,128)(2,1)S(1)} collective-permute-done((bf16[3,72,512]{2,1,0:T(8,128)(2,1)S(1)}, bf16[3,72,512]{2,1,0:T(8,128)(2,1)S(1)}, u32[]{:S(2)}, u32[]{:S(2)}) %collective-permute-start.4) | collective-permute-done | bytes 221216 | tf_op jit(solution)/shard_map/ppermute | solution.py:41
  65.3 4.0 %shard_map.65 = (bf16[3,72,512]{2,1,0:T(8,128)(2,1)S(1)}, bf16[3,64,512]{2,1,0:T(8,128)(2,1)S(1)}) custom-call(s32[1]{0:T(128)} %bitcast.4.refs_0_, bf16[3,3,64,512]{3,2,1,0:T(8,128)(2,1)S(1)} %copy-done.2, bf16[24,8,512]{2,1,0:T(8,128)(2,1)S(1)} %collective-permute-done.low_ref.refs_1_.refs_2_, ...), custom_call_target="tpu_custom_call" | custom-call | flops 1100000000 | bytes 6000000 | tf_op jit(solution)/shard_map/pallas_call | solution.py:197
  69.8 2.6 %shard_map.68.refs_8_ = f32[9,128,512]{2,1,0:T(8,128)S(1)} custom-call(bf16[4,3,72,128]{3,2,1,0:T(8,128)(2,1)S(1)} %get-tuple-element.22.refs_0_, bf16[4,3,72,128]{3,2,1,0:T(8,128)(2,1)S(1)} %collective-permute-done.5.refs_1_, bf16[4,3,72,128]{3,2,1,0:T(8,128)(2,1)S(1)} %collective-permute-done.6.refs_2_, ...), custom_call_target="tpu_custom_call" | custom-call | flops 900000000 | bytes 6000000 | tf_op jit(solution)/shard_map/pallas_call | solution.py:286
  72.4 1.4 %copy-done.3 = f32[9,128,512]{2,1,0:T(8,128)} copy-done((f32[9,128,512]{2,1,0:T(8,128)}, f32[9,128,512]{2,1,0:T(8,128)S(1)}, u32[]{:S(2)}) %copy-start.3) | copy-done | bytes 2359320
  73.8 0.5 collective-permute-start.13
  74.3 1.3 collective-permute-done.9.refs_6_
  75.6 2.6 %shard_map.69.refs_8_ = f32[9,128,512]{2,1,0:T(8,128)S(1)} custom-call(bf16[4,3,72,128]{3,2,1,0:T(8,128)(2,1)S(1)} %get-tuple-element.22.refs_0_, bf16[4,3,72,128]{3,2,1,0:T(8,128)(2,1)S(1)} %collective-permute-done.5.refs_1_, bf16[4,3,72,128]{3,2,1,0:T(8,128)(2,1)S(1)} %collective-permute-done.6.refs_2_, ...), custom_call_target="tpu_custom_call" | custom-call | flops 900000000 | bytes 6000000 | tf_op jit(solution)/shard_map/pallas_call | solution.py:286
  78.2 0.9 shard_map.70
  79.3 2.1 %collective-permute-start.27 = (bf16[9,32,128]{2,1,0:T(8,128)(2,1)S(1)}, bf16[9,32,128]{2,1,0:T(8,128)(2,1)S(1)}, u32[]{:S(2)}, u32[]{:S(2)}) collective-permute-start(bf16[9,32,128]{2,1,0:T(8,128)(2,1)S(1)} %get-tuple-element.36), channel_id=1, source_target_pairs={{0,4},{1,5},{2,6},{3,7},{4,8},{5,9},{6,10},{7,11},{8,12},{9,13},{1... | collective-permute-start | bytes 221192 | tf_op jit(solution)/shard_map/ppermute | solution.py:36
  81.4 3.3 %collective-permute-start.20 = (bf16[9,4,16,256]{3,2,1,0:T(8,128)(2,1)S(1)}, bf16[9,4,16,256]{3,2,1,0:T(8,128)(2,1)S(1)}, u32[]{:S(2)}, u32[]{:S(2)}) collective-permute-start(bf16[9,4,16,256]{3,2,1,0:T(8,128)(2,1)S(1)} %slice_bitcast_fusion.1), channel_id=1, source_target_pairs={{0,16},{1,17},{2,18},{3,19},{4,20},{5,21},{6,22},{7,23},{8,24},{9,... | collective-permute-start | bytes 884744 | tf_op jit(solution)/shard_map/ppermute | solution.py:36
  84.7 2.5 %collective-permute-done.27 = bf16[9,32,128]{2,1,0:T(8,128)(2,1)S(1)} collective-permute-done((bf16[9,32,128]{2,1,0:T(8,128)(2,1)S(1)}, bf16[9,32,128]{2,1,0:T(8,128)(2,1)S(1)}, u32[]{:S(2)}, u32[]{:S(2)}) %collective-permute-start.27) | collective-permute-done | bytes 73760 | tf_op jit(solution)/shard_map/ppermute | solution.py:36
  87.4 1.0 maximum_bitcast_fusion
  88.3 4.1 %collective-permute-start.30 = (bf16[9,32,128]{2,1,0:T(8,128)(2,1)S(1)}, bf16[9,32,128]{2,1,0:T(8,128)(2,1)S(1)}, u32[]{:S(2)}, u32[]{:S(2)}) collective-permute-start(bf16[9,32,128]{2,1,0:T(8,128)(2,1)S(1)} %get-tuple-element.37), channel_id=1, source_target_pairs={{0,12},{1,13},{2,14},{3,15},{4,0},{5,1},{6,2},{7,3},{8,4},{9,5},{1... | collective-permute-start | bytes 221192 | tf_op jit(solution)/shard_map/ppermute | solution.py:36
  92.5 1.6 %collective-permute-done.28 = bf16[9,32,128]{2,1,0:T(8,128)(2,1)S(1)} collective-permute-done((bf16[9,32,128]{2,1,0:T(8,128)(2,1)S(1)}, bf16[9,32,128]{2,1,0:T(8,128)(2,1)S(1)}, u32[]{:S(2)}, u32[]{:S(2)}) %collective-permute-start.28) | collective-permute-done | bytes 73760 | tf_op jit(solution)/shard_map/ppermute | solution.py:36
  94.3 3.8 %collective-permute-start.21 = (bf16[9,16,128]{2,1,0:T(8,128)(2,1)S(1)}, bf16[9,16,128]{2,1,0:T(8,128)(2,1)S(1)}, u32[]{:S(2)}, u32[]{:S(2)}) collective-permute-start(bf16[9,16,128]{2,1,0:T(8,128)(2,1)S(1)} %get-tuple-element.40), channel_id=1, source_target_pairs={{0,4},{1,5},{2,6},{3,7},{4,8},{5,9},{6,10},{7,11},{8,12},{9,13},{1... | collective-permute-start | bytes 110600 | tf_op jit(solution)/shard_map/ppermute | solution.py:36
  98.1 3.2 %collective-permute-done.29 = bf16[9,32,128]{2,1,0:T(8,128)(2,1)S(1)} collective-permute-done((bf16[9,32,128]{2,1,0:T(8,128)(2,1)S(1)}, bf16[9,32,128]{2,1,0:T(8,128)(2,1)S(1)}, u32[]{:S(2)}, u32[]{:S(2)}) %collective-permute-start.29) | collective-permute-done | bytes 73760 | tf_op jit(solution)/shard_map/ppermute | solution.py:36
  101.5 5.2 %collective-permute-start.24 = (bf16[9,16,128]{2,1,0:T(8,128)(2,1)S(1)}, bf16[9,16,128]{2,1,0:T(8,128)(2,1)S(1)}, u32[]{:S(2)}, u32[]{:S(2)}) collective-permute-start(bf16[9,16,128]{2,1,0:T(8,128)(2,1)S(1)} %get-tuple-element.41), channel_id=1, source_target_pairs={{0,12},{1,13},{2,14},{3,15},{4,0},{5,1},{6,2},{7,3},{8,4},{9,5},{1... | collective-permute-start | bytes 110600 | tf_op jit(solution)/shard_map/ppermute | solution.py:36
  106.8 0.9 collective-permute-done.31
  107.8 3.3 %collective-permute-start.32 = (bf16[9,32,128]{2,1,0:T(8,128)(2,1)S(1)}, bf16[9,32,128]{2,1,0:T(8,128)(2,1)S(1)}, u32[]{:S(2)}, u32[]{:S(2)}) collective-permute-start(bf16[9,32,128]{2,1,0:T(8,128)(2,1)S(1)} %fusion.3), channel_id=1, source_target_pairs={{0,12},{1,13},{2,14},{3,15},{4,0},{5,1},{6,2},{7,3},{8,4},{9,5},{1... | collective-permute-start | bytes 221192 | tf_op jit(solution)/shard_map/ppermute | solution.py:36
  111.0 1.9 %collective-permute-done.22 = bf16[9,16,128]{2,1,0:T(8,128)(2,1)S(1)} collective-permute-done((bf16[9,16,128]{2,1,0:T(8,128)(2,1)S(1)}, bf16[9,16,128]{2,1,0:T(8,128)(2,1)S(1)}, u32[]{:S(2)}, u32[]{:S(2)}) %collective-permute-start.22) | collective-permute-done | bytes 36896 | tf_op jit(solution)/shard_map/ppermute | solution.py:36
  113.2 5.9 %collective-permute-done.23 = bf16[9,16,128]{2,1,0:T(8,128)(2,1)S(1)} collective-permute-done((bf16[9,16,128]{2,1,0:T(8,128)(2,1)S(1)}, bf16[9,16,128]{2,1,0:T(8,128)(2,1)S(1)}, u32[]{:S(2)}, u32[]{:S(2)}) %collective-permute-start.23) | collective-permute-done | bytes 36896 | tf_op jit(solution)/shard_map/ppermute | solution.py:36
  119.2 1.4 %collective-permute-start.33 = (bf16[9,16,256]{2,1,0:T(8,128)(2,1)S(1)}, bf16[9,16,256]{2,1,0:T(8,128)(2,1)S(1)}, u32[]{:S(2)}, u32[]{:S(2)}) collective-permute-start(bf16[9,16,256]{2,1,0:T(8,128)(2,1)S(1)} %slice_bitcast_fusion.7), channel_id=1, source_target_pairs={{0,16},{1,17},{2,18},{3,19},{4,20},{5,21},{6,22},{7,23},{8,24},{9,... | collective-permute-start | bytes 221192 | tf_op jit(solution)/shard_map/ppermute | solution.py:36
  120.6 3.7 %collective-permute-done.25 = bf16[9,16,128]{2,1,0:T(8,128)(2,1)S(1)} collective-permute-done((bf16[9,16,128]{2,1,0:T(8,128)(2,1)S(1)}, bf16[9,16,128]{2,1,0:T(8,128)(2,1)S(1)}, u32[]{:S(2)}, u32[]{:S(2)}) %collective-permute-start.25) | collective-permute-done | bytes 36896 | tf_op jit(solution)/shard_map/ppermute | solution.py:36
  124.3 1.5 %collective-permute-start.26 = (bf16[9,16,128]{2,1,0:T(8,128)(2,1)S(1)}, bf16[9,16,128]{2,1,0:T(8,128)(2,1)S(1)}, u32[]{:S(2)}, u32[]{:S(2)}) collective-permute-start(bf16[9,16,128]{2,1,0:T(8,128)(2,1)S(1)} %fusion.9), channel_id=1, source_target_pairs={{0,12},{1,13},{2,14},{3,15},{4,0},{5,1},{6,2},{7,3},{8,4},{9,5},{1... | collective-permute-start | bytes 110600 | tf_op jit(solution)/shard_map/ppermute | solution.py:36
  125.8 3.5 %collective-permute-done.26 = bf16[9,16,128]{2,1,0:T(8,128)(2,1)S(1)} collective-permute-done((bf16[9,16,128]{2,1,0:T(8,128)(2,1)S(1)}, bf16[9,16,128]{2,1,0:T(8,128)(2,1)S(1)}, u32[]{:S(2)}, u32[]{:S(2)}) %collective-permute-start.26) | collective-permute-done | bytes 36896 | tf_op jit(solution)/shard_map/ppermute | solution.py:36
  129.3 0.7 multiply_convert_fusion
  (76 shorter events, 2.9 us)
Async XLA Ops:
  0.6 1.1 copy-start.1
  1.7 1.1 copy-start.5
  2.8 0.9 copy-start.7
  3.8 11.4 %copy-start.6 = (bf16[4,1,3,64,512]{4,3,2,1,0:T(8,128)(2,1)S(1)}, bf16[4,1,3,64,512]{4,3,2,1,0:T(8,128)(2,1)}, u32[]{:S(2)}) copy-start(bf16[4,1,3,64,512]{4,3,2,1,0:T(8,128)(2,1)} %param.4) | copy-start | bytes 2359300
  3.8 11.4 %collective-permute-start = (bf16[24,8,512]{2,1,0:T(8,128)(2,1)S(1)}, bf16[24,8,512]{2,1,0:T(8,128)(2,1)S(1)}, u32[]{:S(2)}, u32[]{:S(2)}) collective-permute-start(bf16[24,8,512]{2,1,0:T(8,128)(2,1)S(1)} %get-tuple-element.16), channel_id=1, source_target_pairs={{0,1},{1,2},{2,3},{3,4},{4,5},{5,6},{6,7},{7,8},{8,9},{9,10},{10,1... | collective-permute-start | bytes 589832 | tf_op jit(solution)/shard_map/ppermute | solution.py:36
  3.9 11.3 %collective-permute-start.1 = (bf16[24,8,512]{2,1,0:T(8,128)(2,1)S(1)}, bf16[24,8,512]{2,1,0:T(8,128)(2,1)S(1)}, u32[]{:S(2)}, u32[]{:S(2)}) collective-permute-start(bf16[24,8,512]{2,1,0:T(8,128)(2,1)S(1)} %get-tuple-element.17), channel_id=1, source_target_pairs={{0,31},{1,0},{2,1},{3,2},{4,3},{5,4},{6,5},{7,6},{8,7},{9,8},{10,9... | collective-permute-start | bytes 589832 | tf_op jit(solution)/shard_map/ppermute | solution.py:36
  15.2 3.8 %copy-start = (bf16[1,3,3,512,512]{4,3,2,1,0:T(8,128)(2,1)S(1)}, bf16[1,3,3,512,512]{4,3,2,1,0:T(8,128)(2,1)}, u32[]{:S(2)}) copy-start(bf16[1,3,3,512,512]{4,3,2,1,0:T(8,128)(2,1)} %param.5) | copy-start | bytes 14155780
  15.2 3.8 %copy-start.8 = (bf16[1,3,64,512]{3,2,1,0:T(8,128)(2,1)S(1)}, bf16[1,3,64,512]{3,2,1,0:T(8,128)(2,1)}, u32[]{:S(2)}) copy-start(bf16[1,3,64,512]{3,2,1,0:T(8,128)(2,1)} %param.6) | copy-start | bytes 589828
  20.6 20.0 %collective-permute-start.18 = (bf16[3,64,512]{2,1,0:T(8,128)(2,1)S(1)}, bf16[3,64,512]{2,1,0:T(8,128)(2,1)S(1)}, u32[]{:S(2)}, u32[]{:S(2)}) collective-permute-start(bf16[3,64,512]{2,1,0:T(8,128)(2,1)S(1)} %get-tuple-element.29.refs_4_), channel_id=1, source_target_pairs={{0,2},{1,3},{2,0},{3,1},{4,6},{5,7},{6,4},{7,5},{8,10},{9,11},{10,... | collective-permute-start | bytes 589832 | tf_op jit(solution)/shard_map/ppermute | solution.py:36
  20.7 31.0 %collective-permute-start.17 = (bf16[3,64,512]{2,1,0:T(8,128)(2,1)S(1)}, bf16[3,64,512]{2,1,0:T(8,128)(2,1)S(1)}, u32[]{:S(2)}, u32[]{:S(2)}) collective-permute-start(bf16[3,64,512]{2,1,0:T(8,128)(2,1)S(1)} %get-tuple-element.29.refs_4_), channel_id=1, source_target_pairs={{0,1},{1,0},{2,3},{3,2},{4,5},{5,4},{6,7},{7,6},{8,9},{9,8},{10,11... | collective-permute-start | bytes 589832 | tf_op jit(solution)/shard_map/ppermute | solution.py:36
  20.8 11.8 %collective-permute-start.2 = (bf16[3,72,512]{2,1,0:T(8,128)(2,1)S(1)}, bf16[3,72,512]{2,1,0:T(8,128)(2,1)S(1)}, u32[]{:S(2)}, u32[]{:S(2)}) collective-permute-start(bf16[3,72,512]{2,1,0:T(8,128)(2,1)S(1)} %get-tuple-element.18), channel_id=1, source_target_pairs={{32,0},{64,32},{96,64},{128,96},{160,128},{192,160},{224,192},{33,... | collective-permute-start | bytes 663560 | tf_op jit(solution)/shard_map/ppermute | solution.py:41
  25.4 7.2 %copy-start.2 = (bf16[3,3,64,512]{3,2,1,0:T(8,128)(2,1)S(1)}, bf16[3,3,64,512]{3,2,1,0:T(8,128)(2,1)}, u32[]{:S(2)}) copy-start(bf16[3,3,64,512]{3,2,1,0:T(8,128)(2,1)} %refs_1_.5) | copy-start | bytes 1769476
  25.4 28.3 %collective-permute-start.5 = (bf16[4,3,72,128]{3,2,1,0:T(8,128)(2,1)S(1)}, bf16[4,3,72,128]{3,2,1,0:T(8,128)(2,1)S(1)}, u32[]{:S(2)}, u32[]{:S(2)}) collective-permute-start(bf16[4,3,72,128]{3,2,1,0:T(8,128)(2,1)S(1)} %get-tuple-element.23), channel_id=1, source_target_pairs={{0,1},{1,0},{2,3},{3,2},{4,5},{5,4},{6,7},{7,6},{8,9},{9,8},{10,11... | collective-permute-start | bytes 663560 | tf_op jit(solution)/shard_map/ppermute | solution.py:36
  36.6 11.0 %collective-permute-start.3 = (bf16[3,72,512]{2,1,0:T(8,128)(2,1)S(1)}, bf16[3,72,512]{2,1,0:T(8,128)(2,1)S(1)}, u32[]{:S(2)}, u32[]{:S(2)}) collective-permute-start(bf16[3,72,512]{2,1,0:T(8,128)(2,1)S(1)} %get-tuple-element.19), channel_id=1, source_target_pairs={{32,0},{64,32},{96,64},{128,96},{160,128},{192,160},{224,192},{33,... | collective-permute-start | bytes 663560 | tf_op jit(solution)/shard_map/ppermute | solution.py:41
  38.6 17.1 %collective-permute-start.6 = (bf16[4,3,72,128]{3,2,1,0:T(8,128)(2,1)S(1)}, bf16[4,3,72,128]{3,2,1,0:T(8,128)(2,1)S(1)}, u32[]{:S(2)}, u32[]{:S(2)}) collective-permute-start(bf16[4,3,72,128]{3,2,1,0:T(8,128)(2,1)S(1)} %get-tuple-element.24), channel_id=1, source_target_pairs={{0,2},{1,3},{2,0},{3,1},{4,6},{5,7},{6,4},{7,5},{8,10},{9,11},{10,... | collective-permute-start | bytes 663560 | tf_op jit(solution)/shard_map/ppermute | solution.py:36
  40.6 15.4 %collective-permute-start.7 = (bf16[4,3,72,128]{3,2,1,0:T(8,128)(2,1)S(1)}, bf16[4,3,72,128]{3,2,1,0:T(8,128)(2,1)S(1)}, u32[]{:S(2)}, u32[]{:S(2)}) collective-permute-start(bf16[4,3,72,128]{3,2,1,0:T(8,128)(2,1)S(1)} %get-tuple-element.25), channel_id=1, source_target_pairs={{0,3},{1,2},{2,1},{3,0},{4,7},{5,6},{6,5},{7,4},{8,11},{9,10},{10,... | collective-permute-start | bytes 663560 | tf_op jit(solution)/shard_map/ppermute | solution.py:36
  47.7 8.3 %collective-permute-start.19 = (bf16[3,64,512]{2,1,0:T(8,128)(2,1)S(1)}, bf16[3,64,512]{2,1,0:T(8,128)(2,1)S(1)}, u32[]{:S(2)}, u32[]{:S(2)}) collective-permute-start(bf16[3,64,512]{2,1,0:T(8,128)(2,1)S(1)} %collective-permute-done.18.refs_6_), channel_id=1, source_target_pairs={{0,1},{1,0},{2,3},{3,2},{4,5},{5,4},{6,7},{7,6},{8,9},{9,8},{10,11... | collective-permute-start | bytes 589832 | tf_op jit(solution)/shard_map/ppermute | solution.py:36
  51.7 7.6 %collective-permute-start.15 = (bf16[3,64,512]{2,1,0:T(8,128)(2,1)S(1)}, bf16[3,64,512]{2,1,0:T(8,128)(2,1)S(1)}, u32[]{:S(2)}, u32[]{:S(2)}) collective-permute-start(bf16[3,64,512]{2,1,0:T(8,128)(2,1)S(1)} %get-tuple-element.28.refs_4_), channel_id=1, source_target_pairs={{0,2},{1,3},{2,0},{3,1},{4,6},{5,7},{6,4},{7,5},{8,10},{9,11},{10,... | collective-permute-start | bytes 589832 | tf_op jit(solution)/shard_map/ppermute | solution.py:36
  53.7 11.6 %collective-permute-start.4 = (bf16[3,72,512]{2,1,0:T(8,128)(2,1)S(1)}, bf16[3,72,512]{2,1,0:T(8,128)(2,1)S(1)}, u32[]{:S(2)}, u32[]{:S(2)}) collective-permute-start(bf16[3,72,512]{2,1,0:T(8,128)(2,1)S(1)} %get-tuple-element.20), channel_id=1, source_target_pairs={{32,0},{64,32},{96,64},{128,96},{160,128},{192,160},{224,192},{33,... | collective-permute-start | bytes 663560 | tf_op jit(solution)/shard_map/ppermute | solution.py:41
  55.7 14.1 %collective-permute-start.14 = (bf16[3,64,512]{2,1,0:T(8,128)(2,1)S(1)}, bf16[3,64,512]{2,1,0:T(8,128)(2,1)S(1)}, u32[]{:S(2)}, u32[]{:S(2)}) collective-permute-start(bf16[3,64,512]{2,1,0:T(8,128)(2,1)S(1)} %get-tuple-element.28.refs_4_), channel_id=1, source_target_pairs={{0,1},{1,0},{2,3},{3,2},{4,5},{5,4},{6,7},{7,6},{8,9},{9,8},{10,11... | collective-permute-start | bytes 589832 | tf_op jit(solution)/shard_map/ppermute | solution.py:36
  56.9 1.4 %copy-start.4 = (f32[9,128,512]{2,1,0:T(8,128)}, f32[9,128,512]{2,1,0:T(8,128)S(1)}, u32[]{:S(2)}) copy-start(f32[9,128,512]{2,1,0:T(8,128)S(1)} %shard_map.67.refs_8_) | copy-start | bytes 7077892
  59.3 10.5 %collective-permute-start.16 = (bf16[3,64,512]{2,1,0:T(8,128)(2,1)S(1)}, bf16[3,64,512]{2,1,0:T(8,128)(2,1)S(1)}, u32[]{:S(2)}, u32[]{:S(2)}) collective-permute-start(bf16[3,64,512]{2,1,0:T(8,128)(2,1)S(1)} %collective-permute-done.15.refs_6_), channel_id=1, source_target_pairs={{0,1},{1,0},{2,3},{3,2},{4,5},{5,4},{6,7},{7,6},{8,9},{9,8},{10,11... | collective-permute-start | bytes 589832 | tf_op jit(solution)/shard_map/ppermute | solution.py:36
  59.3 14.5 %collective-permute-start.12 = (bf16[3,64,512]{2,1,0:T(8,128)(2,1)S(1)}, bf16[3,64,512]{2,1,0:T(8,128)(2,1)S(1)}, u32[]{:S(2)}, u32[]{:S(2)}) collective-permute-start(bf16[3,64,512]{2,1,0:T(8,128)(2,1)S(1)} %get-tuple-element.27.refs_4_), channel_id=1, source_target_pairs={{0,2},{1,3},{2,0},{3,1},{4,6},{5,7},{6,4},{7,5},{8,10},{9,11},{10,... | collective-permute-start | bytes 589832 | tf_op jit(solution)/shard_map/ppermute | solution.py:36
  69.3 6.3 %collective-permute-start.9 = (bf16[3,64,512]{2,1,0:T(8,128)(2,1)S(1)}, bf16[3,64,512]{2,1,0:T(8,128)(2,1)S(1)}, u32[]{:S(2)}, u32[]{:S(2)}) collective-permute-start(bf16[3,64,512]{2,1,0:T(8,128)(2,1)S(1)} %get-tuple-element.26.refs_4_), channel_id=1, source_target_pairs={{0,2},{1,3},{2,0},{3,1},{4,6},{5,7},{6,4},{7,5},{8,10},{9,11},{10,... | collective-permute-start | bytes 589832 | tf_op jit(solution)/shard_map/ppermute | solution.py:36
  69.7 5.9 %collective-permute-start.11 = (bf16[3,64,512]{2,1,0:T(8,128)(2,1)S(1)}, bf16[3,64,512]{2,1,0:T(8,128)(2,1)S(1)}, u32[]{:S(2)}, u32[]{:S(2)}) collective-permute-start(bf16[3,64,512]{2,1,0:T(8,128)(2,1)S(1)} %get-tuple-element.27.refs_4_), channel_id=1, source_target_pairs={{0,1},{1,0},{2,3},{3,2},{4,5},{5,4},{6,7},{7,6},{8,9},{9,8},{10,11... | collective-permute-start | bytes 589832 | tf_op jit(solution)/shard_map/ppermute | solution.py:36
  72.4 1.4 %copy-start.3 = (f32[9,128,512]{2,1,0:T(8,128)}, f32[9,128,512]{2,1,0:T(8,128)S(1)}, u32[]{:S(2)}) copy-start(f32[9,128,512]{2,1,0:T(8,128)S(1)} %shard_map.68.refs_8_) | copy-start | bytes 7077892
  73.8 1.8 %collective-permute-start.13 = (bf16[3,64,512]{2,1,0:T(8,128)(2,1)S(1)}, bf16[3,64,512]{2,1,0:T(8,128)(2,1)S(1)}, u32[]{:S(2)}, u32[]{:S(2)}) collective-permute-start(bf16[3,64,512]{2,1,0:T(8,128)(2,1)S(1)} %collective-permute-done.12.refs_6_), channel_id=1, source_target_pairs={{0,1},{1,0},{2,3},{3,2},{4,5},{5,4},{6,7},{7,6},{8,9},{9,8},{10,11... | collective-permute-start | bytes 589832 | tf_op jit(solution)/shard_map/ppermute | solution.py:36
  74.3 3.9 %collective-permute-start.8 = (bf16[3,64,512]{2,1,0:T(8,128)(2,1)S(1)}, bf16[3,64,512]{2,1,0:T(8,128)(2,1)S(1)}, u32[]{:S(2)}, u32[]{:S(2)}) collective-permute-start(bf16[3,64,512]{2,1,0:T(8,128)(2,1)S(1)} %get-tuple-element.26.refs_4_), channel_id=1, source_target_pairs={{0,1},{1,0},{2,3},{3,2},{4,5},{5,4},{6,7},{7,6},{8,9},{9,8},{10,11... | collective-permute-start | bytes 589832 | tf_op jit(solution)/shard_map/ppermute | solution.py:36
  75.6 2.6 %collective-permute-start.10 = (bf16[3,64,512]{2,1,0:T(8,128)(2,1)S(1)}, bf16[3,64,512]{2,1,0:T(8,128)(2,1)S(1)}, u32[]{:S(2)}, u32[]{:S(2)}) collective-permute-start(bf16[3,64,512]{2,1,0:T(8,128)(2,1)S(1)} %collective-permute-done.9.refs_6_), channel_id=1, source_target_pairs={{0,1},{1,0},{2,3},{3,2},{4,5},{5,4},{6,7},{7,6},{8,9},{9,8},{10,11... | collective-permute-start | bytes 589832 | tf_op jit(solution)/shard_map/ppermute | solution.py:36
  79.3 7.9 %collective-permute-start.27 = (bf16[9,32,128]{2,1,0:T(8,128)(2,1)S(1)}, bf16[9,32,128]{2,1,0:T(8,128)(2,1)S(1)}, u32[]{:S(2)}, u32[]{:S(2)}) collective-permute-start(bf16[9,32,128]{2,1,0:T(8,128)(2,1)S(1)} %get-tuple-element.36), channel_id=1, source_target_pairs={{0,4},{1,5},{2,6},{3,7},{4,8},{5,9},{6,10},{7,11},{8,12},{9,13},{1... | collective-permute-start | bytes 221192 | tf_op jit(solution)/shard_map/ppermute | solution.py:36
  81.4 12.7 %collective-permute-start.20 = (bf16[9,4,16,256]{3,2,1,0:T(8,128)(2,1)S(1)}, bf16[9,4,16,256]{3,2,1,0:T(8,128)(2,1)S(1)}, u32[]{:S(2)}, u32[]{:S(2)}) collective-permute-start(bf16[9,4,16,256]{3,2,1,0:T(8,128)(2,1)S(1)} %slice_bitcast_fusion.1), channel_id=1, source_target_pairs={{0,16},{1,17},{2,18},{3,19},{4,20},{5,21},{6,22},{7,23},{8,24},{9,... | collective-permute-start | bytes 884744 | tf_op jit(solution)/shard_map/ppermute | solution.py:36
  87.3 6.8 %collective-permute-start.28 = (bf16[9,32,128]{2,1,0:T(8,128)(2,1)S(1)}, bf16[9,32,128]{2,1,0:T(8,128)(2,1)S(1)}, u32[]{:S(2)}, u32[]{:S(2)}) collective-permute-start(bf16[9,32,128]{2,1,0:T(8,128)(2,1)S(1)} %fusion.7), channel_id=1, source_target_pairs={{0,4},{1,5},{2,6},{3,7},{4,8},{5,9},{6,10},{7,11},{8,12},{9,13},{1... | collective-permute-start | bytes 221192 | tf_op jit(solution)/shard_map/ppermute | solution.py:36
  88.3 9.7 %collective-permute-start.30 = (bf16[9,32,128]{2,1,0:T(8,128)(2,1)S(1)}, bf16[9,32,128]{2,1,0:T(8,128)(2,1)S(1)}, u32[]{:S(2)}, u32[]{:S(2)}) collective-permute-start(bf16[9,32,128]{2,1,0:T(8,128)(2,1)S(1)} %get-tuple-element.37), channel_id=1, source_target_pairs={{0,12},{1,13},{2,14},{3,15},{4,0},{5,1},{6,2},{7,3},{8,4},{9,5},{1... | collective-permute-start | bytes 221192 | tf_op jit(solution)/shard_map/ppermute | solution.py:36
  94.1 7.2 %collective-permute-start.29 = (bf16[9,32,128]{2,1,0:T(8,128)(2,1)S(1)}, bf16[9,32,128]{2,1,0:T(8,128)(2,1)S(1)}, u32[]{:S(2)}, u32[]{:S(2)}) collective-permute-start(bf16[9,32,128]{2,1,0:T(8,128)(2,1)S(1)} %fusion.6), channel_id=1, source_target_pairs={{0,4},{1,5},{2,6},{3,7},{4,8},{5,9},{6,10},{7,11},{8,12},{9,13},{1... | collective-permute-start | bytes 221192 | tf_op jit(solution)/shard_map/ppermute | solution.py:36
  94.3 12.4 %collective-permute-start.21 = (bf16[9,16,128]{2,1,0:T(8,128)(2,1)S(1)}, bf16[9,16,128]{2,1,0:T(8,128)(2,1)S(1)}, u32[]{:S(2)}, u32[]{:S(2)}) collective-permute-start(bf16[9,16,128]{2,1,0:T(8,128)(2,1)S(1)} %get-tuple-element.40), channel_id=1, source_target_pairs={{0,4},{1,5},{2,6},{3,7},{4,8},{5,9},{6,10},{7,11},{8,12},{9,13},{1... | collective-permute-start | bytes 110600 | tf_op jit(solution)/shard_map/ppermute | solution.py:36
  101.4 6.4 %collective-permute-start.31 = (bf16[9,32,128]{2,1,0:T(8,128)(2,1)S(1)}, bf16[9,32,128]{2,1,0:T(8,128)(2,1)S(1)}, u32[]{:S(2)}, u32[]{:S(2)}) collective-permute-start(bf16[9,32,128]{2,1,0:T(8,128)(2,1)S(1)} %get-tuple-element.35), channel_id=1, source_target_pairs={{0,12},{1,13},{2,14},{3,15},{4,0},{5,1},{6,2},{7,3},{8,4},{9,5},{1... | collective-permute-start | bytes 221192 | tf_op jit(solution)/shard_map/ppermute | solution.py:36
  101.5 11.7 %collective-permute-start.24 = (bf16[9,16,128]{2,1,0:T(8,128)(2,1)S(1)}, bf16[9,16,128]{2,1,0:T(8,128)(2,1)S(1)}, u32[]{:S(2)}, u32[]{:S(2)}) collective-permute-start(bf16[9,16,128]{2,1,0:T(8,128)(2,1)S(1)} %get-tuple-element.41), channel_id=1, source_target_pairs={{0,12},{1,13},{2,14},{3,15},{4,0},{5,1},{6,2},{7,3},{8,4},{9,5},{1... | collective-permute-start | bytes 110600 | tf_op jit(solution)/shard_map/ppermute | solution.py:36
  106.7 6.2 %collective-permute-start.22 = (bf16[9,16,128]{2,1,0:T(8,128)(2,1)S(1)}, bf16[9,16,128]{2,1,0:T(8,128)(2,1)S(1)}, u32[]{:S(2)}, u32[]{:S(2)}) collective-permute-start(bf16[9,16,128]{2,1,0:T(8,128)(2,1)S(1)} %fusion.13), channel_id=1, source_target_pairs={{0,4},{1,5},{2,6},{3,7},{4,8},{5,9},{6,10},{7,11},{8,12},{9,13},{1... | collective-permute-start | bytes 110600 | tf_op jit(solution)/shard_map/ppermute | solution.py:36
  107.8 5.3 %collective-permute-start.32 = (bf16[9,32,128]{2,1,0:T(8,128)(2,1)S(1)}, bf16[9,32,128]{2,1,0:T(8,128)(2,1)S(1)}, u32[]{:S(2)}, u32[]{:S(2)}) collective-permute-start(bf16[9,32,128]{2,1,0:T(8,128)(2,1)S(1)} %fusion.3), channel_id=1, source_target_pairs={{0,12},{1,13},{2,14},{3,15},{4,0},{5,1},{6,2},{7,3},{8,4},{9,5},{1... | collective-permute-start | bytes 221192 | tf_op jit(solution)/shard_map/ppermute | solution.py:36
  112.9 6.1 %collective-permute-start.23 = (bf16[9,16,128]{2,1,0:T(8,128)(2,1)S(1)}, bf16[9,16,128]{2,1,0:T(8,128)(2,1)S(1)}, u32[]{:S(2)}, u32[]{:S(2)}) collective-permute-start(bf16[9,16,128]{2,1,0:T(8,128)(2,1)S(1)} %fusion.12), channel_id=1, source_target_pairs={{0,4},{1,5},{2,6},{3,7},{4,8},{5,9},{6,10},{7,11},{8,12},{9,13},{1... | collective-permute-start | bytes 110600 | tf_op jit(solution)/shard_map/ppermute | solution.py:36
  119.1 5.2 %collective-permute-start.25 = (bf16[9,16,128]{2,1,0:T(8,128)(2,1)S(1)}, bf16[9,16,128]{2,1,0:T(8,128)(2,1)S(1)}, u32[]{:S(2)}, u32[]{:S(2)}) collective-permute-start(bf16[9,16,128]{2,1,0:T(8,128)(2,1)S(1)} %get-tuple-element.39), channel_id=1, source_target_pairs={{0,12},{1,13},{2,14},{3,15},{4,0},{5,1},{6,2},{7,3},{8,4},{9,5},{1... | collective-permute-start | bytes 110600 | tf_op jit(solution)/shard_map/ppermute | solution.py:36
  119.2 6.5 %collective-permute-start.33 = (bf16[9,16,256]{2,1,0:T(8,128)(2,1)S(1)}, bf16[9,16,256]{2,1,0:T(8,128)(2,1)S(1)}, u32[]{:S(2)}, u32[]{:S(2)}) collective-permute-start(bf16[9,16,256]{2,1,0:T(8,128)(2,1)S(1)} %slice_bitcast_fusion.7), channel_id=1, source_target_pairs={{0,16},{1,17},{2,18},{3,19},{4,20},{5,21},{6,22},{7,23},{8,24},{9,... | collective-permute-start | bytes 221192 | tf_op jit(solution)/shard_map/ppermute | solution.py:36
  124.3 5.0 %collective-permute-start.26 = (bf16[9,16,128]{2,1,0:T(8,128)(2,1)S(1)}, bf16[9,16,128]{2,1,0:T(8,128)(2,1)S(1)}, u32[]{:S(2)}, u32[]{:S(2)}) collective-permute-start(bf16[9,16,128]{2,1,0:T(8,128)(2,1)S(1)} %fusion.9), channel_id=1, source_target_pairs={{0,12},{1,13},{2,14},{3,15},{4,0},{5,1},{6,2},{7,3},{8,4},{9,5},{1... | collective-permute-start | bytes 110600 | tf_op jit(solution)/shard_map/ppermute | solution.py:36
where the time goes:
time: 130 us
  starting transfers between devices  47.4 us (36%)
  waiting for transfers between devices  41.2 us (32%)
  Pallas kernels  31.9 us (25%)
  local copies, waits for them, and re-layouts  6.3 us (5%)
  other arithmetic  2.11 us (2%)
    ppermute x31, starting transfers between devices, send(): return lax.ppermute(block, 'az', route)  40.8 us
    ppermute x31, waiting for transfers between devices, send(): return lax.ppermute(block, 'az', route)  28.8 us
    pallas_call x4, Pallas kernels, back_step(): pl.pallas_call(lambda *refs: back_kernel(first, *refs), grid=(1,), out_sh...  13.6 us
    ppermute x3, waiting for transfers between devices, relay(): return lax.ppermute(block, 'segment', [(i, i - 1) for i in range(1, count)])  12.5 us
    pallas_call x2, Pallas kernels, slope_factors(): pl.pallas_call(factor_kernel, grid=(count,), out_shape=jax.ShapeDtypeStru...  9.35 us
    pallas_call x4, Pallas kernels, weight_step(): pl.pallas_call(lambda *refs: weight_kernel(more, last, *refs), grid=(1,),...  6.97 us
    ppermute x3, starting transfers between devices, relay(): return lax.ppermute(block, 'segment', [(i, i - 1) for i in range(1, count)])  6.55 us
    unnamed x19, local copies, waits for them, and re-layouts  6.13 us
  transfers between devices with their start and end apart: 34, of which 15 were waited for; matrix products, arithmetic and copies ran while one was open for 1% of the time, Pallas kernels for 20%

commit v1 on v0

v1 whole, which is shorter than its diff:
```python
import math

import jax
import jax.numpy as jnp
from jax import lax
from jax.experimental import pallas as pl
from jax.experimental.pallas import tpu as pltpu
from jax.sharding import PartitionSpec as P

BF = jnp.bfloat16
F32 = jnp.float32
ROWS, WIDTH, CH, STEPS = 3, 64, 512, 4
WIDE = WIDTH + 8
HALF = CH // 2


def az_route(move):
    route = []
    for i in range(32):
        h, z, c = move(i // 16, (i // 2) % 8, i % 2)
        route.append((i, (h % 2) * 16 + (z % 8) * 2 + c % 2))
    return route


RIGHT = [(i, (i + 1) % 32) for i in range(32)]
LEFT = [(i, (i - 1) % 32) for i in range(32)]
CORE = az_route(lambda h, z, c: (h, z, c + 1))
PAIR = az_route(lambda h, z, c: (h, z ^ 1, c))
FAR = az_route(lambda h, z, c: (h + 1, z, c))
UP = az_route(lambda h, z, c: (h, z + 2, c))
ACROSS = az_route(lambda h, z, c: (h, z + 4, c))
DOWN = az_route(lambda h, z, c: (h, z - 2, c))


def send(block, route):
    return lax.ppermute(block, "az", route)


def relay(block):
    count = lax.axis_size("segment")
    return lax.ppermute(block, "segment", [(i, i - 1) for i in range(1, count)])


def params(mib=24):
    return pltpu.CompilerParams(vmem_limit_bytes=mib * 1024 * 1024)


def cost(flops, size):
    return pl.CostEstimate(flops=int(flops), bytes_accessed=int(size), transcendentals=0)


VMEM = pl.BlockSpec(memory_space=pltpu.VMEM)
SMEM = pl.BlockSpec(memory_space=pltpu.SMEM)


def block(shape, *index):
    return pl.BlockSpec(shape, lambda *_: index)


def pack_kernel(x_right, p_right, t_right, x_left, p_left, t_left, right_ref, left_ref):
    for refs, first, out in (((x_right, p_right, t_right), 8, right_ref), ((x_left, p_left, t_left), 0, left_ref)):
        xs, ps, ts = refs
        for r in range(ROWS):
            planes = [xs[t, r] for t in range(STEPS)] + [ps[r]] + [ts[t, r] for t in range(STEPS - 1)]
            for n, plane in enumerate(planes):
                out[n * ROWS + r] = plane.astype(F32)[first : first + 8].astype(BF)


def pack_edges(x, pending, top):
    def specs(edge):
        return [
            block((STEPS, ROWS, 16, CH), 0, 0, edge, 0),
            block((ROWS, 16, CH), 0, edge, 0),
            block((STEPS - 1, ROWS, 16, CH), 0, 0, edge, 0),
        ]

    x, pending, top = (pltpu.with_memory_space_constraint(v, pltpu.HBM) for v in (x, pending, top))
    shape = jax.ShapeDtypeStruct((24, 8, CH), BF)
    return pl.pallas_call(
        pack_kernel,
        grid=(1,),
        out_shape=(shape, shape),
        in_specs=specs(3) + specs(0),
        out_specs=(block((24, 8, CH), 0, 0, 0),) * 2,
        compiler_params=params(),
        cost_estimate=cost(0, 1 << 20),
    )(x, pending, top, x, pending, top)


def first_four(high, low):
    pick = lax.broadcasted_iota(jnp.int32, high.shape, 0) < 4
    return jnp.where(pick, high, low)


def widen(own, high, low):
    return jnp.concatenate([own.astype(F32), first_four(high.astype(F32), low.astype(F32))], axis=0)


def factor_kernel(x_ref, low_ref, high_ref, w_ref, out_ref):
    wide = WIDTH + 16
    planes = [
        jnp.concatenate(
            [x_ref[0, r].astype(F32), high_ref[r].astype(F32), low_ref[r].astype(F32)], axis=0
        )
        for r in range(ROWS)
    ]
    field = jnp.concatenate(planes, axis=0).astype(BF)
    sums = []
    for b in range(3):
        up = jnp.dot(field[: 2 * wide], w_ref[b], preferred_element_type=F32)
        mid = jnp.dot(field, w_ref[3 + b], preferred_element_type=F32)
        down = jnp.dot(field[wide:], w_ref[6 + b], preferred_element_type=F32)
        rows = []
        for r in range(ROWS):
            value = mid[r * wide : (r + 1) * wide]
            if r > 0:
                value = value + up[(r - 1) * wide : r * wide]
            if r < 2:
                value = value + down[r * wide : (r + 1) * wide]
            rows.append(value)
        sums.append(rows)
    for r in range(ROWS):
        preact = pltpu.roll(sums[0][r], 1, 0) + sums[1][r] + pltpu.roll(sums[2][r], wide - 1, 0)
        gate = jax.nn.sigmoid(preact)
        value = gate * (1.0 + preact * (1.0 - gate))
        out_ref[0, r, :WIDTH] = value[:WIDTH]
        out_ref[0, r, WIDTH:] = first_four(value[WIDTH : WIDTH + 8], value[WIDTH + 8 :])


def slope_factors(x, low, high, weights, first):
    return pl.pallas_call(
        factor_kernel,
        grid=(1,),
        out_shape=jax.ShapeDtypeStruct((1, ROWS, WIDE, CH), F32),
        in_specs=[
            pl.BlockSpec((1, ROWS, WIDTH, CH), lambda n: (first + n, 0, 0, 0)),
            pl.BlockSpec((ROWS, 8, CH), lambda n: (first + n, 0, 0)),
            pl.BlockSpec((ROWS, 8, CH), lambda n: (first + n, 0, 0)),
            VMEM,
        ],
        out_specs=pl.BlockSpec((1, ROWS, WIDE, CH), lambda n: (n, 0, 0, 0)),
        compiler_params=params(),
        cost_estimate=cost(1.2e9, 5e6),
    )(x, low, high, weights)


def back_kernel(first, *refs):
    if first:
        own_ref, low_ref, high_ref, factor_ref, w_ref, sent_ref, grad_ref = refs
    else:
        flag_ref, own_ref, low_ref, high_ref, relay_ref, factor_ref, w_ref, sent_ref, grad_ref = refs
    slopes = []
    for r in range(ROWS):
        own = own_ref[r] if first else own_ref[0, r]
        slope = widen(own, high_ref[r], low_ref[r])
        if not first:
            slope = jnp.where(flag_ref[0] == 1, slope, relay_ref[r].astype(F32))
        slopes.append(slope)
    grads = []
    for r in range(ROWS):
        grad = slopes[r] * factor_ref[0, r]
        grad_ref[r] = grad.astype(BF)
        grads.append(grad)
    field = jnp.concatenate(grads, axis=0).astype(BF)
    above = jnp.concatenate(grads[1:], axis=0).astype(BF)
    below = jnp.concatenate(grads[:2], axis=0).astype(BF)
    turned = (((1,), (1,)), ((), ()))
    sums = []
    for b in range(3):
        up = lax.dot_general(above, w_ref[b], turned, preferred_element_type=F32)
        mid = lax.dot_general(field, w_ref[3 + b], turned, preferred_element_type=F32)
        down = lax.dot_general(below, w_ref[6 + b], turned, preferred_element_type=F32)
        rows = []
        for r in range(ROWS):
            value = mid[r * WIDE : (r + 1) * WIDE]
            if r < 2:
                value = value + up[r * WIDE : (r + 1) * WIDE]
            if r > 0:
                value = value + down[(r - 1) * WIDE : r * WIDE]
            rows.append(value)
        sums.append(rows)
    for r in range(ROWS):
        value = pltpu.roll(sums[0][r], WIDE - 1, 0) + sums[1][r] + pltpu.roll(sums[2][r], 1, 0)
        sent_ref[r] = (slopes[r] + value).astype(BF)


def back_step(own, low, high, factors, weights, t, flag=None, arrived=None):
    first = t == 0
    edge = block((ROWS, 8, CH), 4 + t, 0, 0)
    operands = [own, low, high]
    if first:
        specs = [block((ROWS, WIDTH, CH), 0, 0, 0), edge, edge]
    else:
        specs = [SMEM, block((1, ROWS, WIDTH, CH), t - 1, 0, 0, 0), edge, edge]
        specs += [block((ROWS, WIDE, CH), 0, 0, 0)]
        operands = [flag, *operands, arrived]
    specs += [block((1, ROWS, WIDE, CH), 0, 0, 0, 0), VMEM]
    return pl.pallas_call(
        lambda *refs: back_kernel(first, *refs),
        grid=(1,),
        out_shape=(
            jax.ShapeDtypeStruct((ROWS, WIDE, CH), BF),
            jax.ShapeDtypeStruct((ROWS, WIDE, CH), BF),
        ),
        in_specs=specs,
        out_specs=(block((ROWS, WIDE, CH), 0, 0, 0), block((ROWS, WIDE, CH), 0, 0, 0)),
        compiler_params=params(),
        cost_estimate=cost(1.1e9, 6e6),
    )(*operands, factors, weights)


def spread_kernel(place_ref, x_ref, out0, out1, order_ref):
    @pl.when(pl.program_id(0) == 0)
    def _():
        h, j, k, c = (place_ref[n] for n in range(4))
        lane = lax.broadcasted_iota(jnp.int32, (8, CH), 1)
        chip = jnp.bitwise_xor(lane // HALF, k)
        core = jnp.bitwise_xor(lane // 128 % 2, c)
        far = jnp.bitwise_xor(lane // 64 % 2, h)
        turn = jnp.bitwise_and(lane // 16 + j, 3)
        source = ((far * 4 + turn) * 4 + chip * 2 + core) * 16 + lane % 16
        row = lax.broadcasted_iota(jnp.int32, (CH, CH), 0)
        order_ref[...] = jnp.where(row == source[:1], 1.0, 0.0).astype(BF)

    field = jnp.concatenate([x_ref[0, r] for r in range(ROWS)], axis=0)
    value = jnp.dot(field, order_ref[...], preferred_element_type=F32)
    for n, out in enumerate((out0, out1)):
        for r in range(ROWS):
            out[0, r] = value[r * WIDTH : (r + 1) * WIDTH, n * HALF : (n + 1) * HALF].astype(BF)


def spread(place, x):
    shape = jax.ShapeDtypeStruct((STEPS, ROWS, WIDTH, HALF), BF)
    return pl.pallas_call(
        spread_kernel,
        grid=(STEPS,),
        out_shape=(shape,) * 2,
        in_specs=[
            SMEM,
            pl.BlockSpec((1, ROWS, WIDTH, CH), lambda n: (n, 0, 0, 0)),
        ],
        out_specs=(pl.BlockSpec((1, ROWS, WIDTH, HALF), lambda n: (n, 0, 0, 0)),) * 2,
        scratch_shapes=[pltpu.VMEM((CH, CH), BF)],
        compiler_params=params(),
        cost_estimate=cost(4.5e8, 2e6),
    )(place, x)


def tap_products(xs, gs):
    left, right = [], []
    for r in range(ROWS):
        left.append(jnp.concatenate([x[r] for x in xs], axis=0))
        taps = [[], [], []]
        for g in gs:
            plane = g[r].astype(F32)
            for b, shift in enumerate((WIDE - 1, 0, 1)):
                moved = pltpu.roll(plane, shift, 0) if shift else plane
                taps[b].append(moved[:WIDTH])
        right.append(
            jnp.concatenate([jnp.concatenate(parts, axis=0).astype(BF) for parts in taps], axis=1)
        )
    pairs = ((left[:2], right[1:]), (left, right), (left[1:], right[:2]))
    return [
        lax.dot_general(
            jnp.concatenate(ls, axis=0),
            jnp.concatenate(rs, axis=0),
            (((0,), (0,)), ((), ())),
            preferred_element_type=F32,
        )
        for ls, rs in pairs
    ]


def early_kernel(x0, x1, *refs):
    gs, out_ref = refs[:6], refs[6]
    for t in range(STEPS - 1):
        values = tap_products((x0[t], x1[t]), (gs[2 * t], gs[2 * t + 1]))
        for a, value in enumerate(values):
            out_ref[a] = value if t == 0 else out_ref[a] + value


def early_products(xs, gs):
    return pl.pallas_call(
        early_kernel,
        out_shape=jax.ShapeDtypeStruct((3, HALF, 3 * CH), F32),
        in_specs=[VMEM] * 8,
        out_specs=VMEM,
        compiler_params=params(),
        cost_estimate=cost(3e9, 8e6),
    )(*xs, *gs)


def late_kernel(x0, x1, g0, g1, total_ref, mine_ref, other_ref):
    for a, value in enumerate(tap_products((x0[0], x1[0]), (g0, g1))):
        value = value + total_ref[a]
        for b in range(3):
            for n, out in enumerate((mine_ref, other_ref)):
                for far in range(2):
                    for turn in range(4):
                        at = ((n * 2 + far) * 4 + turn) * 16
                        out[far, turn, a * 3 + b] = value[at : at + 16, b * CH : (b + 1) * CH].astype(BF)


def late_products(xs, gs, total):
    shape = jax.ShapeDtypeStruct((2, 4, 9, 16, CH), BF)
    whole = block((2, 4, 9, 16, CH), 0, 0, 0, 0, 0)
    return pl.pallas_call(
        late_kernel,
        grid=(1,),
        out_shape=(shape, shape),
        in_specs=[block((1, ROWS, WIDTH, HALF), STEPS - 1, 0, 0, 0)] * 2
        + [block((ROWS, WIDE, CH), 0, 0, 0)] * 2
        + [block((3, HALF, 3 * CH), 0, 0, 0)],
        out_specs=(whole, whole),
        compiler_params=params(),
        cost_estimate=cost(1e9, 8e6),
    )(*xs, *gs, total)


def grad_kernel(flag_ref, own_ref, low_ref, high_ref, relay_ref, factor_ref, grad_ref):
    for r in range(ROWS):
        slope = widen(own_ref[0, r], high_ref[r], low_ref[r])
        slope = jnp.where(flag_ref[0] == 1, slope, relay_ref[r].astype(F32))
        grad_ref[r] = (slope * factor_ref[0, r]).astype(BF)


def last_grad(flag, top, low, high, arrived, factors):
    edge = block((ROWS, 8, CH), 3 + STEPS, 0, 0)
    return pl.pallas_call(
        grad_kernel,
        grid=(1,),
        out_shape=jax.ShapeDtypeStruct((ROWS, WIDE, CH), BF),
        in_specs=[
            SMEM,
            block((1, ROWS, WIDTH, CH), STEPS - 2, 0, 0, 0),
            edge,
            edge,
            block((ROWS, WIDE, CH), 0, 0, 0),
            block((1, ROWS, WIDE, CH), 0, 0, 0, 0),
        ],
        out_specs=block((ROWS, WIDE, CH), 0, 0, 0),
        compiler_params=params(),
        cost_estimate=cost(1e6, 1e6),
    )(flag, top, low, high, arrived, factors)


def load_kernel(source_ref, out_ref, done):
    copy = pltpu.make_async_copy(source_ref, out_ref, done)
    copy.start()
    copy.wait()


def load(weights):
    return pl.pallas_call(
        load_kernel,
        out_shape=pltpu.VMEM(weights.shape, BF),
        in_specs=[pl.BlockSpec(memory_space=pltpu.HBM)],
        out_specs=VMEM,
        scratch_shapes=[pltpu.SemaphoreType.DMA],
        compiler_params=params(),
        cost_estimate=cost(0, 9e6),
    )(weights)


def total_of(*parts):
    value = parts[0].astype(F32)
    for part in parts[1:]:
        value = value + part.astype(F32)
    return value


def after(value, *others):
    return lax.optimization_barrier((value, *others))[0]


def body(stored_inputs, filter_weights, pending_slopes, topmost_slopes):
    x = stored_inputs[:, 0]
    pending = pending_slopes[0]
    top = topmost_slopes
    az = lax.axis_index("az")
    place = jnp.stack([az // 16, (az // 4) % 4, (az // 2) % 2, az % 2]).astype(jnp.int32)
    last = lax.axis_index("segment") == lax.axis_size("segment") - 1
    flag = last.astype(jnp.int32).reshape(1)
    scale = 1.0 / math.sqrt(STEPS * ROWS * WIDTH * lax.axis_size("az"))

    right_edge, left_edge = pack_edges(x, pending, top)
    low = send(right_edge, RIGHT)
    high = send(left_edge, LEFT)
    weights = load(after(filter_weights[0].reshape(9, CH, CH), right_edge))
    mine, other = spread(after(place, left_edge), x)
    xs = (mine, send(other, PAIR))

    emitted, fields = [], []
    slope, arrived = pending, None
    weights = pltpu.with_memory_space_constraint(weights, pltpu.VMEM)
    factors = slope_factors(after(x, mine), low, high, weights, 0)
    for t in range(STEPS):
        if t == STEPS - 1:
            own = last_grad(flag, top, low, high, arrived, factors)
            arrived, factors = lax.optimization_barrier((arrived, factors, own))[:2]
        sent, grad = back_step(slope, low, high, factors, weights, t, flag, arrived)
        emitted.append(sent[:, :WIDTH])
        slope = top
        if t < STEPS - 1:
            own = grad
            arrived = relay(sent)
            factors = slope_factors(after(x, sent), low, high, weights, t + 1)
            own = after(own, factors)
        fields.append((own, send(own, PAIR)))

    total = early_products(xs, [g for pair in fields[:-1] for g in pair])
    mine, other = late_products(xs, fields[-1], total)
    other = send(other, CORE)
    near = [total_of(mine[n], other[n]).astype(BF) for n in range(2)]
    near = total_of(near[0], send(near[1], FAR)).astype(BF)
    ups, across, downs = send(near[1], UP), send(near[2], ACROSS), send(near[3], DOWN)
    weight_grads = (total_of(near[0], ups, across, downs) * scale).astype(BF).reshape(1, 3, 3, 16, CH)
    return (jnp.stack(emitted)[:, None], weight_grads)


def solution(mesh):
    return jax.shard_map(
        body,
        mesh=mesh,
        in_specs=(
            P(None, "segment", None, "az", None),
            P("segment", None, None, None, None),
            P("segment", None, "az", None),
            P(None, None, "az", None),
        ),
        out_specs=(P(None, "segment", None, "az", None), P("segment", None, None, "az", None)),
        check_vma=False,
    )
```

time: 130 us -> 104 us (0.80)
  the two profiles are of different devices: /device:TPU:6 before, /device:TPU:24 now
where the time goes in v1:
time: 104 us; the launch traced here: 103 us
  waiting for transfers between devices  38.9 us (37%)
  starting transfers between devices  36 us (35%)
  Pallas kernels  18.5 us (18%)
  local copies, waits for them, and re-layouts  6.9 us (7%)
  other arithmetic  2.34 us (2%)
    ppermute x12, waiting for transfers between devices, send(): return lax.ppermute(block, 'az', route)  37.3 us
    ppermute x12, starting transfers between devices, send(): return lax.ppermute(block, 'az', route)  20.2 us
    ppermute x3, starting transfers between devices, relay(): return lax.ppermute(block, 'segment', [(i, i - 1) for i in range(1, count)])  15.8 us
    unnamed x14, local copies, waits for them, and re-layouts  6.81 us
    pallas_call x4, Pallas kernels, back_step(): pl.pallas_call(lambda *refs: back_kernel(first, *refs), grid=(1,), out_sh...  6.65 us
    pallas_call x4, Pallas kernels, slope_factors(): pl.pallas_call(factor_kernel, grid=(1,), out_shape=jax.ShapeDtypeStruct((...  4.49 us
    pallas_call x1, Pallas kernels, early_products(): pl.pallas_call(early_kernel, out_shape=jax.ShapeDtypeStruct((3, HALF, 3 *...  2.74 us
  transfers between devices with their start and end apart: 15, of which 9 were waited for; matrix products, arithmetic and copies ran while one was open for 1% of the time, Pallas kernels for 11%

profile of v1, /device:TPU:24, one launch (start us, length us, event | category | flops | bytes accessed | tf_op | source)
XLA Modules:
  0.0 103.4 jit_solution(3127465421923176341)
XLA Ops:
  0.6 1.3 %shard_map.59 = (bf16[24,8,512]{2,1,0:T(8,128)(2,1)S(1)}, bf16[24,8,512]{2,1,0:T(8,128)(2,1)S(1)}) custom-call(bf16[4,3,64,512]{3,2,1,0:T(8,128)(2,1)} %bitcast.39, bf16[3,64,512]{2,1,0:T(8,128)(2,1)} %bitcast.47, bf16[3,3,64,512]{3,2,1,0:T(8,128)(2,1)} %refs_1_.5, bf16[4,3,64,512]{3,2,1,0:T(8,128)(2,1)} %bitcast.40, bf16[3,64,512]{2,1,0:T(8,128)(2,1)} %bitcast.48, ...), custom_call_target="tpu_custom_call" | custom-call | bytes 1048576 | tf_op jit(solution)/shard_map/pallas_call | solution.py:79
  2.0 0.1 collective-permute-start
  2.1 6.0 %collective-permute-start.1 = (bf16[24,8,512]{2,1,0:T(8,128)(2,1)S(1)}, bf16[24,8,512]{2,1,0:T(8,128)(2,1)S(1)}, u32[]{:S(2)}, u32[]{:S(2)}) collective-permute-start(bf16[24,8,512]{2,1,0:T(8,128)(2,1)S(1)} %get-tuple-element.27), channel_id=1, source_target_pairs={{0,31},{1,0},{2,1},{3,2},{4,3},{5,4},{6,5},{7,6},{8,7},{9,8},{10,9... | collective-permute-start | bytes 589832 | tf_op jit(solution)/shard_map/ppermute | solution.py:36
  8.1 0.1 pad_add_fusion.place_ref
  8.2 1.8 %shard_map.60 = (bf16[4,3,64,256]{3,2,1,0:T(8,128)(2,1)S(1)}, bf16[4,3,64,256]{3,2,1,0:T(8,128)(2,1)S(1)}) custom-call(s32[4]{0:T(128)S(1)} %pad_add_fusion.place_ref, bf16[4,3,64,512]{3,2,1,0:T(8,128)(2,1)S(1)} %bitcast.41), custom_call_target="tpu_custom_call" | custom-call | flops 450000000 | bytes 2000000 | tf_op jit(solution)/shard_map/pallas_call | solution.py:234
  10.0 2.3 %copy-done.5 = bf16[1,3,3,512,512]{4,3,2,1,0:T(8,128)(2,1)S(1)} copy-done((bf16[1,3,3,512,512]{4,3,2,1,0:T(8,128)(2,1)S(1)}, bf16[1,3,3,512,512]{4,3,2,1,0:T(8,128)(2,1)}, u32[]{:S(2)}) %copy-start.5) | copy-done | bytes 4718616
  12.3 0.3 shard_map.61.w_ref.refs_4_.refs_6_
  12.7 1.1 %shard_map.62.refs_3_ = f32[1,3,72,512]{3,2,1,0:T(8,128)S(1)} custom-call(bf16[4,3,64,512]{3,2,1,0:T(8,128)(2,1)S(1)} %bitcast.42, bf16[24,8,512]{2,1,0:T(8,128)(2,1)S(1)} %collective-permute-done.low_ref.refs_1_.refs_2_, bf16[24,8,512]{2,1,0:T(8,128)(2,1)S(1)} %collective-permute-done.1.high_ref.refs_2_.refs_3_, ...), custom_call_target="tpu_custom_call" | custom-call | flops 1200000000 | bytes 5000000 | tf_op jit(solution)/shard_map/pallas_call | solution.py:131
  13.8 1.0 copy-done
  14.8 1.7 %shard_map.63 = (bf16[3,72,512]{2,1,0:T(8,128)(2,1)S(1)}, bf16[3,72,512]{2,1,0:T(8,128)(2,1)S(1)}) custom-call(bf16[3,64,512]{2,1,0:T(8,128)(2,1)S(1)} %bitcast.49, bf16[24,8,512]{2,1,0:T(8,128)(2,1)S(1)} %collective-permute-done.low_ref.refs_1_.refs_2_, bf16[24,8,512]{2,1,0:T(8,128)(2,1)S(1)} %collective-permute-done.1.high_ref.refs_2_.refs_3_, ...), custom_call_target="tpu_custom_call" | custom-call | flops 1100000000 | bytes 6000000 | tf_op jit(solution)/shard_map/pallas_call | solution.py:198
  16.5 4.1 %collective-permute-start.2 = (bf16[3,72,512]{2,1,0:T(8,128)(2,1)S(1)}, bf16[3,72,512]{2,1,0:T(8,128)(2,1)S(1)}, u32[]{:S(2)}, u32[]{:S(2)}) collective-permute-start(bf16[3,72,512]{2,1,0:T(8,128)(2,1)S(1)} %get-tuple-element.32), channel_id=1, source_target_pairs={{32,0},{64,32},{96,64},{128,96},{160,128},{192,160},{224,192},{33,... | collective-permute-start | bytes 663560 | tf_op jit(solution)/shard_map/ppermute | solution.py:41
  20.6 2.3 %copy-done.1 = bf16[9,512,512]{2,1,0:T(8,128)(2,1)S(1)} copy-done((bf16[9,512,512]{2,1,0:T(8,128)(2,1)S(1)}, bf16[9,512,512]{2,1,0:T(8,128)(2,1)}, u32[]{:S(2)}) %copy-start.1) | copy-done | bytes 4718616
  23.0 1.1 %shard_map.64.refs_5_ = f32[1,3,72,512]{3,2,1,0:T(8,128)S(1)} custom-call(bf16[4,3,64,512]{3,2,1,0:T(8,128)(2,1)S(1)} %bitcast.43, bf16[24,8,512]{2,1,0:T(8,128)(2,1)S(1)} %collective-permute-done.low_ref.refs_1_.refs_2_, bf16[24,8,512]{2,1,0:T(8,128)(2,1)S(1)} %collective-permute-done.1.high_ref.refs_2_.refs_3_, bf16[9,512,512]{2,1,0:T(8,128)(2,1)S(1)} %copy-done.1), custom_call_target="tpu_custom_call" | custom-call | flops 1200000000 | bytes 5000000 | tf_op jit(solution)/shard_map/pallas_call | solution.py:131
  24.1 0.2 collective-permute-done.2.refs_4_
  24.3 1.0 copy-done.2
  25.3 0.1 copy-done.4
  25.4 1.7 %shard_map.65 = (bf16[3,72,512]{2,1,0:T(8,128)(2,1)S(1)}, bf16[3,72,512]{2,1,0:T(8,128)(2,1)S(1)}) custom-call(s32[1]{0:T(128)} %bitcast.8.refs_0_.flag_ref, bf16[3,3,64,512]{3,2,1,0:T(8,128)(2,1)S(1)} %copy-done.4, bf16[24,8,512]{2,1,0:T(8,128)(2,1)S(1)} %collective-permute-done.low_ref.refs_1_.refs_2_, ...), custom_call_target="tpu_custom_call" | custom-call | flops 1100000000 | bytes 6000000 | tf_op jit(solution)/shard_map/pallas_call | solution.py:198
  27.1 5.1 %collective-permute-start.3 = (bf16[3,72,512]{2,1,0:T(8,128)(2,1)S(1)}, bf16[3,72,512]{2,1,0:T(8,128)(2,1)S(1)}, u32[]{:S(2)}, u32[]{:S(2)}) collective-permute-start(bf16[3,72,512]{2,1,0:T(8,128)(2,1)S(1)} %get-tuple-element.34), channel_id=1, source_target_pairs={{32,0},{64,32},{96,64},{128,96},{160,128},{192,160},{224,192},{33,... | collective-permute-start | bytes 663560 | tf_op jit(solution)/shard_map/ppermute | solution.py:41
  32.2 0.1 collective-permute-start.5
  32.3 2.0 %collective-permute-start.7 = (bf16[3,72,512]{2,1,0:T(8,128)(2,1)S(1)}, bf16[3,72,512]{2,1,0:T(8,128)(2,1)S(1)}, u32[]{:S(2)}, u32[]{:S(2)}) collective-permute-start(bf16[3,72,512]{2,1,0:T(8,128)(2,1)S(1)} %get-tuple-element.43.refs_0_), channel_id=1, source_target_pairs={{0,2},{1,3},{2,0},{3,1},{4,6},{5,7},{6,4},{7,5},{8,10},{9,11},{10,... | collective-permute-start | bytes 663560 | tf_op jit(solution)/shard_map/ppermute | solution.py:36
  34.3 1.1 %shard_map.66.refs_5_ = f32[1,3,72,512]{3,2,1,0:T(8,128)S(1)} custom-call(bf16[4,3,64,512]{3,2,1,0:T(8,128)(2,1)S(1)} %bitcast.44, bf16[24,8,512]{2,1,0:T(8,128)(2,1)S(1)} %collective-permute-done.low_ref.refs_1_.refs_2_, bf16[24,8,512]{2,1,0:T(8,128)(2,1)S(1)} %collective-permute-done.1.high_ref.refs_2_.refs_3_, bf16[9,512,512]{2,1,0:T(8,128)(2,1)S(1)} %copy-done.2), custom_call_target="tpu_custom_call" | custom-call | flops 1200000000 | bytes 5000000 | tf_op jit(solution)/shard_map/pallas_call | solution.py:131
  35.5 0.2 collective-permute-start.8
  35.7 1.7 %shard_map.67 = (bf16[3,72,512]{2,1,0:T(8,128)(2,1)S(1)}, bf16[3,72,512]{2,1,0:T(8,128)(2,1)S(1)}) custom-call(s32[1]{0:T(128)} %bitcast.8.refs_0_.flag_ref, bf16[3,3,64,512]{3,2,1,0:T(8,128)(2,1)S(1)} %copy-done.4, bf16[24,8,512]{2,1,0:T(8,128)(2,1)S(1)} %collective-permute-done.low_ref.refs_1_.refs_2_, ...), custom_call_target="tpu_custom_call" | custom-call | flops 1100000000 | bytes 6000000 | tf_op jit(solution)/shard_map/pallas_call | solution.py:198
  37.3 6.5 %collective-permute-start.4 = (bf16[3,72,512]{2,1,0:T(8,128)(2,1)S(1)}, bf16[3,72,512]{2,1,0:T(8,128)(2,1)S(1)}, u32[]{:S(2)}, u32[]{:S(2)}) collective-permute-start(bf16[3,72,512]{2,1,0:T(8,128)(2,1)S(1)} %get-tuple-element.36), channel_id=1, source_target_pairs={{32,0},{64,32},{96,64},{128,96},{160,128},{192,160},{224,192},{33,... | collective-permute-start | bytes 663560 | tf_op jit(solution)/shard_map/ppermute | solution.py:41
  43.8 1.1 %shard_map.68.factor_ref.refs_5_ = f32[1,3,72,512]{3,2,1,0:T(8,128)S(1)} custom-call(bf16[4,3,64,512]{3,2,1,0:T(8,128)(2,1)S(1)} %bitcast.45, bf16[24,8,512]{2,1,0:T(8,128)(2,1)S(1)} %collective-permute-done.low_ref.refs_1_.refs_2_, bf16[24,8,512]{2,1,0:T(8,128)(2,1)S(1)} %collective-permute-done.1.high_ref.refs_2_.refs_3_, bf16[9,512,512]{2,1,0:T(8,128)(2,1)S(1)} %copy-done.2), custom_call_target="tpu_custom_call" | custom-call | flops 1200000000 | bytes 5000000 | tf_op jit(solution)/shard_map/pallas_call | solution.py:131
  45.0 1.0 collective-permute-start.9
  45.9 1.3 %collective-permute-done.4.relay_ref.refs_4_ = bf16[3,72,512]{2,1,0:T(8,128)(2,1)S(1)} collective-permute-done((bf16[3,72,512]{2,1,0:T(8,128)(2,1)S(1)}, bf16[3,72,512]{2,1,0:T(8,128)(2,1)S(1)}, u32[]{:S(2)}, u32[]{:S(2)}) %collective-permute-start.4) | collective-permute-done | bytes 221216 | tf_op jit(solution)/shard_map/ppermute | solution.py:41
  47.3 0.1 shard_map.69.g0
  47.4 1.1 %collective-permute-start.6 = (bf16[3,72,512]{2,1,0:T(8,128)(2,1)S(1)}, bf16[3,72,512]{2,1,0:T(8,128)(2,1)S(1)}, u32[]{:S(2)}, u32[]{:S(2)}) collective-permute-start(bf16[3,72,512]{2,1,0:T(8,128)(2,1)S(1)} %shard_map.69.g0), channel_id=1, source_target_pairs={{0,2},{1,3},{2,0},{3,1},{4,6},{5,7},{6,4},{7,5},{8,10},{9,11},{10,... | collective-permute-start | bytes 663560 | tf_op jit(solution)/shard_map/ppermute | solution.py:36
  48.5 0.6 collective-permute-done.7.refs_1_
  49.1 4.7 %collective-permute-done.8.refs_3_ = bf16[3,72,512]{2,1,0:T(8,128)(2,1)S(1)} collective-permute-done((bf16[3,72,512]{2,1,0:T(8,128)(2,1)S(1)}, bf16[3,72,512]{2,1,0:T(8,128)(2,1)S(1)}, u32[]{:S(2)}, u32[]{:S(2)}) %collective-permute-start.8) | collective-permute-done | bytes 221216 | tf_op jit(solution)/shard_map/ppermute | solution.py:36
  53.8 3.5 %collective-permute-done.9.refs_5_ = bf16[3,72,512]{2,1,0:T(8,128)(2,1)S(1)} collective-permute-done((bf16[3,72,512]{2,1,0:T(8,128)(2,1)S(1)}, bf16[3,72,512]{2,1,0:T(8,128)(2,1)S(1)}, u32[]{:S(2)}, u32[]{:S(2)}) %collective-permute-start.9) | collective-permute-done | bytes 221216 | tf_op jit(solution)/shard_map/ppermute | solution.py:36
  57.4 2.7 %shard_map.71.total_ref = f32[3,256,1536]{2,1,0:T(8,128)S(1)} custom-call(bf16[4,3,64,256]{3,2,1,0:T(8,128)(2,1)S(1)} %get-tuple-element.29.x0, bf16[4,3,64,256]{3,2,1,0:T(8,128)(2,1)S(1)} %collective-permute-done.5.x1, bf16[3,72,512]{2,1,0:T(8,128)(2,1)S(1)} %get-tuple-element.43.refs_0_, bf16[3,72,512]{2,1,0:T(8,128)(2,1)S(1)} %collective-permute-done.7.refs_1_, ...), custom_call_target="tpu_custom_call" | custom-call | flops 3000000000 | bytes 8000000 | tf_op jit(solution)/shard_map/pallas_call | solution.py:283
  60.1 1.1 %shard_map.72 = (bf16[2,4,9,16,512]{4,3,2,1,0:T(8,128)(2,1)S(1)}, bf16[2,4,9,16,512]{4,3,2,1,0:T(8,128)(2,1)S(1)}) custom-call(bf16[4,3,64,256]{3,2,1,0:T(8,128)(2,1)S(1)} %get-tuple-element.29.x0, bf16[4,3,64,256]{3,2,1,0:T(8,128)(2,1)S(1)} %collective-permute-done.5.x1, bf16[3,72,512]{2,1,0:T(8,128)(2,1)S(1)} %shard_map.69.g0, ...), custom_call_target="tpu_custom_call" | custom-call | flops 1000000000 | bytes 8000000 | tf_op jit(solution)/shard_map/pallas_call | solution.py:307
  61.2 0.1 collective-permute-start.10
  61.3 2.8 %collective-permute-done.10 = bf16[2,4,9,16,512]{4,3,2,1,0:T(8,128)(2,1)S(1)} collective-permute-done((bf16[2,4,9,16,512]{4,3,2,1,0:T(8,128)(2,1)S(1)}, bf16[2,4,9,16,512]{4,3,2,1,0:T(8,128)(2,1)S(1)}, u32[]{:S(2)}, u32[]{:S(2)}) %collective-permute-start.10) | collective-permute-done | bytes 1179680 | tf_op jit(solution)/shard_map/ppermute | solution.py:36
  64.1 0.2 fusion.2
  64.4 1.0 collective-permute-start.11
  65.5 1.7 %shard_map.70 = (bf16[3,72,512]{2,1,0:T(8,128)(2,1)S(1)}, bf16[3,72,512]{2,1,0:T(8,128)(2,1)}) custom-call(s32[1]{0:T(128)} %bitcast.8.refs_0_.flag_ref, bf16[3,3,64,512]{3,2,1,0:T(8,128)(2,1)S(1)} %copy-done.4, bf16[24,8,512]{2,1,0:T(8,128)(2,1)S(1)} %collective-permute-done.low_ref.refs_1_.refs_2_, ...), custom_call_target="tpu_custom_call" | custom-call | flops 1100000000 | bytes 6000000 | tf_op jit(solution)/shard_map/pallas_call | solution.py:198
  67.1 14.2 %collective-permute-done.11 = bf16[4,9,16,512]{3,2,1,0:T(8,128)(2,1)S(1)} collective-permute-done((bf16[4,9,16,512]{3,2,1,0:T(8,128)(2,1)S(1)}, bf16[4,9,16,512]{3,2,1,0:T(8,128)(2,1)S(1)}, u32[]{:S(2)}, u32[]{:S(2)}) %collective-permute-start.11) | collective-permute-done | bytes 589856 | tf_op jit(solution)/shard_map/ppermute | solution.py:36
  81.3 0.3 fusion
  81.7 4.0 %collective-permute-start.12 = (bf16[9,16,512]{2,1,0:T(8,128)(2,1)S(1)}, bf16[9,16,512]{2,1,0:T(8,128)(2,1)S(1)}, u32[]{:S(2)}, u32[]{:S(2)}) collective-permute-start(bf16[9,16,512]{2,1,0:T(8,128)(2,1)S(1)} %get-tuple-element.52), channel_id=1, source_target_pairs={{0,4},{1,5},{2,6},{3,7},{4,8},{5,9},{6,10},{7,11},{8,12},{9,13},{1... | collective-permute-start | bytes 442376 | tf_op jit(solution)/shard_map/ppermute | solution.py:36
  85.6 2.2 %collective-permute-start.14 = (bf16[9,16,512]{2,1,0:T(8,128)(2,1)S(1)}, bf16[9,16,512]{2,1,0:T(8,128)(2,1)S(1)}, u32[]{:S(2)}, u32[]{:S(2)}) collective-permute-start(bf16[9,16,512]{2,1,0:T(8,128)(2,1)S(1)} %get-tuple-element.53), channel_id=1, source_target_pairs={{0,12},{1,13},{2,14},{3,15},{4,0},{5,1},{6,2},{7,3},{8,4},{9,5},{1... | collective-permute-start | bytes 442376 | tf_op jit(solution)/shard_map/ppermute | solution.py:36
  87.9 2.4 %collective-permute-start.13 = (bf16[9,16,512]{2,1,0:T(8,128)(2,1)S(1)}, bf16[9,16,512]{2,1,0:T(8,128)(2,1)S(1)}, u32[]{:S(2)}, u32[]{:S(2)}) collective-permute-start(bf16[9,16,512]{2,1,0:T(8,128)(2,1)S(1)} %get-tuple-element.54), channel_id=1, source_target_pairs={{0,8},{1,9},{2,10},{3,11},{4,12},{5,13},{6,14},{7,15},{8,0},{9,1},... | collective-permute-start | bytes 442376 | tf_op jit(solution)/shard_map/ppermute | solution.py:36
  90.3 1.0 maximum_bitcast_fusion
  91.3 2.0 %collective-permute-done.14 = bf16[9,16,512]{2,1,0:T(8,128)(2,1)S(1)} collective-permute-done((bf16[9,16,512]{2,1,0:T(8,128)(2,1)S(1)}, bf16[9,16,512]{2,1,0:T(8,128)(2,1)S(1)}, u32[]{:S(2)}, u32[]{:S(2)}) %collective-permute-start.14) | collective-permute-done | bytes 147488 | tf_op jit(solution)/shard_map/ppermute | solution.py:36
  93.3 9.4 %collective-permute-done.13 = bf16[9,16,512]{2,1,0:T(8,128)(2,1)S(1)} collective-permute-done((bf16[9,16,512]{2,1,0:T(8,128)(2,1)S(1)}, bf16[9,16,512]{2,1,0:T(8,128)(2,1)S(1)}, u32[]{:S(2)}, u32[]{:S(2)}) %collective-permute-start.13) | collective-permute-done | bytes 147488 | tf_op jit(solution)/shard_map/ppermute | solution.py:36
  102.7 0.8 fusion.6
  (20 shorter events, 0.1 us)
Async XLA Ops:
  0.6 7.5 %copy-start.3 = (bf16[4,1,3,64,512]{4,3,2,1,0:T(8,128)(2,1)S(1)}, bf16[4,1,3,64,512]{4,3,2,1,0:T(8,128)(2,1)}, u32[]{:S(2)}) copy-start(bf16[4,1,3,64,512]{4,3,2,1,0:T(8,128)(2,1)} %param.4) | copy-start | bytes 2359300
  2.0 10.7 %collective-permute-start = (bf16[24,8,512]{2,1,0:T(8,128)(2,1)S(1)}, bf16[24,8,512]{2,1,0:T(8,128)(2,1)S(1)}, u32[]{:S(2)}, u32[]{:S(2)}) collective-permute-start(bf16[24,8,512]{2,1,0:T(8,128)(2,1)S(1)} %get-tuple-element.26), channel_id=1, source_target_pairs={{0,1},{1,2},{2,3},{3,4},{4,5},{5,6},{6,7},{7,8},{8,9},{9,10},{10,1... | collective-permute-start | bytes 589832 | tf_op jit(solution)/shard_map/ppermute | solution.py:36
  2.1 10.6 %collective-permute-start.1 = (bf16[24,8,512]{2,1,0:T(8,128)(2,1)S(1)}, bf16[24,8,512]{2,1,0:T(8,128)(2,1)S(1)}, u32[]{:S(2)}, u32[]{:S(2)}) collective-permute-start(bf16[24,8,512]{2,1,0:T(8,128)(2,1)S(1)} %get-tuple-element.27), channel_id=1, source_target_pairs={{0,31},{1,0},{2,1},{3,2},{4,3},{5,4},{6,5},{7,6},{8,7},{9,8},{10,9... | collective-permute-start | bytes 589832 | tf_op jit(solution)/shard_map/ppermute | solution.py:36
  10.0 2.3 %copy-start.5 = (bf16[1,3,3,512,512]{4,3,2,1,0:T(8,128)(2,1)S(1)}, bf16[1,3,3,512,512]{4,3,2,1,0:T(8,128)(2,1)}, u32[]{:S(2)}) copy-start(bf16[1,3,3,512,512]{4,3,2,1,0:T(8,128)(2,1)} %param.5) | copy-start | bytes 14155780
  12.6 2.1 %copy-start = (bf16[9,512,512]{2,1,0:T(8,128)(2,1)}, bf16[9,512,512]{2,1,0:T(8,128)(2,1)S(1)}, u32[]{:S(2)}) copy-start(bf16[9,512,512]{2,1,0:T(8,128)(2,1)S(1)} %shard_map.61.w_ref.refs_4_.refs_6_) | copy-start | bytes 14155780
  12.7 2.1 %copy-start.6 = (bf16[1,3,64,512]{3,2,1,0:T(8,128)(2,1)S(1)}, bf16[1,3,64,512]{3,2,1,0:T(8,128)(2,1)}, u32[]{:S(2)}) copy-start(bf16[1,3,64,512]{3,2,1,0:T(8,128)(2,1)} %param.6) | copy-start | bytes 589828
  16.5 7.8 %collective-permute-start.2 = (bf16[3,72,512]{2,1,0:T(8,128)(2,1)S(1)}, bf16[3,72,512]{2,1,0:T(8,128)(2,1)S(1)}, u32[]{:S(2)}, u32[]{:S(2)}) collective-permute-start(bf16[3,72,512]{2,1,0:T(8,128)(2,1)S(1)} %get-tuple-element.32), channel_id=1, source_target_pairs={{32,0},{64,32},{96,64},{128,96},{160,128},{192,160},{224,192},{33,... | collective-permute-start | bytes 663560 | tf_op jit(solution)/shard_map/ppermute | solution.py:41
  20.6 2.3 %copy-start.1 = (bf16[9,512,512]{2,1,0:T(8,128)(2,1)S(1)}, bf16[9,512,512]{2,1,0:T(8,128)(2,1)}, u32[]{:S(2)}) copy-start(bf16[9,512,512]{2,1,0:T(8,128)(2,1)} %copy-done) | copy-start | bytes 14155780
  23.0 2.3 %copy-start.2 = (bf16[9,512,512]{2,1,0:T(8,128)(2,1)S(1)}, bf16[9,512,512]{2,1,0:T(8,128)(2,1)}, u32[]{:S(2)}) copy-start(bf16[9,512,512]{2,1,0:T(8,128)(2,1)} %copy-done) | copy-start | bytes 14155780
  23.0 2.5 %copy-start.4 = (bf16[3,3,64,512]{3,2,1,0:T(8,128)(2,1)S(1)}, bf16[3,3,64,512]{3,2,1,0:T(8,128)(2,1)}, u32[]{:S(2)}) copy-start(bf16[3,3,64,512]{3,2,1,0:T(8,128)(2,1)} %refs_1_.5) | copy-start | bytes 1769476
  27.1 8.6 %collective-permute-start.3 = (bf16[3,72,512]{2,1,0:T(8,128)(2,1)S(1)}, bf16[3,72,512]{2,1,0:T(8,128)(2,1)S(1)}, u32[]{:S(2)}, u32[]{:S(2)}) collective-permute-start(bf16[3,72,512]{2,1,0:T(8,128)(2,1)S(1)} %get-tuple-element.34), channel_id=1, source_target_pairs={{32,0},{64,32},{96,64},{128,96},{160,128},{192,160},{224,192},{33,... | collective-permute-start | bytes 663560 | tf_op jit(solution)/shard_map/ppermute | solution.py:41
  32.2 16.3 %collective-permute-start.5 = (bf16[4,3,64,256]{3,2,1,0:T(8,128)(2,1)S(1)}, bf16[4,3,64,256]{3,2,1,0:T(8,128)(2,1)S(1)}, u32[]{:S(2)}, u32[]{:S(2)}) collective-permute-start(bf16[4,3,64,256]{3,2,1,0:T(8,128)(2,1)S(1)} %get-tuple-element.41), channel_id=1, source_target_pairs={{0,2},{1,3},{2,0},{3,1},{4,6},{5,7},{6,4},{7,5},{8,10},{9,11},{10,... | collective-permute-start | bytes 1179656 | tf_op jit(solution)/shard_map/ppermute | solution.py:36
  32.3 16.8 %collective-permute-start.7 = (bf16[3,72,512]{2,1,0:T(8,128)(2,1)S(1)}, bf16[3,72,512]{2,1,0:T(8,128)(2,1)S(1)}, u32[]{:S(2)}, u32[]{:S(2)}) collective-permute-start(bf16[3,72,512]{2,1,0:T(8,128)(2,1)S(1)} %get-tuple-element.43.refs_0_), channel_id=1, source_target_pairs={{0,2},{1,3},{2,0},{3,1},{4,6},{5,7},{6,4},{7,5},{8,10},{9,11},{10,... | collective-permute-start | bytes 663560 | tf_op jit(solution)/shard_map/ppermute | solution.py:36
  35.5 18.4 %collective-permute-start.8 = (bf16[3,72,512]{2,1,0:T(8,128)(2,1)S(1)}, bf16[3,72,512]{2,1,0:T(8,128)(2,1)S(1)}, u32[]{:S(2)}, u32[]{:S(2)}) collective-permute-start(bf16[3,72,512]{2,1,0:T(8,128)(2,1)S(1)} %get-tuple-element.45.refs_2_), channel_id=1, source_target_pairs={{0,2},{1,3},{2,0},{3,1},{4,6},{5,7},{6,4},{7,5},{8,10},{9,11},{10,... | collective-permute-start | bytes 663560 | tf_op jit(solution)/shard_map/ppermute | solution.py:36
  37.3 9.9 %collective-permute-start.4 = (bf16[3,72,512]{2,1,0:T(8,128)(2,1)S(1)}, bf16[3,72,512]{2,1,0:T(8,128)(2,1)S(1)}, u32[]{:S(2)}, u32[]{:S(2)}) collective-permute-start(bf16[3,72,512]{2,1,0:T(8,128)(2,1)S(1)} %get-tuple-element.36), channel_id=1, source_target_pairs={{32,0},{64,32},{96,64},{128,96},{160,128},{192,160},{224,192},{33,... | collective-permute-start | bytes 663560 | tf_op jit(solution)/shard_map/ppermute | solution.py:41
  45.0 12.4 %collective-permute-start.9 = (bf16[3,72,512]{2,1,0:T(8,128)(2,1)S(1)}, bf16[3,72,512]{2,1,0:T(8,128)(2,1)S(1)}, u32[]{:S(2)}, u32[]{:S(2)}) collective-permute-start(bf16[3,72,512]{2,1,0:T(8,128)(2,1)S(1)} %get-tuple-element.47.refs_4_), channel_id=1, source_target_pairs={{0,2},{1,3},{2,0},{3,1},{4,6},{5,7},{6,4},{7,5},{8,10},{9,11},{10,... | collective-permute-start | bytes 663560 | tf_op jit(solution)/shard_map/ppermute | solution.py:36
  47.4 12.8 %collective-permute-start.6 = (bf16[3,72,512]{2,1,0:T(8,128)(2,1)S(1)}, bf16[3,72,512]{2,1,0:T(8,128)(2,1)S(1)}, u32[]{:S(2)}, u32[]{:S(2)}) collective-permute-start(bf16[3,72,512]{2,1,0:T(8,128)(2,1)S(1)} %shard_map.69.g0), channel_id=1, source_target_pairs={{0,2},{1,3},{2,0},{3,1},{4,6},{5,7},{6,4},{7,5},{8,10},{9,11},{10,... | collective-permute-start | bytes 663560 | tf_op jit(solution)/shard_map/ppermute | solution.py:36
  61.2 2.9 %collective-permute-start.10 = (bf16[2,4,9,16,512]{4,3,2,1,0:T(8,128)(2,1)S(1)}, bf16[2,4,9,16,512]{4,3,2,1,0:T(8,128)(2,1)S(1)}, u32[]{:S(2)}, u32[]{:S(2)}) collective-permute-start(bf16[2,4,9,16,512]{4,3,2,1,0:T(8,128)(2,1)S(1)} %get-tuple-element.49), channel_id=1, source_target_pairs={{0,1},{1,0},{2,3},{3,2},{4,5},{5,4},{6,7},{7,6},{8,9},{9,8},{10,11... | collective-permute-start | bytes 3538952 | tf_op jit(solution)/shard_map/ppermute | solution.py:36
  64.4 17.0 %collective-permute-start.11 = (bf16[4,9,16,512]{3,2,1,0:T(8,128)(2,1)S(1)}, bf16[4,9,16,512]{3,2,1,0:T(8,128)(2,1)S(1)}, u32[]{:S(2)}, u32[]{:S(2)}) collective-permute-start(bf16[4,9,16,512]{3,2,1,0:T(8,128)(2,1)S(1)} %fusion.2), channel_id=1, source_target_pairs={{0,16},{1,17},{2,18},{3,19},{4,20},{5,21},{6,22},{7,23},{8,24},{9,... | collective-permute-start | bytes 1769480 | tf_op jit(solution)/shard_map/ppermute | solution.py:36
  81.7 9.6 %collective-permute-start.12 = (bf16[9,16,512]{2,1,0:T(8,128)(2,1)S(1)}, bf16[9,16,512]{2,1,0:T(8,128)(2,1)S(1)}, u32[]{:S(2)}, u32[]{:S(2)}) collective-permute-start(bf16[9,16,512]{2,1,0:T(8,128)(2,1)S(1)} %get-tuple-element.52), channel_id=1, source_target_pairs={{0,4},{1,5},{2,6},{3,7},{4,8},{5,9},{6,10},{7,11},{8,12},{9,13},{1... | collective-permute-start | bytes 442376 | tf_op jit(solution)/shard_map/ppermute | solution.py:36
  85.6 7.6 %collective-permute-start.14 = (bf16[9,16,512]{2,1,0:T(8,128)(2,1)S(1)}, bf16[9,16,512]{2,1,0:T(8,128)(2,1)S(1)}, u32[]{:S(2)}, u32[]{:S(2)}) collective-permute-start(bf16[9,16,512]{2,1,0:T(8,128)(2,1)S(1)} %get-tuple-element.53), channel_id=1, source_target_pairs={{0,12},{1,13},{2,14},{3,15},{4,0},{5,1},{6,2},{7,3},{8,4},{9,5},{1... | collective-permute-start | bytes 442376 | tf_op jit(solution)/shard_map/ppermute | solution.py:36
  87.9 14.8 %collective-permute-start.13 = (bf16[9,16,512]{2,1,0:T(8,128)(2,1)S(1)}, bf16[9,16,512]{2,1,0:T(8,128)(2,1)S(1)}, u32[]{:S(2)}, u32[]{:S(2)}) collective-permute-start(bf16[9,16,512]{2,1,0:T(8,128)(2,1)S(1)} %get-tuple-element.54), channel_id=1, source_target_pairs={{0,8},{1,9},{2,10},{3,11},{4,12},{5,13},{6,14},{7,15},{8,0},{9,1},... | collective-permute-start | bytes 442376 | tf_op jit(solution)/shard_map/ppermute | solution.py:36

commit v2 on v1

--- a/solution.py
+++ b/solution.py
@@ -128,6 +128,7 @@
 
 
 def slope_factors(x, low, high, weights, first):
+    weights = pltpu.with_memory_space_constraint(weights, pltpu.VMEM)
     return pl.pallas_call(
         factor_kernel,
         grid=(1,),
@@ -186,6 +187,7 @@
 
 def back_step(own, low, high, factors, weights, t, flag=None, arrived=None):
     first = t == 0
+    weights = pltpu.with_memory_space_constraint(weights, pltpu.VMEM)
     edge = block((ROWS, 8, CH), 4 + t, 0, 0)
     operands = [own, low, high]
     if first:
@@ -209,41 +211,40 @@
     )(*operands, factors, weights)
 
 
-def spread_kernel(place_ref, x_ref, out0, out1, order_ref):
-    @pl.when(pl.program_id(0) == 0)
-    def _():
-        h, j, k, c = (place_ref[n] for n in range(4))
-        lane = lax.broadcasted_iota(jnp.int32, (8, CH), 1)
-        chip = jnp.bitwise_xor(lane // HALF, k)
-        core = jnp.bitwise_xor(lane // 128 % 2, c)
-        far = jnp.bitwise_xor(lane // 64 % 2, h)
-        turn = jnp.bitwise_and(lane // 16 + j, 3)
-        source = ((far * 4 + turn) * 4 + chip * 2 + core) * 16 + lane % 16
-        row = lax.broadcasted_iota(jnp.int32, (CH, CH), 0)
-        order_ref[...] = jnp.where(row == source[:1], 1.0, 0.0).astype(BF)
-
-    field = jnp.concatenate([x_ref[0, r] for r in range(ROWS)], axis=0)
-    value = jnp.dot(field, order_ref[...], preferred_element_type=F32)
+def spread_kernel(place_ref, x_ref, source_ref, out0, out1, w_ref, done):
+    copy = pltpu.make_async_copy(source_ref, w_ref, done)
+    copy.start()
+    h, j, k, c = (place_ref[n] for n in range(4))
+    lane = lax.broadcasted_iota(jnp.int32, (8, CH), 1)
+    chip = jnp.bitwise_xor(lane // HALF, k)
+    core = jnp.bitwise_xor(lane // 128 % 2, c)
+    far = jnp.bitwise_xor(lane // 64 % 2, h)
+    turn = jnp.bitwise_and(lane // 16 + j, 3)
+    source = ((far * 4 + turn) * 4 + chip * 2 + core) * 16 + lane % 16
+    row = lax.broadcasted_iota(jnp.int32, (CH, CH), 0)
+    order = jnp.where(row == source[:1], 1.0, 0.0).astype(BF)
+    field = jnp.concatenate([x_ref[t, r] for t in range(STEPS) for r in range(ROWS)], axis=0)
+    value = jnp.dot(field, order, preferred_element_type=F32).astype(BF)
     for n, out in enumerate((out0, out1)):
-        for r in range(ROWS):
-            out[0, r] = value[r * WIDTH : (r + 1) * WIDTH, n * HALF : (n + 1) * HALF].astype(BF)
-
-
-def spread(place, x):
+        for t in range(STEPS):
+            for r in range(ROWS):
+                at = (t * ROWS + r) * WIDTH
+                out[t, r] = value[at : at + WIDTH, n * HALF : (n + 1) * HALF]
+    copy.wait()
+
+
+def spread(place, x, weights):
+    weights = pltpu.with_memory_space_constraint(weights, pltpu.HBM)
     shape = jax.ShapeDtypeStruct((STEPS, ROWS, WIDTH, HALF), BF)
     return pl.pallas_call(
         spread_kernel,
-        grid=(STEPS,),
-        out_shape=(shape,) * 2,
-        in_specs=[
-            SMEM,
-            pl.BlockSpec((1, ROWS, WIDTH, CH), lambda n: (n, 0, 0, 0)),
-        ],
-        out_specs=(pl.BlockSpec((1, ROWS, WIDTH, HALF), lambda n: (n, 0, 0, 0)),) * 2,
-        scratch_shapes=[pltpu.VMEM((CH, CH), BF)],
-        compiler_params=params(),
-        cost_estimate=cost(4.5e8, 2e6),
-    )(place, x)
+        out_shape=(shape, shape, pltpu.VMEM(weights.shape, BF)),
+        in_specs=[SMEM, VMEM, pl.BlockSpec(memory_space=pltpu.HBM)],
+        out_specs=(VMEM, VMEM, VMEM),
+        scratch_shapes=[pltpu.SemaphoreType.DMA],
+        compiler_params=params(),
+        cost_estimate=cost(4.5e8, 1.2e7),
+    )(place, x, weights)
 
 
 def tap_products(xs, gs):
@@ -271,47 +272,48 @@
     ]
 
 
-def early_kernel(x0, x1, *refs):
-    gs, out_ref = refs[:6], refs[6]
+def early_kernel(x0, x1, both0, both1, third0, third1, out_ref):
     for t in range(STEPS - 1):
-        values = tap_products((x0[t], x1[t]), (gs[2 * t], gs[2 * t + 1]))
+        gs = (both0[t], both1[t]) if t < 2 else (third0, third1)
+        values = tap_products((x0[t], x1[t]), gs)
         for a, value in enumerate(values):
             out_ref[a] = value if t == 0 else out_ref[a] + value
 
 
-def early_products(xs, gs):
+def early_products(xs, *gs):
     return pl.pallas_call(
         early_kernel,
         out_shape=jax.ShapeDtypeStruct((3, HALF, 3 * CH), F32),
-        in_specs=[VMEM] * 8,
+        in_specs=[VMEM] * 6,
         out_specs=VMEM,
         compiler_params=params(),
         cost_estimate=cost(3e9, 8e6),
     )(*xs, *gs)
 
 
-def late_kernel(x0, x1, g0, g1, total_ref, mine_ref, other_ref):
+def late_kernel(x0, x1, g0, g1, total_ref, *outs):
     for a, value in enumerate(tap_products((x0[0], x1[0]), (g0, g1))):
         value = value + total_ref[a]
         for b in range(3):
-            for n, out in enumerate((mine_ref, other_ref)):
+            for n, out in enumerate(outs):
+                core, lanes = n // 2, b * CH + n % 2 * HALF
                 for far in range(2):
                     for turn in range(4):
-                        at = ((n * 2 + far) * 4 + turn) * 16
-                        out[far, turn, a * 3 + b] = value[at : at + 16, b * CH : (b + 1) * CH].astype(BF)
+                        at = ((core * 2 + far) * 4 + turn) * 16
+                        out[far, turn, a * 3 + b] = value[at : at + 16, lanes : lanes + HALF].astype(BF)
 
 
 def late_products(xs, gs, total):
-    shape = jax.ShapeDtypeStruct((2, 4, 9, 16, CH), BF)
-    whole = block((2, 4, 9, 16, CH), 0, 0, 0, 0, 0)
+    shape = jax.ShapeDtypeStruct((2, 4, 9, 16, HALF), BF)
+    whole = block((2, 4, 9, 16, HALF), 0, 0, 0, 0, 0)
     return pl.pallas_call(
         late_kernel,
         grid=(1,),
-        out_shape=(shape, shape),
+        out_shape=(shape,) * 4,
         in_specs=[block((1, ROWS, WIDTH, HALF), STEPS - 1, 0, 0, 0)] * 2
         + [block((ROWS, WIDE, CH), 0, 0, 0)] * 2
         + [block((3, HALF, 3 * CH), 0, 0, 0)],
-        out_specs=(whole, whole),
+        out_specs=(whole,) * 4,
         compiler_params=params(),
         cost_estimate=cost(1e9, 8e6),
     )(*xs, *gs, total)
@@ -344,24 +346,6 @@
     )(flag, top, low, high, arrived, factors)
 
 
-def load_kernel(source_ref, out_ref, done):
-    copy = pltpu.make_async_copy(source_ref, out_ref, done)
-    copy.start()
-    copy.wait()
-
-
-def load(weights):
-    return pl.pallas_call(
-        load_kernel,
-        out_shape=pltpu.VMEM(weights.shape, BF),
-        in_specs=[pl.BlockSpec(memory_space=pltpu.HBM)],
-        out_specs=VMEM,
-        scratch_shapes=[pltpu.SemaphoreType.DMA],
-        compiler_params=params(),
-        cost_estimate=cost(0, 9e6),
-    )(weights)
-
-
 def total_of(*parts):
     value = parts[0].astype(F32)
     for part in parts[1:]:
@@ -386,35 +370,45 @@
     right_edge, left_edge = pack_edges(x, pending, top)
     low = send(right_edge, RIGHT)
     high = send(left_edge, LEFT)
-    weights = load(after(filter_weights[0].reshape(9, CH, CH), right_edge))
-    mine, other = spread(after(place, left_edge), x)
+    taps = filter_weights[0].reshape(9, CH, CH)
+    mine, other, weights = spread(after(place, left_edge), x, taps)
     xs = (mine, send(other, PAIR))
 
     emitted, fields = [], []
     slope, arrived = pending, None
     weights = pltpu.with_memory_space_constraint(weights, pltpu.VMEM)
-    factors = slope_factors(after(x, mine), low, high, weights, 0)
+    factors = slope_factors(x, low, high, weights, 0)
     for t in range(STEPS):
         if t == STEPS - 1:
             own = last_grad(flag, top, low, high, arrived, factors)
-            arrived, factors = lax.optimization_barrier((arrived, factors, own))[:2]
-        sent, grad = back_step(slope, low, high, factors, weights, t, flag, arrived)
-        emitted.append(sent[:, :WIDTH])
-        slope = top
-        if t < STEPS - 1:
+        else:
+            sent, grad = back_step(slope, low, high, factors, weights, t, flag, arrived)
+            emitted.append(sent[:, :WIDTH])
+            slope, weights = top, taps
             own = grad
             arrived = relay(sent)
-            factors = slope_factors(after(x, sent), low, high, weights, t + 1)
+            waits = (sent, *xs) if t == 1 else (sent,)
+            factors = slope_factors(after(x, *waits), low, high, weights, t + 1)
             own = after(own, factors)
-        fields.append((own, send(own, PAIR)))
-
-    total = early_products(xs, [g for pair in fields[:-1] for g in pair])
-    mine, other = late_products(xs, fields[-1], total)
-    other = send(other, CORE)
-    near = [total_of(mine[n], other[n]).astype(BF) for n in range(2)]
-    near = total_of(near[0], send(near[1], FAR)).astype(BF)
-    ups, across, downs = send(near[1], UP), send(near[2], ACROSS), send(near[3], DOWN)
-    weight_grads = (total_of(near[0], ups, across, downs) * scale).astype(BF).reshape(1, 3, 3, 16, CH)
+            if t == 1:
+                own = jnp.stack([fields[0], own])
+                fields = []
+        fields.append(own if t == 0 else (own, send(own, PAIR)))
+
+    total = early_products(xs, *fields[0], *fields[1])
+    parts = late_products(xs, fields[-1], total)
+    sums = []
+    for n in range(2):
+        mine, other = parts[n], send(parts[2 + n], CORE)
+        near = [total_of(mine[m], other[m]).astype(BF) for m in range(2)]
+        if n == 1:
+            arrived = after(arrived, near[1])
+        near = total_of(near[0], send(near[1], FAR)).astype(BF)
+        across, ups, downs = send(near[2], ACROSS), send(near[1], UP), send(near[3], DOWN)
+        sums.append(total_of(near[0], ups, across, downs))
+    sent, _ = back_step(top, low, high, factors, taps, STEPS - 1, flag, arrived)
+    emitted.append(sent[:, :WIDTH])
+    weight_grads = (jnp.concatenate(sums, axis=-1) * scale).astype(BF).reshape(1, 3, 3, 16, CH)
     return (jnp.stack(emitted)[:, None], weight_grads)
 
 

time: 104 us -> 93.5 us (0.90)
  the two profiles are of different devices: /device:TPU:24 before, /device:TPU:6 now
where the time goes in v2:
time: 93.5 us; the launch traced here: 92.7 us
  starting transfers between devices  40.2 us (43%)
  waiting for transfers between devices  25.8 us (28%)
  Pallas kernels  19.9 us (21%)
  local copies, waits for them, and re-layouts  3.58 us (4%)
  other arithmetic  2.28 us (2%)
  between operations  0.94 us (1%)
    ppermute x16, starting transfers between devices, send(): return lax.ppermute(block, 'az', route)  33.6 us
    ppermute x3, waiting for transfers between devices, relay(): return lax.ppermute(block, 'segment', [(i, i - 1) for i in range(1, count)])  13.2 us
    ppermute x16, waiting for transfers between devices, send(): return lax.ppermute(block, 'az', route)  12.5 us
    pallas_call x4, Pallas kernels, back_step(): pl.pallas_call(lambda *refs: back_kernel(first, *refs), grid=(1,), out_sh...  6.66 us
    ppermute x3, starting transfers between devices, relay(): return lax.ppermute(block, 'segment', [(i, i - 1) for i in range(1, count)])  6.57 us
    pallas_call x4, Pallas kernels, slope_factors(): pl.pallas_call(factor_kernel, grid=(1,), out_shape=jax.ShapeDtypeStruct((...  4.5 us
    pallas_call x1, Pallas kernels, spread(): pl.pallas_call(spread_kernel, out_shape=(shape, shape, pltpu.VMEM(weights...  3.63 us
    unnamed x12, local copies, waits for them, and re-layouts  3.49 us
  transfers between devices with their start and end apart: 19, of which 9 were waited for; matrix products, arithmetic and copies ran while one was open for 2% of the time, Pallas kernels for 19%

profile of v2, /device:TPU:6, one launch (start us, length us, event | category | flops | bytes accessed | tf_op | source)
XLA Modules:
  0.0 92.7 jit_solution(15282146579333619960)
XLA Ops:
  0.6 1.3 %shard_map.59 = (bf16[24,8,512]{2,1,0:T(8,128)(2,1)S(1)}, bf16[24,8,512]{2,1,0:T(8,128)(2,1)S(1)}) custom-call(bf16[4,3,64,512]{3,2,1,0:T(8,128)(2,1)} %bitcast.67, bf16[3,64,512]{2,1,0:T(8,128)(2,1)} %bitcast.74, bf16[3,3,64,512]{3,2,1,0:T(8,128)(2,1)} %refs_1_.5, bf16[4,3,64,512]{3,2,1,0:T(8,128)(2,1)} %bitcast.68, bf16[3,64,512]{2,1,0:T(8,128)(2,1)} %bitcast.75, ...), custom_call_target="tpu_custom_call" | custom-call | bytes 1048576 | tf_op jit(solution)/shard_map/pallas_call | solution.py:79
  1.9 0.1 collective-permute-start
  2.0 8.0 %collective-permute-start.1 = (bf16[24,8,512]{2,1,0:T(8,128)(2,1)S(1)}, bf16[24,8,512]{2,1,0:T(8,128)(2,1)S(1)}, u32[]{:S(2)}, u32[]{:S(2)}) collective-permute-start(bf16[24,8,512]{2,1,0:T(8,128)(2,1)S(1)} %get-tuple-element.27), channel_id=1, source_target_pairs={{0,31},{1,0},{2,1},{3,2},{4,3},{5,4},{6,5},{7,6},{8,7},{9,8},{10,9... | collective-permute-start | bytes 589832 | tf_op jit(solution)/shard_map/ppermute | solution.py:36
  10.1 1.1 %copy-done.2 = bf16[4,1,3,64,512]{4,3,2,1,0:T(8,128)(2,1)S(1)} copy-done((bf16[4,1,3,64,512]{4,3,2,1,0:T(8,128)(2,1)S(1)}, bf16[4,1,3,64,512]{4,3,2,1,0:T(8,128)(2,1)}, u32[]{:S(2)}) %copy-start.2) | copy-done | bytes 786456
  11.2 3.6 %shard_map.60 = (bf16[4,3,64,256]{3,2,1,0:T(8,128)(2,1)S(1)}, bf16[4,3,64,256]{3,2,1,0:T(8,128)(2,1)}, bf16[9,512,512]{2,1,0:T(8,128)(2,1)S(1)}) custom-call(s32[4]{0:T(128)S(1)} %pad_add_fusion.place_ref, bf16[4,3,64,512]{3,2,1,0:T(8,128)(2,1)S(1)} %bitcast.69, bf16[9,512,512]{2,1,0:T(8,128)(2,1)} %bitcast.60), custom_call_target="tpu_custom_call" | custom-call | flops 450000000 | bytes 12000000 | tf_op jit(solution)/shard_map/pallas_call | solution.py:239
  14.9 0.1 collective-permute-start.4
  15.0 1.1 %shard_map.61.refs_3_ = f32[1,3,72,512]{3,2,1,0:T(8,128)S(1)} custom-call(bf16[4,3,64,512]{3,2,1,0:T(8,128)(2,1)S(1)} %bitcast.70, bf16[24,8,512]{2,1,0:T(8,128)(2,1)S(1)} %collective-permute-done.low_ref.refs_1_.refs_2_, bf16[24,8,512]{2,1,0:T(8,128)(2,1)S(1)} %collective-permute-done.1.high_ref.refs_2_.refs_3_, ...), custom_call_target="tpu_custom_call" | custom-call | flops 1200000000 | bytes 5000000 | tf_op jit(solution)/shard_map/pallas_call | solution.py:132
  16.1 1.7 %shard_map.62 = (bf16[3,72,512]{2,1,0:T(8,128)(2,1)S(1)}, bf16[3,72,512]{2,1,0:T(8,128)(2,1)S(1)}) custom-call(bf16[3,64,512]{2,1,0:T(8,128)(2,1)S(1)} %bitcast.76, bf16[24,8,512]{2,1,0:T(8,128)(2,1)S(1)} %collective-permute-done.low_ref.refs_1_.refs_2_, bf16[24,8,512]{2,1,0:T(8,128)(2,1)S(1)} %collective-permute-done.1.high_ref.refs_2_.refs_3_, ...), custom_call_target="tpu_custom_call" | custom-call | flops 1100000000 | bytes 6000000 | tf_op jit(solution)/shard_map/pallas_call | solution.py:200
  17.8 2.7 %collective-permute-start.2 = (bf16[3,72,512]{2,1,0:T(8,128)(2,1)S(1)}, bf16[3,72,512]{2,1,0:T(8,128)(2,1)S(1)}, u32[]{:S(2)}, u32[]{:S(2)}) collective-permute-start(bf16[3,72,512]{2,1,0:T(8,128)(2,1)S(1)} %get-tuple-element.30), channel_id=1, source_target_pairs={{32,0},{64,32},{96,64},{128,96},{160,128},{192,160},{224,192},{33,... | collective-permute-start | bytes 663560 | tf_op jit(solution)/shard_map/ppermute | solution.py:41
  20.6 2.3 %copy-done = bf16[1,3,3,512,512]{4,3,2,1,0:T(8,128)(2,1)S(1)} copy-done((bf16[1,3,3,512,512]{4,3,2,1,0:T(8,128)(2,1)S(1)}, bf16[1,3,3,512,512]{4,3,2,1,0:T(8,128)(2,1)}, u32[]{:S(2)}) %copy-start) | copy-done | bytes 4718616
  22.9 1.1 %shard_map.63.refs_5_ = f32[1,3,72,512]{3,2,1,0:T(8,128)S(1)} custom-call(bf16[4,3,64,512]{3,2,1,0:T(8,128)(2,1)S(1)} %bitcast.71, bf16[24,8,512]{2,1,0:T(8,128)(2,1)S(1)} %collective-permute-done.low_ref.refs_1_.refs_2_, bf16[24,8,512]{2,1,0:T(8,128)(2,1)S(1)} %collective-permute-done.1.high_ref.refs_2_.refs_3_, bf16[9,512,512]{2,1,0:T(8,128)(2,1)S(1)} %bitcast.61), custom_call_target="tpu_custom_call" | custom-call | flops 1200000000 | bytes 5000000 | tf_op jit(solution)/shard_map/pallas_call | solution.py:132
  24.0 3.7 %collective-permute-done.2.refs_4_ = bf16[3,72,512]{2,1,0:T(8,128)(2,1)S(1)} collective-permute-done((bf16[3,72,512]{2,1,0:T(8,128)(2,1)S(1)}, bf16[3,72,512]{2,1,0:T(8,128)(2,1)S(1)}, u32[]{:S(2)}, u32[]{:S(2)}) %collective-permute-start.2) | collective-permute-done | bytes 221216 | tf_op jit(solution)/shard_map/ppermute | solution.py:41
  27.8 1.7 %shard_map.64 = (bf16[3,72,512]{2,1,0:T(8,128)(2,1)S(1)}, bf16[3,72,512]{2,1,0:T(8,128)(2,1)S(1)}) custom-call(s32[1]{0:T(128)} %bitcast.8.refs_0_.flag_ref, bf16[3,3,64,512]{3,2,1,0:T(8,128)(2,1)S(1)} %copy-done.4, bf16[24,8,512]{2,1,0:T(8,128)(2,1)S(1)} %collective-permute-done.low_ref.refs_1_.refs_2_, ...), custom_call_target="tpu_custom_call" | custom-call | flops 1100000000 | bytes 6000000 | tf_op jit(solution)/shard_map/pallas_call | solution.py:200
  29.4 1.9 %collective-permute-start.3 = (bf16[3,72,512]{2,1,0:T(8,128)(2,1)S(1)}, bf16[3,72,512]{2,1,0:T(8,128)(2,1)S(1)}, u32[]{:S(2)}, u32[]{:S(2)}) collective-permute-start(bf16[3,72,512]{2,1,0:T(8,128)(2,1)S(1)} %get-tuple-element.32), channel_id=1, source_target_pairs={{32,0},{64,32},{96,64},{128,96},{160,128},{192,160},{224,192},{33,... | collective-permute-start | bytes 663560 | tf_op jit(solution)/shard_map/ppermute | solution.py:41
  31.4 1.1 %shard_map.65.refs_5_ = f32[1,3,72,512]{3,2,1,0:T(8,128)S(1)} custom-call(bf16[4,3,64,512]{3,2,1,0:T(8,128)(2,1)S(1)} %bitcast.72, bf16[24,8,512]{2,1,0:T(8,128)(2,1)S(1)} %collective-permute-done.low_ref.refs_1_.refs_2_, bf16[24,8,512]{2,1,0:T(8,128)(2,1)S(1)} %collective-permute-done.1.high_ref.refs_2_.refs_3_, bf16[9,512,512]{2,1,0:T(8,128)(2,1)S(1)} %bitcast.63), custom_call_target="tpu_custom_call" | custom-call | flops 1200000000 | bytes 5000000 | tf_op jit(solution)/shard_map/pallas_call | solution.py:132
  32.5 2.1 %collective-permute-start.7 = (bf16[2,3,72,512]{3,2,1,0:T(8,128)(2,1)S(1)}, bf16[2,3,72,512]{3,2,1,0:T(8,128)(2,1)S(1)}, u32[]{:S(2)}, u32[]{:S(2)}) collective-permute-start(bf16[2,3,72,512]{3,2,1,0:T(8,128)(2,1)S(1)} %pad_maximum_fusion.both0), channel_id=1, source_target_pairs={{0,2},{1,3},{2,0},{3,1},{4,6},{5,7},{6,4},{7,5},{8,10},{9,11},{10,... | collective-permute-start | bytes 1327112 | tf_op jit(solution)/shard_map/ppermute | solution.py:36
  34.6 4.7 %collective-permute-done.3.refs_4_ = bf16[3,72,512]{2,1,0:T(8,128)(2,1)S(1)} collective-permute-done((bf16[3,72,512]{2,1,0:T(8,128)(2,1)S(1)}, bf16[3,72,512]{2,1,0:T(8,128)(2,1)S(1)}, u32[]{:S(2)}, u32[]{:S(2)}) %collective-permute-start.3) | collective-permute-done | bytes 221216 | tf_op jit(solution)/shard_map/ppermute | solution.py:41
  39.4 1.7 %shard_map.66 = (bf16[3,72,512]{2,1,0:T(8,128)(2,1)S(1)}, bf16[3,72,512]{2,1,0:T(8,128)(2,1)S(1)}) custom-call(s32[1]{0:T(128)} %bitcast.8.refs_0_.flag_ref, bf16[3,3,64,512]{3,2,1,0:T(8,128)(2,1)S(1)} %copy-done.4, bf16[24,8,512]{2,1,0:T(8,128)(2,1)S(1)} %collective-permute-done.low_ref.refs_1_.refs_2_, ...), custom_call_target="tpu_custom_call" | custom-call | flops 1100000000 | bytes 6000000 | tf_op jit(solution)/shard_map/pallas_call | solution.py:200
  41.0 1.9 %collective-permute-start.5 = (bf16[3,72,512]{2,1,0:T(8,128)(2,1)S(1)}, bf16[3,72,512]{2,1,0:T(8,128)(2,1)S(1)}, u32[]{:S(2)}, u32[]{:S(2)}) collective-permute-start(bf16[3,72,512]{2,1,0:T(8,128)(2,1)S(1)} %get-tuple-element.36), channel_id=1, source_target_pairs={{32,0},{64,32},{96,64},{128,96},{160,128},{192,160},{224,192},{33,... | collective-permute-start | bytes 663560 | tf_op jit(solution)/shard_map/ppermute | solution.py:41
  43.0 1.1 %shard_map.67.factor_ref.refs_5_ = f32[1,3,72,512]{3,2,1,0:T(8,128)S(1)} custom-call(bf16[4,3,64,512]{3,2,1,0:T(8,128)(2,1)S(1)} %bitcast.73, bf16[24,8,512]{2,1,0:T(8,128)(2,1)S(1)} %collective-permute-done.low_ref.refs_1_.refs_2_, bf16[24,8,512]{2,1,0:T(8,128)(2,1)S(1)} %collective-permute-done.1.high_ref.refs_2_.refs_3_, bf16[9,512,512]{2,1,0:T(8,128)(2,1)S(1)} %bitcast.65), custom_call_target="tpu_custom_call" | custom-call | flops 1200000000 | bytes 5000000 | tf_op jit(solution)/shard_map/pallas_call | solution.py:132
  44.1 2.1 %collective-permute-start.8 = (bf16[3,72,512]{2,1,0:T(8,128)(2,1)S(1)}, bf16[3,72,512]{2,1,0:T(8,128)(2,1)S(1)}, u32[]{:S(2)}, u32[]{:S(2)}) collective-permute-start(bf16[3,72,512]{2,1,0:T(8,128)(2,1)S(1)} %get-tuple-element.43.third0), channel_id=1, source_target_pairs={{0,2},{1,3},{2,0},{3,1},{4,6},{5,7},{6,4},{7,5},{8,10},{9,11},{10,... | collective-permute-start | bytes 663560 | tf_op jit(solution)/shard_map/ppermute | solution.py:36
  46.2 4.8 %collective-permute-done.5.relay_ref.refs_4_ = bf16[3,72,512]{2,1,0:T(8,128)(2,1)S(1)} collective-permute-done((bf16[3,72,512]{2,1,0:T(8,128)(2,1)S(1)}, bf16[3,72,512]{2,1,0:T(8,128)(2,1)S(1)}, u32[]{:S(2)}, u32[]{:S(2)}) %collective-permute-start.5) | collective-permute-done | bytes 221216 | tf_op jit(solution)/shard_map/ppermute | solution.py:41
  51.1 2.3 %collective-permute-start.6 = (bf16[3,72,512]{2,1,0:T(8,128)(2,1)S(1)}, bf16[3,72,512]{2,1,0:T(8,128)(2,1)S(1)}, u32[]{:S(2)}, u32[]{:S(2)}) collective-permute-start(bf16[3,72,512]{2,1,0:T(8,128)(2,1)S(1)} %shard_map.68.g0), channel_id=1, source_target_pairs={{0,2},{1,3},{2,0},{3,1},{4,6},{5,7},{6,4},{7,5},{8,10},{9,11},{10,... | collective-permute-start | bytes 663560 | tf_op jit(solution)/shard_map/ppermute | solution.py:36
  53.3 2.8 %shard_map.69.total_ref = f32[3,256,1536]{2,1,0:T(8,128)S(1)} custom-call(bf16[4,3,64,256]{3,2,1,0:T(8,128)(2,1)S(1)} %get-tuple-element.33.x0, bf16[4,3,64,256]{3,2,1,0:T(8,128)(2,1)S(1)} %collective-permute-done.4.x1, bf16[2,3,72,512]{3,2,1,0:T(8,128)(2,1)S(1)} %pad_maximum_fusion.both0, bf16[2,3,72,512]{3,2,1,0:T(8,128)(2,1)S(1)} %collective-permute-done.7.both1, ...), custom_call_target="tpu_custom_call" | custom-call | flops 3000000000 | bytes 8000000 | tf_op jit(solution)/shard_map/pallas_call | solution.py:284
  56.1 1.2 %collective-permute-done.6.g1 = bf16[3,72,512]{2,1,0:T(8,128)(2,1)S(1)} collective-permute-done((bf16[3,72,512]{2,1,0:T(8,128)(2,1)S(1)}, bf16[3,72,512]{2,1,0:T(8,128)(2,1)S(1)}, u32[]{:S(2)}, u32[]{:S(2)}) %collective-permute-start.6) | collective-permute-done | bytes 221216 | tf_op jit(solution)/shard_map/ppermute | solution.py:36
  57.3 1.1 %shard_map.70 = (bf16[2,4,9,16,256]{4,3,2,1,0:T(8,128)(2,1)S(1)}, bf16[2,4,9,16,256]{4,3,2,1,0:T(8,128)(2,1)S(1)}, bf16[2,4,9,16,256]{4,3,2,1,0:T(8,128)(2,1)S(1)}, bf16[2,4,9,16,256]{4,3,2,1,0:T(8,128)(2,1)S(1)}) custom-call(bf16[4,3,64,256]{3,2,1,0:T(8,128)(2,1)S(1)} %get-tuple-element.33.x0, bf16[4,3,64,256]{3,2,1,0:T(8,128)(2,1)S(1)} %collective-permute-done.4.x1, ...), custom_call_target="tpu_custom_call" | custom-call | flops 1000000000 | bytes 8000000 | tf_op jit(solution)/shard_map/pallas_call | solution.py:309
  58.3 0.1 collective-permute-start.9
  58.4 0.6 collective-permute-start.10
  59.1 1.4 %collective-permute-done.9 = bf16[2,4,9,16,256]{4,3,2,1,0:T(8,128)(2,1)S(1)} collective-permute-done((bf16[2,4,9,16,256]{4,3,2,1,0:T(8,128)(2,1)S(1)}, bf16[2,4,9,16,256]{4,3,2,1,0:T(8,128)(2,1)S(1)}, u32[]{:S(2)}, u32[]{:S(2)}) %collective-permute-start.9) | collective-permute-done | bytes 589856 | tf_op jit(solution)/shard_map/ppermute | solution.py:36
  60.4 0.1 fusion.2
  60.5 0.6 collective-permute-start.15
  61.1 0.1 collective-permute-done.10
  61.3 0.1 fusion.4
  61.4 3.0 %collective-permute-start.11 = (bf16[4,9,16,256]{3,2,1,0:T(8,128)(2,1)S(1)}, bf16[4,9,16,256]{3,2,1,0:T(8,128)(2,1)S(1)}, u32[]{:S(2)}, u32[]{:S(2)}) collective-permute-start(bf16[4,9,16,256]{3,2,1,0:T(8,128)(2,1)S(1)} %fusion.4), channel_id=1, source_target_pairs={{0,16},{1,17},{2,18},{3,19},{4,20},{5,21},{6,22},{7,23},{8,24},{9,... | collective-permute-start | bytes 884744 | tf_op jit(solution)/shard_map/ppermute | solution.py:36
  64.3 1.7 %shard_map.71 = (bf16[3,72,512]{2,1,0:T(8,128)(2,1)S(1)}, bf16[3,72,512]{2,1,0:T(8,128)(2,1)}) custom-call(s32[1]{0:T(128)} %bitcast.8.refs_0_.flag_ref, bf16[3,3,64,512]{3,2,1,0:T(8,128)(2,1)S(1)} %copy-done.4, bf16[24,8,512]{2,1,0:T(8,128)(2,1)S(1)} %collective-permute-done.low_ref.refs_1_.refs_2_, ...), custom_call_target="tpu_custom_call" | custom-call | flops 1100000000 | bytes 6000000 | tf_op jit(solution)/shard_map/pallas_call | solution.py:200
  66.0 1.0 %maximum_bitcast_fusion = bf16[4,1,3,64,512]{4,3,2,1,0:T(8,128)(2,1)} fusion(bf16[1,3,64,512]{3,2,1,0:T(8,128)(2,1)S(1)} %slice_bitcast_fusion, bf16[1,3,64,512]{3,2,1,0:T(8,128)(2,1)S(1)} %slice_bitcast_fusion.1, bf16[1,3,64,512]{3,2,1,0:T(8,128)(2,1)S(1)} %slice_bitcast_fusion.2, bf16[1,3,64,512]{3,2,1,0:T(8,128)(2,1)S(1)} %slice_bitcast_fusion.3), kind=kLoop, calls=%fused_computation | loop fusion | flops 1179648 | bytes 1572864
  67.0 5.0 %collective-permute-done.15 = bf16[4,9,16,256]{3,2,1,0:T(8,128)(2,1)S(1)} collective-permute-done((bf16[4,9,16,256]{3,2,1,0:T(8,128)(2,1)S(1)}, bf16[4,9,16,256]{3,2,1,0:T(8,128)(2,1)S(1)}, u32[]{:S(2)}, u32[]{:S(2)}) %collective-permute-start.15) | collective-permute-done | bytes 294944 | tf_op jit(solution)/shard_map/ppermute | solution.py:36
  71.9 0.1 fusion
  72.1 3.3 %collective-permute-start.16 = (bf16[9,16,256]{2,1,0:T(8,128)(2,1)S(1)}, bf16[9,16,256]{2,1,0:T(8,128)(2,1)S(1)}, u32[]{:S(2)}, u32[]{:S(2)}) collective-permute-start(bf16[9,16,256]{2,1,0:T(8,128)(2,1)S(1)} %get-tuple-element.55), channel_id=1, source_target_pairs={{0,4},{1,5},{2,6},{3,7},{4,8},{5,9},{6,10},{7,11},{8,12},{9,13},{1... | collective-permute-start | bytes 221192 | tf_op jit(solution)/shard_map/ppermute | solution.py:36
  75.4 1.4 %collective-permute-start.18 = (bf16[9,16,256]{2,1,0:T(8,128)(2,1)S(1)}, bf16[9,16,256]{2,1,0:T(8,128)(2,1)S(1)}, u32[]{:S(2)}, u32[]{:S(2)}) collective-permute-start(bf16[9,16,256]{2,1,0:T(8,128)(2,1)S(1)} %get-tuple-element.56), channel_id=1, source_target_pairs={{0,12},{1,13},{2,14},{3,15},{4,0},{5,1},{6,2},{7,3},{8,4},{9,5},{1... | collective-permute-start | bytes 221192 | tf_op jit(solution)/shard_map/ppermute | solution.py:36
  76.7 2.3 %collective-permute-start.17 = (bf16[9,16,256]{2,1,0:T(8,128)(2,1)S(1)}, bf16[9,16,256]{2,1,0:T(8,128)(2,1)S(1)}, u32[]{:S(2)}, u32[]{:S(2)}) collective-permute-start(bf16[9,16,256]{2,1,0:T(8,128)(2,1)S(1)} %get-tuple-element.57), channel_id=1, source_target_pairs={{0,8},{1,9},{2,10},{3,11},{4,12},{5,13},{6,14},{7,15},{8,0},{9,1},... | collective-permute-start | bytes 221192 | tf_op jit(solution)/shard_map/ppermute | solution.py:36
  79.0 0.1 fusion.1
  79.2 3.0 %collective-permute-start.12 = (bf16[9,16,256]{2,1,0:T(8,128)(2,1)S(1)}, bf16[9,16,256]{2,1,0:T(8,128)(2,1)S(1)}, u32[]{:S(2)}, u32[]{:S(2)}) collective-permute-start(bf16[9,16,256]{2,1,0:T(8,128)(2,1)S(1)} %get-tuple-element.52), channel_id=1, source_target_pairs={{0,4},{1,5},{2,6},{3,7},{4,8},{5,9},{6,10},{7,11},{8,12},{9,13},{1... | collective-permute-start | bytes 221192 | tf_op jit(solution)/shard_map/ppermute | solution.py:36
  82.1 1.2 %collective-permute-start.14 = (bf16[9,16,256]{2,1,0:T(8,128)(2,1)S(1)}, bf16[9,16,256]{2,1,0:T(8,128)(2,1)S(1)}, u32[]{:S(2)}, u32[]{:S(2)}) collective-permute-start(bf16[9,16,256]{2,1,0:T(8,128)(2,1)S(1)} %get-tuple-element.53), channel_id=1, source_target_pairs={{0,12},{1,13},{2,14},{3,15},{4,0},{5,1},{6,2},{7,3},{8,4},{9,5},{1... | collective-permute-start | bytes 221192 | tf_op jit(solution)/shard_map/ppermute | solution.py:36
  83.4 3.6 %collective-permute-start.13 = (bf16[9,16,256]{2,1,0:T(8,128)(2,1)S(1)}, bf16[9,16,256]{2,1,0:T(8,128)(2,1)S(1)}, u32[]{:S(2)}, u32[]{:S(2)}) collective-permute-start(bf16[9,16,256]{2,1,0:T(8,128)(2,1)S(1)} %get-tuple-element.54), channel_id=1, source_target_pairs={{0,8},{1,9},{2,10},{3,11},{4,12},{5,13},{6,14},{7,15},{8,0},{9,1},... | collective-permute-start | bytes 221192 | tf_op jit(solution)/shard_map/ppermute | solution.py:36
  87.1 1.8 %collective-permute-done.14 = bf16[9,16,256]{2,1,0:T(8,128)(2,1)S(1)} collective-permute-done((bf16[9,16,256]{2,1,0:T(8,128)(2,1)S(1)}, bf16[9,16,256]{2,1,0:T(8,128)(2,1)S(1)}, u32[]{:S(2)}, u32[]{:S(2)}) %collective-permute-start.14) | collective-permute-done | bytes 73760 | tf_op jit(solution)/shard_map/ppermute | solution.py:36
  88.9 3.0 %collective-permute-done.13 = bf16[9,16,256]{2,1,0:T(8,128)(2,1)S(1)} collective-permute-done((bf16[9,16,256]{2,1,0:T(8,128)(2,1)S(1)}, bf16[9,16,256]{2,1,0:T(8,128)(2,1)S(1)}, u32[]{:S(2)}, u32[]{:S(2)}) %collective-permute-start.13) | collective-permute-done | bytes 73760 | tf_op jit(solution)/shard_map/ppermute | solution.py:36
  92.0 0.7 fusion.6
  (31 shorter events, 0.4 us)
Async XLA Ops:
  1.9 13.0 %collective-permute-start = (bf16[24,8,512]{2,1,0:T(8,128)(2,1)S(1)}, bf16[24,8,512]{2,1,0:T(8,128)(2,1)S(1)}, u32[]{:S(2)}, u32[]{:S(2)}) collective-permute-start(bf16[24,8,512]{2,1,0:T(8,128)(2,1)S(1)} %get-tuple-element.26), channel_id=1, source_target_pairs={{0,1},{1,2},{2,3},{3,4},{4,5},{5,6},{6,7},{7,8},{8,9},{9,10},{10,1... | collective-permute-start | bytes 589832 | tf_op jit(solution)/shard_map/ppermute | solution.py:36
  2.0 13.0 %collective-permute-start.1 = (bf16[24,8,512]{2,1,0:T(8,128)(2,1)S(1)}, bf16[24,8,512]{2,1,0:T(8,128)(2,1)S(1)}, u32[]{:S(2)}, u32[]{:S(2)}) collective-permute-start(bf16[24,8,512]{2,1,0:T(8,128)(2,1)S(1)} %get-tuple-element.27), channel_id=1, source_target_pairs={{0,31},{1,0},{2,1},{3,2},{4,3},{5,4},{6,5},{7,6},{8,7},{9,8},{10,9... | collective-permute-start | bytes 589832 | tf_op jit(solution)/shard_map/ppermute | solution.py:36
  10.1 1.1 %copy-start.2 = (bf16[4,1,3,64,512]{4,3,2,1,0:T(8,128)(2,1)S(1)}, bf16[4,1,3,64,512]{4,3,2,1,0:T(8,128)(2,1)}, u32[]{:S(2)}) copy-start(bf16[4,1,3,64,512]{4,3,2,1,0:T(8,128)(2,1)} %param.4) | copy-start | bytes 2359300
  11.2 4.9 %copy-start.5 = (bf16[1,3,64,512]{3,2,1,0:T(8,128)(2,1)S(1)}, bf16[1,3,64,512]{3,2,1,0:T(8,128)(2,1)}, u32[]{:S(2)}) copy-start(bf16[1,3,64,512]{3,2,1,0:T(8,128)(2,1)} %param.6) | copy-start | bytes 589828
  14.9 16.5 %collective-permute-start.4 = (bf16[4,3,64,256]{3,2,1,0:T(8,128)(2,1)}, bf16[4,3,64,256]{3,2,1,0:T(8,128)(2,1)S(1)}, u32[]{:S(2)}, u32[]{:S(2)}) collective-permute-start(bf16[4,3,64,256]{3,2,1,0:T(8,128)(2,1)} %get-tuple-element.34), channel_id=1, source_target_pairs={{0,2},{1,3},{2,0},{3,1},{4,6},{5,7},{6,4},{7,5},{8,10},{9,11},{10,... | collective-permute-start | bytes 1179656 | tf_op jit(solution)/shard_map/ppermute | solution.py:36
  15.0 5.6 %copy-start.3 = (bf16[4,1,3,64,512]{4,3,2,1,0:T(8,128)(2,1)S(1)}, bf16[4,1,3,64,512]{4,3,2,1,0:T(8,128)(2,1)}, u32[]{:S(2)}) copy-start(bf16[4,1,3,64,512]{4,3,2,1,0:T(8,128)(2,1)} %param.4) | copy-start | bytes 2359300
  16.1 11.6 %copy-start.4 = (bf16[3,3,64,512]{3,2,1,0:T(8,128)(2,1)S(1)}, bf16[3,3,64,512]{3,2,1,0:T(8,128)(2,1)}, u32[]{:S(2)}) copy-start(bf16[3,3,64,512]{3,2,1,0:T(8,128)(2,1)} %refs_1_.5) | copy-start | bytes 1769476
  17.8 9.9 %collective-permute-start.2 = (bf16[3,72,512]{2,1,0:T(8,128)(2,1)S(1)}, bf16[3,72,512]{2,1,0:T(8,128)(2,1)S(1)}, u32[]{:S(2)}, u32[]{:S(2)}) collective-permute-start(bf16[3,72,512]{2,1,0:T(8,128)(2,1)S(1)} %get-tuple-element.30), channel_id=1, source_target_pairs={{32,0},{64,32},{96,64},{128,96},{160,128},{192,160},{224,192},{33,... | collective-permute-start | bytes 663560 | tf_op jit(solution)/shard_map/ppermute | solution.py:41
  20.6 2.3 %copy-start = (bf16[1,3,3,512,512]{4,3,2,1,0:T(8,128)(2,1)S(1)}, bf16[1,3,3,512,512]{4,3,2,1,0:T(8,128)(2,1)}, u32[]{:S(2)}) copy-start(bf16[1,3,3,512,512]{4,3,2,1,0:T(8,128)(2,1)} %param.5) | copy-start | bytes 14155780
  22.9 4.8 %copy-start.1 = (bf16[1,3,3,512,512]{4,3,2,1,0:T(8,128)(2,1)S(1)}, bf16[1,3,3,512,512]{4,3,2,1,0:T(8,128)(2,1)}, u32[]{:S(2)}) copy-start(bf16[1,3,3,512,512]{4,3,2,1,0:T(8,128)(2,1)} %param.5) | copy-start | bytes 14155780
  29.4 9.9 %collective-permute-start.3 = (bf16[3,72,512]{2,1,0:T(8,128)(2,1)S(1)}, bf16[3,72,512]{2,1,0:T(8,128)(2,1)S(1)}, u32[]{:S(2)}, u32[]{:S(2)}) collective-permute-start(bf16[3,72,512]{2,1,0:T(8,128)(2,1)S(1)} %get-tuple-element.32), channel_id=1, source_target_pairs={{32,0},{64,32},{96,64},{128,96},{160,128},{192,160},{224,192},{33,... | collective-permute-start | bytes 663560 | tf_op jit(solution)/shard_map/ppermute | solution.py:41
  32.5 20.8 %collective-permute-start.7 = (bf16[2,3,72,512]{3,2,1,0:T(8,128)(2,1)S(1)}, bf16[2,3,72,512]{3,2,1,0:T(8,128)(2,1)S(1)}, u32[]{:S(2)}, u32[]{:S(2)}) collective-permute-start(bf16[2,3,72,512]{3,2,1,0:T(8,128)(2,1)S(1)} %pad_maximum_fusion.both0), channel_id=1, source_target_pairs={{0,2},{1,3},{2,0},{3,1},{4,6},{5,7},{6,4},{7,5},{8,10},{9,11},{10,... | collective-permute-start | bytes 1327112 | tf_op jit(solution)/shard_map/ppermute | solution.py:36
  41.0 9.9 %collective-permute-start.5 = (bf16[3,72,512]{2,1,0:T(8,128)(2,1)S(1)}, bf16[3,72,512]{2,1,0:T(8,128)(2,1)S(1)}, u32[]{:S(2)}, u32[]{:S(2)}) collective-permute-start(bf16[3,72,512]{2,1,0:T(8,128)(2,1)S(1)} %get-tuple-element.36), channel_id=1, source_target_pairs={{32,0},{64,32},{96,64},{128,96},{160,128},{192,160},{224,192},{33,... | collective-permute-start | bytes 663560 | tf_op jit(solution)/shard_map/ppermute | solution.py:41
  44.1 9.2 %collective-permute-start.8 = (bf16[3,72,512]{2,1,0:T(8,128)(2,1)S(1)}, bf16[3,72,512]{2,1,0:T(8,128)(2,1)S(1)}, u32[]{:S(2)}, u32[]{:S(2)}) collective-permute-start(bf16[3,72,512]{2,1,0:T(8,128)(2,1)S(1)} %get-tuple-element.43.third0), channel_id=1, source_target_pairs={{0,2},{1,3},{2,0},{3,1},{4,6},{5,7},{6,4},{7,5},{8,10},{9,11},{10,... | collective-permute-start | bytes 663560 | tf_op jit(solution)/shard_map/ppermute | solution.py:36
  51.1 6.2 %collective-permute-start.6 = (bf16[3,72,512]{2,1,0:T(8,128)(2,1)S(1)}, bf16[3,72,512]{2,1,0:T(8,128)(2,1)S(1)}, u32[]{:S(2)}, u32[]{:S(2)}) collective-permute-start(bf16[3,72,512]{2,1,0:T(8,128)(2,1)S(1)} %shard_map.68.g0), channel_id=1, source_target_pairs={{0,2},{1,3},{2,0},{3,1},{4,6},{5,7},{6,4},{7,5},{8,10},{9,11},{10,... | collective-permute-start | bytes 663560 | tf_op jit(solution)/shard_map/ppermute | solution.py:36
  58.3 2.1 %collective-permute-start.9 = (bf16[2,4,9,16,256]{4,3,2,1,0:T(8,128)(2,1)S(1)}, bf16[2,4,9,16,256]{4,3,2,1,0:T(8,128)(2,1)S(1)}, u32[]{:S(2)}, u32[]{:S(2)}) collective-permute-start(bf16[2,4,9,16,256]{4,3,2,1,0:T(8,128)(2,1)S(1)} %get-tuple-element.45), channel_id=1, source_target_pairs={{0,1},{1,0},{2,3},{3,2},{4,5},{5,4},{6,7},{7,6},{8,9},{9,8},{10,11... | collective-permute-start | bytes 1769480 | tf_op jit(solution)/shard_map/ppermute | solution.py:36
  58.4 2.8 %collective-permute-start.10 = (bf16[2,4,9,16,256]{4,3,2,1,0:T(8,128)(2,1)S(1)}, bf16[2,4,9,16,256]{4,3,2,1,0:T(8,128)(2,1)S(1)}, u32[]{:S(2)}, u32[]{:S(2)}) collective-permute-start(bf16[2,4,9,16,256]{4,3,2,1,0:T(8,128)(2,1)S(1)} %get-tuple-element.49), channel_id=1, source_target_pairs={{0,1},{1,0},{2,3},{3,2},{4,5},{5,4},{6,7},{7,6},{8,9},{9,8},{10,11... | collective-permute-start | bytes 1769480 | tf_op jit(solution)/shard_map/ppermute | solution.py:36
  60.5 11.4 %collective-permute-start.15 = (bf16[4,9,16,256]{3,2,1,0:T(8,128)(2,1)S(1)}, bf16[4,9,16,256]{3,2,1,0:T(8,128)(2,1)S(1)}, u32[]{:S(2)}, u32[]{:S(2)}) collective-permute-start(bf16[4,9,16,256]{3,2,1,0:T(8,128)(2,1)S(1)} %fusion.2), channel_id=1, source_target_pairs={{0,16},{1,17},{2,18},{3,19},{4,20},{5,21},{6,22},{7,23},{8,24},{9,... | collective-permute-start | bytes 884744 | tf_op jit(solution)/shard_map/ppermute | solution.py:36
  61.4 17.7 %collective-permute-start.11 = (bf16[4,9,16,256]{3,2,1,0:T(8,128)(2,1)S(1)}, bf16[4,9,16,256]{3,2,1,0:T(8,128)(2,1)S(1)}, u32[]{:S(2)}, u32[]{:S(2)}) collective-permute-start(bf16[4,9,16,256]{3,2,1,0:T(8,128)(2,1)S(1)} %fusion.4), channel_id=1, source_target_pairs={{0,16},{1,17},{2,18},{3,19},{4,20},{5,21},{6,22},{7,23},{8,24},{9,... | collective-permute-start | bytes 884744 | tf_op jit(solution)/shard_map/ppermute | solution.py:36
  72.1 11.3 %collective-permute-start.16 = (bf16[9,16,256]{2,1,0:T(8,128)(2,1)S(1)}, bf16[9,16,256]{2,1,0:T(8,128)(2,1)S(1)}, u32[]{:S(2)}, u32[]{:S(2)}) collective-permute-start(bf16[9,16,256]{2,1,0:T(8,128)(2,1)S(1)} %get-tuple-element.55), channel_id=1, source_target_pairs={{0,4},{1,5},{2,6},{3,7},{4,8},{5,9},{6,10},{7,11},{8,12},{9,13},{1... | collective-permute-start | bytes 221192 | tf_op jit(solution)/shard_map/ppermute | solution.py:36
  75.4 11.7 %collective-permute-start.18 = (bf16[9,16,256]{2,1,0:T(8,128)(2,1)S(1)}, bf16[9,16,256]{2,1,0:T(8,128)(2,1)S(1)}, u32[]{:S(2)}, u32[]{:S(2)}) collective-permute-start(bf16[9,16,256]{2,1,0:T(8,128)(2,1)S(1)} %get-tuple-element.56), channel_id=1, source_target_pairs={{0,12},{1,13},{2,14},{3,15},{4,0},{5,1},{6,2},{7,3},{8,4},{9,5},{1... | collective-permute-start | bytes 221192 | tf_op jit(solution)/shard_map/ppermute | solution.py:36
  76.7 10.3 %collective-permute-start.17 = (bf16[9,16,256]{2,1,0:T(8,128)(2,1)S(1)}, bf16[9,16,256]{2,1,0:T(8,128)(2,1)S(1)}, u32[]{:S(2)}, u32[]{:S(2)}) collective-permute-start(bf16[9,16,256]{2,1,0:T(8,128)(2,1)S(1)} %get-tuple-element.57), channel_id=1, source_target_pairs={{0,8},{1,9},{2,10},{3,11},{4,12},{5,13},{6,14},{7,15},{8,0},{9,1},... | collective-permute-start | bytes 221192 | tf_op jit(solution)/shard_map/ppermute | solution.py:36
  79.2 7.9 %collective-permute-start.12 = (bf16[9,16,256]{2,1,0:T(8,128)(2,1)S(1)}, bf16[9,16,256]{2,1,0:T(8,128)(2,1)S(1)}, u32[]{:S(2)}, u32[]{:S(2)}) collective-permute-start(bf16[9,16,256]{2,1,0:T(8,128)(2,1)S(1)} %get-tuple-element.52), channel_id=1, source_target_pairs={{0,4},{1,5},{2,6},{3,7},{4,8},{5,9},{6,10},{7,11},{8,12},{9,13},{1... | collective-permute-start | bytes 221192 | tf_op jit(solution)/shard_map/ppermute | solution.py:36
  82.1 6.8 %collective-permute-start.14 = (bf16[9,16,256]{2,1,0:T(8,128)(2,1)S(1)}, bf16[9,16,256]{2,1,0:T(8,128)(2,1)S(1)}, u32[]{:S(2)}, u32[]{:S(2)}) collective-permute-start(bf16[9,16,256]{2,1,0:T(8,128)(2,1)S(1)} %get-tuple-element.53), channel_id=1, source_target_pairs={{0,12},{1,13},{2,14},{3,15},{4,0},{5,1},{6,2},{7,3},{8,4},{9,5},{1... | collective-permute-start | bytes 221192 | tf_op jit(solution)/shard_map/ppermute | solution.py:36
  83.4 8.6 %collective-permute-start.13 = (bf16[9,16,256]{2,1,0:T(8,128)(2,1)S(1)}, bf16[9,16,256]{2,1,0:T(8,128)(2,1)S(1)}, u32[]{:S(2)}, u32[]{:S(2)}) collective-permute-start(bf16[9,16,256]{2,1,0:T(8,128)(2,1)S(1)} %get-tuple-element.54), channel_id=1, source_target_pairs={{0,8},{1,9},{2,10},{3,11},{4,12},{5,13},{6,14},{7,15},{8,0},{9,1},... | collective-permute-start | bytes 221192 | tf_op jit(solution)/shard_map/ppermute | solution.py:36

commit v3 on v2

--- a/solution.py
+++ b/solution.py
@@ -211,9 +211,11 @@
     )(*operands, factors, weights)
 
 
-def spread_kernel(place_ref, x_ref, source_ref, out0, out1, w_ref, done):
-    copy = pltpu.make_async_copy(source_ref, w_ref, done)
-    copy.start()
+def spread_kernel(place_ref, x_ref, source_ref, out0, out1, w_ref, field_ref, done):
+    copies = [pltpu.make_async_copy(x_ref.at[t], field_ref.at[t], done.at[t]) for t in range(STEPS)]
+    copies.append(pltpu.make_async_copy(source_ref, w_ref, done.at[STEPS]))
+    for copy in copies:
+        copy.start()
     h, j, k, c = (place_ref[n] for n in range(4))
     lane = lax.broadcasted_iota(jnp.int32, (8, CH), 1)
     chip = jnp.bitwise_xor(lane // HALF, k)
@@ -223,25 +225,28 @@
     source = ((far * 4 + turn) * 4 + chip * 2 + core) * 16 + lane % 16
     row = lax.broadcasted_iota(jnp.int32, (CH, CH), 0)
     order = jnp.where(row == source[:1], 1.0, 0.0).astype(BF)
-    field = jnp.concatenate([x_ref[t, r] for t in range(STEPS) for r in range(ROWS)], axis=0)
-    value = jnp.dot(field, order, preferred_element_type=F32).astype(BF)
-    for n, out in enumerate((out0, out1)):
-        for t in range(STEPS):
+    for t in range(STEPS):
+        copies[t].wait()
+        field = jnp.concatenate([field_ref[t, r] for r in range(ROWS)], axis=0)
+        value = jnp.dot(field, order, preferred_element_type=F32).astype(BF)
+        for n, out in enumerate((out0, out1)):
             for r in range(ROWS):
-                at = (t * ROWS + r) * WIDTH
-                out[t, r] = value[at : at + WIDTH, n * HALF : (n + 1) * HALF]
-    copy.wait()
+                out[t, r] = value[r * WIDTH : (r + 1) * WIDTH, n * HALF : (n + 1) * HALF]
+    copies[STEPS].wait()
 
 
 def spread(place, x, weights):
-    weights = pltpu.with_memory_space_constraint(weights, pltpu.HBM)
+    x, weights = (pltpu.with_memory_space_constraint(v, pltpu.HBM) for v in (x, weights))
     shape = jax.ShapeDtypeStruct((STEPS, ROWS, WIDTH, HALF), BF)
     return pl.pallas_call(
         spread_kernel,
         out_shape=(shape, shape, pltpu.VMEM(weights.shape, BF)),
-        in_specs=[SMEM, VMEM, pl.BlockSpec(memory_space=pltpu.HBM)],
+        in_specs=[SMEM, pl.BlockSpec(memory_space=pltpu.HBM), pl.BlockSpec(memory_space=pltpu.HBM)],
         out_specs=(VMEM, VMEM, VMEM),
-        scratch_shapes=[pltpu.SemaphoreType.DMA],
+        scratch_shapes=[
+            pltpu.VMEM((STEPS, ROWS, WIDTH, CH), BF),
+            pltpu.SemaphoreType.DMA((STEPS + 1,)),
+        ],
         compiler_params=params(),
         cost_estimate=cost(4.5e8, 1.2e7),
     )(place, x, weights)
@@ -291,29 +296,35 @@
     )(*xs, *gs)
 
 
+FIRST = 6
+
+
 def late_kernel(x0, x1, g0, g1, total_ref, *outs):
     for a, value in enumerate(tap_products((x0[0], x1[0]), (g0, g1))):
         value = value + total_ref[a]
         for b in range(3):
-            for n, out in enumerate(outs):
-                core, lanes = n // 2, b * CH + n % 2 * HALF
+            tap = a * 3 + b
+            for core in range(2):
                 for far in range(2):
                     for turn in range(4):
                         at = ((core * 2 + far) * 4 + turn) * 16
-                        out[far, turn, a * 3 + b] = value[at : at + 16, lanes : lanes + HALF].astype(BF)
+                        part = value[at : at + 16, b * CH : (b + 1) * CH].astype(BF)
+                        if tap < FIRST:
+                            outs[core][far, turn, tap] = part
+                        else:
+                            outs[2 + core][turn, far, tap - FIRST] = part
 
 
 def late_products(xs, gs, total):
-    shape = jax.ShapeDtypeStruct((2, 4, 9, 16, HALF), BF)
-    whole = block((2, 4, 9, 16, HALF), 0, 0, 0, 0, 0)
+    shapes = [(2, 4, FIRST, 16, CH)] * 2 + [(4, 2, 9 - FIRST, 16, CH)] * 2
     return pl.pallas_call(
         late_kernel,
         grid=(1,),
-        out_shape=(shape,) * 4,
+        out_shape=tuple(jax.ShapeDtypeStruct(shape, BF) for shape in shapes),
         in_specs=[block((1, ROWS, WIDTH, HALF), STEPS - 1, 0, 0, 0)] * 2
         + [block((ROWS, WIDE, CH), 0, 0, 0)] * 2
         + [block((3, HALF, 3 * CH), 0, 0, 0)],
-        out_specs=(whole,) * 4,
+        out_specs=tuple(block(shape, 0, 0, 0, 0, 0) for shape in shapes),
         compiler_params=params(),
         cost_estimate=cost(1e9, 8e6),
     )(*xs, *gs, total)
@@ -396,19 +407,23 @@
         fields.append(own if t == 0 else (own, send(own, PAIR)))
 
     total = early_products(xs, *fields[0], *fields[1])
-    parts = late_products(xs, fields[-1], total)
-    sums = []
-    for n in range(2):
-        mine, other = parts[n], send(parts[2 + n], CORE)
-        near = [total_of(mine[m], other[m]).astype(BF) for m in range(2)]
-        if n == 1:
-            arrived = after(arrived, near[1])
-        near = total_of(near[0], send(near[1], FAR)).astype(BF)
-        across, ups, downs = send(near[2], ACROSS), send(near[1], UP), send(near[3], DOWN)
-        sums.append(total_of(near[0], ups, across, downs))
+    mine, other, mine_b, other_b = late_products(xs, fields[-1], total)
+    other = send(other, CORE)
+    near = [total_of(mine[m], other[m]).astype(BF) for m in range(2)]
+    far = send(near[1], FAR)
+    other_b = send(after(other_b, near[1]), CORE)
+    turns = [total_of(mine_b[m], other_b[m]).astype(BF) for m in range(4)]
+    arrived = after(arrived, turns[1], turns[2], turns[3])
+    arriving = (send(turns[2], ACROSS), send(turns[1], UP), send(turns[3], DOWN))
+    near = total_of(near[0], far).astype(BF)
+    across, ups, downs = send(near[2], ACROSS), send(near[1], UP), send(near[3], DOWN)
+    arriving = lax.optimization_barrier((*arriving, near))[:3]
+    turned = total_of(turns[0], *arriving).astype(BF)
+    far = send(turned[1], FAR)
+    sums = [total_of(near[0], ups, across, downs), total_of(turned[0], far)]
     sent, _ = back_step(top, low, high, factors, taps, STEPS - 1, flag, arrived)
     emitted.append(sent[:, :WIDTH])
-    weight_grads = (jnp.concatenate(sums, axis=-1) * scale).astype(BF).reshape(1, 3, 3, 16, CH)
+    weight_grads = (jnp.concatenate(sums, axis=0) * scale).astype(BF).reshape(1, 3, 3, 16, CH)
     return (jnp.stack(emitted)[:, None], weight_grads)
 
 

time: 93.5 us -> 92.6 us (level)
  starting transfers between devices: 40.2 us -> 42.4 us
  waiting for transfers between devices: 25.8 us -> 23.8 us
  local copies, waits for them, and re-layouts: 3.58 us -> 2.44 us
    ppermute x16, starting transfers between devices: 33.6 us -> 35.8 us  [send(): return lax.ppermute(block, 'az', route)]
    ppermute x16, waiting for transfers between devices: 12.5 us -> 10.6 us  [send(): return lax.ppermute(block, 'az', route)]
    unnamed x12 -> x10, local copies, waits for them, and re-layouts: 3.49 us -> 2.35 us
  transfers between devices with their start and end apart: 19 -> 19, of which waited for: 9 -> 8; matrix products, arithmetic and copies ran while one was open for 2% -> 2% of each run, Pallas kernels for 19% -> 20%
where the time goes in v3:
time: 92.6 us; the launch traced here: 92.3 us
  starting transfers between devices  42.4 us (46%)
  waiting for transfers between devices  23.8 us (26%)
  Pallas kernels  20.4 us (22%)
  local copies, waits for them, and re-layouts  2.44 us (3%)
  other arithmetic  2.35 us (3%)
  between operations  0.95 us (1%)
    ppermute x16, starting transfers between devices, send(): return lax.ppermute(block, 'az', route)  35.8 us
    ppermute x3, waiting for transfers between devices, relay(): return lax.ppermute(block, 'segment', [(i, i - 1) for i in range(1, count)])  13.2 us
    ppermute x16, waiting for transfers between devices, send(): return lax.ppermute(block, 'az', route)  10.6 us
    pallas_call x4, Pallas kernels, back_step(): pl.pallas_call(lambda *refs: back_kernel(first, *refs), grid=(1,), out_sh...  6.65 us
    ppermute x3, starting transfers between devices, relay(): return lax.ppermute(block, 'segment', [(i, i - 1) for i in range(1, count)])  6.57 us
    pallas_call x4, Pallas kernels, slope_factors(): pl.pallas_call(factor_kernel, grid=(1,), out_shape=jax.ShapeDtypeStruct((...  4.5 us
    pallas_call x1, Pallas kernels, spread(): pl.pallas_call(spread_kernel, out_shape=(shape, shape, pltpu.VMEM(weights...  4.04 us
    pallas_call x1, Pallas kernels, early_products(): pl.pallas_call(early_kernel, out_shape=jax.ShapeDtypeStruct((3, HALF, 3 *...  2.75 us
  transfers between devices with their start and end apart: 19, of which 8 were waited for; matrix products, arithmetic and copies ran while one was open for 2% of the time, Pallas kernels for 20%

profile of v3, /device:TPU:6, one launch (start us, length us, event | category | flops | bytes accessed | tf_op | source)
XLA Modules:
  0.0 92.3 jit_solution(14306761837109547414)
XLA Ops:
  0.6 1.3 %shard_map.59 = (bf16[24,8,512]{2,1,0:T(8,128)(2,1)S(1)}, bf16[24,8,512]{2,1,0:T(8,128)(2,1)S(1)}) custom-call(bf16[4,3,64,512]{3,2,1,0:T(8,128)(2,1)} %bitcast.66, bf16[3,64,512]{2,1,0:T(8,128)(2,1)} %bitcast.73, bf16[3,3,64,512]{3,2,1,0:T(8,128)(2,1)} %refs_1_.5, bf16[4,3,64,512]{3,2,1,0:T(8,128)(2,1)} %bitcast.67, bf16[3,64,512]{2,1,0:T(8,128)(2,1)} %bitcast.74, ...), custom_call_target="tpu_custom_call" | custom-call | bytes 1048576 | tf_op jit(solution)/shard_map/pallas_call | solution.py:79
  2.0 0.1 collective-permute-start
  2.1 8.0 %collective-permute-start.1 = (bf16[24,8,512]{2,1,0:T(8,128)(2,1)S(1)}, bf16[24,8,512]{2,1,0:T(8,128)(2,1)S(1)}, u32[]{:S(2)}, u32[]{:S(2)}) collective-permute-start(bf16[24,8,512]{2,1,0:T(8,128)(2,1)S(1)} %get-tuple-element.31), channel_id=1, source_target_pairs={{0,31},{1,0},{2,1},{3,2},{4,3},{5,4},{6,5},{7,6},{8,7},{9,8},{10,9... | collective-permute-start | bytes 589832 | tf_op jit(solution)/shard_map/ppermute | solution.py:36
  10.1 0.1 pad_add_fusion.place_ref
  10.1 4.0 %shard_map.60 = (bf16[4,3,64,256]{3,2,1,0:T(8,128)(2,1)S(1)}, bf16[4,3,64,256]{3,2,1,0:T(8,128)(2,1)}, bf16[9,512,512]{2,1,0:T(8,128)(2,1)S(1)}) custom-call(s32[4]{0:T(128)S(1)} %pad_add_fusion.place_ref, bf16[4,3,64,512]{3,2,1,0:T(8,128)(2,1)} %bitcast.68, bf16[9,512,512]{2,1,0:T(8,128)(2,1)} %bitcast.59), custom_call_target="tpu_custom_call" | custom-call | flops 450000000 | bytes 12000000 | tf_op jit(solution)/shard_map/pallas_call | solution.py:241
  14.2 0.1 collective-permute-start.4
  14.3 1.1 %shard_map.61.refs_3_ = f32[1,3,72,512]{3,2,1,0:T(8,128)S(1)} custom-call(bf16[4,3,64,512]{3,2,1,0:T(8,128)(2,1)S(1)} %bitcast.69, bf16[24,8,512]{2,1,0:T(8,128)(2,1)S(1)} %collective-permute-done.low_ref.refs_1_.refs_2_, bf16[24,8,512]{2,1,0:T(8,128)(2,1)S(1)} %collective-permute-done.1.high_ref.refs_2_.refs_3_, ...), custom_call_target="tpu_custom_call" | custom-call | flops 1200000000 | bytes 5000000 | tf_op jit(solution)/shard_map/pallas_call | solution.py:132
  15.5 1.7 %shard_map.62 = (bf16[3,72,512]{2,1,0:T(8,128)(2,1)S(1)}, bf16[3,72,512]{2,1,0:T(8,128)(2,1)S(1)}) custom-call(bf16[3,64,512]{2,1,0:T(8,128)(2,1)S(1)} %bitcast.75, bf16[24,8,512]{2,1,0:T(8,128)(2,1)S(1)} %collective-permute-done.low_ref.refs_1_.refs_2_, bf16[24,8,512]{2,1,0:T(8,128)(2,1)S(1)} %collective-permute-done.1.high_ref.refs_2_.refs_3_, ...), custom_call_target="tpu_custom_call" | custom-call | flops 1100000000 | bytes 6000000 | tf_op jit(solution)/shard_map/pallas_call | solution.py:200
  17.1 2.7 %collective-permute-start.2 = (bf16[3,72,512]{2,1,0:T(8,128)(2,1)S(1)}, bf16[3,72,512]{2,1,0:T(8,128)(2,1)S(1)}, u32[]{:S(2)}, u32[]{:S(2)}) collective-permute-start(bf16[3,72,512]{2,1,0:T(8,128)(2,1)S(1)} %get-tuple-element.34), channel_id=1, source_target_pairs={{32,0},{64,32},{96,64},{128,96},{160,128},{192,160},{224,192},{33,... | collective-permute-start | bytes 663560 | tf_op jit(solution)/shard_map/ppermute | solution.py:41
  19.9 2.3 %copy-done = bf16[1,3,3,512,512]{4,3,2,1,0:T(8,128)(2,1)S(1)} copy-done((bf16[1,3,3,512,512]{4,3,2,1,0:T(8,128)(2,1)S(1)}, bf16[1,3,3,512,512]{4,3,2,1,0:T(8,128)(2,1)}, u32[]{:S(2)}) %copy-start) | copy-done | bytes 4718616
  22.2 1.1 %shard_map.63.refs_5_ = f32[1,3,72,512]{3,2,1,0:T(8,128)S(1)} custom-call(bf16[4,3,64,512]{3,2,1,0:T(8,128)(2,1)S(1)} %bitcast.70, bf16[24,8,512]{2,1,0:T(8,128)(2,1)S(1)} %collective-permute-done.low_ref.refs_1_.refs_2_, bf16[24,8,512]{2,1,0:T(8,128)(2,1)S(1)} %collective-permute-done.1.high_ref.refs_2_.refs_3_, bf16[9,512,512]{2,1,0:T(8,128)(2,1)S(1)} %bitcast.60), custom_call_target="tpu_custom_call" | custom-call | flops 1200000000 | bytes 5000000 | tf_op jit(solution)/shard_map/pallas_call | solution.py:132
  23.4 3.7 %collective-permute-done.2.refs_4_ = bf16[3,72,512]{2,1,0:T(8,128)(2,1)S(1)} collective-permute-done((bf16[3,72,512]{2,1,0:T(8,128)(2,1)S(1)}, bf16[3,72,512]{2,1,0:T(8,128)(2,1)S(1)}, u32[]{:S(2)}, u32[]{:S(2)}) %collective-permute-start.2) | collective-permute-done | bytes 221216 | tf_op jit(solution)/shard_map/ppermute | solution.py:41
  27.1 1.7 %shard_map.64 = (bf16[3,72,512]{2,1,0:T(8,128)(2,1)S(1)}, bf16[3,72,512]{2,1,0:T(8,128)(2,1)S(1)}) custom-call(s32[1]{0:T(128)} %bitcast.8.refs_0_.flag_ref, bf16[3,3,64,512]{3,2,1,0:T(8,128)(2,1)S(1)} %copy-done.3, bf16[24,8,512]{2,1,0:T(8,128)(2,1)S(1)} %collective-permute-done.low_ref.refs_1_.refs_2_, ...), custom_call_target="tpu_custom_call" | custom-call | flops 1100000000 | bytes 6000000 | tf_op jit(solution)/shard_map/pallas_call | solution.py:200
  28.7 1.9 %collective-permute-start.3 = (bf16[3,72,512]{2,1,0:T(8,128)(2,1)S(1)}, bf16[3,72,512]{2,1,0:T(8,128)(2,1)S(1)}, u32[]{:S(2)}, u32[]{:S(2)}) collective-permute-start(bf16[3,72,512]{2,1,0:T(8,128)(2,1)S(1)} %get-tuple-element.36), channel_id=1, source_target_pairs={{32,0},{64,32},{96,64},{128,96},{160,128},{192,160},{224,192},{33,... | collective-permute-start | bytes 663560 | tf_op jit(solution)/shard_map/ppermute | solution.py:41
  30.7 1.1 %shard_map.65.refs_5_ = f32[1,3,72,512]{3,2,1,0:T(8,128)S(1)} custom-call(bf16[4,3,64,512]{3,2,1,0:T(8,128)(2,1)S(1)} %bitcast.71, bf16[24,8,512]{2,1,0:T(8,128)(2,1)S(1)} %collective-permute-done.low_ref.refs_1_.refs_2_, bf16[24,8,512]{2,1,0:T(8,128)(2,1)S(1)} %collective-permute-done.1.high_ref.refs_2_.refs_3_, bf16[9,512,512]{2,1,0:T(8,128)(2,1)S(1)} %bitcast.62), custom_call_target="tpu_custom_call" | custom-call | flops 1200000000 | bytes 5000000 | tf_op jit(solution)/shard_map/pallas_call | solution.py:132
  31.9 2.1 %collective-permute-start.7 = (bf16[2,3,72,512]{3,2,1,0:T(8,128)(2,1)S(1)}, bf16[2,3,72,512]{3,2,1,0:T(8,128)(2,1)S(1)}, u32[]{:S(2)}, u32[]{:S(2)}) collective-permute-start(bf16[2,3,72,512]{3,2,1,0:T(8,128)(2,1)S(1)} %pad_maximum_fusion.both0), channel_id=1, source_target_pairs={{0,2},{1,3},{2,0},{3,1},{4,6},{5,7},{6,4},{7,5},{8,10},{9,11},{10,... | collective-permute-start | bytes 1327112 | tf_op jit(solution)/shard_map/ppermute | solution.py:36
  33.9 4.7 %collective-permute-done.3.refs_4_ = bf16[3,72,512]{2,1,0:T(8,128)(2,1)S(1)} collective-permute-done((bf16[3,72,512]{2,1,0:T(8,128)(2,1)S(1)}, bf16[3,72,512]{2,1,0:T(8,128)(2,1)S(1)}, u32[]{:S(2)}, u32[]{:S(2)}) %collective-permute-start.3) | collective-permute-done | bytes 221216 | tf_op jit(solution)/shard_map/ppermute | solution.py:41
  38.7 1.7 %shard_map.66 = (bf16[3,72,512]{2,1,0:T(8,128)(2,1)S(1)}, bf16[3,72,512]{2,1,0:T(8,128)(2,1)S(1)}) custom-call(s32[1]{0:T(128)} %bitcast.8.refs_0_.flag_ref, bf16[3,3,64,512]{3,2,1,0:T(8,128)(2,1)S(1)} %copy-done.3, bf16[24,8,512]{2,1,0:T(8,128)(2,1)S(1)} %collective-permute-done.low_ref.refs_1_.refs_2_, ...), custom_call_target="tpu_custom_call" | custom-call | flops 1100000000 | bytes 6000000 | tf_op jit(solution)/shard_map/pallas_call | solution.py:200
  40.4 1.9 %collective-permute-start.5 = (bf16[3,72,512]{2,1,0:T(8,128)(2,1)S(1)}, bf16[3,72,512]{2,1,0:T(8,128)(2,1)S(1)}, u32[]{:S(2)}, u32[]{:S(2)}) collective-permute-start(bf16[3,72,512]{2,1,0:T(8,128)(2,1)S(1)} %get-tuple-element.40), channel_id=1, source_target_pairs={{32,0},{64,32},{96,64},{128,96},{160,128},{192,160},{224,192},{33,... | collective-permute-start | bytes 663560 | tf_op jit(solution)/shard_map/ppermute | solution.py:41
  42.3 1.1 %shard_map.67.factor_ref.refs_5_ = f32[1,3,72,512]{3,2,1,0:T(8,128)S(1)} custom-call(bf16[4,3,64,512]{3,2,1,0:T(8,128)(2,1)S(1)} %bitcast.72, bf16[24,8,512]{2,1,0:T(8,128)(2,1)S(1)} %collective-permute-done.low_ref.refs_1_.refs_2_, bf16[24,8,512]{2,1,0:T(8,128)(2,1)S(1)} %collective-permute-done.1.high_ref.refs_2_.refs_3_, bf16[9,512,512]{2,1,0:T(8,128)(2,1)S(1)} %bitcast.64), custom_call_target="tpu_custom_call" | custom-call | flops 1200000000 | bytes 5000000 | tf_op jit(solution)/shard_map/pallas_call | solution.py:132
  43.4 2.1 %collective-permute-start.8 = (bf16[3,72,512]{2,1,0:T(8,128)(2,1)S(1)}, bf16[3,72,512]{2,1,0:T(8,128)(2,1)S(1)}, u32[]{:S(2)}, u32[]{:S(2)}) collective-permute-start(bf16[3,72,512]{2,1,0:T(8,128)(2,1)S(1)} %get-tuple-element.47.third0), channel_id=1, source_target_pairs={{0,2},{1,3},{2,0},{3,1},{4,6},{5,7},{6,4},{7,5},{8,10},{9,11},{10,... | collective-permute-start | bytes 663560 | tf_op jit(solution)/shard_map/ppermute | solution.py:36
  45.5 4.8 %collective-permute-done.5.relay_ref.refs_4_ = bf16[3,72,512]{2,1,0:T(8,128)(2,1)S(1)} collective-permute-done((bf16[3,72,512]{2,1,0:T(8,128)(2,1)S(1)}, bf16[3,72,512]{2,1,0:T(8,128)(2,1)S(1)}, u32[]{:S(2)}, u32[]{:S(2)}) %collective-permute-start.5) | collective-permute-done | bytes 221216 | tf_op jit(solution)/shard_map/ppermute | solution.py:41
  50.3 0.1 shard_map.68.g0
  50.4 2.3 %collective-permute-start.6 = (bf16[3,72,512]{2,1,0:T(8,128)(2,1)S(1)}, bf16[3,72,512]{2,1,0:T(8,128)(2,1)S(1)}, u32[]{:S(2)}, u32[]{:S(2)}) collective-permute-start(bf16[3,72,512]{2,1,0:T(8,128)(2,1)S(1)} %shard_map.68.g0), channel_id=1, source_target_pairs={{0,2},{1,3},{2,0},{3,1},{4,6},{5,7},{6,4},{7,5},{8,10},{9,11},{10,... | collective-permute-start | bytes 663560 | tf_op jit(solution)/shard_map/ppermute | solution.py:36
  52.6 2.8 %shard_map.69.total_ref = f32[3,256,1536]{2,1,0:T(8,128)S(1)} custom-call(bf16[4,3,64,256]{3,2,1,0:T(8,128)(2,1)S(1)} %get-tuple-element.37.x0, bf16[4,3,64,256]{3,2,1,0:T(8,128)(2,1)S(1)} %collective-permute-done.4.x1, bf16[2,3,72,512]{3,2,1,0:T(8,128)(2,1)S(1)} %pad_maximum_fusion.both0, bf16[2,3,72,512]{3,2,1,0:T(8,128)(2,1)S(1)} %collective-permute-done.7.both1, ...), custom_call_target="tpu_custom_call" | custom-call | flops 3000000000 | bytes 8000000 | tf_op jit(solution)/shard_map/pallas_call | solution.py:289
  55.4 1.2 %collective-permute-done.6.g1 = bf16[3,72,512]{2,1,0:T(8,128)(2,1)S(1)} collective-permute-done((bf16[3,72,512]{2,1,0:T(8,128)(2,1)S(1)}, bf16[3,72,512]{2,1,0:T(8,128)(2,1)S(1)}, u32[]{:S(2)}, u32[]{:S(2)}) %collective-permute-start.6) | collective-permute-done | bytes 221216 | tf_op jit(solution)/shard_map/ppermute | solution.py:36
  56.6 1.1 %shard_map.70 = (bf16[2,4,6,16,512]{4,3,2,1,0:T(8,128)(2,1)S(1)}, bf16[2,4,6,16,512]{4,3,2,1,0:T(8,128)(2,1)S(1)}, bf16[4,2,3,16,512]{4,3,2,1,0:T(8,128)(2,1)S(1)}, bf16[4,2,3,16,512]{4,3,2,1,0:T(8,128)(2,1)S(1)}) custom-call(bf16[4,3,64,256]{3,2,1,0:T(8,128)(2,1)S(1)} %get-tuple-element.37.x0, bf16[4,3,64,256]{3,2,1,0:T(8,128)(2,1)S(1)} %collective-permute-done.4.x1, ...), custom_call_target="tpu_custom_call" | custom-call | flops 1000000000 | bytes 8000000 | tf_op jit(solution)/shard_map/pallas_call | solution.py:320
  57.7 0.1 collective-permute-start.9
  57.8 2.2 %collective-permute-done.9 = bf16[2,4,6,16,512]{4,3,2,1,0:T(8,128)(2,1)S(1)} collective-permute-done((bf16[2,4,6,16,512]{4,3,2,1,0:T(8,128)(2,1)S(1)}, bf16[2,4,6,16,512]{4,3,2,1,0:T(8,128)(2,1)S(1)}, u32[]{:S(2)}, u32[]{:S(2)}) %collective-permute-start.9) | collective-permute-done | bytes 786464 | tf_op jit(solution)/shard_map/ppermute | solution.py:36
  60.0 0.1 fusion.1
  60.2 0.2 collective-permute-start.10
  60.4 0.6 collective-permute-start.11
  61.1 0.9 collective-permute-done.10
  62.0 0.1 fusion.11
  62.1 6.9 %collective-permute-start.17 = (bf16[2,3,16,512]{3,2,1,0:T(8,128)(2,1)S(1)}, bf16[2,3,16,512]{3,2,1,0:T(8,128)(2,1)S(1)}, u32[]{:S(2)}, u32[]{:S(2)}) collective-permute-start(bf16[2,3,16,512]{3,2,1,0:T(8,128)(2,1)S(1)} %get-tuple-element.60), channel_id=1, source_target_pairs={{0,12},{1,13},{2,14},{3,15},{4,0},{5,1},{6,2},{7,3},{8,4},{9,5},{1... | collective-permute-start | bytes 294920 | tf_op jit(solution)/shard_map/ppermute | solution.py:36
  69.0 1.6 %collective-permute-start.15 = (bf16[2,3,16,512]{3,2,1,0:T(8,128)(2,1)S(1)}, bf16[2,3,16,512]{3,2,1,0:T(8,128)(2,1)S(1)}, u32[]{:S(2)}, u32[]{:S(2)}) collective-permute-start(bf16[2,3,16,512]{3,2,1,0:T(8,128)(2,1)S(1)} %get-tuple-element.61), channel_id=1, source_target_pairs={{0,8},{1,9},{2,10},{3,11},{4,12},{5,13},{6,14},{7,15},{8,0},{9,1},... | collective-permute-start | bytes 294920 | tf_op jit(solution)/shard_map/ppermute | solution.py:36
  70.7 0.8 collective-permute-start.16
  71.5 1.7 %shard_map.71 = (bf16[3,72,512]{2,1,0:T(8,128)(2,1)S(1)}, bf16[3,72,512]{2,1,0:T(8,128)(2,1)}) custom-call(s32[1]{0:T(128)} %bitcast.8.refs_0_.flag_ref, bf16[3,3,64,512]{3,2,1,0:T(8,128)(2,1)S(1)} %copy-done.3, bf16[24,8,512]{2,1,0:T(8,128)(2,1)S(1)} %collective-permute-done.low_ref.refs_1_.refs_2_, ...), custom_call_target="tpu_custom_call" | custom-call | flops 1100000000 | bytes 6000000 | tf_op jit(solution)/shard_map/pallas_call | solution.py:200
  73.2 0.2 collective-permute-done.11
  73.4 0.2 fusion
  73.6 3.9 %collective-permute-start.12 = (bf16[6,16,512]{2,1,0:T(8,128)(2,1)S(1)}, bf16[6,16,512]{2,1,0:T(8,128)(2,1)S(1)}, u32[]{:S(2)}, u32[]{:S(2)}) collective-permute-start(bf16[6,16,512]{2,1,0:T(8,128)(2,1)S(1)} %get-tuple-element.63), channel_id=1, source_target_pairs={{0,4},{1,5},{2,6},{3,7},{4,8},{5,9},{6,10},{7,11},{8,12},{9,13},{1... | collective-permute-start | bytes 294920 | tf_op jit(solution)/shard_map/ppermute | solution.py:36
  77.5 1.8 %collective-permute-start.14 = (bf16[6,16,512]{2,1,0:T(8,128)(2,1)S(1)}, bf16[6,16,512]{2,1,0:T(8,128)(2,1)S(1)}, u32[]{:S(2)}, u32[]{:S(2)}) collective-permute-start(bf16[6,16,512]{2,1,0:T(8,128)(2,1)S(1)} %get-tuple-element.64), channel_id=1, source_target_pairs={{0,12},{1,13},{2,14},{3,15},{4,0},{5,1},{6,2},{7,3},{8,4},{9,5},{1... | collective-permute-start | bytes 294920 | tf_op jit(solution)/shard_map/ppermute | solution.py:36
  79.3 1.0 %maximum_bitcast_fusion = bf16[4,1,3,64,512]{4,3,2,1,0:T(8,128)(2,1)} fusion(bf16[1,3,64,512]{3,2,1,0:T(8,128)(2,1)S(1)} %slice_bitcast_fusion, bf16[1,3,64,512]{3,2,1,0:T(8,128)(2,1)S(1)} %slice_bitcast_fusion.1, bf16[1,3,64,512]{3,2,1,0:T(8,128)(2,1)S(1)} %slice_bitcast_fusion.2, bf16[1,3,64,512]{3,2,1,0:T(8,128)(2,1)S(1)} %slice_bitcast_fusion.3), kind=kLoop, calls=%fused_computation | loop fusion | flops 1179648 | bytes 1572864
  80.3 2.3 %collective-permute-start.13 = (bf16[6,16,512]{2,1,0:T(8,128)(2,1)S(1)}, bf16[6,16,512]{2,1,0:T(8,128)(2,1)S(1)}, u32[]{:S(2)}, u32[]{:S(2)}) collective-permute-start(bf16[6,16,512]{2,1,0:T(8,128)(2,1)S(1)} %get-tuple-element.65), channel_id=1, source_target_pairs={{0,8},{1,9},{2,10},{3,11},{4,12},{5,13},{6,14},{7,15},{8,0},{9,1},... | collective-permute-start | bytes 294920 | tf_op jit(solution)/shard_map/ppermute | solution.py:36
  82.6 0.1 fusion.6
  82.7 2.9 %collective-permute-start.18 = (bf16[3,16,512]{2,1,0:T(8,128)(2,1)S(1)}, bf16[3,16,512]{2,1,0:T(8,128)(2,1)S(1)}, u32[]{:S(2)}, u32[]{:S(2)}) collective-permute-start(bf16[3,16,512]{2,1,0:T(8,128)(2,1)S(1)} %slice_bitcast_fusion.8), channel_id=1, source_target_pairs={{0,16},{1,17},{2,18},{3,19},{4,20},{5,21},{6,22},{7,23},{8,24},{9,... | collective-permute-start | bytes 147464 | tf_op jit(solution)/shard_map/ppermute | solution.py:36
  85.6 6.0 %collective-permute-done.13 = bf16[6,16,512]{2,1,0:T(8,128)(2,1)S(1)} collective-permute-done((bf16[6,16,512]{2,1,0:T(8,128)(2,1)S(1)}, bf16[6,16,512]{2,1,0:T(8,128)(2,1)S(1)}, u32[]{:S(2)}, u32[]{:S(2)}) %collective-permute-start.13) | collective-permute-done | bytes 98336 | tf_op jit(solution)/shard_map/ppermute | solution.py:36
  91.6 0.7 fusion.3
  (29 shorter events, 0.2 us)
Async XLA Ops:
  0.6 13.7 %copy-start.2 = (bf16[4,1,3,64,512]{4,3,2,1,0:T(8,128)(2,1)S(1)}, bf16[4,1,3,64,512]{4,3,2,1,0:T(8,128)(2,1)}, u32[]{:S(2)}) copy-start(bf16[4,1,3,64,512]{4,3,2,1,0:T(8,128)(2,1)} %param.4) | copy-start | bytes 2359300
  2.0 12.3 %collective-permute-start = (bf16[24,8,512]{2,1,0:T(8,128)(2,1)S(1)}, bf16[24,8,512]{2,1,0:T(8,128)(2,1)S(1)}, u32[]{:S(2)}, u32[]{:S(2)}) collective-permute-start(bf16[24,8,512]{2,1,0:T(8,128)(2,1)S(1)} %get-tuple-element.30), channel_id=1, source_target_pairs={{0,1},{1,2},{2,3},{3,4},{4,5},{5,6},{6,7},{7,8},{8,9},{9,10},{10,1... | collective-permute-start | bytes 589832 | tf_op jit(solution)/shard_map/ppermute | solution.py:36
  2.1 12.2 %collective-permute-start.1 = (bf16[24,8,512]{2,1,0:T(8,128)(2,1)S(1)}, bf16[24,8,512]{2,1,0:T(8,128)(2,1)S(1)}, u32[]{:S(2)}, u32[]{:S(2)}) collective-permute-start(bf16[24,8,512]{2,1,0:T(8,128)(2,1)S(1)} %get-tuple-element.31), channel_id=1, source_target_pairs={{0,31},{1,0},{2,1},{3,2},{4,3},{5,4},{6,5},{7,6},{8,7},{9,8},{10,9... | collective-permute-start | bytes 589832 | tf_op jit(solution)/shard_map/ppermute | solution.py:36
  10.1 5.3 %copy-start.4 = (bf16[1,3,64,512]{3,2,1,0:T(8,128)(2,1)S(1)}, bf16[1,3,64,512]{3,2,1,0:T(8,128)(2,1)}, u32[]{:S(2)}) copy-start(bf16[1,3,64,512]{3,2,1,0:T(8,128)(2,1)} %param.6) | copy-start | bytes 589828
  14.2 16.5 %collective-permute-start.4 = (bf16[4,3,64,256]{3,2,1,0:T(8,128)(2,1)}, bf16[4,3,64,256]{3,2,1,0:T(8,128)(2,1)S(1)}, u32[]{:S(2)}, u32[]{:S(2)}) collective-permute-start(bf16[4,3,64,256]{3,2,1,0:T(8,128)(2,1)} %get-tuple-element.38), channel_id=1, source_target_pairs={{0,2},{1,3},{2,0},{3,1},{4,6},{5,7},{6,4},{7,5},{8,10},{9,11},{10,... | collective-permute-start | bytes 1179656 | tf_op jit(solution)/shard_map/ppermute | solution.py:36
  15.5 11.6 %copy-start.3 = (bf16[3,3,64,512]{3,2,1,0:T(8,128)(2,1)S(1)}, bf16[3,3,64,512]{3,2,1,0:T(8,128)(2,1)}, u32[]{:S(2)}) copy-start(bf16[3,3,64,512]{3,2,1,0:T(8,128)(2,1)} %refs_1_.5) | copy-start | bytes 1769476
  17.1 9.9 %collective-permute-start.2 = (bf16[3,72,512]{2,1,0:T(8,128)(2,1)S(1)}, bf16[3,72,512]{2,1,0:T(8,128)(2,1)S(1)}, u32[]{:S(2)}, u32[]{:S(2)}) collective-permute-start(bf16[3,72,512]{2,1,0:T(8,128)(2,1)S(1)} %get-tuple-element.34), channel_id=1, source_target_pairs={{32,0},{64,32},{96,64},{128,96},{160,128},{192,160},{224,192},{33,... | collective-permute-start | bytes 663560 | tf_op jit(solution)/shard_map/ppermute | solution.py:41
  19.9 2.3 %copy-start = (bf16[1,3,3,512,512]{4,3,2,1,0:T(8,128)(2,1)S(1)}, bf16[1,3,3,512,512]{4,3,2,1,0:T(8,128)(2,1)}, u32[]{:S(2)}) copy-start(bf16[1,3,3,512,512]{4,3,2,1,0:T(8,128)(2,1)} %param.5) | copy-start | bytes 14155780
  22.2 4.9 %copy-start.1 = (bf16[1,3,3,512,512]{4,3,2,1,0:T(8,128)(2,1)S(1)}, bf16[1,3,3,512,512]{4,3,2,1,0:T(8,128)(2,1)}, u32[]{:S(2)}) copy-start(bf16[1,3,3,512,512]{4,3,2,1,0:T(8,128)(2,1)} %param.5) | copy-start | bytes 14155780
  28.7 9.9 %collective-permute-start.3 = (bf16[3,72,512]{2,1,0:T(8,128)(2,1)S(1)}, bf16[3,72,512]{2,1,0:T(8,128)(2,1)S(1)}, u32[]{:S(2)}, u32[]{:S(2)}) collective-permute-start(bf16[3,72,512]{2,1,0:T(8,128)(2,1)S(1)} %get-tuple-element.36), channel_id=1, source_target_pairs={{32,0},{64,32},{96,64},{128,96},{160,128},{192,160},{224,192},{33,... | collective-permute-start | bytes 663560 | tf_op jit(solution)/shard_map/ppermute | solution.py:41
  31.9 20.8 %collective-permute-start.7 = (bf16[2,3,72,512]{3,2,1,0:T(8,128)(2,1)S(1)}, bf16[2,3,72,512]{3,2,1,0:T(8,128)(2,1)S(1)}, u32[]{:S(2)}, u32[]{:S(2)}) collective-permute-start(bf16[2,3,72,512]{3,2,1,0:T(8,128)(2,1)S(1)} %pad_maximum_fusion.both0), channel_id=1, source_target_pairs={{0,2},{1,3},{2,0},{3,1},{4,6},{5,7},{6,4},{7,5},{8,10},{9,11},{10,... | collective-permute-start | bytes 1327112 | tf_op jit(solution)/shard_map/ppermute | solution.py:36
  40.4 9.9 %collective-permute-start.5 = (bf16[3,72,512]{2,1,0:T(8,128)(2,1)S(1)}, bf16[3,72,512]{2,1,0:T(8,128)(2,1)S(1)}, u32[]{:S(2)}, u32[]{:S(2)}) collective-permute-start(bf16[3,72,512]{2,1,0:T(8,128)(2,1)S(1)} %get-tuple-element.40), channel_id=1, source_target_pairs={{32,0},{64,32},{96,64},{128,96},{160,128},{192,160},{224,192},{33,... | collective-permute-start | bytes 663560 | tf_op jit(solution)/shard_map/ppermute | solution.py:41
  43.4 9.2 %collective-permute-start.8 = (bf16[3,72,512]{2,1,0:T(8,128)(2,1)S(1)}, bf16[3,72,512]{2,1,0:T(8,128)(2,1)S(1)}, u32[]{:S(2)}, u32[]{:S(2)}) collective-permute-start(bf16[3,72,512]{2,1,0:T(8,128)(2,1)S(1)} %get-tuple-element.47.third0), channel_id=1, source_target_pairs={{0,2},{1,3},{2,0},{3,1},{4,6},{5,7},{6,4},{7,5},{8,10},{9,11},{10,... | collective-permute-start | bytes 663560 | tf_op jit(solution)/shard_map/ppermute | solution.py:36
  50.4 6.2 %collective-permute-start.6 = (bf16[3,72,512]{2,1,0:T(8,128)(2,1)S(1)}, bf16[3,72,512]{2,1,0:T(8,128)(2,1)S(1)}, u32[]{:S(2)}, u32[]{:S(2)}) collective-permute-start(bf16[3,72,512]{2,1,0:T(8,128)(2,1)S(1)} %shard_map.68.g0), channel_id=1, source_target_pairs={{0,2},{1,3},{2,0},{3,1},{4,6},{5,7},{6,4},{7,5},{8,10},{9,11},{10,... | collective-permute-start | bytes 663560 | tf_op jit(solution)/shard_map/ppermute | solution.py:36
  57.7 2.4 %collective-permute-start.9 = (bf16[2,4,6,16,512]{4,3,2,1,0:T(8,128)(2,1)S(1)}, bf16[2,4,6,16,512]{4,3,2,1,0:T(8,128)(2,1)S(1)}, u32[]{:S(2)}, u32[]{:S(2)}) collective-permute-start(bf16[2,4,6,16,512]{4,3,2,1,0:T(8,128)(2,1)S(1)} %get-tuple-element.51), channel_id=1, source_target_pairs={{0,1},{1,0},{2,3},{3,2},{4,5},{5,4},{6,7},{7,6},{8,9},{9,8},{10,11... | collective-permute-start | bytes 2359304 | tf_op jit(solution)/shard_map/ppermute | solution.py:36
  60.2 1.8 %collective-permute-start.10 = (bf16[4,2,3,16,512]{4,3,2,1,0:T(8,128)(2,1)S(1)}, bf16[4,2,3,16,512]{4,3,2,1,0:T(8,128)(2,1)S(1)}, u32[]{:S(2)}, u32[]{:S(2)}) collective-permute-start(bf16[4,2,3,16,512]{4,3,2,1,0:T(8,128)(2,1)S(1)} %get-tuple-element.52), channel_id=1, source_target_pairs={{0,1},{1,0},{2,3},{3,2},{4,5},{5,4},{6,7},{7,6},{8,9},{9,8},{10,11... | collective-permute-start | bytes 1179656 | tf_op jit(solution)/shard_map/ppermute | solution.py:36
  60.4 13.0 %collective-permute-start.11 = (bf16[4,6,16,512]{3,2,1,0:T(8,128)(2,1)S(1)}, bf16[4,6,16,512]{3,2,1,0:T(8,128)(2,1)S(1)}, u32[]{:S(2)}, u32[]{:S(2)}) collective-permute-start(bf16[4,6,16,512]{3,2,1,0:T(8,128)(2,1)S(1)} %fusion.1), channel_id=1, source_target_pairs={{0,16},{1,17},{2,18},{3,19},{4,20},{5,21},{6,22},{7,23},{8,24},{9,... | collective-permute-start | bytes 1179656 | tf_op jit(solution)/shard_map/ppermute | solution.py:36
  62.1 18.2 %collective-permute-start.17 = (bf16[2,3,16,512]{3,2,1,0:T(8,128)(2,1)S(1)}, bf16[2,3,16,512]{3,2,1,0:T(8,128)(2,1)S(1)}, u32[]{:S(2)}, u32[]{:S(2)}) collective-permute-start(bf16[2,3,16,512]{3,2,1,0:T(8,128)(2,1)S(1)} %get-tuple-element.60), channel_id=1, source_target_pairs={{0,12},{1,13},{2,14},{3,15},{4,0},{5,1},{6,2},{7,3},{8,4},{9,5},{1... | collective-permute-start | bytes 294920 | tf_op jit(solution)/shard_map/ppermute | solution.py:36
  69.0 13.6 %collective-permute-start.15 = (bf16[2,3,16,512]{3,2,1,0:T(8,128)(2,1)S(1)}, bf16[2,3,16,512]{3,2,1,0:T(8,128)(2,1)S(1)}, u32[]{:S(2)}, u32[]{:S(2)}) collective-permute-start(bf16[2,3,16,512]{3,2,1,0:T(8,128)(2,1)S(1)} %get-tuple-element.61), channel_id=1, source_target_pairs={{0,8},{1,9},{2,10},{3,11},{4,12},{5,13},{6,14},{7,15},{8,0},{9,1},... | collective-permute-start | bytes 294920 | tf_op jit(solution)/shard_map/ppermute | solution.py:36
  70.7 11.9 %collective-permute-start.16 = (bf16[2,3,16,512]{3,2,1,0:T(8,128)(2,1)S(1)}, bf16[2,3,16,512]{3,2,1,0:T(8,128)(2,1)S(1)}, u32[]{:S(2)}, u32[]{:S(2)}) collective-permute-start(bf16[2,3,16,512]{3,2,1,0:T(8,128)(2,1)S(1)} %get-tuple-element.62), channel_id=1, source_target_pairs={{0,4},{1,5},{2,6},{3,7},{4,8},{5,9},{6,10},{7,11},{8,12},{9,13},{1... | collective-permute-start | bytes 294920 | tf_op jit(solution)/shard_map/ppermute | solution.py:36
  73.6 11.9 %collective-permute-start.12 = (bf16[6,16,512]{2,1,0:T(8,128)(2,1)S(1)}, bf16[6,16,512]{2,1,0:T(8,128)(2,1)S(1)}, u32[]{:S(2)}, u32[]{:S(2)}) collective-permute-start(bf16[6,16,512]{2,1,0:T(8,128)(2,1)S(1)} %get-tuple-element.63), channel_id=1, source_target_pairs={{0,4},{1,5},{2,6},{3,7},{4,8},{5,9},{6,10},{7,11},{8,12},{9,13},{1... | collective-permute-start | bytes 294920 | tf_op jit(solution)/shard_map/ppermute | solution.py:36
  77.5 8.0 %collective-permute-start.14 = (bf16[6,16,512]{2,1,0:T(8,128)(2,1)S(1)}, bf16[6,16,512]{2,1,0:T(8,128)(2,1)S(1)}, u32[]{:S(2)}, u32[]{:S(2)}) collective-permute-start(bf16[6,16,512]{2,1,0:T(8,128)(2,1)S(1)} %get-tuple-element.64), channel_id=1, source_target_pairs={{0,12},{1,13},{2,14},{3,15},{4,0},{5,1},{6,2},{7,3},{8,4},{9,5},{1... | collective-permute-start | bytes 294920 | tf_op jit(solution)/shard_map/ppermute | solution.py:36
  80.3 11.2 %collective-permute-start.13 = (bf16[6,16,512]{2,1,0:T(8,128)(2,1)S(1)}, bf16[6,16,512]{2,1,0:T(8,128)(2,1)S(1)}, u32[]{:S(2)}, u32[]{:S(2)}) collective-permute-start(bf16[6,16,512]{2,1,0:T(8,128)(2,1)S(1)} %get-tuple-element.65), channel_id=1, source_target_pairs={{0,8},{1,9},{2,10},{3,11},{4,12},{5,13},{6,14},{7,15},{8,0},{9,1},... | collective-permute-start | bytes 294920 | tf_op jit(solution)/shard_map/ppermute | solution.py:36
  82.7 8.9 %collective-permute-start.18 = (bf16[3,16,512]{2,1,0:T(8,128)(2,1)S(1)}, bf16[3,16,512]{2,1,0:T(8,128)(2,1)S(1)}, u32[]{:S(2)}, u32[]{:S(2)}) collective-permute-start(bf16[3,16,512]{2,1,0:T(8,128)(2,1)S(1)} %slice_bitcast_fusion.8), channel_id=1, source_target_pairs={{0,16},{1,17},{2,18},{3,19},{4,20},{5,21},{6,22},{7,23},{8,24},{9,... | collective-permute-start | bytes 147464 | tf_op jit(solution)/shard_map/ppermute | solution.py:36

commit v4 on v3

--- a/solution.py
+++ b/solution.py
@@ -225,13 +225,15 @@
     source = ((far * 4 + turn) * 4 + chip * 2 + core) * 16 + lane % 16
     row = lax.broadcasted_iota(jnp.int32, (CH, CH), 0)
     order = jnp.where(row == source[:1], 1.0, 0.0).astype(BF)
-    for t in range(STEPS):
-        copies[t].wait()
-        field = jnp.concatenate([field_ref[t, r] for r in range(ROWS)], axis=0)
-        value = jnp.dot(field, order, preferred_element_type=F32).astype(BF)
-        for n, out in enumerate((out0, out1)):
+    for copy in copies[:STEPS]:
+        copy.wait()
+    field = jnp.concatenate([field_ref[t, r] for t in range(STEPS) for r in range(ROWS)], axis=0)
+    value = jnp.dot(field, order, preferred_element_type=F32).astype(BF)
+    for n, out in enumerate((out0, out1)):
+        for t in range(STEPS):
             for r in range(ROWS):
-                out[t, r] = value[r * WIDTH : (r + 1) * WIDTH, n * HALF : (n + 1) * HALF]
+                at = (t * ROWS + r) * WIDTH
+                out[t, r] = value[at : at + WIDTH, n * HALF : (n + 1) * HALF]
     copies[STEPS].wait()
 
 
@@ -309,14 +311,14 @@
                     for turn in range(4):
                         at = ((core * 2 + far) * 4 + turn) * 16
                         part = value[at : at + 16, b * CH : (b + 1) * CH].astype(BF)
-                        if tap < FIRST:
-                            outs[core][far, turn, tap] = part
+                        if tap >= FIRST:
+                            outs[4 + core][turn, far, tap - FIRST] = part
                         else:
-                            outs[2 + core][turn, far, tap - FIRST] = part
+                            outs[2 * far + core][turn, tap] = part
 
 
 def late_products(xs, gs, total):
-    shapes = [(2, 4, FIRST, 16, CH)] * 2 + [(4, 2, 9 - FIRST, 16, CH)] * 2
+    shapes = [(4, FIRST, 16, CH)] * 4 + [(4, 2, 9 - FIRST, 16, CH)] * 2
     return pl.pallas_call(
         late_kernel,
         grid=(1,),
@@ -324,7 +326,7 @@
         in_specs=[block((1, ROWS, WIDTH, HALF), STEPS - 1, 0, 0, 0)] * 2
         + [block((ROWS, WIDE, CH), 0, 0, 0)] * 2
         + [block((3, HALF, 3 * CH), 0, 0, 0)],
-        out_specs=tuple(block(shape, 0, 0, 0, 0, 0) for shape in shapes),
+        out_specs=tuple(block(shape, *(0,) * len(shape)) for shape in shapes),
         compiler_params=params(),
         cost_estimate=cost(1e9, 8e6),
     )(*xs, *gs, total)
@@ -407,15 +409,16 @@
         fields.append(own if t == 0 else (own, send(own, PAIR)))
 
     total = early_products(xs, *fields[0], *fields[1])
-    mine, other, mine_b, other_b = late_products(xs, fields[-1], total)
-    other = send(other, CORE)
-    near = [total_of(mine[m], other[m]).astype(BF) for m in range(2)]
-    far = send(near[1], FAR)
-    other_b = send(after(other_b, near[1]), CORE)
-    turns = [total_of(mine_b[m], other_b[m]).astype(BF) for m in range(4)]
-    arrived = after(arrived, turns[1], turns[2], turns[3])
+    near, near_other, out_going, out_other, turns, turns_other = late_products(xs, fields[-1], total)
+    out_going = total_of(out_going, send(out_other, CORE)).astype(BF)
+    far = send(out_going, FAR)
+    turns_other, near_other = lax.optimization_barrier((turns_other, near_other, out_going))[:2]
+    turns_other, near_other = send(turns_other, CORE), send(near_other, CORE)
+    turns = [total_of(turns[m], turns_other[m]).astype(BF) for m in range(4)]
+    arrived = after(arrived, *turns[1:])
     arriving = (send(turns[2], ACROSS), send(turns[1], UP), send(turns[3], DOWN))
-    near = total_of(near[0], far).astype(BF)
+    near = total_of(near, near_other).astype(BF)
+    near = total_of(near, far).astype(BF)
     across, ups, downs = send(near[2], ACROSS), send(near[1], UP), send(near[3], DOWN)
     arriving = lax.optimization_barrier((*arriving, near))[:3]
     turned = total_of(turns[0], *arriving).astype(BF)

time: 92.6 us -> 91.9 us (level)
    ppermute x16 -> x17, waiting for transfers between devices: 10.6 us -> 9.77 us  [send(): return lax.ppermute(block, 'az', route)]
    ppermute x16 -> x17, starting transfers between devices: 35.8 us -> 35.9 us  [send(): return lax.ppermute(block, 'az', route)]
  transfers between devices with their start and end apart: 19 -> 20, of which waited for: 8 -> 8; matrix products, arithmetic and copies ran while one was open for 2% -> 2% of each run, Pallas kernels for 20% -> 20%
where the time goes in v4:
time: 91.9 us; the launch traced here: 91.7 us
  starting transfers between devices  42.5 us (46%)
  waiting for transfers between devices  23 us (25%)
  Pallas kernels  20.4 us (22%)
  local copies, waits for them, and re-layouts  2.44 us (3%)
  other arithmetic  2.34 us (3%)
  between operations  0.96 us (1%)
    ppermute x17, starting transfers between devices, send(): return lax.ppermute(block, 'az', route)  35.9 us
    ppermute x3, waiting for transfers between devices, relay(): return lax.ppermute(block, 'segment', [(i, i - 1) for i in range(1, count)])  13.2 us
    ppermute x17, waiting for transfers between devices, send(): return lax.ppermute(block, 'az', route)  9.77 us
    pallas_call x4, Pallas kernels, back_step(): pl.pallas_call(lambda *refs: back_kernel(first, *refs), grid=(1,), out_sh...  6.65 us
    ppermute x3, starting transfers between devices, relay(): return lax.ppermute(block, 'segment', [(i, i - 1) for i in range(1, count)])  6.57 us
    pallas_call x4, Pallas kernels, slope_factors(): pl.pallas_call(factor_kernel, grid=(1,), out_shape=jax.ShapeDtypeStruct((...  4.5 us
    pallas_call x1, Pallas kernels, spread(): pl.pallas_call(spread_kernel, out_shape=(shape, shape, pltpu.VMEM(weights...  4.04 us
    pallas_call x1, Pallas kernels, early_products(): pl.pallas_call(early_kernel, out_shape=jax.ShapeDtypeStruct((3, HALF, 3 *...  2.75 us
  transfers between devices with their start and end apart: 20, of which 8 were waited for; matrix products, arithmetic and copies ran while one was open for 2% of the time, Pallas kernels for 20%

profile of v4, /device:TPU:6, one launch (start us, length us, event | category | flops | bytes accessed | tf_op | source)
XLA Modules:
  0.0 91.7 jit_solution(13166305522953605063)
XLA Ops:
  0.6 1.3 %shard_map.59 = (bf16[24,8,512]{2,1,0:T(8,128)(2,1)S(1)}, bf16[24,8,512]{2,1,0:T(8,128)(2,1)S(1)}) custom-call(bf16[4,3,64,512]{3,2,1,0:T(8,128)(2,1)} %bitcast.59, bf16[3,64,512]{2,1,0:T(8,128)(2,1)} %bitcast.66, bf16[3,3,64,512]{3,2,1,0:T(8,128)(2,1)} %refs_1_.5, bf16[4,3,64,512]{3,2,1,0:T(8,128)(2,1)} %bitcast.60, bf16[3,64,512]{2,1,0:T(8,128)(2,1)} %bitcast.67, ...), custom_call_target="tpu_custom_call" | custom-call | bytes 1048576 | tf_op jit(solution)/shard_map/pallas_call | solution.py:79
  2.0 0.1 collective-permute-start
  2.1 8.0 %collective-permute-start.1 = (bf16[24,8,512]{2,1,0:T(8,128)(2,1)S(1)}, bf16[24,8,512]{2,1,0:T(8,128)(2,1)S(1)}, u32[]{:S(2)}, u32[]{:S(2)}) collective-permute-start(bf16[24,8,512]{2,1,0:T(8,128)(2,1)S(1)} %get-tuple-element.34), channel_id=1, source_target_pairs={{0,31},{1,0},{2,1},{3,2},{4,3},{5,4},{6,5},{7,6},{8,7},{9,8},{10,9... | collective-permute-start | bytes 589832 | tf_op jit(solution)/shard_map/ppermute | solution.py:36
  10.1 0.1 pad_add_fusion.place_ref
  10.1 4.0 %shard_map.60 = (bf16[4,3,64,256]{3,2,1,0:T(8,128)(2,1)S(1)}, bf16[4,3,64,256]{3,2,1,0:T(8,128)(2,1)}, bf16[9,512,512]{2,1,0:T(8,128)(2,1)S(1)}) custom-call(s32[4]{0:T(128)S(1)} %pad_add_fusion.place_ref, bf16[4,3,64,512]{3,2,1,0:T(8,128)(2,1)} %bitcast.61, bf16[9,512,512]{2,1,0:T(8,128)(2,1)} %bitcast.52), custom_call_target="tpu_custom_call" | custom-call | flops 450000000 | bytes 12000000 | tf_op jit(solution)/shard_map/pallas_call | solution.py:243
  14.2 0.1 collective-permute-start.4
  14.3 1.1 %shard_map.61.refs_3_ = f32[1,3,72,512]{3,2,1,0:T(8,128)S(1)} custom-call(bf16[4,3,64,512]{3,2,1,0:T(8,128)(2,1)S(1)} %bitcast.62, bf16[24,8,512]{2,1,0:T(8,128)(2,1)S(1)} %collective-permute-done.low_ref.refs_1_.refs_2_, bf16[24,8,512]{2,1,0:T(8,128)(2,1)S(1)} %collective-permute-done.1.high_ref.refs_2_.refs_3_, ...), custom_call_target="tpu_custom_call" | custom-call | flops 1200000000 | bytes 5000000 | tf_op jit(solution)/shard_map/pallas_call | solution.py:132
  15.5 1.7 %shard_map.62 = (bf16[3,72,512]{2,1,0:T(8,128)(2,1)S(1)}, bf16[3,72,512]{2,1,0:T(8,128)(2,1)S(1)}) custom-call(bf16[3,64,512]{2,1,0:T(8,128)(2,1)S(1)} %bitcast.68, bf16[24,8,512]{2,1,0:T(8,128)(2,1)S(1)} %collective-permute-done.low_ref.refs_1_.refs_2_, bf16[24,8,512]{2,1,0:T(8,128)(2,1)S(1)} %collective-permute-done.1.high_ref.refs_2_.refs_3_, ...), custom_call_target="tpu_custom_call" | custom-call | flops 1100000000 | bytes 6000000 | tf_op jit(solution)/shard_map/pallas_call | solution.py:200
  17.1 2.7 %collective-permute-start.2 = (bf16[3,72,512]{2,1,0:T(8,128)(2,1)S(1)}, bf16[3,72,512]{2,1,0:T(8,128)(2,1)S(1)}, u32[]{:S(2)}, u32[]{:S(2)}) collective-permute-start(bf16[3,72,512]{2,1,0:T(8,128)(2,1)S(1)} %get-tuple-element.37), channel_id=1, source_target_pairs={{32,0},{64,32},{96,64},{128,96},{160,128},{192,160},{224,192},{33,... | collective-permute-start | bytes 663560 | tf_op jit(solution)/shard_map/ppermute | solution.py:41
  19.9 2.3 %copy-done = bf16[1,3,3,512,512]{4,3,2,1,0:T(8,128)(2,1)S(1)} copy-done((bf16[1,3,3,512,512]{4,3,2,1,0:T(8,128)(2,1)S(1)}, bf16[1,3,3,512,512]{4,3,2,1,0:T(8,128)(2,1)}, u32[]{:S(2)}) %copy-start) | copy-done | bytes 4718616
  22.2 1.1 %shard_map.63.refs_5_ = f32[1,3,72,512]{3,2,1,0:T(8,128)S(1)} custom-call(bf16[4,3,64,512]{3,2,1,0:T(8,128)(2,1)S(1)} %bitcast.63, bf16[24,8,512]{2,1,0:T(8,128)(2,1)S(1)} %collective-permute-done.low_ref.refs_1_.refs_2_, bf16[24,8,512]{2,1,0:T(8,128)(2,1)S(1)} %collective-permute-done.1.high_ref.refs_2_.refs_3_, bf16[9,512,512]{2,1,0:T(8,128)(2,1)S(1)} %bitcast.53), custom_call_target="tpu_custom_call" | custom-call | flops 1200000000 | bytes 5000000 | tf_op jit(solution)/shard_map/pallas_call | solution.py:132
  23.4 3.7 %collective-permute-done.2.refs_4_ = bf16[3,72,512]{2,1,0:T(8,128)(2,1)S(1)} collective-permute-done((bf16[3,72,512]{2,1,0:T(8,128)(2,1)S(1)}, bf16[3,72,512]{2,1,0:T(8,128)(2,1)S(1)}, u32[]{:S(2)}, u32[]{:S(2)}) %collective-permute-start.2) | collective-permute-done | bytes 221216 | tf_op jit(solution)/shard_map/ppermute | solution.py:41
  27.1 1.7 %shard_map.64 = (bf16[3,72,512]{2,1,0:T(8,128)(2,1)S(1)}, bf16[3,72,512]{2,1,0:T(8,128)(2,1)S(1)}) custom-call(s32[1]{0:T(128)} %bitcast.8.refs_0_.flag_ref, bf16[3,3,64,512]{3,2,1,0:T(8,128)(2,1)S(1)} %copy-done.3, bf16[24,8,512]{2,1,0:T(8,128)(2,1)S(1)} %collective-permute-done.low_ref.refs_1_.refs_2_, ...), custom_call_target="tpu_custom_call" | custom-call | flops 1100000000 | bytes 6000000 | tf_op jit(solution)/shard_map/pallas_call | solution.py:200
  28.7 1.9 %collective-permute-start.3 = (bf16[3,72,512]{2,1,0:T(8,128)(2,1)S(1)}, bf16[3,72,512]{2,1,0:T(8,128)(2,1)S(1)}, u32[]{:S(2)}, u32[]{:S(2)}) collective-permute-start(bf16[3,72,512]{2,1,0:T(8,128)(2,1)S(1)} %get-tuple-element.39), channel_id=1, source_target_pairs={{32,0},{64,32},{96,64},{128,96},{160,128},{192,160},{224,192},{33,... | collective-permute-start | bytes 663560 | tf_op jit(solution)/shard_map/ppermute | solution.py:41
  30.7 1.1 %shard_map.65.refs_5_ = f32[1,3,72,512]{3,2,1,0:T(8,128)S(1)} custom-call(bf16[4,3,64,512]{3,2,1,0:T(8,128)(2,1)S(1)} %bitcast.64, bf16[24,8,512]{2,1,0:T(8,128)(2,1)S(1)} %collective-permute-done.low_ref.refs_1_.refs_2_, bf16[24,8,512]{2,1,0:T(8,128)(2,1)S(1)} %collective-permute-done.1.high_ref.refs_2_.refs_3_, bf16[9,512,512]{2,1,0:T(8,128)(2,1)S(1)} %bitcast.55), custom_call_target="tpu_custom_call" | custom-call | flops 1200000000 | bytes 5000000 | tf_op jit(solution)/shard_map/pallas_call | solution.py:132
  31.9 2.1 %collective-permute-start.7 = (bf16[2,3,72,512]{3,2,1,0:T(8,128)(2,1)S(1)}, bf16[2,3,72,512]{3,2,1,0:T(8,128)(2,1)S(1)}, u32[]{:S(2)}, u32[]{:S(2)}) collective-permute-start(bf16[2,3,72,512]{3,2,1,0:T(8,128)(2,1)S(1)} %pad_maximum_fusion.both0), channel_id=1, source_target_pairs={{0,2},{1,3},{2,0},{3,1},{4,6},{5,7},{6,4},{7,5},{8,10},{9,11},{10,... | collective-permute-start | bytes 1327112 | tf_op jit(solution)/shard_map/ppermute | solution.py:36
  33.9 4.7 %collective-permute-done.3.refs_4_ = bf16[3,72,512]{2,1,0:T(8,128)(2,1)S(1)} collective-permute-done((bf16[3,72,512]{2,1,0:T(8,128)(2,1)S(1)}, bf16[3,72,512]{2,1,0:T(8,128)(2,1)S(1)}, u32[]{:S(2)}, u32[]{:S(2)}) %collective-permute-start.3) | collective-permute-done | bytes 221216 | tf_op jit(solution)/shard_map/ppermute | solution.py:41
  38.7 1.7 %shard_map.66 = (bf16[3,72,512]{2,1,0:T(8,128)(2,1)S(1)}, bf16[3,72,512]{2,1,0:T(8,128)(2,1)S(1)}) custom-call(s32[1]{0:T(128)} %bitcast.8.refs_0_.flag_ref, bf16[3,3,64,512]{3,2,1,0:T(8,128)(2,1)S(1)} %copy-done.3, bf16[24,8,512]{2,1,0:T(8,128)(2,1)S(1)} %collective-permute-done.low_ref.refs_1_.refs_2_, ...), custom_call_target="tpu_custom_call" | custom-call | flops 1100000000 | bytes 6000000 | tf_op jit(solution)/shard_map/pallas_call | solution.py:200
  40.4 1.9 %collective-permute-start.5 = (bf16[3,72,512]{2,1,0:T(8,128)(2,1)S(1)}, bf16[3,72,512]{2,1,0:T(8,128)(2,1)S(1)}, u32[]{:S(2)}, u32[]{:S(2)}) collective-permute-start(bf16[3,72,512]{2,1,0:T(8,128)(2,1)S(1)} %get-tuple-element.43), channel_id=1, source_target_pairs={{32,0},{64,32},{96,64},{128,96},{160,128},{192,160},{224,192},{33,... | collective-permute-start | bytes 663560 | tf_op jit(solution)/shard_map/ppermute | solution.py:41
  42.3 1.1 %shard_map.67.factor_ref.refs_5_ = f32[1,3,72,512]{3,2,1,0:T(8,128)S(1)} custom-call(bf16[4,3,64,512]{3,2,1,0:T(8,128)(2,1)S(1)} %bitcast.65, bf16[24,8,512]{2,1,0:T(8,128)(2,1)S(1)} %collective-permute-done.low_ref.refs_1_.refs_2_, bf16[24,8,512]{2,1,0:T(8,128)(2,1)S(1)} %collective-permute-done.1.high_ref.refs_2_.refs_3_, bf16[9,512,512]{2,1,0:T(8,128)(2,1)S(1)} %bitcast.57), custom_call_target="tpu_custom_call" | custom-call | flops 1200000000 | bytes 5000000 | tf_op jit(solution)/shard_map/pallas_call | solution.py:132
  43.4 2.1 %collective-permute-start.8 = (bf16[3,72,512]{2,1,0:T(8,128)(2,1)S(1)}, bf16[3,72,512]{2,1,0:T(8,128)(2,1)S(1)}, u32[]{:S(2)}, u32[]{:S(2)}) collective-permute-start(bf16[3,72,512]{2,1,0:T(8,128)(2,1)S(1)} %get-tuple-element.50.third0), channel_id=1, source_target_pairs={{0,2},{1,3},{2,0},{3,1},{4,6},{5,7},{6,4},{7,5},{8,10},{9,11},{10,... | collective-permute-start | bytes 663560 | tf_op jit(solution)/shard_map/ppermute | solution.py:36
  45.5 4.8 %collective-permute-done.5.relay_ref.refs_4_ = bf16[3,72,512]{2,1,0:T(8,128)(2,1)S(1)} collective-permute-done((bf16[3,72,512]{2,1,0:T(8,128)(2,1)S(1)}, bf16[3,72,512]{2,1,0:T(8,128)(2,1)S(1)}, u32[]{:S(2)}, u32[]{:S(2)}) %collective-permute-start.5) | collective-permute-done | bytes 221216 | tf_op jit(solution)/shard_map/ppermute | solution.py:41
  50.4 2.3 %collective-permute-start.6 = (bf16[3,72,512]{2,1,0:T(8,128)(2,1)S(1)}, bf16[3,72,512]{2,1,0:T(8,128)(2,1)S(1)}, u32[]{:S(2)}, u32[]{:S(2)}) collective-permute-start(bf16[3,72,512]{2,1,0:T(8,128)(2,1)S(1)} %shard_map.68.g0), channel_id=1, source_target_pairs={{0,2},{1,3},{2,0},{3,1},{4,6},{5,7},{6,4},{7,5},{8,10},{9,11},{10,... | collective-permute-start | bytes 663560 | tf_op jit(solution)/shard_map/ppermute | solution.py:36
  52.6 2.7 %shard_map.69.total_ref = f32[3,256,1536]{2,1,0:T(8,128)S(1)} custom-call(bf16[4,3,64,256]{3,2,1,0:T(8,128)(2,1)S(1)} %get-tuple-element.40.x0, bf16[4,3,64,256]{3,2,1,0:T(8,128)(2,1)S(1)} %collective-permute-done.4.x1, bf16[2,3,72,512]{3,2,1,0:T(8,128)(2,1)S(1)} %pad_maximum_fusion.both0, bf16[2,3,72,512]{3,2,1,0:T(8,128)(2,1)S(1)} %collective-permute-done.7.both1, ...), custom_call_target="tpu_custom_call" | custom-call | flops 3000000000 | bytes 8000000 | tf_op jit(solution)/shard_map/pallas_call | solution.py:291
  55.4 1.2 %collective-permute-done.6.g1 = bf16[3,72,512]{2,1,0:T(8,128)(2,1)S(1)} collective-permute-done((bf16[3,72,512]{2,1,0:T(8,128)(2,1)S(1)}, bf16[3,72,512]{2,1,0:T(8,128)(2,1)S(1)}, u32[]{:S(2)}, u32[]{:S(2)}) %collective-permute-start.6) | collective-permute-done | bytes 221216 | tf_op jit(solution)/shard_map/ppermute | solution.py:36
  56.6 1.1 %shard_map.70 = (bf16[4,6,16,512]{3,2,1,0:T(8,128)(2,1)S(1)}, bf16[4,6,16,512]{3,2,1,0:T(8,128)(2,1)S(1)}, bf16[4,6,16,512]{3,2,1,0:T(8,128)(2,1)S(1)}, bf16[4,6...) custom-call(bf16[4,3,64,256]{3,2,1,0:T(8,128)(2,1)S(1)} %get-tuple-elem, ...), custom_call_target="tpu_custom_call" | custom-call | flops 1000000000 | bytes 8000000 | tf_op jit(solution)/shard_map/pallas_call | solution.py:322
  57.7 0.1 collective-permute-start.9
  57.8 1.7 %collective-permute-done.9 = bf16[4,6,16,512]{3,2,1,0:T(8,128)(2,1)S(1)} collective-permute-done((bf16[4,6,16,512]{3,2,1,0:T(8,128)(2,1)S(1)}, bf16[4,6,16,512]{3,2,1,0:T(8,128)(2,1)S(1)}, u32[]{:S(2)}, u32[]{:S(2)}) %collective-permute-start.9) | collective-permute-done | bytes 393248 | tf_op jit(solution)/shard_map/ppermute | solution.py:36
  59.5 0.1 add_convert_fusion.2
  59.6 0.2 collective-permute-start.10
  59.9 0.6 collective-permute-start.12
  60.5 0.1 collective-permute-start.11
  60.6 0.8 collective-permute-done.10
  61.4 0.1 fusion.8
  61.5 7.0 %collective-permute-start.18 = (bf16[2,3,16,512]{3,2,1,0:T(8,128)(2,1)S(1)}, bf16[2,3,16,512]{3,2,1,0:T(8,128)(2,1)S(1)}, u32[]{:S(2)}, u32[]{:S(2)}) collective-permute-start(bf16[2,3,16,512]{3,2,1,0:T(8,128)(2,1)S(1)} %get-tuple-element.66), channel_id=1, source_target_pairs={{0,12},{1,13},{2,14},{3,15},{4,0},{5,1},{6,2},{7,3},{8,4},{9,5},{1... | collective-permute-start | bytes 294920 | tf_op jit(solution)/shard_map/ppermute | solution.py:36
  68.5 1.6 %collective-permute-start.16 = (bf16[2,3,16,512]{3,2,1,0:T(8,128)(2,1)S(1)}, bf16[2,3,16,512]{3,2,1,0:T(8,128)(2,1)S(1)}, u32[]{:S(2)}, u32[]{:S(2)}) collective-permute-start(bf16[2,3,16,512]{3,2,1,0:T(8,128)(2,1)S(1)} %get-tuple-element.67), channel_id=1, source_target_pairs={{0,8},{1,9},{2,10},{3,11},{4,12},{5,13},{6,14},{7,15},{8,0},{9,1},... | collective-permute-start | bytes 294920 | tf_op jit(solution)/shard_map/ppermute | solution.py:36
  70.2 0.8 collective-permute-start.17
  71.0 1.7 %shard_map.71 = (bf16[3,72,512]{2,1,0:T(8,128)(2,1)S(1)}, bf16[3,72,512]{2,1,0:T(8,128)(2,1)}) custom-call(s32[1]{0:T(128)} %bitcast.8.refs_0_.flag_ref, bf16[3,3,64,512]{3,2,1,0:T(8,128)(2,1)S(1)} %copy-done.3, bf16[24,8,512]{2,1,0:T(8,128)(2,1)S(1)} %collective-permute-done.low_ref.refs_1_.refs_2_, ...), custom_call_target="tpu_custom_call" | custom-call | flops 1100000000 | bytes 6000000 | tf_op jit(solution)/shard_map/pallas_call | solution.py:200
  72.7 0.2 collective-permute-done.12
  72.8 0.2 add_convert_fusion
  73.1 4.0 %collective-permute-start.13 = (bf16[6,16,512]{2,1,0:T(8,128)(2,1)S(1)}, bf16[6,16,512]{2,1,0:T(8,128)(2,1)S(1)}, u32[]{:S(2)}, u32[]{:S(2)}) collective-permute-start(bf16[6,16,512]{2,1,0:T(8,128)(2,1)S(1)} %get-tuple-element.69), channel_id=1, source_target_pairs={{0,4},{1,5},{2,6},{3,7},{4,8},{5,9},{6,10},{7,11},{8,12},{9,13},{1... | collective-permute-start | bytes 294920 | tf_op jit(solution)/shard_map/ppermute | solution.py:36
  77.0 1.7 %collective-permute-start.15 = (bf16[6,16,512]{2,1,0:T(8,128)(2,1)S(1)}, bf16[6,16,512]{2,1,0:T(8,128)(2,1)S(1)}, u32[]{:S(2)}, u32[]{:S(2)}) collective-permute-start(bf16[6,16,512]{2,1,0:T(8,128)(2,1)S(1)} %get-tuple-element.70), channel_id=1, source_target_pairs={{0,12},{1,13},{2,14},{3,15},{4,0},{5,1},{6,2},{7,3},{8,4},{9,5},{1... | collective-permute-start | bytes 294920 | tf_op jit(solution)/shard_map/ppermute | solution.py:36
  78.7 1.0 %maximum_bitcast_fusion = bf16[4,1,3,64,512]{4,3,2,1,0:T(8,128)(2,1)} fusion(bf16[1,3,64,512]{3,2,1,0:T(8,128)(2,1)S(1)} %slice_bitcast_fusion, bf16[1,3,64,512]{3,2,1,0:T(8,128)(2,1)S(1)} %slice_bitcast_fusion.1, bf16[1,3,64,512]{3,2,1,0:T(8,128)(2,1)S(1)} %slice_bitcast_fusion.2, bf16[1,3,64,512]{3,2,1,0:T(8,128)(2,1)S(1)} %slice_bitcast_fusion.3), kind=kLoop, calls=%fused_computation | loop fusion | flops 1179648 | bytes 1572864
  79.7 2.3 %collective-permute-start.14 = (bf16[6,16,512]{2,1,0:T(8,128)(2,1)S(1)}, bf16[6,16,512]{2,1,0:T(8,128)(2,1)S(1)}, u32[]{:S(2)}, u32[]{:S(2)}) collective-permute-start(bf16[6,16,512]{2,1,0:T(8,128)(2,1)S(1)} %get-tuple-element.71), channel_id=1, source_target_pairs={{0,8},{1,9},{2,10},{3,11},{4,12},{5,13},{6,14},{7,15},{8,0},{9,1},... | collective-permute-start | bytes 294920 | tf_op jit(solution)/shard_map/ppermute | solution.py:36
  82.0 0.1 fusion.3
  82.1 2.9 %collective-permute-start.19 = (bf16[3,16,512]{2,1,0:T(8,128)(2,1)S(1)}, bf16[3,16,512]{2,1,0:T(8,128)(2,1)S(1)}, u32[]{:S(2)}, u32[]{:S(2)}) collective-permute-start(bf16[3,16,512]{2,1,0:T(8,128)(2,1)S(1)} %slice_bitcast_fusion.8), channel_id=1, source_target_pairs={{0,16},{1,17},{2,18},{3,19},{4,20},{5,21},{6,22},{7,23},{8,24},{9,... | collective-permute-start | bytes 147464 | tf_op jit(solution)/shard_map/ppermute | solution.py:36
  85.0 5.9 %collective-permute-done.14 = bf16[6,16,512]{2,1,0:T(8,128)(2,1)S(1)} collective-permute-done((bf16[6,16,512]{2,1,0:T(8,128)(2,1)S(1)}, bf16[6,16,512]{2,1,0:T(8,128)(2,1)S(1)}, u32[]{:S(2)}, u32[]{:S(2)}) %collective-permute-start.14) | collective-permute-done | bytes 98336 | tf_op jit(solution)/shard_map/ppermute | solution.py:36
  91.0 0.7 fusion
  (31 shorter events, 0.3 us)
Async XLA Ops:
  0.6 13.7 %copy-start.2 = (bf16[4,1,3,64,512]{4,3,2,1,0:T(8,128)(2,1)S(1)}, bf16[4,1,3,64,512]{4,3,2,1,0:T(8,128)(2,1)}, u32[]{:S(2)}) copy-start(bf16[4,1,3,64,512]{4,3,2,1,0:T(8,128)(2,1)} %param.4) | copy-start | bytes 2359300
  2.0 12.3 %collective-permute-start = (bf16[24,8,512]{2,1,0:T(8,128)(2,1)S(1)}, bf16[24,8,512]{2,1,0:T(8,128)(2,1)S(1)}, u32[]{:S(2)}, u32[]{:S(2)}) collective-permute-start(bf16[24,8,512]{2,1,0:T(8,128)(2,1)S(1)} %get-tuple-element.33), channel_id=1, source_target_pairs={{0,1},{1,2},{2,3},{3,4},{4,5},{5,6},{6,7},{7,8},{8,9},{9,10},{10,1... | collective-permute-start | bytes 589832 | tf_op jit(solution)/shard_map/ppermute | solution.py:36
  2.1 12.2 %collective-permute-start.1 = (bf16[24,8,512]{2,1,0:T(8,128)(2,1)S(1)}, bf16[24,8,512]{2,1,0:T(8,128)(2,1)S(1)}, u32[]{:S(2)}, u32[]{:S(2)}) collective-permute-start(bf16[24,8,512]{2,1,0:T(8,128)(2,1)S(1)} %get-tuple-element.34), channel_id=1, source_target_pairs={{0,31},{1,0},{2,1},{3,2},{4,3},{5,4},{6,5},{7,6},{8,7},{9,8},{10,9... | collective-permute-start | bytes 589832 | tf_op jit(solution)/shard_map/ppermute | solution.py:36
  10.1 5.3 %copy-start.4 = (bf16[1,3,64,512]{3,2,1,0:T(8,128)(2,1)S(1)}, bf16[1,3,64,512]{3,2,1,0:T(8,128)(2,1)}, u32[]{:S(2)}) copy-start(bf16[1,3,64,512]{3,2,1,0:T(8,128)(2,1)} %param.6) | copy-start | bytes 589828
  14.2 16.5 %collective-permute-start.4 = (bf16[4,3,64,256]{3,2,1,0:T(8,128)(2,1)}, bf16[4,3,64,256]{3,2,1,0:T(8,128)(2,1)S(1)}, u32[]{:S(2)}, u32[]{:S(2)}) collective-permute-start(bf16[4,3,64,256]{3,2,1,0:T(8,128)(2,1)} %get-tuple-element.41), channel_id=1, source_target_pairs={{0,2},{1,3},{2,0},{3,1},{4,6},{5,7},{6,4},{7,5},{8,10},{9,11},{10,... | collective-permute-start | bytes 1179656 | tf_op jit(solution)/shard_map/ppermute | solution.py:36
  15.5 11.6 %copy-start.3 = (bf16[3,3,64,512]{3,2,1,0:T(8,128)(2,1)S(1)}, bf16[3,3,64,512]{3,2,1,0:T(8,128)(2,1)}, u32[]{:S(2)}) copy-start(bf16[3,3,64,512]{3,2,1,0:T(8,128)(2,1)} %refs_1_.5) | copy-start | bytes 1769476
  17.1 9.9 %collective-permute-start.2 = (bf16[3,72,512]{2,1,0:T(8,128)(2,1)S(1)}, bf16[3,72,512]{2,1,0:T(8,128)(2,1)S(1)}, u32[]{:S(2)}, u32[]{:S(2)}) collective-permute-start(bf16[3,72,512]{2,1,0:T(8,128)(2,1)S(1)} %get-tuple-element.37), channel_id=1, source_target_pairs={{32,0},{64,32},{96,64},{128,96},{160,128},{192,160},{224,192},{33,... | collective-permute-start | bytes 663560 | tf_op jit(solution)/shard_map/ppermute | solution.py:41
  19.9 2.3 %copy-start = (bf16[1,3,3,512,512]{4,3,2,1,0:T(8,128)(2,1)S(1)}, bf16[1,3,3,512,512]{4,3,2,1,0:T(8,128)(2,1)}, u32[]{:S(2)}) copy-start(bf16[1,3,3,512,512]{4,3,2,1,0:T(8,128)(2,1)} %param.5) | copy-start | bytes 14155780
  22.2 4.9 %copy-start.1 = (bf16[1,3,3,512,512]{4,3,2,1,0:T(8,128)(2,1)S(1)}, bf16[1,3,3,512,512]{4,3,2,1,0:T(8,128)(2,1)}, u32[]{:S(2)}) copy-start(bf16[1,3,3,512,512]{4,3,2,1,0:T(8,128)(2,1)} %param.5) | copy-start | bytes 14155780
  28.7 9.9 %collective-permute-start.3 = (bf16[3,72,512]{2,1,0:T(8,128)(2,1)S(1)}, bf16[3,72,512]{2,1,0:T(8,128)(2,1)S(1)}, u32[]{:S(2)}, u32[]{:S(2)}) collective-permute-start(bf16[3,72,512]{2,1,0:T(8,128)(2,1)S(1)} %get-tuple-element.39), channel_id=1, source_target_pairs={{32,0},{64,32},{96,64},{128,96},{160,128},{192,160},{224,192},{33,... | collective-permute-start | bytes 663560 | tf_op jit(solution)/shard_map/ppermute | solution.py:41
  31.9 20.8 %collective-permute-start.7 = (bf16[2,3,72,512]{3,2,1,0:T(8,128)(2,1)S(1)}, bf16[2,3,72,512]{3,2,1,0:T(8,128)(2,1)S(1)}, u32[]{:S(2)}, u32[]{:S(2)}) collective-permute-start(bf16[2,3,72,512]{3,2,1,0:T(8,128)(2,1)S(1)} %pad_maximum_fusion.both0), channel_id=1, source_target_pairs={{0,2},{1,3},{2,0},{3,1},{4,6},{5,7},{6,4},{7,5},{8,10},{9,11},{10,... | collective-permute-start | bytes 1327112 | tf_op jit(solution)/shard_map/ppermute | solution.py:36
  40.4 9.9 %collective-permute-start.5 = (bf16[3,72,512]{2,1,0:T(8,128)(2,1)S(1)}, bf16[3,72,512]{2,1,0:T(8,128)(2,1)S(1)}, u32[]{:S(2)}, u32[]{:S(2)}) collective-permute-start(bf16[3,72,512]{2,1,0:T(8,128)(2,1)S(1)} %get-tuple-element.43), channel_id=1, source_target_pairs={{32,0},{64,32},{96,64},{128,96},{160,128},{192,160},{224,192},{33,... | collective-permute-start | bytes 663560 | tf_op jit(solution)/shard_map/ppermute | solution.py:41
  43.4 9.2 %collective-permute-start.8 = (bf16[3,72,512]{2,1,0:T(8,128)(2,1)S(1)}, bf16[3,72,512]{2,1,0:T(8,128)(2,1)S(1)}, u32[]{:S(2)}, u32[]{:S(2)}) collective-permute-start(bf16[3,72,512]{2,1,0:T(8,128)(2,1)S(1)} %get-tuple-element.50.third0), channel_id=1, source_target_pairs={{0,2},{1,3},{2,0},{3,1},{4,6},{5,7},{6,4},{7,5},{8,10},{9,11},{10,... | collective-permute-start | bytes 663560 | tf_op jit(solution)/shard_map/ppermute | solution.py:36
  50.4 6.2 %collective-permute-start.6 = (bf16[3,72,512]{2,1,0:T(8,128)(2,1)S(1)}, bf16[3,72,512]{2,1,0:T(8,128)(2,1)S(1)}, u32[]{:S(2)}, u32[]{:S(2)}) collective-permute-start(bf16[3,72,512]{2,1,0:T(8,128)(2,1)S(1)} %shard_map.68.g0), channel_id=1, source_target_pairs={{0,2},{1,3},{2,0},{3,1},{4,6},{5,7},{6,4},{7,5},{8,10},{9,11},{10,... | collective-permute-start | bytes 663560 | tf_op jit(solution)/shard_map/ppermute | solution.py:36
  57.7 1.8 %collective-permute-start.9 = (bf16[4,6,16,512]{3,2,1,0:T(8,128)(2,1)S(1)}, bf16[4,6,16,512]{3,2,1,0:T(8,128)(2,1)S(1)}, u32[]{:S(2)}, u32[]{:S(2)}) collective-permute-start(bf16[4,6,16,512]{3,2,1,0:T(8,128)(2,1)S(1)} %get-tuple-element.55), channel_id=1, source_target_pairs={{0,1},{1,0},{2,3},{3,2},{4,5},{5,4},{6,7},{7,6},{8,9},{9,8},{10,11... | collective-permute-start | bytes 1179656 | tf_op jit(solution)/shard_map/ppermute | solution.py:36
  59.6 1.8 %collective-permute-start.10 = (bf16[4,2,3,16,512]{4,3,2,1,0:T(8,128)(2,1)S(1)}, bf16[4,2,3,16,512]{4,3,2,1,0:T(8,128)(2,1)S(1)}, u32[]{:S(2)}, u32[]{:S(2)}) collective-permute-start(bf16[4,2,3,16,512]{4,3,2,1,0:T(8,128)(2,1)S(1)} %get-tuple-element.56), channel_id=1, source_target_pairs={{0,1},{1,0},{2,3},{3,2},{4,5},{5,4},{6,7},{7,6},{8,9},{9,8},{10,11... | collective-permute-start | bytes 1179656 | tf_op jit(solution)/shard_map/ppermute | solution.py:36
  59.9 13.0 %collective-permute-start.12 = (bf16[4,6,16,512]{3,2,1,0:T(8,128)(2,1)S(1)}, bf16[4,6,16,512]{3,2,1,0:T(8,128)(2,1)S(1)}, u32[]{:S(2)}, u32[]{:S(2)}) collective-permute-start(bf16[4,6,16,512]{3,2,1,0:T(8,128)(2,1)S(1)} %add_convert_fusion.2), channel_id=1, source_target_pairs={{0,16},{1,17},{2,18},{3,19},{4,20},{5,21},{6,22},{7,23},{8,24},{9,... | collective-permute-start | bytes 1179656 | tf_op jit(solution)/shard_map/ppermute | solution.py:36
  60.5 12.2 %collective-permute-start.11 = (bf16[4,6,16,512]{3,2,1,0:T(8,128)(2,1)S(1)}, bf16[4,6,16,512]{3,2,1,0:T(8,128)(2,1)S(1)}, u32[]{:S(2)}, u32[]{:S(2)}) collective-permute-start(bf16[4,6,16,512]{3,2,1,0:T(8,128)(2,1)S(1)} %get-tuple-element.60), channel_id=1, source_target_pairs={{0,1},{1,0},{2,3},{3,2},{4,5},{5,4},{6,7},{7,6},{8,9},{9,8},{10,11... | collective-permute-start | bytes 1179656 | tf_op jit(solution)/shard_map/ppermute | solution.py:36
  61.5 18.2 %collective-permute-start.18 = (bf16[2,3,16,512]{3,2,1,0:T(8,128)(2,1)S(1)}, bf16[2,3,16,512]{3,2,1,0:T(8,128)(2,1)S(1)}, u32[]{:S(2)}, u32[]{:S(2)}) collective-permute-start(bf16[2,3,16,512]{3,2,1,0:T(8,128)(2,1)S(1)} %get-tuple-element.66), channel_id=1, source_target_pairs={{0,12},{1,13},{2,14},{3,15},{4,0},{5,1},{6,2},{7,3},{8,4},{9,5},{1... | collective-permute-start | bytes 294920 | tf_op jit(solution)/shard_map/ppermute | solution.py:36
  68.5 13.5 %collective-permute-start.16 = (bf16[2,3,16,512]{3,2,1,0:T(8,128)(2,1)S(1)}, bf16[2,3,16,512]{3,2,1,0:T(8,128)(2,1)S(1)}, u32[]{:S(2)}, u32[]{:S(2)}) collective-permute-start(bf16[2,3,16,512]{3,2,1,0:T(8,128)(2,1)S(1)} %get-tuple-element.67), channel_id=1, source_target_pairs={{0,8},{1,9},{2,10},{3,11},{4,12},{5,13},{6,14},{7,15},{8,0},{9,1},... | collective-permute-start | bytes 294920 | tf_op jit(solution)/shard_map/ppermute | solution.py:36
  70.2 11.8 %collective-permute-start.17 = (bf16[2,3,16,512]{3,2,1,0:T(8,128)(2,1)S(1)}, bf16[2,3,16,512]{3,2,1,0:T(8,128)(2,1)S(1)}, u32[]{:S(2)}, u32[]{:S(2)}) collective-permute-start(bf16[2,3,16,512]{3,2,1,0:T(8,128)(2,1)S(1)} %get-tuple-element.68), channel_id=1, source_target_pairs={{0,4},{1,5},{2,6},{3,7},{4,8},{5,9},{6,10},{7,11},{8,12},{9,13},{1... | collective-permute-start | bytes 294920 | tf_op jit(solution)/shard_map/ppermute | solution.py:36
  73.1 11.9 %collective-permute-start.13 = (bf16[6,16,512]{2,1,0:T(8,128)(2,1)S(1)}, bf16[6,16,512]{2,1,0:T(8,128)(2,1)S(1)}, u32[]{:S(2)}, u32[]{:S(2)}) collective-permute-start(bf16[6,16,512]{2,1,0:T(8,128)(2,1)S(1)} %get-tuple-element.69), channel_id=1, source_target_pairs={{0,4},{1,5},{2,6},{3,7},{4,8},{5,9},{6,10},{7,11},{8,12},{9,13},{1... | collective-permute-start | bytes 294920 | tf_op jit(solution)/shard_map/ppermute | solution.py:36
  77.0 8.0 %collective-permute-start.15 = (bf16[6,16,512]{2,1,0:T(8,128)(2,1)S(1)}, bf16[6,16,512]{2,1,0:T(8,128)(2,1)S(1)}, u32[]{:S(2)}, u32[]{:S(2)}) collective-permute-start(bf16[6,16,512]{2,1,0:T(8,128)(2,1)S(1)} %get-tuple-element.70), channel_id=1, source_target_pairs={{0,12},{1,13},{2,14},{3,15},{4,0},{5,1},{6,2},{7,3},{8,4},{9,5},{1... | collective-permute-start | bytes 294920 | tf_op jit(solution)/shard_map/ppermute | solution.py:36
  79.7 11.2 %collective-permute-start.14 = (bf16[6,16,512]{2,1,0:T(8,128)(2,1)S(1)}, bf16[6,16,512]{2,1,0:T(8,128)(2,1)S(1)}, u32[]{:S(2)}, u32[]{:S(2)}) collective-permute-start(bf16[6,16,512]{2,1,0:T(8,128)(2,1)S(1)} %get-tuple-element.71), channel_id=1, source_target_pairs={{0,8},{1,9},{2,10},{3,11},{4,12},{5,13},{6,14},{7,15},{8,0},{9,1},... | collective-permute-start | bytes 294920 | tf_op jit(solution)/shard_map/ppermute | solution.py:36
  82.1 8.9 %collective-permute-start.19 = (bf16[3,16,512]{2,1,0:T(8,128)(2,1)S(1)}, bf16[3,16,512]{2,1,0:T(8,128)(2,1)S(1)}, u32[]{:S(2)}, u32[]{:S(2)}) collective-permute-start(bf16[3,16,512]{2,1,0:T(8,128)(2,1)S(1)} %slice_bitcast_fusion.8), channel_id=1, source_target_pairs={{0,16},{1,17},{2,18},{3,19},{4,20},{5,21},{6,22},{7,23},{8,24},{9,... | collective-permute-start | bytes 147464 | tf_op jit(solution)/shard_map/ppermute | solution.py:36

commit v5 on v4

--- a/solution.py
+++ b/solution.py
@@ -145,11 +145,12 @@
     )(x, low, high, weights)
 
 
-def back_kernel(first, *refs):
+def back_kernel(first, last, *refs):
     if first:
         own_ref, low_ref, high_ref, factor_ref, w_ref, sent_ref, grad_ref = refs
     else:
-        flag_ref, own_ref, low_ref, high_ref, relay_ref, factor_ref, w_ref, sent_ref, grad_ref = refs
+        flag_ref, own_ref, low_ref, high_ref, relay_ref, factor_ref, w_ref = refs[:7]
+        sent_ref, grad_ref = (refs[10], None) if last else refs[7:]
     slopes = []
     for r in range(ROWS):
         own = own_ref[r] if first else own_ref[0, r]
@@ -160,7 +161,8 @@
     grads = []
     for r in range(ROWS):
         grad = slopes[r] * factor_ref[0, r]
-        grad_ref[r] = grad.astype(BF)
+        if not last:
+            grad_ref[r] = grad.astype(BF)
         grads.append(grad)
     field = jnp.concatenate(grads, axis=0).astype(BF)
     above = jnp.concatenate(grads[1:], axis=0).astype(BF)
@@ -182,11 +184,16 @@
         sums.append(rows)
     for r in range(ROWS):
         value = pltpu.roll(sums[0][r], WIDE - 1, 0) + sums[1][r] + pltpu.roll(sums[2][r], 1, 0)
-        sent_ref[r] = (slopes[r] + value).astype(BF)
-
-
-def back_step(own, low, high, factors, weights, t, flag=None, arrived=None):
-    first = t == 0
+        if last:
+            sent_ref[STEPS - 1, r] = (slopes[r] + value)[:WIDTH].astype(BF)
+            for t in range(STEPS - 1):
+                sent_ref[t, r] = refs[7 + t][r, :WIDTH]
+        else:
+            sent_ref[r] = (slopes[r] + value).astype(BF)
+
+
+def back_step(own, low, high, factors, weights, t, flag=None, arrived=None, earlier=()):
+    first, last = t == 0, t == STEPS - 1
     weights = pltpu.with_memory_space_constraint(weights, pltpu.VMEM)
     edge = block((ROWS, 8, CH), 4 + t, 0, 0)
     operands = [own, low, high]
@@ -197,23 +204,27 @@
         specs += [block((ROWS, WIDE, CH), 0, 0, 0)]
         operands = [flag, *operands, arrived]
     specs += [block((1, ROWS, WIDE, CH), 0, 0, 0, 0), VMEM]
-    return pl.pallas_call(
-        lambda *refs: back_kernel(first, *refs),
+    wide = block((ROWS, WIDE, CH), 0, 0, 0)
+    shape = jax.ShapeDtypeStruct((ROWS, WIDE, CH), BF)
+    if last:
+        specs += [wide] * len(earlier)
+        out_shape = jax.ShapeDtypeStruct((STEPS, ROWS, WIDTH, CH), BF)
+        out_specs = block((STEPS, ROWS, WIDTH, CH), 0, 0, 0, 0)
+    else:
+        out_shape, out_specs = (shape, shape), (wide, wide)
+    return pl.pallas_call(
+        lambda *refs: back_kernel(first, last, *refs),
         grid=(1,),
-        out_shape=(
-            jax.ShapeDtypeStruct((ROWS, WIDE, CH), BF),
-            jax.ShapeDtypeStruct((ROWS, WIDE, CH), BF),
-        ),
+        out_shape=out_shape,
         in_specs=specs,
-        out_specs=(block((ROWS, WIDE, CH), 0, 0, 0), block((ROWS, WIDE, CH), 0, 0, 0)),
+        out_specs=out_specs,
         compiler_params=params(),
         cost_estimate=cost(1.1e9, 6e6),
-    )(*operands, factors, weights)
+    )(*operands, factors, weights, *earlier)
 
 
 def spread_kernel(place_ref, x_ref, source_ref, out0, out1, w_ref, field_ref, done):
     copies = [pltpu.make_async_copy(x_ref.at[t], field_ref.at[t], done.at[t]) for t in range(STEPS)]
-    copies.append(pltpu.make_async_copy(source_ref, w_ref, done.at[STEPS]))
     for copy in copies:
         copy.start()
     h, j, k, c = (place_ref[n] for n in range(4))
@@ -225,8 +236,10 @@
     source = ((far * 4 + turn) * 4 + chip * 2 + core) * 16 + lane % 16
     row = lax.broadcasted_iota(jnp.int32, (CH, CH), 0)
     order = jnp.where(row == source[:1], 1.0, 0.0).astype(BF)
-    for copy in copies[:STEPS]:
+    for copy in copies:
         copy.wait()
+    load = pltpu.make_async_copy(source_ref, w_ref, done.at[STEPS])
+    load.start()
     field = jnp.concatenate([field_ref[t, r] for t in range(STEPS) for r in range(ROWS)], axis=0)
     value = jnp.dot(field, order, preferred_element_type=F32).astype(BF)
     for n, out in enumerate((out0, out1)):
@@ -234,7 +247,7 @@
             for r in range(ROWS):
                 at = (t * ROWS + r) * WIDTH
                 out[t, r] = value[at : at + WIDTH, n * HALF : (n + 1) * HALF]
-    copies[STEPS].wait()
+    load.wait()
 
 
 def spread(place, x, weights):
@@ -396,7 +409,7 @@
             own = last_grad(flag, top, low, high, arrived, factors)
         else:
             sent, grad = back_step(slope, low, high, factors, weights, t, flag, arrived)
-            emitted.append(sent[:, :WIDTH])
+            emitted.append(sent)
             slope, weights = top, taps
             own = grad
             arrived = relay(sent)
@@ -409,13 +422,14 @@
         fields.append(own if t == 0 else (own, send(own, PAIR)))
 
     total = early_products(xs, *fields[0], *fields[1])
+    sent = back_step(top, low, high, factors, taps, STEPS - 1, flag, after(arrived, total), emitted)
+    total = after(total, sent)
     near, near_other, out_going, out_other, turns, turns_other = late_products(xs, fields[-1], total)
     out_going = total_of(out_going, send(out_other, CORE)).astype(BF)
     far = send(out_going, FAR)
     turns_other, near_other = lax.optimization_barrier((turns_other, near_other, out_going))[:2]
     turns_other, near_other = send(turns_other, CORE), send(near_other, CORE)
     turns = [total_of(turns[m], turns_other[m]).astype(BF) for m in range(4)]
-    arrived = after(arrived, *turns[1:])
     arriving = (send(turns[2], ACROSS), send(turns[1], UP), send(turns[3], DOWN))
     near = total_of(near, near_other).astype(BF)
     near = total_of(near, far).astype(BF)
@@ -424,10 +438,8 @@
     turned = total_of(turns[0], *arriving).astype(BF)
     far = send(turned[1], FAR)
     sums = [total_of(near[0], ups, across, downs), total_of(turned[0], far)]
-    sent, _ = back_step(top, low, high, factors, taps, STEPS - 1, flag, arrived)
-    emitted.append(sent[:, :WIDTH])
     weight_grads = (jnp.concatenate(sums, axis=0) * scale).astype(BF).reshape(1, 3, 3, 16, CH)
-    return (jnp.stack(emitted)[:, None], weight_grads)
+    return (sent[:, None], weight_grads)
 
 
 def solution(mesh):

time: 91.9 us -> 94.1 us (1.024)
  the two profiles are of different devices: /device:TPU:6 before, /device:TPU:24 now
where the time goes in v5:
time: 94.1 us; the launch traced here: 93.8 us
  starting transfers between devices  53.8 us (57%)
  Pallas kernels  22.4 us (24%)
  waiting for transfers between devices  12 us (13%)
  local copies, waits for them, and re-layouts  3.4 us (4%)
  other arithmetic  1.38 us (1%)
    ppermute x17, starting transfers between devices, send(): return lax.ppermute(block, 'az', route)  37.8 us
    ppermute x3, starting transfers between devices, relay(): return lax.ppermute(block, 'segment', [(i, i - 1) for i in range(1, count)])  15.9 us
    ppermute x17, waiting for transfers between devices, send(): return lax.ppermute(block, 'az', route)  11.4 us
    pallas_call x4, Pallas kernels, back_step(): pl.pallas_call(lambda *refs: back_kernel(first, last, *refs), grid=(1,),...  7.63 us
    pallas_call x1, Pallas kernels, spread(): pl.pallas_call(spread_kernel, out_shape=(shape, shape, pltpu.VMEM(weights...  4.88 us
    pallas_call x4, Pallas kernels, slope_factors(): pl.pallas_call(factor_kernel, grid=(1,), out_shape=jax.ShapeDtypeStruct((...  4.55 us
    unnamed x10, local copies, waits for them, and re-layouts  3.37 us
    pallas_call x1, Pallas kernels, early_products(): pl.pallas_call(early_kernel, out_shape=jax.ShapeDtypeStruct((3, HALF, 3 *...  2.8 us
  transfers between devices with their start and end apart: 20, of which 9 were waited for; matrix products, arithmetic and copies ran while one was open for 1% of the time, Pallas kernels for 21%

profile of v5, /device:TPU:24, one launch (start us, length us, event | category | flops | bytes accessed | tf_op | source)
XLA Modules:
  0.0 93.8 jit_solution(9367347066390014530)
XLA Ops:
  0.6 1.3 %shard_map.59 = (bf16[24,8,512]{2,1,0:T(8,128)(2,1)S(1)}, bf16[24,8,512]{2,1,0:T(8,128)(2,1)S(1)}) custom-call(bf16[4,3,64,512]{3,2,1,0:T(8,128)(2,1)} %bitcast.50, bf16[3,64,512]{2,1,0:T(8,128)(2,1)} %bitcast.57, bf16[3,3,64,512]{3,2,1,0:T(8,128)(2,1)} %own_ref.1, bf16[4,3,64,512]{3,2,1,0:T(8,128)(2,1)} %bitcast.51, bf16[3,64,512]{2,1,0:T(8,128)(2,1)} %bitcast.58, ...), custom_call_target="tpu_custom_call" | custom-call | bytes 1048576 | tf_op jit(solution)/shard_map/pallas_call | solution.py:79
  2.0 0.1 collective-permute-start
  2.1 6.0 %collective-permute-start.1 = (bf16[24,8,512]{2,1,0:T(8,128)(2,1)S(1)}, bf16[24,8,512]{2,1,0:T(8,128)(2,1)S(1)}, u32[]{:S(2)}, u32[]{:S(2)}) collective-permute-start(bf16[24,8,512]{2,1,0:T(8,128)(2,1)S(1)} %get-tuple-element.34), channel_id=1, source_target_pairs={{0,31},{1,0},{2,1},{3,2},{4,3},{5,4},{6,5},{7,6},{8,7},{9,8},{10,9... | collective-permute-start | bytes 589832 | tf_op jit(solution)/shard_map/ppermute | solution.py:36
  8.1 0.1 pad_add_fusion.place_ref
  8.2 4.9 %shard_map.60 = (bf16[4,3,64,256]{3,2,1,0:T(8,128)(2,1)S(1)}, bf16[4,3,64,256]{3,2,1,0:T(8,128)(2,1)}, bf16[9,512,512]{2,1,0:T(8,128)(2,1)S(1)}) custom-call(s32[4]{0:T(128)S(1)} %pad_add_fusion.place_ref, bf16[4,3,64,512]{3,2,1,0:T(8,128)(2,1)} %bitcast.52, bf16[9,512,512]{2,1,0:T(8,128)(2,1)} %bitcast.43), custom_call_target="tpu_custom_call" | custom-call | flops 450000000 | bytes 12000000 | tf_op jit(solution)/shard_map/pallas_call | solution.py:256
  13.1 0.1 collective-permute-start.4
  13.2 1.1 %shard_map.61.refs_3_ = f32[1,3,72,512]{3,2,1,0:T(8,128)S(1)} custom-call(bf16[4,3,64,512]{3,2,1,0:T(8,128)(2,1)S(1)} %bitcast.53, bf16[24,8,512]{2,1,0:T(8,128)(2,1)S(1)} %collective-permute-done.low_ref.refs_1_.refs_2_, bf16[24,8,512]{2,1,0:T(8,128)(2,1)S(1)} %collective-permute-done.1.high_ref.refs_2_.refs_3_, ...), custom_call_target="tpu_custom_call" | custom-call | flops 1200000000 | bytes 5000000 | tf_op jit(solution)/shard_map/pallas_call | solution.py:132
  14.4 1.7 %shard_map.62 = (bf16[3,72,512]{2,1,0:T(8,128)(2,1)S(1)}, bf16[3,72,512]{2,1,0:T(8,128)(2,1)S(1)}) custom-call(bf16[3,64,512]{2,1,0:T(8,128)(2,1)S(1)} %bitcast.59, bf16[24,8,512]{2,1,0:T(8,128)(2,1)S(1)} %collective-permute-done.low_ref.refs_1_.refs_2_, bf16[24,8,512]{2,1,0:T(8,128)(2,1)S(1)} %collective-permute-done.1.high_ref.refs_2_.refs_3_, ...), custom_call_target="tpu_custom_call" | custom-call | flops 1100000000 | bytes 6000000 | tf_op jit(solution)/shard_map/pallas_call | solution.py:215
  16.0 4.2 %collective-permute-start.2 = (bf16[3,72,512]{2,1,0:T(8,128)(2,1)S(1)}, bf16[3,72,512]{2,1,0:T(8,128)(2,1)S(1)}, u32[]{:S(2)}, u32[]{:S(2)}) collective-permute-start(bf16[3,72,512]{2,1,0:T(8,128)(2,1)S(1)} %get-tuple-element.37.refs_7_), channel_id=1, source_target_pairs={{32,0},{64,32},{96,64},{128,96},{160,128},{192,160},{224,192},{33,... | collective-permute-start | bytes 663560 | tf_op jit(solution)/shard_map/ppermute | solution.py:41
  20.2 2.3 %copy-done = bf16[1,3,3,512,512]{4,3,2,1,0:T(8,128)(2,1)S(1)} copy-done((bf16[1,3,3,512,512]{4,3,2,1,0:T(8,128)(2,1)S(1)}, bf16[1,3,3,512,512]{4,3,2,1,0:T(8,128)(2,1)}, u32[]{:S(2)}) %copy-start) | copy-done | bytes 4718616
  22.5 1.1 %shard_map.63.refs_5_ = f32[1,3,72,512]{3,2,1,0:T(8,128)S(1)} custom-call(bf16[4,3,64,512]{3,2,1,0:T(8,128)(2,1)S(1)} %bitcast.54, bf16[24,8,512]{2,1,0:T(8,128)(2,1)S(1)} %collective-permute-done.low_ref.refs_1_.refs_2_, bf16[24,8,512]{2,1,0:T(8,128)(2,1)S(1)} %collective-permute-done.1.high_ref.refs_2_.refs_3_, bf16[9,512,512]{2,1,0:T(8,128)(2,1)S(1)} %bitcast.44), custom_call_target="tpu_custom_call" | custom-call | flops 1200000000 | bytes 5000000 | tf_op jit(solution)/shard_map/pallas_call | solution.py:132
  23.7 0.2 collective-permute-done.2.refs_4_
  23.8 1.0 %copy-done.1 = bf16[1,3,3,512,512]{4,3,2,1,0:T(8,128)(2,1)S(1)} copy-done((bf16[1,3,3,512,512]{4,3,2,1,0:T(8,128)(2,1)S(1)}, bf16[1,3,3,512,512]{4,3,2,1,0:T(8,128)(2,1)}, u32[]{:S(2)}) %copy-start.1) | copy-done | bytes 4718616
  24.9 1.7 %shard_map.64 = (bf16[3,72,512]{2,1,0:T(8,128)(2,1)S(1)}, bf16[3,72,512]{2,1,0:T(8,128)(2,1)S(1)}) custom-call(s32[1]{0:T(128)} %bitcast.refs_0_.flag_ref, bf16[3,3,64,512]{3,2,1,0:T(8,128)(2,1)S(1)} %copy-done.3, bf16[24,8,512]{2,1,0:T(8,128)(2,1)S(1)} %collective-permute-done.low_ref.refs_1_.refs_2_, ...), custom_call_target="tpu_custom_call" | custom-call | flops 1100000000 | bytes 6000000 | tf_op jit(solution)/shard_map/pallas_call | solution.py:215
  26.6 5.3 %collective-permute-start.3 = (bf16[3,72,512]{2,1,0:T(8,128)(2,1)S(1)}, bf16[3,72,512]{2,1,0:T(8,128)(2,1)S(1)}, u32[]{:S(2)}, u32[]{:S(2)}) collective-permute-start(bf16[3,72,512]{2,1,0:T(8,128)(2,1)S(1)} %get-tuple-element.39.refs_8_), channel_id=1, source_target_pairs={{32,0},{64,32},{96,64},{128,96},{160,128},{192,160},{224,192},{33,... | collective-permute-start | bytes 663560 | tf_op jit(solution)/shard_map/ppermute | solution.py:41
  31.8 1.2 %shard_map.65.refs_5_ = f32[1,3,72,512]{3,2,1,0:T(8,128)S(1)} custom-call(bf16[4,3,64,512]{3,2,1,0:T(8,128)(2,1)S(1)} %bitcast.55, bf16[24,8,512]{2,1,0:T(8,128)(2,1)S(1)} %collective-permute-done.low_ref.refs_1_.refs_2_, bf16[24,8,512]{2,1,0:T(8,128)(2,1)S(1)} %collective-permute-done.1.high_ref.refs_2_.refs_3_, bf16[9,512,512]{2,1,0:T(8,128)(2,1)S(1)} %bitcast.46), custom_call_target="tpu_custom_call" | custom-call | flops 1200000000 | bytes 5000000 | tf_op jit(solution)/shard_map/pallas_call | solution.py:132
  33.1 2.1 %collective-permute-start.6 = (bf16[2,3,72,512]{3,2,1,0:T(8,128)(2,1)S(1)}, bf16[2,3,72,512]{3,2,1,0:T(8,128)(2,1)S(1)}, u32[]{:S(2)}, u32[]{:S(2)}) collective-permute-start(bf16[2,3,72,512]{3,2,1,0:T(8,128)(2,1)S(1)} %pad_maximum_fusion.both0), channel_id=1, source_target_pairs={{0,2},{1,3},{2,0},{3,1},{4,6},{5,7},{6,4},{7,5},{8,10},{9,11},{10,... | collective-permute-start | bytes 1327112 | tf_op jit(solution)/shard_map/ppermute | solution.py:36
  35.1 0.1 collective-permute-done.3.refs_4_
  35.3 1.7 %shard_map.66 = (bf16[3,72,512]{2,1,0:T(8,128)(2,1)S(1)}, bf16[3,72,512]{2,1,0:T(8,128)(2,1)S(1)}) custom-call(s32[1]{0:T(128)} %bitcast.refs_0_.flag_ref, bf16[3,3,64,512]{3,2,1,0:T(8,128)(2,1)S(1)} %copy-done.3, bf16[24,8,512]{2,1,0:T(8,128)(2,1)S(1)} %collective-permute-done.low_ref.refs_1_.refs_2_, ...), custom_call_target="tpu_custom_call" | custom-call | flops 1100000000 | bytes 6000000 | tf_op jit(solution)/shard_map/pallas_call | solution.py:215
  37.0 6.5 %collective-permute-start.5 = (bf16[3,72,512]{2,1,0:T(8,128)(2,1)S(1)}, bf16[3,72,512]{2,1,0:T(8,128)(2,1)S(1)}, u32[]{:S(2)}, u32[]{:S(2)}) collective-permute-start(bf16[3,72,512]{2,1,0:T(8,128)(2,1)S(1)} %get-tuple-element.43.refs_9_), channel_id=1, source_target_pairs={{32,0},{64,32},{96,64},{128,96},{160,128},{192,160},{224,192},{33,... | collective-permute-start | bytes 663560 | tf_op jit(solution)/shard_map/ppermute | solution.py:41
  43.5 1.2 %shard_map.67.refs_5_.factor_ref = f32[1,3,72,512]{3,2,1,0:T(8,128)S(1)} custom-call(bf16[4,3,64,512]{3,2,1,0:T(8,128)(2,1)S(1)} %bitcast.56, bf16[24,8,512]{2,1,0:T(8,128)(2,1)S(1)} %collective-permute-done.low_ref.refs_1_.refs_2_, bf16[24,8,512]{2,1,0:T(8,128)(2,1)S(1)} %collective-permute-done.1.high_ref.refs_2_.refs_3_, bf16[9,512,512]{2,1,0:T(8,128)(2,1)S(1)} %bitcast.48), custom_call_target="tpu_custom_call" | custom-call | flops 1200000000 | bytes 5000000 | tf_op jit(solution)/shard_map/pallas_call | solution.py:132
  44.6 2.1 %collective-permute-start.7 = (bf16[3,72,512]{2,1,0:T(8,128)(2,1)S(1)}, bf16[3,72,512]{2,1,0:T(8,128)(2,1)S(1)}, u32[]{:S(2)}, u32[]{:S(2)}) collective-permute-start(bf16[3,72,512]{2,1,0:T(8,128)(2,1)S(1)} %get-tuple-element.50.third0), channel_id=1, source_target_pairs={{0,2},{1,3},{2,0},{3,1},{4,6},{5,7},{6,4},{7,5},{8,10},{9,11},{10,... | collective-permute-start | bytes 663560 | tf_op jit(solution)/shard_map/ppermute | solution.py:36
  46.7 0.2 collective-permute-done.5.refs_4_.relay_ref
  46.9 0.1 shard_map.70.g0
  47.0 2.3 %collective-permute-start.8 = (bf16[3,72,512]{2,1,0:T(8,128)(2,1)S(1)}, bf16[3,72,512]{2,1,0:T(8,128)(2,1)S(1)}, u32[]{:S(2)}, u32[]{:S(2)}) collective-permute-start(bf16[3,72,512]{2,1,0:T(8,128)(2,1)S(1)} %shard_map.70.g0), channel_id=1, source_target_pairs={{0,2},{1,3},{2,0},{3,1},{4,6},{5,7},{6,4},{7,5},{8,10},{9,11},{10,... | collective-permute-start | bytes 663560 | tf_op jit(solution)/shard_map/ppermute | solution.py:36
  49.2 1.4 %collective-permute-done.7.third1 = bf16[3,72,512]{2,1,0:T(8,128)(2,1)S(1)} collective-permute-done((bf16[3,72,512]{2,1,0:T(8,128)(2,1)S(1)}, bf16[3,72,512]{2,1,0:T(8,128)(2,1)S(1)}, u32[]{:S(2)}, u32[]{:S(2)}) %collective-permute-start.7) | collective-permute-done | bytes 221216 | tf_op jit(solution)/shard_map/ppermute | solution.py:36
  50.7 2.8 %shard_map.68.total_ref = f32[3,256,1536]{2,1,0:T(8,128)S(1)} custom-call(bf16[4,3,64,256]{3,2,1,0:T(8,128)(2,1)S(1)} %get-tuple-element.40.x0, bf16[4,3,64,256]{3,2,1,0:T(8,128)(2,1)S(1)} %collective-permute-done.4.x1, bf16[2,3,72,512]{3,2,1,0:T(8,128)(2,1)S(1)} %pad_maximum_fusion.both0, bf16[2,3,72,512]{3,2,1,0:T(8,128)(2,1)S(1)} %collective-permute-done.6.both1, ...), custom_call_target="tpu_custom_call" | custom-call | flops 3000000000 | bytes 8000000 | tf_op jit(solution)/shard_map/pallas_call | solution.py:304
  53.5 2.6 %shard_map.69 = bf16[4,3,64,512]{3,2,1,0:T(8,128)(2,1)} custom-call(s32[1]{0:T(128)} %bitcast.refs_0_.flag_ref, bf16[3,3,64,512]{3,2,1,0:T(8,128)(2,1)S(1)} %copy-done.3, bf16[24,8,512]{2,1,0:T(8,128)(2,1)S(1)} %collective-permute-done.low_ref.refs_1_.refs_2_, bf16[24,8,512]{2,1,0:T(8,128)(2,1)S(1)} %collective-permute-done.1.high_ref.refs_2_.refs_3_, ...), custom_call_target="tpu_custom_call" | custom-call | flops 1100000000 | bytes 6000000 | tf_op jit(solution)/shard_map/pallas_call | solution.py:215
  56.1 1.1 %shard_map.71 = (bf16[4,6,16,512]{3,2,1,0:T(8,128)(2,1)S(1)}, bf16[4,6,16,512]{3,2,1,0:T(8,128)(2,1)S(1)}, bf16[4,6,16,512]{3,2,1,0:T(8,128)(2,1)S(1)}, bf16[4,6...) custom-call(bf16[4,3,64,256]{3,2,1,0:T(8,128)(2,1)S(1)} %get-tuple-elem, ...), custom_call_target="tpu_custom_call" | custom-call | flops 1000000000 | bytes 8000000 | tf_op jit(solution)/shard_map/pallas_call | solution.py:335
  57.2 0.1 collective-permute-start.9
  57.3 1.7 %collective-permute-done.9 = bf16[4,6,16,512]{3,2,1,0:T(8,128)(2,1)S(1)} collective-permute-done((bf16[4,6,16,512]{3,2,1,0:T(8,128)(2,1)S(1)}, bf16[4,6,16,512]{3,2,1,0:T(8,128)(2,1)S(1)}, u32[]{:S(2)}, u32[]{:S(2)}) %collective-permute-start.9) | collective-permute-done | bytes 393248 | tf_op jit(solution)/shard_map/ppermute | solution.py:36
  59.0 0.1 add_convert_fusion.2
  59.1 0.2 collective-permute-start.15
  59.3 0.4 collective-permute-start.10
  59.7 3.6 %collective-permute-start.11 = (bf16[4,6,16,512]{3,2,1,0:T(8,128)(2,1)S(1)}, bf16[4,6,16,512]{3,2,1,0:T(8,128)(2,1)S(1)}, u32[]{:S(2)}, u32[]{:S(2)}) collective-permute-start(bf16[4,6,16,512]{3,2,1,0:T(8,128)(2,1)S(1)} %add_convert_fusion.2), channel_id=1, source_target_pairs={{0,16},{1,17},{2,18},{3,19},{4,20},{5,21},{6,22},{7,23},{8,24},{9,... | collective-permute-start | bytes 1179656 | tf_op jit(solution)/shard_map/ppermute | solution.py:36
  63.3 0.1 fusion.9
  63.4 6.4 %collective-permute-start.18 = (bf16[2,3,16,512]{3,2,1,0:T(8,128)(2,1)S(1)}, bf16[2,3,16,512]{3,2,1,0:T(8,128)(2,1)S(1)}, u32[]{:S(2)}, u32[]{:S(2)}) collective-permute-start(bf16[2,3,16,512]{3,2,1,0:T(8,128)(2,1)S(1)} %get-tuple-element.66), channel_id=1, source_target_pairs={{0,12},{1,13},{2,14},{3,15},{4,0},{5,1},{6,2},{7,3},{8,4},{9,5},{1... | collective-permute-start | bytes 294920 | tf_op jit(solution)/shard_map/ppermute | solution.py:36
  69.8 2.5 %collective-permute-start.16 = (bf16[2,3,16,512]{3,2,1,0:T(8,128)(2,1)S(1)}, bf16[2,3,16,512]{3,2,1,0:T(8,128)(2,1)S(1)}, u32[]{:S(2)}, u32[]{:S(2)}) collective-permute-start(bf16[2,3,16,512]{3,2,1,0:T(8,128)(2,1)S(1)} %get-tuple-element.68), channel_id=1, source_target_pairs={{0,8},{1,9},{2,10},{3,11},{4,12},{5,13},{6,14},{7,15},{8,0},{9,1},... | collective-permute-start | bytes 294920 | tf_op jit(solution)/shard_map/ppermute | solution.py:36
  72.3 0.4 collective-permute-done.11
  72.7 0.2 add_convert_fusion
  72.9 7.3 %collective-permute-start.12 = (bf16[6,16,512]{2,1,0:T(8,128)(2,1)S(1)}, bf16[6,16,512]{2,1,0:T(8,128)(2,1)S(1)}, u32[]{:S(2)}, u32[]{:S(2)}) collective-permute-start(bf16[6,16,512]{2,1,0:T(8,128)(2,1)S(1)} %get-tuple-element.69), channel_id=1, source_target_pairs={{0,4},{1,5},{2,6},{3,7},{4,8},{5,9},{6,10},{7,11},{8,12},{9,13},{1... | collective-permute-start | bytes 294920 | tf_op jit(solution)/shard_map/ppermute | solution.py:36
  80.3 1.1 %collective-permute-start.14 = (bf16[6,16,512]{2,1,0:T(8,128)(2,1)S(1)}, bf16[6,16,512]{2,1,0:T(8,128)(2,1)S(1)}, u32[]{:S(2)}, u32[]{:S(2)}) collective-permute-start(bf16[6,16,512]{2,1,0:T(8,128)(2,1)S(1)} %get-tuple-element.70), channel_id=1, source_target_pairs={{0,12},{1,13},{2,14},{3,15},{4,0},{5,1},{6,2},{7,3},{8,4},{9,5},{1... | collective-permute-start | bytes 294920 | tf_op jit(solution)/shard_map/ppermute | solution.py:36
  81.4 2.5 %collective-permute-start.13 = (bf16[6,16,512]{2,1,0:T(8,128)(2,1)S(1)}, bf16[6,16,512]{2,1,0:T(8,128)(2,1)S(1)}, u32[]{:S(2)}, u32[]{:S(2)}) collective-permute-start(bf16[6,16,512]{2,1,0:T(8,128)(2,1)S(1)} %get-tuple-element.71), channel_id=1, source_target_pairs={{0,8},{1,9},{2,10},{3,11},{4,12},{5,13},{6,14},{7,15},{8,0},{9,1},... | collective-permute-start | bytes 294920 | tf_op jit(solution)/shard_map/ppermute | solution.py:36
  84.0 1.1 %collective-permute-start.19 = (bf16[3,16,512]{2,1,0:T(8,128)(2,1)S(1)}, bf16[3,16,512]{2,1,0:T(8,128)(2,1)S(1)}, u32[]{:S(2)}, u32[]{:S(2)}) collective-permute-start(bf16[3,16,512]{2,1,0:T(8,128)(2,1)S(1)} %slice_bitcast_fusion.4), channel_id=1, source_target_pairs={{0,16},{1,17},{2,18},{3,19},{4,20},{5,21},{6,22},{7,23},{8,24},{9,... | collective-permute-start | bytes 147464 | tf_op jit(solution)/shard_map/ppermute | solution.py:36
  85.1 0.5 collective-permute-done.12
  85.6 1.1 %collective-permute-done.14 = bf16[6,16,512]{2,1,0:T(8,128)(2,1)S(1)} collective-permute-done((bf16[6,16,512]{2,1,0:T(8,128)(2,1)S(1)}, bf16[6,16,512]{2,1,0:T(8,128)(2,1)S(1)}, u32[]{:S(2)}, u32[]{:S(2)}) %collective-permute-start.14) | collective-permute-done | bytes 98336 | tf_op jit(solution)/shard_map/ppermute | solution.py:36
  86.7 6.2 %collective-permute-done.13 = bf16[6,16,512]{2,1,0:T(8,128)(2,1)S(1)} collective-permute-done((bf16[6,16,512]{2,1,0:T(8,128)(2,1)S(1)}, bf16[6,16,512]{2,1,0:T(8,128)(2,1)S(1)}, u32[]{:S(2)}, u32[]{:S(2)}) %collective-permute-start.13) | collective-permute-done | bytes 98336 | tf_op jit(solution)/shard_map/ppermute | solution.py:36
  93.1 0.7 fusion
  (26 shorter events, 0.3 us)
Async XLA Ops:
  0.6 12.6 %copy-start.2 = (bf16[4,1,3,64,512]{4,3,2,1,0:T(8,128)(2,1)S(1)}, bf16[4,1,3,64,512]{4,3,2,1,0:T(8,128)(2,1)}, u32[]{:S(2)}) copy-start(bf16[4,1,3,64,512]{4,3,2,1,0:T(8,128)(2,1)} %param.4) | copy-start | bytes 2359300
  2.0 11.2 %collective-permute-start = (bf16[24,8,512]{2,1,0:T(8,128)(2,1)S(1)}, bf16[24,8,512]{2,1,0:T(8,128)(2,1)S(1)}, u32[]{:S(2)}, u32[]{:S(2)}) collective-permute-start(bf16[24,8,512]{2,1,0:T(8,128)(2,1)S(1)} %get-tuple-element.33), channel_id=1, source_target_pairs={{0,1},{1,2},{2,3},{3,4},{4,5},{5,6},{6,7},{7,8},{8,9},{9,10},{10,1... | collective-permute-start | bytes 589832 | tf_op jit(solution)/shard_map/ppermute | solution.py:36
  2.1 11.1 %collective-permute-start.1 = (bf16[24,8,512]{2,1,0:T(8,128)(2,1)S(1)}, bf16[24,8,512]{2,1,0:T(8,128)(2,1)S(1)}, u32[]{:S(2)}, u32[]{:S(2)}) collective-permute-start(bf16[24,8,512]{2,1,0:T(8,128)(2,1)S(1)} %get-tuple-element.34), channel_id=1, source_target_pairs={{0,31},{1,0},{2,1},{3,2},{4,3},{5,4},{6,5},{7,6},{8,7},{9,8},{10,9... | collective-permute-start | bytes 589832 | tf_op jit(solution)/shard_map/ppermute | solution.py:36
  8.2 6.2 %copy-start.4 = (bf16[1,3,64,512]{3,2,1,0:T(8,128)(2,1)S(1)}, bf16[1,3,64,512]{3,2,1,0:T(8,128)(2,1)}, u32[]{:S(2)}) copy-start(bf16[1,3,64,512]{3,2,1,0:T(8,128)(2,1)} %param.6) | copy-start | bytes 589828
  13.1 18.8 %collective-permute-start.4 = (bf16[4,3,64,256]{3,2,1,0:T(8,128)(2,1)}, bf16[4,3,64,256]{3,2,1,0:T(8,128)(2,1)S(1)}, u32[]{:S(2)}, u32[]{:S(2)}) collective-permute-start(bf16[4,3,64,256]{3,2,1,0:T(8,128)(2,1)} %get-tuple-element.41), channel_id=1, source_target_pairs={{0,2},{1,3},{2,0},{3,1},{4,6},{5,7},{6,4},{7,5},{8,10},{9,11},{10,... | collective-permute-start | bytes 1179656 | tf_op jit(solution)/shard_map/ppermute | solution.py:36
  14.3 9.5 %copy-start.3 = (bf16[3,3,64,512]{3,2,1,0:T(8,128)(2,1)S(1)}, bf16[3,3,64,512]{3,2,1,0:T(8,128)(2,1)}, u32[]{:S(2)}) copy-start(bf16[3,3,64,512]{3,2,1,0:T(8,128)(2,1)} %own_ref.1) | copy-start | bytes 1769476
  16.0 7.8 %collective-permute-start.2 = (bf16[3,72,512]{2,1,0:T(8,128)(2,1)S(1)}, bf16[3,72,512]{2,1,0:T(8,128)(2,1)S(1)}, u32[]{:S(2)}, u32[]{:S(2)}) collective-permute-start(bf16[3,72,512]{2,1,0:T(8,128)(2,1)S(1)} %get-tuple-element.37.refs_7_), channel_id=1, source_target_pairs={{32,0},{64,32},{96,64},{128,96},{160,128},{192,160},{224,192},{33,... | collective-permute-start | bytes 663560 | tf_op jit(solution)/shard_map/ppermute | solution.py:41
  20.2 2.3 %copy-start = (bf16[1,3,3,512,512]{4,3,2,1,0:T(8,128)(2,1)S(1)}, bf16[1,3,3,512,512]{4,3,2,1,0:T(8,128)(2,1)}, u32[]{:S(2)}) copy-start(bf16[1,3,3,512,512]{4,3,2,1,0:T(8,128)(2,1)} %param.5) | copy-start | bytes 14155780
  22.5 2.3 %copy-start.1 = (bf16[1,3,3,512,512]{4,3,2,1,0:T(8,128)(2,1)S(1)}, bf16[1,3,3,512,512]{4,3,2,1,0:T(8,128)(2,1)}, u32[]{:S(2)}) copy-start(bf16[1,3,3,512,512]{4,3,2,1,0:T(8,128)(2,1)} %param.5) | copy-start | bytes 14155780
  26.6 8.7 %collective-permute-start.3 = (bf16[3,72,512]{2,1,0:T(8,128)(2,1)S(1)}, bf16[3,72,512]{2,1,0:T(8,128)(2,1)S(1)}, u32[]{:S(2)}, u32[]{:S(2)}) collective-permute-start(bf16[3,72,512]{2,1,0:T(8,128)(2,1)S(1)} %get-tuple-element.39.refs_8_), channel_id=1, source_target_pairs={{32,0},{64,32},{96,64},{128,96},{160,128},{192,160},{224,192},{33,... | collective-permute-start | bytes 663560 | tf_op jit(solution)/shard_map/ppermute | solution.py:41
  33.1 17.6 %collective-permute-start.6 = (bf16[2,3,72,512]{3,2,1,0:T(8,128)(2,1)S(1)}, bf16[2,3,72,512]{3,2,1,0:T(8,128)(2,1)S(1)}, u32[]{:S(2)}, u32[]{:S(2)}) collective-permute-start(bf16[2,3,72,512]{3,2,1,0:T(8,128)(2,1)S(1)} %pad_maximum_fusion.both0), channel_id=1, source_target_pairs={{0,2},{1,3},{2,0},{3,1},{4,6},{5,7},{6,4},{7,5},{8,10},{9,11},{10,... | collective-permute-start | bytes 1327112 | tf_op jit(solution)/shard_map/ppermute | solution.py:36
  37.0 9.9 %collective-permute-start.5 = (bf16[3,72,512]{2,1,0:T(8,128)(2,1)S(1)}, bf16[3,72,512]{2,1,0:T(8,128)(2,1)S(1)}, u32[]{:S(2)}, u32[]{:S(2)}) collective-permute-start(bf16[3,72,512]{2,1,0:T(8,128)(2,1)S(1)} %get-tuple-element.43.refs_9_), channel_id=1, source_target_pairs={{32,0},{64,32},{96,64},{128,96},{160,128},{192,160},{224,192},{33,... | collective-permute-start | bytes 663560 | tf_op jit(solution)/shard_map/ppermute | solution.py:41
  44.6 6.0 %collective-permute-start.7 = (bf16[3,72,512]{2,1,0:T(8,128)(2,1)S(1)}, bf16[3,72,512]{2,1,0:T(8,128)(2,1)S(1)}, u32[]{:S(2)}, u32[]{:S(2)}) collective-permute-start(bf16[3,72,512]{2,1,0:T(8,128)(2,1)S(1)} %get-tuple-element.50.third0), channel_id=1, source_target_pairs={{0,2},{1,3},{2,0},{3,1},{4,6},{5,7},{6,4},{7,5},{8,10},{9,11},{10,... | collective-permute-start | bytes 663560 | tf_op jit(solution)/shard_map/ppermute | solution.py:36
  47.0 9.1 %collective-permute-start.8 = (bf16[3,72,512]{2,1,0:T(8,128)(2,1)S(1)}, bf16[3,72,512]{2,1,0:T(8,128)(2,1)S(1)}, u32[]{:S(2)}, u32[]{:S(2)}) collective-permute-start(bf16[3,72,512]{2,1,0:T(8,128)(2,1)S(1)} %shard_map.70.g0), channel_id=1, source_target_pairs={{0,2},{1,3},{2,0},{3,1},{4,6},{5,7},{6,4},{7,5},{8,10},{9,11},{10,... | collective-permute-start | bytes 663560 | tf_op jit(solution)/shard_map/ppermute | solution.py:36
  57.2 1.8 %collective-permute-start.9 = (bf16[4,6,16,512]{3,2,1,0:T(8,128)(2,1)S(1)}, bf16[4,6,16,512]{3,2,1,0:T(8,128)(2,1)S(1)}, u32[]{:S(2)}, u32[]{:S(2)}) collective-permute-start(bf16[4,6,16,512]{3,2,1,0:T(8,128)(2,1)S(1)} %get-tuple-element.57), channel_id=1, source_target_pairs={{0,1},{1,0},{2,3},{3,2},{4,5},{5,4},{6,7},{7,6},{8,9},{9,8},{10,11... | collective-permute-start | bytes 1179656 | tf_op jit(solution)/shard_map/ppermute | solution.py:36
  59.1 4.2 %collective-permute-start.15 = (bf16[4,2,3,16,512]{4,3,2,1,0:T(8,128)(2,1)S(1)}, bf16[4,2,3,16,512]{4,3,2,1,0:T(8,128)(2,1)S(1)}, u32[]{:S(2)}, u32[]{:S(2)}) collective-permute-start(bf16[4,2,3,16,512]{4,3,2,1,0:T(8,128)(2,1)S(1)} %get-tuple-element.60), channel_id=1, source_target_pairs={{0,1},{1,0},{2,3},{3,2},{4,5},{5,4},{6,7},{7,6},{8,9},{9,8},{10,11... | collective-permute-start | bytes 1179656 | tf_op jit(solution)/shard_map/ppermute | solution.py:36
  59.3 13.0 %collective-permute-start.10 = (bf16[4,6,16,512]{3,2,1,0:T(8,128)(2,1)S(1)}, bf16[4,6,16,512]{3,2,1,0:T(8,128)(2,1)S(1)}, u32[]{:S(2)}, u32[]{:S(2)}) collective-permute-start(bf16[4,6,16,512]{3,2,1,0:T(8,128)(2,1)S(1)} %get-tuple-element.58), channel_id=1, source_target_pairs={{0,1},{1,0},{2,3},{3,2},{4,5},{5,4},{6,7},{7,6},{8,9},{9,8},{10,11... | collective-permute-start | bytes 1179656 | tf_op jit(solution)/shard_map/ppermute | solution.py:36
  59.7 13.0 %collective-permute-start.11 = (bf16[4,6,16,512]{3,2,1,0:T(8,128)(2,1)S(1)}, bf16[4,6,16,512]{3,2,1,0:T(8,128)(2,1)S(1)}, u32[]{:S(2)}, u32[]{:S(2)}) collective-permute-start(bf16[4,6,16,512]{3,2,1,0:T(8,128)(2,1)S(1)} %add_convert_fusion.2), channel_id=1, source_target_pairs={{0,16},{1,17},{2,18},{3,19},{4,20},{5,21},{6,22},{7,23},{8,24},{9,... | collective-permute-start | bytes 1179656 | tf_op jit(solution)/shard_map/ppermute | solution.py:36
  63.4 18.0 %collective-permute-start.18 = (bf16[2,3,16,512]{3,2,1,0:T(8,128)(2,1)S(1)}, bf16[2,3,16,512]{3,2,1,0:T(8,128)(2,1)S(1)}, u32[]{:S(2)}, u32[]{:S(2)}) collective-permute-start(bf16[2,3,16,512]{3,2,1,0:T(8,128)(2,1)S(1)} %get-tuple-element.66), channel_id=1, source_target_pairs={{0,12},{1,13},{2,14},{3,15},{4,0},{5,1},{6,2},{7,3},{8,4},{9,5},{1... | collective-permute-start | bytes 294920 | tf_op jit(solution)/shard_map/ppermute | solution.py:36
  69.8 14.2 %collective-permute-start.17 = (bf16[2,3,16,512]{3,2,1,0:T(8,128)(2,1)S(1)}, bf16[2,3,16,512]{3,2,1,0:T(8,128)(2,1)S(1)}, u32[]{:S(2)}, u32[]{:S(2)}) collective-permute-start(bf16[2,3,16,512]{3,2,1,0:T(8,128)(2,1)S(1)} %get-tuple-element.67), channel_id=1, source_target_pairs={{0,4},{1,5},{2,6},{3,7},{4,8},{5,9},{6,10},{7,11},{8,12},{9,13},{1... | collective-permute-start | bytes 294920 | tf_op jit(solution)/shard_map/ppermute | solution.py:36
  69.8 14.2 %collective-permute-start.16 = (bf16[2,3,16,512]{3,2,1,0:T(8,128)(2,1)S(1)}, bf16[2,3,16,512]{3,2,1,0:T(8,128)(2,1)S(1)}, u32[]{:S(2)}, u32[]{:S(2)}) collective-permute-start(bf16[2,3,16,512]{3,2,1,0:T(8,128)(2,1)S(1)} %get-tuple-element.68), channel_id=1, source_target_pairs={{0,8},{1,9},{2,10},{3,11},{4,12},{5,13},{6,14},{7,15},{8,0},{9,1},... | collective-permute-start | bytes 294920 | tf_op jit(solution)/shard_map/ppermute | solution.py:36
  72.9 12.7 %collective-permute-start.12 = (bf16[6,16,512]{2,1,0:T(8,128)(2,1)S(1)}, bf16[6,16,512]{2,1,0:T(8,128)(2,1)S(1)}, u32[]{:S(2)}, u32[]{:S(2)}) collective-permute-start(bf16[6,16,512]{2,1,0:T(8,128)(2,1)S(1)} %get-tuple-element.69), channel_id=1, source_target_pairs={{0,4},{1,5},{2,6},{3,7},{4,8},{5,9},{6,10},{7,11},{8,12},{9,13},{1... | collective-permute-start | bytes 294920 | tf_op jit(solution)/shard_map/ppermute | solution.py:36
  80.3 6.5 %collective-permute-start.14 = (bf16[6,16,512]{2,1,0:T(8,128)(2,1)S(1)}, bf16[6,16,512]{2,1,0:T(8,128)(2,1)S(1)}, u32[]{:S(2)}, u32[]{:S(2)}) collective-permute-start(bf16[6,16,512]{2,1,0:T(8,128)(2,1)S(1)} %get-tuple-element.70), channel_id=1, source_target_pairs={{0,12},{1,13},{2,14},{3,15},{4,0},{5,1},{6,2},{7,3},{8,4},{9,5},{1... | collective-permute-start | bytes 294920 | tf_op jit(solution)/shard_map/ppermute | solution.py:36
  81.4 11.6 %collective-permute-start.13 = (bf16[6,16,512]{2,1,0:T(8,128)(2,1)S(1)}, bf16[6,16,512]{2,1,0:T(8,128)(2,1)S(1)}, u32[]{:S(2)}, u32[]{:S(2)}) collective-permute-start(bf16[6,16,512]{2,1,0:T(8,128)(2,1)S(1)} %get-tuple-element.71), channel_id=1, source_target_pairs={{0,8},{1,9},{2,10},{3,11},{4,12},{5,13},{6,14},{7,15},{8,0},{9,1},... | collective-permute-start | bytes 294920 | tf_op jit(solution)/shard_map/ppermute | solution.py:36
  84.0 9.0 %collective-permute-start.19 = (bf16[3,16,512]{2,1,0:T(8,128)(2,1)S(1)}, bf16[3,16,512]{2,1,0:T(8,128)(2,1)S(1)}, u32[]{:S(2)}, u32[]{:S(2)}) collective-permute-start(bf16[3,16,512]{2,1,0:T(8,128)(2,1)S(1)} %slice_bitcast_fusion.4), channel_id=1, source_target_pairs={{0,16},{1,17},{2,18},{3,19},{4,20},{5,21},{6,22},{7,23},{8,24},{9,... | collective-permute-start | bytes 147464 | tf_op jit(solution)/shard_map/ppermute | solution.py:36

commit v6 on v4

--- a/solution.py
+++ b/solution.py
@@ -57,19 +57,27 @@
     return pl.BlockSpec(shape, lambda *_: index)
 
 
-def pack_kernel(x_right, p_right, t_right, x_left, p_left, t_left, right_ref, left_ref):
-    for refs, first, out in (((x_right, p_right, t_right), 8, right_ref), ((x_left, p_left, t_left), 0, left_ref)):
-        xs, ps, ts = refs
+def pack_kernel(source_ref, p_right, t_right, p_left, t_left, right_ref, left_ref, x_ref, done):
+    copies = [pltpu.make_async_copy(source_ref.at[t], x_ref.at[t], done.at[t]) for t in range(STEPS)]
+    for copy in copies:
+        copy.start()
+    sides = ((p_right, t_right, 8, right_ref), (p_left, t_left, 0, left_ref))
+    for ps, ts, first, out in sides:
         for r in range(ROWS):
-            planes = [xs[t, r] for t in range(STEPS)] + [ps[r]] + [ts[t, r] for t in range(STEPS - 1)]
+            planes = [ps[r]] + [ts[t, r] for t in range(STEPS - 1)]
             for n, plane in enumerate(planes):
-                out[n * ROWS + r] = plane.astype(F32)[first : first + 8].astype(BF)
+                out[(STEPS + n) * ROWS + r] = plane.astype(F32)[first : first + 8].astype(BF)
+    for t, copy in enumerate(copies):
+        copy.wait()
+        for ps, ts, first, out in sides:
+            for r in range(ROWS):
+                plane = x_ref[t, r, WIDTH - 16 :] if first else x_ref[t, r, :16]
+                out[t * ROWS + r] = plane.astype(F32)[first : first + 8].astype(BF)
 
 
 def pack_edges(x, pending, top):
     def specs(edge):
         return [
-            block((STEPS, ROWS, 16, CH), 0, 0, edge, 0),
             block((ROWS, 16, CH), 0, edge, 0),
             block((STEPS - 1, ROWS, 16, CH), 0, 0, edge, 0),
         ]
@@ -79,12 +87,13 @@
     return pl.pallas_call(
         pack_kernel,
         grid=(1,),
-        out_shape=(shape, shape),
-        in_specs=specs(3) + specs(0),
-        out_specs=(block((24, 8, CH), 0, 0, 0),) * 2,
-        compiler_params=params(),
-        cost_estimate=cost(0, 1 << 20),
-    )(x, pending, top, x, pending, top)
+        out_shape=(shape, shape, pltpu.VMEM(x.shape, BF)),
+        in_specs=[pl.BlockSpec(memory_space=pltpu.HBM)] + specs(3) + specs(0),
+        out_specs=(block((24, 8, CH), 0, 0, 0),) * 2 + (VMEM,),
+        scratch_shapes=[pltpu.SemaphoreType.DMA((STEPS,))],
+        compiler_params=params(),
+        cost_estimate=cost(0, 2 << 20),
+    )(x, pending, top, pending, top)
 
 
 def first_four(high, low):
@@ -211,11 +220,9 @@
     )(*operands, factors, weights)
 
 
-def spread_kernel(place_ref, x_ref, source_ref, out0, out1, w_ref, field_ref, done):
-    copies = [pltpu.make_async_copy(x_ref.at[t], field_ref.at[t], done.at[t]) for t in range(STEPS)]
-    copies.append(pltpu.make_async_copy(source_ref, w_ref, done.at[STEPS]))
-    for copy in copies:
-        copy.start()
+def spread_kernel(place_ref, x_ref, source_ref, out0, out1, w_ref, done):
+    copy = pltpu.make_async_copy(source_ref, w_ref, done)
+    copy.start()
     h, j, k, c = (place_ref[n] for n in range(4))
     lane = lax.broadcasted_iota(jnp.int32, (8, CH), 1)
     chip = jnp.bitwise_xor(lane // HALF, k)
@@ -225,30 +232,26 @@
     source = ((far * 4 + turn) * 4 + chip * 2 + core) * 16 + lane % 16
     row = lax.broadcasted_iota(jnp.int32, (CH, CH), 0)
     order = jnp.where(row == source[:1], 1.0, 0.0).astype(BF)
-    for copy in copies[:STEPS]:
-        copy.wait()
-    field = jnp.concatenate([field_ref[t, r] for t in range(STEPS) for r in range(ROWS)], axis=0)
+    field = jnp.concatenate([x_ref[t, r] for t in range(STEPS) for r in range(ROWS)], axis=0)
     value = jnp.dot(field, order, preferred_element_type=F32).astype(BF)
     for n, out in enumerate((out0, out1)):
         for t in range(STEPS):
             for r in range(ROWS):
                 at = (t * ROWS + r) * WIDTH
                 out[t, r] = value[at : at + WIDTH, n * HALF : (n + 1) * HALF]
-    copies[STEPS].wait()
+    copy.wait()
 
 
 def spread(place, x, weights):
-    x, weights = (pltpu.with_memory_space_constraint(v, pltpu.HBM) for v in (x, weights))
+    x = pltpu.with_memory_space_constraint(x, pltpu.VMEM)
+    weights = pltpu.with_memory_space_constraint(weights, pltpu.HBM)
     shape = jax.ShapeDtypeStruct((STEPS, ROWS, WIDTH, HALF), BF)
     return pl.pallas_call(
         spread_kernel,
         out_shape=(shape, shape, pltpu.VMEM(weights.shape, BF)),
-        in_specs=[SMEM, pl.BlockSpec(memory_space=pltpu.HBM), pl.BlockSpec(memory_space=pltpu.HBM)],
+        in_specs=[SMEM, VMEM, pl.BlockSpec(memory_space=pltpu.HBM)],
         out_specs=(VMEM, VMEM, VMEM),
-        scratch_shapes=[
-            pltpu.VMEM((STEPS, ROWS, WIDTH, CH), BF),
-            pltpu.SemaphoreType.DMA((STEPS + 1,)),
-        ],
+        scratch_shapes=[pltpu.SemaphoreType.DMA],
         compiler_params=params(),
         cost_estimate=cost(4.5e8, 1.2e7),
     )(place, x, weights)
@@ -380,11 +383,11 @@
     flag = last.astype(jnp.int32).reshape(1)
     scale = 1.0 / math.sqrt(STEPS * ROWS * WIDTH * lax.axis_size("az"))
 
-    right_edge, left_edge = pack_edges(x, pending, top)
+    right_edge, left_edge, near_x = pack_edges(x, pending, top)
     low = send(right_edge, RIGHT)
     high = send(left_edge, LEFT)
     taps = filter_weights[0].reshape(9, CH, CH)
-    mine, other, weights = spread(after(place, left_edge), x, taps)
+    mine, other, weights = spread(after(place, left_edge), near_x, taps)
     xs = (mine, send(other, PAIR))
 
     emitted, fields = [], []

time: 91.9 us -> 94.3 us (1.026)
  starting transfers between devices: 42.5 us -> 43.5 us
    pallas_call x1, Pallas kernels: 1.32 us -> 2.37 us  [pack_edges(): pl.pallas_call(pack_kernel, grid=(1,), out_shape=(shape, shape, pltpu.VME...]
    ppermute x17, starting transfers between devices: 35.9 us -> 37 us  [send(): return lax.ppermute(block, 'az', route)]
  transfers between devices with their start and end apart: 20 -> 20, of which waited for: 8 -> 7; matrix products, arithmetic and copies ran while one was open for 2% -> 2% of each run, Pallas kernels for 20% -> 19%
where the time goes in v6:
time: 94.3 us; the launch traced here: 94 us
  starting transfers between devices  43.5 us (46%)
  waiting for transfers between devices  23.7 us (25%)
  Pallas kernels  21 us (22%)
  local copies, waits for them, and re-layouts  2.43 us (3%)
  other arithmetic  2.35 us (2%)
  between operations  0.97 us (1%)
    ppermute x17, starting transfers between devices, send(): return lax.ppermute(block, 'az', route)  37 us
    ppermute x3, waiting for transfers between devices, relay(): return lax.ppermute(block, 'segment', [(i, i - 1) for i in range(1, count)])  13.2 us
    ppermute x17, waiting for transfers between devices, send(): return lax.ppermute(block, 'az', route)  10.4 us
    pallas_call x4, Pallas kernels, back_step(): pl.pallas_call(lambda *refs: back_kernel(first, *refs), grid=(1,), out_sh...  6.65 us
    ppermute x3, starting transfers between devices, relay(): return lax.ppermute(block, 'segment', [(i, i - 1) for i in range(1, count)])  6.58 us
    pallas_call x4, Pallas kernels, slope_factors(): pl.pallas_call(factor_kernel, grid=(1,), out_shape=jax.ShapeDtypeStruct((...  4.5 us
    pallas_call x1, Pallas kernels, spread(): pl.pallas_call(spread_kernel, out_shape=(shape, shape, pltpu.VMEM(weights...  3.63 us
    pallas_call x1, Pallas kernels, early_products(): pl.pallas_call(early_kernel, out_shape=jax.ShapeDtypeStruct((3, HALF, 3 *...  2.75 us
  transfers between devices with their start and end apart: 20, of which 7 were waited for; matrix products, arithmetic and copies ran while one was open for 2% of the time, Pallas kernels for 19%

profile of v6, /device:TPU:6, one launch (start us, length us, event | category | flops | bytes accessed | tf_op | source)
XLA Modules:
  0.0 94.0 jit_solution(1631339530954946401)
XLA Ops:
  0.6 2.4 %shard_map.59 = (bf16[24,8,512]{2,1,0:T(8,128)(2,1)S(1)}, bf16[24,8,512]{2,1,0:T(8,128)(2,1)S(1)}, bf16[4,3,64,512]{3,2,1,0:T(8,128)(2,1)S(1)}) custom-call(bf16[4,3,64,512]{3,2,1,0:T(8,128)(2,1)} %bitcast.59, bf16[3,64,512]{2,1,0:T(8,128)(2,1)} %bitcast.64, bf16[3,3,64,512]{3,2,1,0:T(8,128)(2,1)} %refs_1_.5, bf16[3,64,512]{2,1,0:T(8,128)(2,1)} %bitcast.65, ...), custom_call_target="tpu_custom_call" | custom-call | bytes 2097152 | tf_op jit(solution)/shard_map/pallas_call | solution.py:87
  3.0 0.1 collective-permute-start
  3.1 8.0 %collective-permute-start.1 = (bf16[24,8,512]{2,1,0:T(8,128)(2,1)S(1)}, bf16[24,8,512]{2,1,0:T(8,128)(2,1)S(1)}, u32[]{:S(2)}, u32[]{:S(2)}) collective-permute-start(bf16[24,8,512]{2,1,0:T(8,128)(2,1)S(1)} %get-tuple-element.35), channel_id=1, source_target_pairs={{0,31},{1,0},{2,1},{3,2},{4,3},{5,4},{6,5},{7,6},{8,7},{9,8},{10,9... | collective-permute-start | bytes 589832 | tf_op jit(solution)/shard_map/ppermute | solution.py:36
  11.1 0.1 pad_add_fusion.place_ref
  11.2 3.6 %shard_map.60 = (bf16[4,3,64,256]{3,2,1,0:T(8,128)(2,1)S(1)}, bf16[4,3,64,256]{3,2,1,0:T(8,128)(2,1)}, bf16[9,512,512]{2,1,0:T(8,128)(2,1)S(1)}) custom-call(s32[4]{0:T(128)S(1)} %pad_add_fusion.place_ref, bf16[4,3,64,512]{3,2,1,0:T(8,128)(2,1)S(1)} %get-tuple-element.37.x_ref, bf16[9,512,512]{2,1,0:T(8,128)(2,1)} %bitcast.52), custom_call_target="tpu_custom_call" | custom-call | flops 450000000 | bytes 12000000 | tf_op jit(solution)/shard_map/pallas_call | solution.py:249
  14.8 0.1 collective-permute-start.4
  15.0 1.1 %shard_map.61.refs_3_ = f32[1,3,72,512]{3,2,1,0:T(8,128)S(1)} custom-call(bf16[4,3,64,512]{3,2,1,0:T(8,128)(2,1)S(1)} %bitcast.60, bf16[24,8,512]{2,1,0:T(8,128)(2,1)S(1)} %collective-permute-done.low_ref.refs_1_.refs_2_, bf16[24,8,512]{2,1,0:T(8,128)(2,1)S(1)} %collective-permute-done.1.high_ref.refs_2_.refs_3_, ...), custom_call_target="tpu_custom_call" | custom-call | flops 1200000000 | bytes 5000000 | tf_op jit(solution)/shard_map/pallas_call | solution.py:141
  16.1 1.7 %shard_map.62 = (bf16[3,72,512]{2,1,0:T(8,128)(2,1)S(1)}, bf16[3,72,512]{2,1,0:T(8,128)(2,1)S(1)}) custom-call(bf16[3,64,512]{2,1,0:T(8,128)(2,1)S(1)} %bitcast.66, bf16[24,8,512]{2,1,0:T(8,128)(2,1)S(1)} %collective-permute-done.low_ref.refs_1_.refs_2_, bf16[24,8,512]{2,1,0:T(8,128)(2,1)S(1)} %collective-permute-done.1.high_ref.refs_2_.refs_3_, ...), custom_call_target="tpu_custom_call" | custom-call | flops 1100000000 | bytes 6000000 | tf_op jit(solution)/shard_map/pallas_call | solution.py:209
  17.8 2.7 %collective-permute-start.2 = (bf16[3,72,512]{2,1,0:T(8,128)(2,1)S(1)}, bf16[3,72,512]{2,1,0:T(8,128)(2,1)S(1)}, u32[]{:S(2)}, u32[]{:S(2)}) collective-permute-start(bf16[3,72,512]{2,1,0:T(8,128)(2,1)S(1)} %get-tuple-element.39), channel_id=1, source_target_pairs={{32,0},{64,32},{96,64},{128,96},{160,128},{192,160},{224,192},{33,... | collective-permute-start | bytes 663560 | tf_op jit(solution)/shard_map/ppermute | solution.py:41
  20.5 2.3 %copy-done = bf16[1,3,3,512,512]{4,3,2,1,0:T(8,128)(2,1)S(1)} copy-done((bf16[1,3,3,512,512]{4,3,2,1,0:T(8,128)(2,1)S(1)}, bf16[1,3,3,512,512]{4,3,2,1,0:T(8,128)(2,1)}, u32[]{:S(2)}) %copy-start) | copy-done | bytes 4718616
  22.9 1.1 %shard_map.63.refs_5_ = f32[1,3,72,512]{3,2,1,0:T(8,128)S(1)} custom-call(bf16[4,3,64,512]{3,2,1,0:T(8,128)(2,1)S(1)} %bitcast.61, bf16[24,8,512]{2,1,0:T(8,128)(2,1)S(1)} %collective-permute-done.low_ref.refs_1_.refs_2_, bf16[24,8,512]{2,1,0:T(8,128)(2,1)S(1)} %collective-permute-done.1.high_ref.refs_2_.refs_3_, bf16[9,512,512]{2,1,0:T(8,128)(2,1)S(1)} %bitcast.53), custom_call_target="tpu_custom_call" | custom-call | flops 1200000000 | bytes 5000000 | tf_op jit(solution)/shard_map/pallas_call | solution.py:141
  24.0 3.7 %collective-permute-done.2.refs_4_ = bf16[3,72,512]{2,1,0:T(8,128)(2,1)S(1)} collective-permute-done((bf16[3,72,512]{2,1,0:T(8,128)(2,1)S(1)}, bf16[3,72,512]{2,1,0:T(8,128)(2,1)S(1)}, u32[]{:S(2)}, u32[]{:S(2)}) %collective-permute-start.2) | collective-permute-done | bytes 221216 | tf_op jit(solution)/shard_map/ppermute | solution.py:41
  27.7 1.7 %shard_map.64 = (bf16[3,72,512]{2,1,0:T(8,128)(2,1)S(1)}, bf16[3,72,512]{2,1,0:T(8,128)(2,1)S(1)}) custom-call(s32[1]{0:T(128)} %bitcast.8.refs_0_.flag_ref, bf16[3,3,64,512]{3,2,1,0:T(8,128)(2,1)S(1)} %copy-done.2, bf16[24,8,512]{2,1,0:T(8,128)(2,1)S(1)} %collective-permute-done.low_ref.refs_1_.refs_2_, ...), custom_call_target="tpu_custom_call" | custom-call | flops 1100000000 | bytes 6000000 | tf_op jit(solution)/shard_map/pallas_call | solution.py:209
  29.4 1.9 %collective-permute-start.3 = (bf16[3,72,512]{2,1,0:T(8,128)(2,1)S(1)}, bf16[3,72,512]{2,1,0:T(8,128)(2,1)S(1)}, u32[]{:S(2)}, u32[]{:S(2)}) collective-permute-start(bf16[3,72,512]{2,1,0:T(8,128)(2,1)S(1)} %get-tuple-element.41), channel_id=1, source_target_pairs={{32,0},{64,32},{96,64},{128,96},{160,128},{192,160},{224,192},{33,... | collective-permute-start | bytes 663560 | tf_op jit(solution)/shard_map/ppermute | solution.py:41
  31.3 1.1 %shard_map.65.refs_5_ = f32[1,3,72,512]{3,2,1,0:T(8,128)S(1)} custom-call(bf16[4,3,64,512]{3,2,1,0:T(8,128)(2,1)S(1)} %bitcast.62, bf16[24,8,512]{2,1,0:T(8,128)(2,1)S(1)} %collective-permute-done.low_ref.refs_1_.refs_2_, bf16[24,8,512]{2,1,0:T(8,128)(2,1)S(1)} %collective-permute-done.1.high_ref.refs_2_.refs_3_, bf16[9,512,512]{2,1,0:T(8,128)(2,1)S(1)} %bitcast.55), custom_call_target="tpu_custom_call" | custom-call | flops 1200000000 | bytes 5000000 | tf_op jit(solution)/shard_map/pallas_call | solution.py:141
  32.5 2.1 %collective-permute-start.7 = (bf16[2,3,72,512]{3,2,1,0:T(8,128)(2,1)S(1)}, bf16[2,3,72,512]{3,2,1,0:T(8,128)(2,1)S(1)}, u32[]{:S(2)}, u32[]{:S(2)}) collective-permute-start(bf16[2,3,72,512]{3,2,1,0:T(8,128)(2,1)S(1)} %pad_maximum_fusion.both0), channel_id=1, source_target_pairs={{0,2},{1,3},{2,0},{3,1},{4,6},{5,7},{6,4},{7,5},{8,10},{9,11},{10,... | collective-permute-start | bytes 1327112 | tf_op jit(solution)/shard_map/ppermute | solution.py:36
  34.6 4.7 %collective-permute-done.3.refs_4_ = bf16[3,72,512]{2,1,0:T(8,128)(2,1)S(1)} collective-permute-done((bf16[3,72,512]{2,1,0:T(8,128)(2,1)S(1)}, bf16[3,72,512]{2,1,0:T(8,128)(2,1)S(1)}, u32[]{:S(2)}, u32[]{:S(2)}) %collective-permute-start.3) | collective-permute-done | bytes 221216 | tf_op jit(solution)/shard_map/ppermute | solution.py:41
  39.3 1.7 %shard_map.66 = (bf16[3,72,512]{2,1,0:T(8,128)(2,1)S(1)}, bf16[3,72,512]{2,1,0:T(8,128)(2,1)S(1)}) custom-call(s32[1]{0:T(128)} %bitcast.8.refs_0_.flag_ref, bf16[3,3,64,512]{3,2,1,0:T(8,128)(2,1)S(1)} %copy-done.2, bf16[24,8,512]{2,1,0:T(8,128)(2,1)S(1)} %collective-permute-done.low_ref.refs_1_.refs_2_, ...), custom_call_target="tpu_custom_call" | custom-call | flops 1100000000 | bytes 6000000 | tf_op jit(solution)/shard_map/pallas_call | solution.py:209
  41.0 1.9 %collective-permute-start.5 = (bf16[3,72,512]{2,1,0:T(8,128)(2,1)S(1)}, bf16[3,72,512]{2,1,0:T(8,128)(2,1)S(1)}, u32[]{:S(2)}, u32[]{:S(2)}) collective-permute-start(bf16[3,72,512]{2,1,0:T(8,128)(2,1)S(1)} %get-tuple-element.45), channel_id=1, source_target_pairs={{32,0},{64,32},{96,64},{128,96},{160,128},{192,160},{224,192},{33,... | collective-permute-start | bytes 663560 | tf_op jit(solution)/shard_map/ppermute | solution.py:41
  42.9 1.1 %shard_map.67.factor_ref.refs_5_ = f32[1,3,72,512]{3,2,1,0:T(8,128)S(1)} custom-call(bf16[4,3,64,512]{3,2,1,0:T(8,128)(2,1)S(1)} %bitcast.63, bf16[24,8,512]{2,1,0:T(8,128)(2,1)S(1)} %collective-permute-done.low_ref.refs_1_.refs_2_, bf16[24,8,512]{2,1,0:T(8,128)(2,1)S(1)} %collective-permute-done.1.high_ref.refs_2_.refs_3_, bf16[9,512,512]{2,1,0:T(8,128)(2,1)S(1)} %bitcast.57), custom_call_target="tpu_custom_call" | custom-call | flops 1200000000 | bytes 5000000 | tf_op jit(solution)/shard_map/pallas_call | solution.py:141
  44.1 2.1 %collective-permute-start.8 = (bf16[3,72,512]{2,1,0:T(8,128)(2,1)S(1)}, bf16[3,72,512]{2,1,0:T(8,128)(2,1)S(1)}, u32[]{:S(2)}, u32[]{:S(2)}) collective-permute-start(bf16[3,72,512]{2,1,0:T(8,128)(2,1)S(1)} %get-tuple-element.52.third0), channel_id=1, source_target_pairs={{0,2},{1,3},{2,0},{3,1},{4,6},{5,7},{6,4},{7,5},{8,10},{9,11},{10,... | collective-permute-start | bytes 663560 | tf_op jit(solution)/shard_map/ppermute | solution.py:36
  46.2 4.8 %collective-permute-done.5.relay_ref.refs_4_ = bf16[3,72,512]{2,1,0:T(8,128)(2,1)S(1)} collective-permute-done((bf16[3,72,512]{2,1,0:T(8,128)(2,1)S(1)}, bf16[3,72,512]{2,1,0:T(8,128)(2,1)S(1)}, u32[]{:S(2)}, u32[]{:S(2)}) %collective-permute-start.5) | collective-permute-done | bytes 221216 | tf_op jit(solution)/shard_map/ppermute | solution.py:41
  50.9 0.1 shard_map.68.g0
  51.0 2.3 %collective-permute-start.6 = (bf16[3,72,512]{2,1,0:T(8,128)(2,1)S(1)}, bf16[3,72,512]{2,1,0:T(8,128)(2,1)S(1)}, u32[]{:S(2)}, u32[]{:S(2)}) collective-permute-start(bf16[3,72,512]{2,1,0:T(8,128)(2,1)S(1)} %shard_map.68.g0), channel_id=1, source_target_pairs={{0,2},{1,3},{2,0},{3,1},{4,6},{5,7},{6,4},{7,5},{8,10},{9,11},{10,... | collective-permute-start | bytes 663560 | tf_op jit(solution)/shard_map/ppermute | solution.py:36
  53.3 2.7 %shard_map.69.total_ref = f32[3,256,1536]{2,1,0:T(8,128)S(1)} custom-call(bf16[4,3,64,256]{3,2,1,0:T(8,128)(2,1)S(1)} %get-tuple-element.42.x0, bf16[4,3,64,256]{3,2,1,0:T(8,128)(2,1)S(1)} %collective-permute-done.4.x1, bf16[2,3,72,512]{3,2,1,0:T(8,128)(2,1)S(1)} %pad_maximum_fusion.both0, bf16[2,3,72,512]{3,2,1,0:T(8,128)(2,1)S(1)} %collective-permute-done.7.both1, ...), custom_call_target="tpu_custom_call" | custom-call | flops 3000000000 | bytes 8000000 | tf_op jit(solution)/shard_map/pallas_call | solution.py:294
  56.1 1.2 %collective-permute-done.6.g1 = bf16[3,72,512]{2,1,0:T(8,128)(2,1)S(1)} collective-permute-done((bf16[3,72,512]{2,1,0:T(8,128)(2,1)S(1)}, bf16[3,72,512]{2,1,0:T(8,128)(2,1)S(1)}, u32[]{:S(2)}, u32[]{:S(2)}) %collective-permute-start.6) | collective-permute-done | bytes 221216 | tf_op jit(solution)/shard_map/ppermute | solution.py:36
  57.2 1.1 %shard_map.70 = (bf16[4,6,16,512]{3,2,1,0:T(8,128)(2,1)S(1)}, bf16[4,6,16,512]{3,2,1,0:T(8,128)(2,1)S(1)}, bf16[4,6,16,512]{3,2,1,0:T(8,128)(2,1)S(1)}, bf16[4,6...) custom-call(bf16[4,3,64,256]{3,2,1,0:T(8,128)(2,1)S(1)} %get-tuple-elem, ...), custom_call_target="tpu_custom_call" | custom-call | flops 1000000000 | bytes 8000000 | tf_op jit(solution)/shard_map/pallas_call | solution.py:325
  58.3 0.1 collective-permute-start.9
  58.4 1.7 %collective-permute-done.9 = bf16[4,6,16,512]{3,2,1,0:T(8,128)(2,1)S(1)} collective-permute-done((bf16[4,6,16,512]{3,2,1,0:T(8,128)(2,1)S(1)}, bf16[4,6,16,512]{3,2,1,0:T(8,128)(2,1)S(1)}, u32[]{:S(2)}, u32[]{:S(2)}) %collective-permute-start.9) | collective-permute-done | bytes 393248 | tf_op jit(solution)/shard_map/ppermute | solution.py:36
  60.1 0.1 add_convert_fusion.2
  60.2 0.2 collective-permute-start.10
  60.5 0.6 collective-permute-start.12
  61.1 0.1 collective-permute-start.11
  61.2 0.8 collective-permute-done.10
  62.0 0.1 fusion.8
  62.1 7.9 %collective-permute-start.18 = (bf16[2,3,16,512]{3,2,1,0:T(8,128)(2,1)S(1)}, bf16[2,3,16,512]{3,2,1,0:T(8,128)(2,1)S(1)}, u32[]{:S(2)}, u32[]{:S(2)}) collective-permute-start(bf16[2,3,16,512]{3,2,1,0:T(8,128)(2,1)S(1)} %get-tuple-element.68), channel_id=1, source_target_pairs={{0,12},{1,13},{2,14},{3,15},{4,0},{5,1},{6,2},{7,3},{8,4},{9,5},{1... | collective-permute-start | bytes 294920 | tf_op jit(solution)/shard_map/ppermute | solution.py:36
  70.0 0.8 collective-permute-start.16
  70.8 1.6 %collective-permute-start.17 = (bf16[2,3,16,512]{3,2,1,0:T(8,128)(2,1)S(1)}, bf16[2,3,16,512]{3,2,1,0:T(8,128)(2,1)S(1)}, u32[]{:S(2)}, u32[]{:S(2)}) collective-permute-start(bf16[2,3,16,512]{3,2,1,0:T(8,128)(2,1)S(1)} %get-tuple-element.70), channel_id=1, source_target_pairs={{0,4},{1,5},{2,6},{3,7},{4,8},{5,9},{6,10},{7,11},{8,12},{9,13},{1... | collective-permute-start | bytes 294920 | tf_op jit(solution)/shard_map/ppermute | solution.py:36
  72.5 1.7 %shard_map.71 = (bf16[3,72,512]{2,1,0:T(8,128)(2,1)S(1)}, bf16[3,72,512]{2,1,0:T(8,128)(2,1)}) custom-call(s32[1]{0:T(128)} %bitcast.8.refs_0_.flag_ref, bf16[3,3,64,512]{3,2,1,0:T(8,128)(2,1)S(1)} %copy-done.2, bf16[24,8,512]{2,1,0:T(8,128)(2,1)S(1)} %collective-permute-done.low_ref.refs_1_.refs_2_, ...), custom_call_target="tpu_custom_call" | custom-call | flops 1100000000 | bytes 6000000 | tf_op jit(solution)/shard_map/pallas_call | solution.py:209
  74.2 0.2 add_convert_fusion
  74.4 4.1 %collective-permute-start.13 = (bf16[6,16,512]{2,1,0:T(8,128)(2,1)S(1)}, bf16[6,16,512]{2,1,0:T(8,128)(2,1)S(1)}, u32[]{:S(2)}, u32[]{:S(2)}) collective-permute-start(bf16[6,16,512]{2,1,0:T(8,128)(2,1)S(1)} %get-tuple-element.71), channel_id=1, source_target_pairs={{0,4},{1,5},{2,6},{3,7},{4,8},{5,9},{6,10},{7,11},{8,12},{9,13},{1... | collective-permute-start | bytes 294920 | tf_op jit(solution)/shard_map/ppermute | solution.py:36
  78.5 1.3 %collective-permute-start.15 = (bf16[6,16,512]{2,1,0:T(8,128)(2,1)S(1)}, bf16[6,16,512]{2,1,0:T(8,128)(2,1)S(1)}, u32[]{:S(2)}, u32[]{:S(2)}) collective-permute-start(bf16[6,16,512]{2,1,0:T(8,128)(2,1)S(1)} %get-tuple-element.72), channel_id=1, source_target_pairs={{0,12},{1,13},{2,14},{3,15},{4,0},{5,1},{6,2},{7,3},{8,4},{9,5},{1... | collective-permute-start | bytes 294920 | tf_op jit(solution)/shard_map/ppermute | solution.py:36
  79.8 1.0 %maximum_bitcast_fusion = bf16[4,1,3,64,512]{4,3,2,1,0:T(8,128)(2,1)} fusion(bf16[1,3,64,512]{3,2,1,0:T(8,128)(2,1)S(1)} %slice_bitcast_fusion, bf16[1,3,64,512]{3,2,1,0:T(8,128)(2,1)S(1)} %slice_bitcast_fusion.1, bf16[1,3,64,512]{3,2,1,0:T(8,128)(2,1)S(1)} %slice_bitcast_fusion.2, bf16[1,3,64,512]{3,2,1,0:T(8,128)(2,1)S(1)} %slice_bitcast_fusion.3), kind=kLoop, calls=%fused_computation | loop fusion | flops 1179648 | bytes 1572864
  80.8 2.4 %collective-permute-start.14 = (bf16[6,16,512]{2,1,0:T(8,128)(2,1)S(1)}, bf16[6,16,512]{2,1,0:T(8,128)(2,1)S(1)}, u32[]{:S(2)}, u32[]{:S(2)}) collective-permute-start(bf16[6,16,512]{2,1,0:T(8,128)(2,1)S(1)} %get-tuple-element.73), channel_id=1, source_target_pairs={{0,8},{1,9},{2,10},{3,11},{4,12},{5,13},{6,14},{7,15},{8,0},{9,1},... | collective-permute-start | bytes 294920 | tf_op jit(solution)/shard_map/ppermute | solution.py:36
  83.2 0.1 fusion.3
  83.3 3.2 %collective-permute-start.19 = (bf16[3,16,512]{2,1,0:T(8,128)(2,1)S(1)}, bf16[3,16,512]{2,1,0:T(8,128)(2,1)S(1)}, u32[]{:S(2)}, u32[]{:S(2)}) collective-permute-start(bf16[3,16,512]{2,1,0:T(8,128)(2,1)S(1)} %slice_bitcast_fusion.8), channel_id=1, source_target_pairs={{0,16},{1,17},{2,18},{3,19},{4,20},{5,21},{6,22},{7,23},{8,24},{9,... | collective-permute-start | bytes 147464 | tf_op jit(solution)/shard_map/ppermute | solution.py:36
  86.5 6.7 %collective-permute-done.14 = bf16[6,16,512]{2,1,0:T(8,128)(2,1)S(1)} collective-permute-done((bf16[6,16,512]{2,1,0:T(8,128)(2,1)S(1)}, bf16[6,16,512]{2,1,0:T(8,128)(2,1)S(1)}, u32[]{:S(2)}, u32[]{:S(2)}) %collective-permute-start.14) | collective-permute-done | bytes 98336 | tf_op jit(solution)/shard_map/ppermute | solution.py:36
  93.3 0.7 fusion
  (31 shorter events, 0.2 us)
Async XLA Ops:
  0.6 14.3 %copy-start.3 = (bf16[4,1,3,64,512]{4,3,2,1,0:T(8,128)(2,1)S(1)}, bf16[4,1,3,64,512]{4,3,2,1,0:T(8,128)(2,1)}, u32[]{:S(2)}) copy-start(bf16[4,1,3,64,512]{4,3,2,1,0:T(8,128)(2,1)} %param.4) | copy-start | bytes 2359300
  3.0 11.9 %collective-permute-start = (bf16[24,8,512]{2,1,0:T(8,128)(2,1)S(1)}, bf16[24,8,512]{2,1,0:T(8,128)(2,1)S(1)}, u32[]{:S(2)}, u32[]{:S(2)}) collective-permute-start(bf16[24,8,512]{2,1,0:T(8,128)(2,1)S(1)} %get-tuple-element.34), channel_id=1, source_target_pairs={{0,1},{1,2},{2,3},{3,4},{4,5},{5,6},{6,7},{7,8},{8,9},{9,10},{10,1... | collective-permute-start | bytes 589832 | tf_op jit(solution)/shard_map/ppermute | solution.py:36
  3.1 11.8 %collective-permute-start.1 = (bf16[24,8,512]{2,1,0:T(8,128)(2,1)S(1)}, bf16[24,8,512]{2,1,0:T(8,128)(2,1)S(1)}, u32[]{:S(2)}, u32[]{:S(2)}) collective-permute-start(bf16[24,8,512]{2,1,0:T(8,128)(2,1)S(1)} %get-tuple-element.35), channel_id=1, source_target_pairs={{0,31},{1,0},{2,1},{3,2},{4,3},{5,4},{6,5},{7,6},{8,7},{9,8},{10,9... | collective-permute-start | bytes 589832 | tf_op jit(solution)/shard_map/ppermute | solution.py:36
  11.2 4.9 %copy-start.4 = (bf16[1,3,64,512]{3,2,1,0:T(8,128)(2,1)S(1)}, bf16[1,3,64,512]{3,2,1,0:T(8,128)(2,1)}, u32[]{:S(2)}) copy-start(bf16[1,3,64,512]{3,2,1,0:T(8,128)(2,1)} %param.6) | copy-start | bytes 589828
  14.8 16.5 %collective-permute-start.4 = (bf16[4,3,64,256]{3,2,1,0:T(8,128)(2,1)}, bf16[4,3,64,256]{3,2,1,0:T(8,128)(2,1)S(1)}, u32[]{:S(2)}, u32[]{:S(2)}) collective-permute-start(bf16[4,3,64,256]{3,2,1,0:T(8,128)(2,1)} %get-tuple-element.43), channel_id=1, source_target_pairs={{0,2},{1,3},{2,0},{3,1},{4,6},{5,7},{6,4},{7,5},{8,10},{9,11},{10,... | collective-permute-start | bytes 1179656 | tf_op jit(solution)/shard_map/ppermute | solution.py:36
  16.1 11.6 %copy-start.2 = (bf16[3,3,64,512]{3,2,1,0:T(8,128)(2,1)S(1)}, bf16[3,3,64,512]{3,2,1,0:T(8,128)(2,1)}, u32[]{:S(2)}) copy-start(bf16[3,3,64,512]{3,2,1,0:T(8,128)(2,1)} %refs_1_.5) | copy-start | bytes 1769476
  17.8 9.9 %collective-permute-start.2 = (bf16[3,72,512]{2,1,0:T(8,128)(2,1)S(1)}, bf16[3,72,512]{2,1,0:T(8,128)(2,1)S(1)}, u32[]{:S(2)}, u32[]{:S(2)}) collective-permute-start(bf16[3,72,512]{2,1,0:T(8,128)(2,1)S(1)} %get-tuple-element.39), channel_id=1, source_target_pairs={{32,0},{64,32},{96,64},{128,96},{160,128},{192,160},{224,192},{33,... | collective-permute-start | bytes 663560 | tf_op jit(solution)/shard_map/ppermute | solution.py:41
  20.5 2.3 %copy-start = (bf16[1,3,3,512,512]{4,3,2,1,0:T(8,128)(2,1)S(1)}, bf16[1,3,3,512,512]{4,3,2,1,0:T(8,128)(2,1)}, u32[]{:S(2)}) copy-start(bf16[1,3,3,512,512]{4,3,2,1,0:T(8,128)(2,1)} %param.5) | copy-start | bytes 14155780
  22.9 4.8 %copy-start.1 = (bf16[1,3,3,512,512]{4,3,2,1,0:T(8,128)(2,1)S(1)}, bf16[1,3,3,512,512]{4,3,2,1,0:T(8,128)(2,1)}, u32[]{:S(2)}) copy-start(bf16[1,3,3,512,512]{4,3,2,1,0:T(8,128)(2,1)} %param.5) | copy-start | bytes 14155780
  29.4 9.9 %collective-permute-start.3 = (bf16[3,72,512]{2,1,0:T(8,128)(2,1)S(1)}, bf16[3,72,512]{2,1,0:T(8,128)(2,1)S(1)}, u32[]{:S(2)}, u32[]{:S(2)}) collective-permute-start(bf16[3,72,512]{2,1,0:T(8,128)(2,1)S(1)} %get-tuple-element.41), channel_id=1, source_target_pairs={{32,0},{64,32},{96,64},{128,96},{160,128},{192,160},{224,192},{33,... | collective-permute-start | bytes 663560 | tf_op jit(solution)/shard_map/ppermute | solution.py:41
  32.5 20.8 %collective-permute-start.7 = (bf16[2,3,72,512]{3,2,1,0:T(8,128)(2,1)S(1)}, bf16[2,3,72,512]{3,2,1,0:T(8,128)(2,1)S(1)}, u32[]{:S(2)}, u32[]{:S(2)}) collective-permute-start(bf16[2,3,72,512]{3,2,1,0:T(8,128)(2,1)S(1)} %pad_maximum_fusion.both0), channel_id=1, source_target_pairs={{0,2},{1,3},{2,0},{3,1},{4,6},{5,7},{6,4},{7,5},{8,10},{9,11},{10,... | collective-permute-start | bytes 1327112 | tf_op jit(solution)/shard_map/ppermute | solution.py:36
  41.0 9.9 %collective-permute-start.5 = (bf16[3,72,512]{2,1,0:T(8,128)(2,1)S(1)}, bf16[3,72,512]{2,1,0:T(8,128)(2,1)S(1)}, u32[]{:S(2)}, u32[]{:S(2)}) collective-permute-start(bf16[3,72,512]{2,1,0:T(8,128)(2,1)S(1)} %get-tuple-element.45), channel_id=1, source_target_pairs={{32,0},{64,32},{96,64},{128,96},{160,128},{192,160},{224,192},{33,... | collective-permute-start | bytes 663560 | tf_op jit(solution)/shard_map/ppermute | solution.py:41
  44.1 9.2 %collective-permute-start.8 = (bf16[3,72,512]{2,1,0:T(8,128)(2,1)S(1)}, bf16[3,72,512]{2,1,0:T(8,128)(2,1)S(1)}, u32[]{:S(2)}, u32[]{:S(2)}) collective-permute-start(bf16[3,72,512]{2,1,0:T(8,128)(2,1)S(1)} %get-tuple-element.52.third0), channel_id=1, source_target_pairs={{0,2},{1,3},{2,0},{3,1},{4,6},{5,7},{6,4},{7,5},{8,10},{9,11},{10,... | collective-permute-start | bytes 663560 | tf_op jit(solution)/shard_map/ppermute | solution.py:36
  51.0 6.2 %collective-permute-start.6 = (bf16[3,72,512]{2,1,0:T(8,128)(2,1)S(1)}, bf16[3,72,512]{2,1,0:T(8,128)(2,1)S(1)}, u32[]{:S(2)}, u32[]{:S(2)}) collective-permute-start(bf16[3,72,512]{2,1,0:T(8,128)(2,1)S(1)} %shard_map.68.g0), channel_id=1, source_target_pairs={{0,2},{1,3},{2,0},{3,1},{4,6},{5,7},{6,4},{7,5},{8,10},{9,11},{10,... | collective-permute-start | bytes 663560 | tf_op jit(solution)/shard_map/ppermute | solution.py:36
  58.3 1.8 %collective-permute-start.9 = (bf16[4,6,16,512]{3,2,1,0:T(8,128)(2,1)S(1)}, bf16[4,6,16,512]{3,2,1,0:T(8,128)(2,1)S(1)}, u32[]{:S(2)}, u32[]{:S(2)}) collective-permute-start(bf16[4,6,16,512]{3,2,1,0:T(8,128)(2,1)S(1)} %get-tuple-element.57), channel_id=1, source_target_pairs={{0,1},{1,0},{2,3},{3,2},{4,5},{5,4},{6,7},{7,6},{8,9},{9,8},{10,11... | collective-permute-start | bytes 1179656 | tf_op jit(solution)/shard_map/ppermute | solution.py:36
  60.2 1.8 %collective-permute-start.10 = (bf16[4,2,3,16,512]{4,3,2,1,0:T(8,128)(2,1)S(1)}, bf16[4,2,3,16,512]{4,3,2,1,0:T(8,128)(2,1)S(1)}, u32[]{:S(2)}, u32[]{:S(2)}) collective-permute-start(bf16[4,2,3,16,512]{4,3,2,1,0:T(8,128)(2,1)S(1)} %get-tuple-element.58), channel_id=1, source_target_pairs={{0,1},{1,0},{2,3},{3,2},{4,5},{5,4},{6,7},{7,6},{8,9},{9,8},{10,11... | collective-permute-start | bytes 1179656 | tf_op jit(solution)/shard_map/ppermute | solution.py:36
  60.5 13.7 %collective-permute-start.12 = (bf16[4,6,16,512]{3,2,1,0:T(8,128)(2,1)S(1)}, bf16[4,6,16,512]{3,2,1,0:T(8,128)(2,1)S(1)}, u32[]{:S(2)}, u32[]{:S(2)}) collective-permute-start(bf16[4,6,16,512]{3,2,1,0:T(8,128)(2,1)S(1)} %add_convert_fusion.2), channel_id=1, source_target_pairs={{0,16},{1,17},{2,18},{3,19},{4,20},{5,21},{6,22},{7,23},{8,24},{9,... | collective-permute-start | bytes 1179656 | tf_op jit(solution)/shard_map/ppermute | solution.py:36
  61.1 13.0 %collective-permute-start.11 = (bf16[4,6,16,512]{3,2,1,0:T(8,128)(2,1)S(1)}, bf16[4,6,16,512]{3,2,1,0:T(8,128)(2,1)S(1)}, u32[]{:S(2)}, u32[]{:S(2)}) collective-permute-start(bf16[4,6,16,512]{3,2,1,0:T(8,128)(2,1)S(1)} %get-tuple-element.62), channel_id=1, source_target_pairs={{0,1},{1,0},{2,3},{3,2},{4,5},{5,4},{6,7},{7,6},{8,9},{9,8},{10,11... | collective-permute-start | bytes 1179656 | tf_op jit(solution)/shard_map/ppermute | solution.py:36
  62.1 18.6 %collective-permute-start.18 = (bf16[2,3,16,512]{3,2,1,0:T(8,128)(2,1)S(1)}, bf16[2,3,16,512]{3,2,1,0:T(8,128)(2,1)S(1)}, u32[]{:S(2)}, u32[]{:S(2)}) collective-permute-start(bf16[2,3,16,512]{3,2,1,0:T(8,128)(2,1)S(1)} %get-tuple-element.68), channel_id=1, source_target_pairs={{0,12},{1,13},{2,14},{3,15},{4,0},{5,1},{6,2},{7,3},{8,4},{9,5},{1... | collective-permute-start | bytes 294920 | tf_op jit(solution)/shard_map/ppermute | solution.py:36
  70.0 13.2 %collective-permute-start.16 = (bf16[2,3,16,512]{3,2,1,0:T(8,128)(2,1)S(1)}, bf16[2,3,16,512]{3,2,1,0:T(8,128)(2,1)S(1)}, u32[]{:S(2)}, u32[]{:S(2)}) collective-permute-start(bf16[2,3,16,512]{3,2,1,0:T(8,128)(2,1)S(1)} %get-tuple-element.69), channel_id=1, source_target_pairs={{0,8},{1,9},{2,10},{3,11},{4,12},{5,13},{6,14},{7,15},{8,0},{9,1},... | collective-permute-start | bytes 294920 | tf_op jit(solution)/shard_map/ppermute | solution.py:36
  70.8 12.4 %collective-permute-start.17 = (bf16[2,3,16,512]{3,2,1,0:T(8,128)(2,1)S(1)}, bf16[2,3,16,512]{3,2,1,0:T(8,128)(2,1)S(1)}, u32[]{:S(2)}, u32[]{:S(2)}) collective-permute-start(bf16[2,3,16,512]{3,2,1,0:T(8,128)(2,1)S(1)} %get-tuple-element.70), channel_id=1, source_target_pairs={{0,4},{1,5},{2,6},{3,7},{4,8},{5,9},{6,10},{7,11},{8,12},{9,13},{1... | collective-permute-start | bytes 294920 | tf_op jit(solution)/shard_map/ppermute | solution.py:36
  74.4 12.1 %collective-permute-start.13 = (bf16[6,16,512]{2,1,0:T(8,128)(2,1)S(1)}, bf16[6,16,512]{2,1,0:T(8,128)(2,1)S(1)}, u32[]{:S(2)}, u32[]{:S(2)}) collective-permute-start(bf16[6,16,512]{2,1,0:T(8,128)(2,1)S(1)} %get-tuple-element.71), channel_id=1, source_target_pairs={{0,4},{1,5},{2,6},{3,7},{4,8},{5,9},{6,10},{7,11},{8,12},{9,13},{1... | collective-permute-start | bytes 294920 | tf_op jit(solution)/shard_map/ppermute | solution.py:36
  78.5 8.0 %collective-permute-start.15 = (bf16[6,16,512]{2,1,0:T(8,128)(2,1)S(1)}, bf16[6,16,512]{2,1,0:T(8,128)(2,1)S(1)}, u32[]{:S(2)}, u32[]{:S(2)}) collective-permute-start(bf16[6,16,512]{2,1,0:T(8,128)(2,1)S(1)} %get-tuple-element.72), channel_id=1, source_target_pairs={{0,12},{1,13},{2,14},{3,15},{4,0},{5,1},{6,2},{7,3},{8,4},{9,5},{1... | collective-permute-start | bytes 294920 | tf_op jit(solution)/shard_map/ppermute | solution.py:36
  80.8 12.4 %collective-permute-start.14 = (bf16[6,16,512]{2,1,0:T(8,128)(2,1)S(1)}, bf16[6,16,512]{2,1,0:T(8,128)(2,1)S(1)}, u32[]{:S(2)}, u32[]{:S(2)}) collective-permute-start(bf16[6,16,512]{2,1,0:T(8,128)(2,1)S(1)} %get-tuple-element.73), channel_id=1, source_target_pairs={{0,8},{1,9},{2,10},{3,11},{4,12},{5,13},{6,14},{7,15},{8,0},{9,1},... | collective-permute-start | bytes 294920 | tf_op jit(solution)/shard_map/ppermute | solution.py:36
  83.3 10.0 %collective-permute-start.19 = (bf16[3,16,512]{2,1,0:T(8,128)(2,1)S(1)}, bf16[3,16,512]{2,1,0:T(8,128)(2,1)S(1)}, u32[]{:S(2)}, u32[]{:S(2)}) collective-permute-start(bf16[3,16,512]{2,1,0:T(8,128)(2,1)S(1)} %slice_bitcast_fusion.8), channel_id=1, source_target_pairs={{0,16},{1,17},{2,18},{3,19},{4,20},{5,21},{6,22},{7,23},{8,24},{9,... | collective-permute-start | bytes 147464 | tf_op jit(solution)/shard_map/ppermute | solution.py:36

commit v7 on v4

--- a/solution.py
+++ b/solution.py
@@ -38,7 +38,7 @@
 
 def relay(block):
     count = lax.axis_size("segment")
-    return lax.ppermute(block, "segment", [(i, i - 1) for i in range(1, count)])
+    return lax.ppermute(block, "segment", [(i, (i - 1) % count) for i in range(count)])
 
 
 def params(mib=24):

time: 91.9 us -> 86.4 us (0.940)
  starting transfers between devices: 42.5 us -> 36.6 us
    ppermute x3, starting transfers between devices: 6.57 us -> 1.07 us  [relay(): lax.ppermute(block, 'segment', [(i, (i - 1) % count) for i in range(count)])]
    ppermute x17, waiting for transfers between devices: 9.77 us -> 10.9 us  [send(): return lax.ppermute(block, 'az', route)]
  transfers between devices with their start and end apart: 20 -> 20, of which waited for: 8 -> 8; matrix products, arithmetic and copies ran while one was open for 2% -> 2% of each run, Pallas kernels for 20% -> 21%
where the time goes in v7:
time: 86.4 us; the launch traced here: 86 us
  starting transfers between devices  36.6 us (42%)
  waiting for transfers between devices  23.3 us (27%)
  Pallas kernels  20.4 us (24%)
  local copies, waits for them, and re-layouts  2.44 us (3%)
  other arithmetic  2.34 us (3%)
  between operations  0.94 us (1%)
    ppermute x17, starting transfers between devices, send(): return lax.ppermute(block, 'az', route)  35.5 us
    ppermute x3, waiting for transfers between devices, relay(): lax.ppermute(block, 'segment', [(i, (i - 1) % count) for i in range(count)])  12.4 us
    ppermute x17, waiting for transfers between devices, send(): return lax.ppermute(block, 'az', route)  10.9 us
    pallas_call x4, Pallas kernels, back_step(): pl.pallas_call(lambda *refs: back_kernel(first, *refs), grid=(1,), out_sh...  6.66 us
    pallas_call x4, Pallas kernels, slope_factors(): pl.pallas_call(factor_kernel, grid=(1,), out_shape=jax.ShapeDtypeStruct((...  4.5 us
    pallas_call x1, Pallas kernels, spread(): pl.pallas_call(spread_kernel, out_shape=(shape, shape, pltpu.VMEM(weights...  4.04 us
    pallas_call x1, Pallas kernels, early_products(): pl.pallas_call(early_kernel, out_shape=jax.ShapeDtypeStruct((3, HALF, 3 *...  2.75 us
    unnamed x10, local copies, waits for them, and re-layouts  2.36 us
  transfers between devices with their start and end apart: 20, of which 8 were waited for; matrix products, arithmetic and copies ran while one was open for 2% of the time, Pallas kernels for 21%

profile of v7, /device:TPU:6, one launch (start us, length us, event | category | flops | bytes accessed | tf_op | source)
XLA Modules:
  0.0 86.0 jit_solution(2311290870134659362)
XLA Ops:
  0.6 1.3 %shard_map.59 = (bf16[24,8,512]{2,1,0:T(8,128)(2,1)S(1)}, bf16[24,8,512]{2,1,0:T(8,128)(2,1)S(1)}) custom-call(bf16[4,3,64,512]{3,2,1,0:T(8,128)(2,1)} %bitcast.59, bf16[3,64,512]{2,1,0:T(8,128)(2,1)} %bitcast.66, bf16[3,3,64,512]{3,2,1,0:T(8,128)(2,1)} %refs_1_.5, bf16[4,3,64,512]{3,2,1,0:T(8,128)(2,1)} %bitcast.60, bf16[3,64,512]{2,1,0:T(8,128)(2,1)} %bitcast.67, ...), custom_call_target="tpu_custom_call" | custom-call | bytes 1048576 | tf_op jit(solution)/shard_map/pallas_call | solution.py:79
  2.0 0.1 collective-permute-start
  2.1 8.0 %collective-permute-start.1 = (bf16[24,8,512]{2,1,0:T(8,128)(2,1)S(1)}, bf16[24,8,512]{2,1,0:T(8,128)(2,1)S(1)}, u32[]{:S(2)}, u32[]{:S(2)}) collective-permute-start(bf16[24,8,512]{2,1,0:T(8,128)(2,1)S(1)} %get-tuple-element.34), channel_id=1, source_target_pairs={{0,31},{1,0},{2,1},{3,2},{4,3},{5,4},{6,5},{7,6},{8,7},{9,8},{10,9... | collective-permute-start | bytes 589832 | tf_op jit(solution)/shard_map/ppermute | solution.py:36
  10.1 0.1 pad_add_fusion.place_ref
  10.1 4.0 %shard_map.60 = (bf16[4,3,64,256]{3,2,1,0:T(8,128)(2,1)S(1)}, bf16[4,3,64,256]{3,2,1,0:T(8,128)(2,1)}, bf16[9,512,512]{2,1,0:T(8,128)(2,1)S(1)}) custom-call(s32[4]{0:T(128)S(1)} %pad_add_fusion.place_ref, bf16[4,3,64,512]{3,2,1,0:T(8,128)(2,1)} %bitcast.61, bf16[9,512,512]{2,1,0:T(8,128)(2,1)} %bitcast.52), custom_call_target="tpu_custom_call" | custom-call | flops 450000000 | bytes 12000000 | tf_op jit(solution)/shard_map/pallas_call | solution.py:243
  14.2 0.1 collective-permute-start.4
  14.3 1.1 %shard_map.61.refs_3_ = f32[1,3,72,512]{3,2,1,0:T(8,128)S(1)} custom-call(bf16[4,3,64,512]{3,2,1,0:T(8,128)(2,1)S(1)} %bitcast.62, bf16[24,8,512]{2,1,0:T(8,128)(2,1)S(1)} %collective-permute-done.low_ref.refs_1_.refs_2_, bf16[24,8,512]{2,1,0:T(8,128)(2,1)S(1)} %collective-permute-done.1.high_ref.refs_2_.refs_3_, ...), custom_call_target="tpu_custom_call" | custom-call | flops 1200000000 | bytes 5000000 | tf_op jit(solution)/shard_map/pallas_call | solution.py:132
  15.5 1.7 %shard_map.62 = (bf16[3,72,512]{2,1,0:T(8,128)(2,1)S(1)}, bf16[3,72,512]{2,1,0:T(8,128)(2,1)S(1)}) custom-call(bf16[3,64,512]{2,1,0:T(8,128)(2,1)S(1)} %bitcast.68, bf16[24,8,512]{2,1,0:T(8,128)(2,1)S(1)} %collective-permute-done.low_ref.refs_1_.refs_2_, bf16[24,8,512]{2,1,0:T(8,128)(2,1)S(1)} %collective-permute-done.1.high_ref.refs_2_.refs_3_, ...), custom_call_target="tpu_custom_call" | custom-call | flops 1100000000 | bytes 6000000 | tf_op jit(solution)/shard_map/pallas_call | solution.py:200
  17.1 0.9 %collective-permute-start.2 = (bf16[3,72,512]{2,1,0:T(8,128)(2,1)S(1)}, bf16[3,72,512]{2,1,0:T(8,128)(2,1)S(1)}, u32[]{:S(2)}, u32[]{:S(2)}) collective-permute-start(bf16[3,72,512]{2,1,0:T(8,128)(2,1)S(1)} %get-tuple-element.37), channel_id=1, source_target_pairs={{0,224},{32,0},{64,32},{96,64},{128,96},{160,128},{192,160},{224,1... | collective-permute-start | bytes 663560 | tf_op jit(solution)/shard_map/ppermute | solution.py:41
  18.0 2.3 %copy-done = bf16[1,3,3,512,512]{4,3,2,1,0:T(8,128)(2,1)S(1)} copy-done((bf16[1,3,3,512,512]{4,3,2,1,0:T(8,128)(2,1)S(1)}, bf16[1,3,3,512,512]{4,3,2,1,0:T(8,128)(2,1)}, u32[]{:S(2)}) %copy-start) | copy-done | bytes 4718616
  20.4 1.1 %shard_map.63.refs_5_ = f32[1,3,72,512]{3,2,1,0:T(8,128)S(1)} custom-call(bf16[4,3,64,512]{3,2,1,0:T(8,128)(2,1)S(1)} %bitcast.63, bf16[24,8,512]{2,1,0:T(8,128)(2,1)S(1)} %collective-permute-done.low_ref.refs_1_.refs_2_, bf16[24,8,512]{2,1,0:T(8,128)(2,1)S(1)} %collective-permute-done.1.high_ref.refs_2_.refs_3_, bf16[9,512,512]{2,1,0:T(8,128)(2,1)S(1)} %bitcast.53), custom_call_target="tpu_custom_call" | custom-call | flops 1200000000 | bytes 5000000 | tf_op jit(solution)/shard_map/pallas_call | solution.py:132
  21.5 3.7 %collective-permute-done.2.refs_4_ = bf16[3,72,512]{2,1,0:T(8,128)(2,1)S(1)} collective-permute-done((bf16[3,72,512]{2,1,0:T(8,128)(2,1)S(1)}, bf16[3,72,512]{2,1,0:T(8,128)(2,1)S(1)}, u32[]{:S(2)}, u32[]{:S(2)}) %collective-permute-start.2) | collective-permute-done | bytes 221216 | tf_op jit(solution)/shard_map/ppermute | solution.py:41
  25.3 1.7 %shard_map.64 = (bf16[3,72,512]{2,1,0:T(8,128)(2,1)S(1)}, bf16[3,72,512]{2,1,0:T(8,128)(2,1)S(1)}) custom-call(s32[1]{0:T(128)} %bitcast.8.refs_0_.flag_ref, bf16[3,3,64,512]{3,2,1,0:T(8,128)(2,1)S(1)} %copy-done.3, bf16[24,8,512]{2,1,0:T(8,128)(2,1)S(1)} %collective-permute-done.low_ref.refs_1_.refs_2_, ...), custom_call_target="tpu_custom_call" | custom-call | flops 1100000000 | bytes 6000000 | tf_op jit(solution)/shard_map/pallas_call | solution.py:200
  26.9 0.1 collective-permute-start.3
  27.0 1.1 %shard_map.65.refs_5_ = f32[1,3,72,512]{3,2,1,0:T(8,128)S(1)} custom-call(bf16[4,3,64,512]{3,2,1,0:T(8,128)(2,1)S(1)} %bitcast.64, bf16[24,8,512]{2,1,0:T(8,128)(2,1)S(1)} %collective-permute-done.low_ref.refs_1_.refs_2_, bf16[24,8,512]{2,1,0:T(8,128)(2,1)S(1)} %collective-permute-done.1.high_ref.refs_2_.refs_3_, bf16[9,512,512]{2,1,0:T(8,128)(2,1)S(1)} %bitcast.55), custom_call_target="tpu_custom_call" | custom-call | flops 1200000000 | bytes 5000000 | tf_op jit(solution)/shard_map/pallas_call | solution.py:132
  28.2 2.1 %collective-permute-start.7 = (bf16[2,3,72,512]{3,2,1,0:T(8,128)(2,1)S(1)}, bf16[2,3,72,512]{3,2,1,0:T(8,128)(2,1)S(1)}, u32[]{:S(2)}, u32[]{:S(2)}) collective-permute-start(bf16[2,3,72,512]{3,2,1,0:T(8,128)(2,1)S(1)} %pad_maximum_fusion.both0), channel_id=1, source_target_pairs={{0,2},{1,3},{2,0},{3,1},{4,6},{5,7},{6,4},{7,5},{8,10},{9,11},{10,... | collective-permute-start | bytes 1327112 | tf_op jit(solution)/shard_map/ppermute | solution.py:36
  30.3 4.9 %collective-permute-done.3.refs_4_ = bf16[3,72,512]{2,1,0:T(8,128)(2,1)S(1)} collective-permute-done((bf16[3,72,512]{2,1,0:T(8,128)(2,1)S(1)}, bf16[3,72,512]{2,1,0:T(8,128)(2,1)S(1)}, u32[]{:S(2)}, u32[]{:S(2)}) %collective-permute-start.3) | collective-permute-done | bytes 221216 | tf_op jit(solution)/shard_map/ppermute | solution.py:41
  35.2 1.7 %shard_map.66 = (bf16[3,72,512]{2,1,0:T(8,128)(2,1)S(1)}, bf16[3,72,512]{2,1,0:T(8,128)(2,1)S(1)}) custom-call(s32[1]{0:T(128)} %bitcast.8.refs_0_.flag_ref, bf16[3,3,64,512]{3,2,1,0:T(8,128)(2,1)S(1)} %copy-done.3, bf16[24,8,512]{2,1,0:T(8,128)(2,1)S(1)} %collective-permute-done.low_ref.refs_1_.refs_2_, ...), custom_call_target="tpu_custom_call" | custom-call | flops 1100000000 | bytes 6000000 | tf_op jit(solution)/shard_map/pallas_call | solution.py:200
  36.9 0.1 collective-permute-start.5
  37.0 1.1 %shard_map.67.factor_ref.refs_5_ = f32[1,3,72,512]{3,2,1,0:T(8,128)S(1)} custom-call(bf16[4,3,64,512]{3,2,1,0:T(8,128)(2,1)S(1)} %bitcast.65, bf16[24,8,512]{2,1,0:T(8,128)(2,1)S(1)} %collective-permute-done.low_ref.refs_1_.refs_2_, bf16[24,8,512]{2,1,0:T(8,128)(2,1)S(1)} %collective-permute-done.1.high_ref.refs_2_.refs_3_, bf16[9,512,512]{2,1,0:T(8,128)(2,1)S(1)} %bitcast.57), custom_call_target="tpu_custom_call" | custom-call | flops 1200000000 | bytes 5000000 | tf_op jit(solution)/shard_map/pallas_call | solution.py:132
  38.1 3.1 %collective-permute-start.8 = (bf16[3,72,512]{2,1,0:T(8,128)(2,1)S(1)}, bf16[3,72,512]{2,1,0:T(8,128)(2,1)S(1)}, u32[]{:S(2)}, u32[]{:S(2)}) collective-permute-start(bf16[3,72,512]{2,1,0:T(8,128)(2,1)S(1)} %get-tuple-element.50.third0), channel_id=1, source_target_pairs={{0,2},{1,3},{2,0},{3,1},{4,6},{5,7},{6,4},{7,5},{8,10},{9,11},{10,... | collective-permute-start | bytes 663560 | tf_op jit(solution)/shard_map/ppermute | solution.py:36
  41.2 3.8 %collective-permute-done.5.relay_ref.refs_4_ = bf16[3,72,512]{2,1,0:T(8,128)(2,1)S(1)} collective-permute-done((bf16[3,72,512]{2,1,0:T(8,128)(2,1)S(1)}, bf16[3,72,512]{2,1,0:T(8,128)(2,1)S(1)}, u32[]{:S(2)}, u32[]{:S(2)}) %collective-permute-start.5) | collective-permute-done | bytes 221216 | tf_op jit(solution)/shard_map/ppermute | solution.py:41
  45.1 2.9 %collective-permute-start.6 = (bf16[3,72,512]{2,1,0:T(8,128)(2,1)S(1)}, bf16[3,72,512]{2,1,0:T(8,128)(2,1)S(1)}, u32[]{:S(2)}, u32[]{:S(2)}) collective-permute-start(bf16[3,72,512]{2,1,0:T(8,128)(2,1)S(1)} %shard_map.68.g0), channel_id=1, source_target_pairs={{0,2},{1,3},{2,0},{3,1},{4,6},{5,7},{6,4},{7,5},{8,10},{9,11},{10,... | collective-permute-start | bytes 663560 | tf_op jit(solution)/shard_map/ppermute | solution.py:36
  48.0 2.7 %shard_map.69.total_ref = f32[3,256,1536]{2,1,0:T(8,128)S(1)} custom-call(bf16[4,3,64,256]{3,2,1,0:T(8,128)(2,1)S(1)} %get-tuple-element.40.x0, bf16[4,3,64,256]{3,2,1,0:T(8,128)(2,1)S(1)} %collective-permute-done.4.x1, bf16[2,3,72,512]{3,2,1,0:T(8,128)(2,1)S(1)} %pad_maximum_fusion.both0, bf16[2,3,72,512]{3,2,1,0:T(8,128)(2,1)S(1)} %collective-permute-done.7.both1, ...), custom_call_target="tpu_custom_call" | custom-call | flops 3000000000 | bytes 8000000 | tf_op jit(solution)/shard_map/pallas_call | solution.py:291
  50.8 1.1 %collective-permute-done.6.g1 = bf16[3,72,512]{2,1,0:T(8,128)(2,1)S(1)} collective-permute-done((bf16[3,72,512]{2,1,0:T(8,128)(2,1)S(1)}, bf16[3,72,512]{2,1,0:T(8,128)(2,1)S(1)}, u32[]{:S(2)}, u32[]{:S(2)}) %collective-permute-start.6) | collective-permute-done | bytes 221216 | tf_op jit(solution)/shard_map/ppermute | solution.py:36
  51.9 1.1 %shard_map.70 = (bf16[4,6,16,512]{3,2,1,0:T(8,128)(2,1)S(1)}, bf16[4,6,16,512]{3,2,1,0:T(8,128)(2,1)S(1)}, bf16[4,6,16,512]{3,2,1,0:T(8,128)(2,1)S(1)}, bf16[4,6...) custom-call(bf16[4,3,64,256]{3,2,1,0:T(8,128)(2,1)S(1)} %get-tuple-elem, ...), custom_call_target="tpu_custom_call" | custom-call | flops 1000000000 | bytes 8000000 | tf_op jit(solution)/shard_map/pallas_call | solution.py:322
  53.0 0.1 collective-permute-start.9
  53.1 1.7 %collective-permute-done.9 = bf16[4,6,16,512]{3,2,1,0:T(8,128)(2,1)S(1)} collective-permute-done((bf16[4,6,16,512]{3,2,1,0:T(8,128)(2,1)S(1)}, bf16[4,6,16,512]{3,2,1,0:T(8,128)(2,1)S(1)}, u32[]{:S(2)}, u32[]{:S(2)}) %collective-permute-start.9) | collective-permute-done | bytes 393248 | tf_op jit(solution)/shard_map/ppermute | solution.py:36
  54.8 0.1 add_convert_fusion.2
  54.9 0.2 collective-permute-start.10
  55.2 0.1 collective-permute-start.12
  55.3 0.5 collective-permute-start.11
  55.8 1.0 %collective-permute-done.10 = bf16[4,2,3,16,512]{4,3,2,1,0:T(8,128)(2,1)S(1)} collective-permute-done((bf16[4,2,3,16,512]{4,3,2,1,0:T(8,128)(2,1)S(1)}, bf16[4,2,3,16,512]{4,3,2,1,0:T(8,128)(2,1)S(1)}, u32[]{:S(2)}, u32[]{:S(2)}) %collective-permute-start.10) | collective-permute-done | bytes 393248 | tf_op jit(solution)/shard_map/ppermute | solution.py:36
  56.8 0.1 fusion.8
  56.8 6.0 %collective-permute-start.18 = (bf16[2,3,16,512]{3,2,1,0:T(8,128)(2,1)S(1)}, bf16[2,3,16,512]{3,2,1,0:T(8,128)(2,1)S(1)}, u32[]{:S(2)}, u32[]{:S(2)}) collective-permute-start(bf16[2,3,16,512]{3,2,1,0:T(8,128)(2,1)S(1)} %get-tuple-element.66), channel_id=1, source_target_pairs={{0,12},{1,13},{2,14},{3,15},{4,0},{5,1},{6,2},{7,3},{8,4},{9,5},{1... | collective-permute-start | bytes 294920 | tf_op jit(solution)/shard_map/ppermute | solution.py:36
  62.9 1.7 %collective-permute-start.16 = (bf16[2,3,16,512]{3,2,1,0:T(8,128)(2,1)S(1)}, bf16[2,3,16,512]{3,2,1,0:T(8,128)(2,1)S(1)}, u32[]{:S(2)}, u32[]{:S(2)}) collective-permute-start(bf16[2,3,16,512]{3,2,1,0:T(8,128)(2,1)S(1)} %get-tuple-element.67), channel_id=1, source_target_pairs={{0,8},{1,9},{2,10},{3,11},{4,12},{5,13},{6,14},{7,15},{8,0},{9,1},... | collective-permute-start | bytes 294920 | tf_op jit(solution)/shard_map/ppermute | solution.py:36
  64.5 0.8 collective-permute-start.17
  65.3 1.7 %shard_map.71 = (bf16[3,72,512]{2,1,0:T(8,128)(2,1)S(1)}, bf16[3,72,512]{2,1,0:T(8,128)(2,1)}) custom-call(s32[1]{0:T(128)} %bitcast.8.refs_0_.flag_ref, bf16[3,3,64,512]{3,2,1,0:T(8,128)(2,1)S(1)} %copy-done.3, bf16[24,8,512]{2,1,0:T(8,128)(2,1)S(1)} %collective-permute-done.low_ref.refs_1_.refs_2_, ...), custom_call_target="tpu_custom_call" | custom-call | flops 1100000000 | bytes 6000000 | tf_op jit(solution)/shard_map/pallas_call | solution.py:200
  67.0 1.1 %collective-permute-done.12 = bf16[4,6,16,512]{3,2,1,0:T(8,128)(2,1)S(1)} collective-permute-done((bf16[4,6,16,512]{3,2,1,0:T(8,128)(2,1)S(1)}, bf16[4,6,16,512]{3,2,1,0:T(8,128)(2,1)S(1)}, u32[]{:S(2)}, u32[]{:S(2)}) %collective-permute-start.12) | collective-permute-done | bytes 393248 | tf_op jit(solution)/shard_map/ppermute | solution.py:36
  68.2 0.2 add_convert_fusion
  68.4 3.0 %collective-permute-start.13 = (bf16[6,16,512]{2,1,0:T(8,128)(2,1)S(1)}, bf16[6,16,512]{2,1,0:T(8,128)(2,1)S(1)}, u32[]{:S(2)}, u32[]{:S(2)}) collective-permute-start(bf16[6,16,512]{2,1,0:T(8,128)(2,1)S(1)} %get-tuple-element.69), channel_id=1, source_target_pairs={{0,4},{1,5},{2,6},{3,7},{4,8},{5,9},{6,10},{7,11},{8,12},{9,13},{1... | collective-permute-start | bytes 294920 | tf_op jit(solution)/shard_map/ppermute | solution.py:36
  71.4 1.7 %collective-permute-start.15 = (bf16[6,16,512]{2,1,0:T(8,128)(2,1)S(1)}, bf16[6,16,512]{2,1,0:T(8,128)(2,1)S(1)}, u32[]{:S(2)}, u32[]{:S(2)}) collective-permute-start(bf16[6,16,512]{2,1,0:T(8,128)(2,1)S(1)} %get-tuple-element.70), channel_id=1, source_target_pairs={{0,12},{1,13},{2,14},{3,15},{4,0},{5,1},{6,2},{7,3},{8,4},{9,5},{1... | collective-permute-start | bytes 294920 | tf_op jit(solution)/shard_map/ppermute | solution.py:36
  73.1 1.0 %maximum_bitcast_fusion = bf16[4,1,3,64,512]{4,3,2,1,0:T(8,128)(2,1)} fusion(bf16[1,3,64,512]{3,2,1,0:T(8,128)(2,1)S(1)} %slice_bitcast_fusion, bf16[1,3,64,512]{3,2,1,0:T(8,128)(2,1)S(1)} %slice_bitcast_fusion.1, bf16[1,3,64,512]{3,2,1,0:T(8,128)(2,1)S(1)} %slice_bitcast_fusion.2, bf16[1,3,64,512]{3,2,1,0:T(8,128)(2,1)S(1)} %slice_bitcast_fusion.3), kind=kLoop, calls=%fused_computation | loop fusion | flops 1179648 | bytes 1572864
  74.1 2.3 %collective-permute-start.14 = (bf16[6,16,512]{2,1,0:T(8,128)(2,1)S(1)}, bf16[6,16,512]{2,1,0:T(8,128)(2,1)S(1)}, u32[]{:S(2)}, u32[]{:S(2)}) collective-permute-start(bf16[6,16,512]{2,1,0:T(8,128)(2,1)S(1)} %get-tuple-element.71), channel_id=1, source_target_pairs={{0,8},{1,9},{2,10},{3,11},{4,12},{5,13},{6,14},{7,15},{8,0},{9,1},... | collective-permute-start | bytes 294920 | tf_op jit(solution)/shard_map/ppermute | solution.py:36
  76.4 0.1 fusion.3
  76.5 2.9 %collective-permute-start.19 = (bf16[3,16,512]{2,1,0:T(8,128)(2,1)S(1)}, bf16[3,16,512]{2,1,0:T(8,128)(2,1)S(1)}, u32[]{:S(2)}, u32[]{:S(2)}) collective-permute-start(bf16[3,16,512]{2,1,0:T(8,128)(2,1)S(1)} %slice_bitcast_fusion.8), channel_id=1, source_target_pairs={{0,16},{1,17},{2,18},{3,19},{4,20},{5,21},{6,22},{7,23},{8,24},{9,... | collective-permute-start | bytes 147464 | tf_op jit(solution)/shard_map/ppermute | solution.py:36
  79.4 5.9 %collective-permute-done.14 = bf16[6,16,512]{2,1,0:T(8,128)(2,1)S(1)} collective-permute-done((bf16[6,16,512]{2,1,0:T(8,128)(2,1)S(1)}, bf16[6,16,512]{2,1,0:T(8,128)(2,1)S(1)}, u32[]{:S(2)}, u32[]{:S(2)}) %collective-permute-start.14) | collective-permute-done | bytes 98336 | tf_op jit(solution)/shard_map/ppermute | solution.py:36
  85.3 0.7 fusion
  (31 shorter events, 0.3 us)
Async XLA Ops:
  0.6 13.7 %copy-start.2 = (bf16[4,1,3,64,512]{4,3,2,1,0:T(8,128)(2,1)S(1)}, bf16[4,1,3,64,512]{4,3,2,1,0:T(8,128)(2,1)}, u32[]{:S(2)}) copy-start(bf16[4,1,3,64,512]{4,3,2,1,0:T(8,128)(2,1)} %param.4) | copy-start | bytes 2359300
  2.0 12.3 %collective-permute-start = (bf16[24,8,512]{2,1,0:T(8,128)(2,1)S(1)}, bf16[24,8,512]{2,1,0:T(8,128)(2,1)S(1)}, u32[]{:S(2)}, u32[]{:S(2)}) collective-permute-start(bf16[24,8,512]{2,1,0:T(8,128)(2,1)S(1)} %get-tuple-element.33), channel_id=1, source_target_pairs={{0,1},{1,2},{2,3},{3,4},{4,5},{5,6},{6,7},{7,8},{8,9},{9,10},{10,1... | collective-permute-start | bytes 589832 | tf_op jit(solution)/shard_map/ppermute | solution.py:36
  2.1 12.2 %collective-permute-start.1 = (bf16[24,8,512]{2,1,0:T(8,128)(2,1)S(1)}, bf16[24,8,512]{2,1,0:T(8,128)(2,1)S(1)}, u32[]{:S(2)}, u32[]{:S(2)}) collective-permute-start(bf16[24,8,512]{2,1,0:T(8,128)(2,1)S(1)} %get-tuple-element.34), channel_id=1, source_target_pairs={{0,31},{1,0},{2,1},{3,2},{4,3},{5,4},{6,5},{7,6},{8,7},{9,8},{10,9... | collective-permute-start | bytes 589832 | tf_op jit(solution)/shard_map/ppermute | solution.py:36
  10.1 5.3 %copy-start.4 = (bf16[1,3,64,512]{3,2,1,0:T(8,128)(2,1)S(1)}, bf16[1,3,64,512]{3,2,1,0:T(8,128)(2,1)}, u32[]{:S(2)}) copy-start(bf16[1,3,64,512]{3,2,1,0:T(8,128)(2,1)} %param.6) | copy-start | bytes 589828
  14.2 12.8 %collective-permute-start.4 = (bf16[4,3,64,256]{3,2,1,0:T(8,128)(2,1)}, bf16[4,3,64,256]{3,2,1,0:T(8,128)(2,1)S(1)}, u32[]{:S(2)}, u32[]{:S(2)}) collective-permute-start(bf16[4,3,64,256]{3,2,1,0:T(8,128)(2,1)} %get-tuple-element.41), channel_id=1, source_target_pairs={{0,2},{1,3},{2,0},{3,1},{4,6},{5,7},{6,4},{7,5},{8,10},{9,11},{10,... | collective-permute-start | bytes 1179656 | tf_op jit(solution)/shard_map/ppermute | solution.py:36
  15.5 9.8 %copy-start.3 = (bf16[3,3,64,512]{3,2,1,0:T(8,128)(2,1)S(1)}, bf16[3,3,64,512]{3,2,1,0:T(8,128)(2,1)}, u32[]{:S(2)}) copy-start(bf16[3,3,64,512]{3,2,1,0:T(8,128)(2,1)} %refs_1_.5) | copy-start | bytes 1769476
  17.1 8.1 %collective-permute-start.2 = (bf16[3,72,512]{2,1,0:T(8,128)(2,1)S(1)}, bf16[3,72,512]{2,1,0:T(8,128)(2,1)S(1)}, u32[]{:S(2)}, u32[]{:S(2)}) collective-permute-start(bf16[3,72,512]{2,1,0:T(8,128)(2,1)S(1)} %get-tuple-element.37), channel_id=1, source_target_pairs={{0,224},{32,0},{64,32},{96,64},{128,96},{160,128},{192,160},{224,1... | collective-permute-start | bytes 663560 | tf_op jit(solution)/shard_map/ppermute | solution.py:41
  18.0 2.3 %copy-start = (bf16[1,3,3,512,512]{4,3,2,1,0:T(8,128)(2,1)S(1)}, bf16[1,3,3,512,512]{4,3,2,1,0:T(8,128)(2,1)}, u32[]{:S(2)}) copy-start(bf16[1,3,3,512,512]{4,3,2,1,0:T(8,128)(2,1)} %param.5) | copy-start | bytes 14155780
  20.4 4.9 %copy-start.1 = (bf16[1,3,3,512,512]{4,3,2,1,0:T(8,128)(2,1)S(1)}, bf16[1,3,3,512,512]{4,3,2,1,0:T(8,128)(2,1)}, u32[]{:S(2)}) copy-start(bf16[1,3,3,512,512]{4,3,2,1,0:T(8,128)(2,1)} %param.5) | copy-start | bytes 14155780
  26.9 8.3 %collective-permute-start.3 = (bf16[3,72,512]{2,1,0:T(8,128)(2,1)S(1)}, bf16[3,72,512]{2,1,0:T(8,128)(2,1)S(1)}, u32[]{:S(2)}, u32[]{:S(2)}) collective-permute-start(bf16[3,72,512]{2,1,0:T(8,128)(2,1)S(1)} %get-tuple-element.39), channel_id=1, source_target_pairs={{0,224},{32,0},{64,32},{96,64},{128,96},{160,128},{192,160},{224,1... | collective-permute-start | bytes 663560 | tf_op jit(solution)/shard_map/ppermute | solution.py:41
  28.2 19.8 %collective-permute-start.7 = (bf16[2,3,72,512]{3,2,1,0:T(8,128)(2,1)S(1)}, bf16[2,3,72,512]{3,2,1,0:T(8,128)(2,1)S(1)}, u32[]{:S(2)}, u32[]{:S(2)}) collective-permute-start(bf16[2,3,72,512]{3,2,1,0:T(8,128)(2,1)S(1)} %pad_maximum_fusion.both0), channel_id=1, source_target_pairs={{0,2},{1,3},{2,0},{3,1},{4,6},{5,7},{6,4},{7,5},{8,10},{9,11},{10,... | collective-permute-start | bytes 1327112 | tf_op jit(solution)/shard_map/ppermute | solution.py:36
  36.9 8.1 %collective-permute-start.5 = (bf16[3,72,512]{2,1,0:T(8,128)(2,1)S(1)}, bf16[3,72,512]{2,1,0:T(8,128)(2,1)S(1)}, u32[]{:S(2)}, u32[]{:S(2)}) collective-permute-start(bf16[3,72,512]{2,1,0:T(8,128)(2,1)S(1)} %get-tuple-element.43), channel_id=1, source_target_pairs={{0,224},{32,0},{64,32},{96,64},{128,96},{160,128},{192,160},{224,1... | collective-permute-start | bytes 663560 | tf_op jit(solution)/shard_map/ppermute | solution.py:41
  38.1 9.9 %collective-permute-start.8 = (bf16[3,72,512]{2,1,0:T(8,128)(2,1)S(1)}, bf16[3,72,512]{2,1,0:T(8,128)(2,1)S(1)}, u32[]{:S(2)}, u32[]{:S(2)}) collective-permute-start(bf16[3,72,512]{2,1,0:T(8,128)(2,1)S(1)} %get-tuple-element.50.third0), channel_id=1, source_target_pairs={{0,2},{1,3},{2,0},{3,1},{4,6},{5,7},{6,4},{7,5},{8,10},{9,11},{10,... | collective-permute-start | bytes 663560 | tf_op jit(solution)/shard_map/ppermute | solution.py:36
  45.1 6.8 %collective-permute-start.6 = (bf16[3,72,512]{2,1,0:T(8,128)(2,1)S(1)}, bf16[3,72,512]{2,1,0:T(8,128)(2,1)S(1)}, u32[]{:S(2)}, u32[]{:S(2)}) collective-permute-start(bf16[3,72,512]{2,1,0:T(8,128)(2,1)S(1)} %shard_map.68.g0), channel_id=1, source_target_pairs={{0,2},{1,3},{2,0},{3,1},{4,6},{5,7},{6,4},{7,5},{8,10},{9,11},{10,... | collective-permute-start | bytes 663560 | tf_op jit(solution)/shard_map/ppermute | solution.py:36
  53.0 1.8 %collective-permute-start.9 = (bf16[4,6,16,512]{3,2,1,0:T(8,128)(2,1)S(1)}, bf16[4,6,16,512]{3,2,1,0:T(8,128)(2,1)S(1)}, u32[]{:S(2)}, u32[]{:S(2)}) collective-permute-start(bf16[4,6,16,512]{3,2,1,0:T(8,128)(2,1)S(1)} %get-tuple-element.55), channel_id=1, source_target_pairs={{0,1},{1,0},{2,3},{3,2},{4,5},{5,4},{6,7},{7,6},{8,9},{9,8},{10,11... | collective-permute-start | bytes 1179656 | tf_op jit(solution)/shard_map/ppermute | solution.py:36
  54.9 1.8 %collective-permute-start.10 = (bf16[4,2,3,16,512]{4,3,2,1,0:T(8,128)(2,1)S(1)}, bf16[4,2,3,16,512]{4,3,2,1,0:T(8,128)(2,1)S(1)}, u32[]{:S(2)}, u32[]{:S(2)}) collective-permute-start(bf16[4,2,3,16,512]{4,3,2,1,0:T(8,128)(2,1)S(1)} %get-tuple-element.56), channel_id=1, source_target_pairs={{0,1},{1,0},{2,3},{3,2},{4,5},{5,4},{6,7},{7,6},{8,9},{9,8},{10,11... | collective-permute-start | bytes 1179656 | tf_op jit(solution)/shard_map/ppermute | solution.py:36
  55.2 13.0 %collective-permute-start.12 = (bf16[4,6,16,512]{3,2,1,0:T(8,128)(2,1)S(1)}, bf16[4,6,16,512]{3,2,1,0:T(8,128)(2,1)S(1)}, u32[]{:S(2)}, u32[]{:S(2)}) collective-permute-start(bf16[4,6,16,512]{3,2,1,0:T(8,128)(2,1)S(1)} %add_convert_fusion.2), channel_id=1, source_target_pairs={{0,16},{1,17},{2,18},{3,19},{4,20},{5,21},{6,22},{7,23},{8,24},{9,... | collective-permute-start | bytes 1179656 | tf_op jit(solution)/shard_map/ppermute | solution.py:36
  55.3 11.7 %collective-permute-start.11 = (bf16[4,6,16,512]{3,2,1,0:T(8,128)(2,1)S(1)}, bf16[4,6,16,512]{3,2,1,0:T(8,128)(2,1)S(1)}, u32[]{:S(2)}, u32[]{:S(2)}) collective-permute-start(bf16[4,6,16,512]{3,2,1,0:T(8,128)(2,1)S(1)} %get-tuple-element.60), channel_id=1, source_target_pairs={{0,1},{1,0},{2,3},{3,2},{4,5},{5,4},{6,7},{7,6},{8,9},{9,8},{10,11... | collective-permute-start | bytes 1179656 | tf_op jit(solution)/shard_map/ppermute | solution.py:36
  56.8 17.2 %collective-permute-start.18 = (bf16[2,3,16,512]{3,2,1,0:T(8,128)(2,1)S(1)}, bf16[2,3,16,512]{3,2,1,0:T(8,128)(2,1)S(1)}, u32[]{:S(2)}, u32[]{:S(2)}) collective-permute-start(bf16[2,3,16,512]{3,2,1,0:T(8,128)(2,1)S(1)} %get-tuple-element.66), channel_id=1, source_target_pairs={{0,12},{1,13},{2,14},{3,15},{4,0},{5,1},{6,2},{7,3},{8,4},{9,5},{1... | collective-permute-start | bytes 294920 | tf_op jit(solution)/shard_map/ppermute | solution.py:36
  62.9 13.5 %collective-permute-start.16 = (bf16[2,3,16,512]{3,2,1,0:T(8,128)(2,1)S(1)}, bf16[2,3,16,512]{3,2,1,0:T(8,128)(2,1)S(1)}, u32[]{:S(2)}, u32[]{:S(2)}) collective-permute-start(bf16[2,3,16,512]{3,2,1,0:T(8,128)(2,1)S(1)} %get-tuple-element.67), channel_id=1, source_target_pairs={{0,8},{1,9},{2,10},{3,11},{4,12},{5,13},{6,14},{7,15},{8,0},{9,1},... | collective-permute-start | bytes 294920 | tf_op jit(solution)/shard_map/ppermute | solution.py:36
  64.5 11.8 %collective-permute-start.17 = (bf16[2,3,16,512]{3,2,1,0:T(8,128)(2,1)S(1)}, bf16[2,3,16,512]{3,2,1,0:T(8,128)(2,1)S(1)}, u32[]{:S(2)}, u32[]{:S(2)}) collective-permute-start(bf16[2,3,16,512]{3,2,1,0:T(8,128)(2,1)S(1)} %get-tuple-element.68), channel_id=1, source_target_pairs={{0,4},{1,5},{2,6},{3,7},{4,8},{5,9},{6,10},{7,11},{8,12},{9,13},{1... | collective-permute-start | bytes 294920 | tf_op jit(solution)/shard_map/ppermute | solution.py:36
  68.4 10.9 %collective-permute-start.13 = (bf16[6,16,512]{2,1,0:T(8,128)(2,1)S(1)}, bf16[6,16,512]{2,1,0:T(8,128)(2,1)S(1)}, u32[]{:S(2)}, u32[]{:S(2)}) collective-permute-start(bf16[6,16,512]{2,1,0:T(8,128)(2,1)S(1)} %get-tuple-element.69), channel_id=1, source_target_pairs={{0,4},{1,5},{2,6},{3,7},{4,8},{5,9},{6,10},{7,11},{8,12},{9,13},{1... | collective-permute-start | bytes 294920 | tf_op jit(solution)/shard_map/ppermute | solution.py:36
  71.4 8.0 %collective-permute-start.15 = (bf16[6,16,512]{2,1,0:T(8,128)(2,1)S(1)}, bf16[6,16,512]{2,1,0:T(8,128)(2,1)S(1)}, u32[]{:S(2)}, u32[]{:S(2)}) collective-permute-start(bf16[6,16,512]{2,1,0:T(8,128)(2,1)S(1)} %get-tuple-element.70), channel_id=1, source_target_pairs={{0,12},{1,13},{2,14},{3,15},{4,0},{5,1},{6,2},{7,3},{8,4},{9,5},{1... | collective-permute-start | bytes 294920 | tf_op jit(solution)/shard_map/ppermute | solution.py:36
  74.1 11.2 %collective-permute-start.14 = (bf16[6,16,512]{2,1,0:T(8,128)(2,1)S(1)}, bf16[6,16,512]{2,1,0:T(8,128)(2,1)S(1)}, u32[]{:S(2)}, u32[]{:S(2)}) collective-permute-start(bf16[6,16,512]{2,1,0:T(8,128)(2,1)S(1)} %get-tuple-element.71), channel_id=1, source_target_pairs={{0,8},{1,9},{2,10},{3,11},{4,12},{5,13},{6,14},{7,15},{8,0},{9,1},... | collective-permute-start | bytes 294920 | tf_op jit(solution)/shard_map/ppermute | solution.py:36
  76.5 8.9 %collective-permute-start.19 = (bf16[3,16,512]{2,1,0:T(8,128)(2,1)S(1)}, bf16[3,16,512]{2,1,0:T(8,128)(2,1)S(1)}, u32[]{:S(2)}, u32[]{:S(2)}) collective-permute-start(bf16[3,16,512]{2,1,0:T(8,128)(2,1)S(1)} %slice_bitcast_fusion.8), channel_id=1, source_target_pairs={{0,16},{1,17},{2,18},{3,19},{4,20},{5,21},{6,22},{7,23},{8,24},{9,... | collective-permute-start | bytes 147464 | tf_op jit(solution)/shard_map/ppermute | solution.py:36

commit v8 on v7

--- a/solution.py
+++ b/solution.py
@@ -279,10 +279,13 @@
     ]
 
 
-def early_kernel(x0, x1, both0, both1, third0, third1, out_ref):
-    for t in range(STEPS - 1):
-        gs = (both0[t], both1[t]) if t < 2 else (third0, third1)
-        values = tap_products((x0[t], x1[t]), gs)
+def early_kernel(x0, x1, both0, both1, third0, third1, last0, out_ref):
+    for t in range(STEPS):
+        if t < STEPS - 1:
+            gs = (both0[t], both1[t]) if t < 2 else (third0, third1)
+            values = tap_products((x0[t], x1[t]), gs)
+        else:
+            values = tap_products((x0[t],), (last0,))
         for a, value in enumerate(values):
             out_ref[a] = value if t == 0 else out_ref[a] + value
 
@@ -291,7 +294,7 @@
     return pl.pallas_call(
         early_kernel,
         out_shape=jax.ShapeDtypeStruct((3, HALF, 3 * CH), F32),
-        in_specs=[VMEM] * 6,
+        in_specs=[VMEM] * 7,
         out_specs=VMEM,
         compiler_params=params(),
         cost_estimate=cost(3e9, 8e6),
@@ -301,8 +304,8 @@
 FIRST = 6
 
 
-def late_kernel(x0, x1, g0, g1, total_ref, *outs):
-    for a, value in enumerate(tap_products((x0[0], x1[0]), (g0, g1))):
+def late_kernel(x_ref, g_ref, total_ref, *outs):
+    for a, value in enumerate(tap_products((x_ref[0],), (g_ref,))):
         value = value + total_ref[a]
         for b in range(3):
             tap = a * 3 + b
@@ -317,19 +320,19 @@
                             outs[2 * far + core][turn, tap] = part
 
 
-def late_products(xs, gs, total):
+def late_products(x, g, total):
     shapes = [(4, FIRST, 16, CH)] * 4 + [(4, 2, 9 - FIRST, 16, CH)] * 2
     return pl.pallas_call(
         late_kernel,
         grid=(1,),
         out_shape=tuple(jax.ShapeDtypeStruct(shape, BF) for shape in shapes),
-        in_specs=[block((1, ROWS, WIDTH, HALF), STEPS - 1, 0, 0, 0)] * 2
-        + [block((ROWS, WIDE, CH), 0, 0, 0)] * 2
+        in_specs=[block((1, ROWS, WIDTH, HALF), STEPS - 1, 0, 0, 0)]
+        + [block((ROWS, WIDE, CH), 0, 0, 0)]
         + [block((3, HALF, 3 * CH), 0, 0, 0)],
         out_specs=tuple(block(shape, *(0,) * len(shape)) for shape in shapes),
         compiler_params=params(),
         cost_estimate=cost(1e9, 8e6),
-    )(*xs, *gs, total)
+    )(x, g, total)
 
 
 def grad_kernel(flag_ref, own_ref, low_ref, high_ref, relay_ref, factor_ref, grad_ref):
@@ -408,8 +411,9 @@
                 fields = []
         fields.append(own if t == 0 else (own, send(own, PAIR)))
 
-    total = early_products(xs, *fields[0], *fields[1])
-    near, near_other, out_going, out_other, turns, turns_other = late_products(xs, fields[-1], total)
+    own, pair = fields[-1]
+    total = early_products(xs, *fields[0], *fields[1], own)
+    near, near_other, out_going, out_other, turns, turns_other = late_products(xs[1], pair, total)
     out_going = total_of(out_going, send(out_other, CORE)).astype(BF)
     far = send(out_going, FAR)
     turns_other, near_other = lax.optimization_barrier((turns_other, near_other, out_going))[:2]

time: 86.4 us -> 86.7 us (level)
  transfers between devices with their start and end apart: 20 -> 20, of which waited for: 8 -> 8; matrix products, arithmetic and copies ran while one was open for 2% -> 2% of each run, Pallas kernels for 21% -> 22%
where the time goes in v8:
time: 86.7 us; the launch traced here: 85.8 us
  starting transfers between devices  36.6 us (42%)
  waiting for transfers between devices  22.6 us (26%)
  Pallas kernels  20.9 us (24%)
  local copies, waits for them, and re-layouts  2.44 us (3%)
  other arithmetic  2.36 us (3%)
  between operations  0.94 us (1%)
    ppermute x17, starting transfers between devices, send(): return lax.ppermute(block, 'az', route)  35.6 us
    ppermute x3, waiting for transfers between devices, relay(): lax.ppermute(block, 'segment', [(i, (i - 1) % count) for i in range(count)])  12.4 us
    ppermute x17, waiting for transfers between devices, send(): return lax.ppermute(block, 'az', route)  10.2 us
    pallas_call x4, Pallas kernels, back_step(): pl.pallas_call(lambda *refs: back_kernel(first, *refs), grid=(1,), out_sh...  6.67 us
    pallas_call x4, Pallas kernels, slope_factors(): pl.pallas_call(factor_kernel, grid=(1,), out_shape=jax.ShapeDtypeStruct((...  4.5 us
    pallas_call x1, Pallas kernels, spread(): pl.pallas_call(spread_kernel, out_shape=(shape, shape, pltpu.VMEM(weights...  4.04 us
    pallas_call x1, Pallas kernels, early_products(): pl.pallas_call(early_kernel, out_shape=jax.ShapeDtypeStruct((3, HALF, 3 *...  3.45 us
    unnamed x10, local copies, waits for them, and re-layouts  2.36 us
  transfers between devices with their start and end apart: 20, of which 8 were waited for; matrix products, arithmetic and copies ran while one was open for 2% of the time, Pallas kernels for 22%

profile of v8, /device:TPU:6, one launch (start us, length us, event | category | flops | bytes accessed | tf_op | source)
XLA Modules:
  0.0 85.8 jit_solution(12807673346876733452)
XLA Ops:
  0.6 1.3 %shard_map.59 = (bf16[24,8,512]{2,1,0:T(8,128)(2,1)S(1)}, bf16[24,8,512]{2,1,0:T(8,128)(2,1)S(1)}) custom-call(bf16[4,3,64,512]{3,2,1,0:T(8,128)(2,1)} %bitcast.59, bf16[3,64,512]{2,1,0:T(8,128)(2,1)} %bitcast.66, bf16[3,3,64,512]{3,2,1,0:T(8,128)(2,1)} %refs_1_.5, bf16[4,3,64,512]{3,2,1,0:T(8,128)(2,1)} %bitcast.60, bf16[3,64,512]{2,1,0:T(8,128)(2,1)} %bitcast.67, ...), custom_call_target="tpu_custom_call" | custom-call | bytes 1048576 | tf_op jit(solution)/shard_map/pallas_call | solution.py:79
  2.0 0.1 collective-permute-start
  2.1 8.0 %collective-permute-start.1 = (bf16[24,8,512]{2,1,0:T(8,128)(2,1)S(1)}, bf16[24,8,512]{2,1,0:T(8,128)(2,1)S(1)}, u32[]{:S(2)}, u32[]{:S(2)}) collective-permute-start(bf16[24,8,512]{2,1,0:T(8,128)(2,1)S(1)} %get-tuple-element.34), channel_id=1, source_target_pairs={{0,31},{1,0},{2,1},{3,2},{4,3},{5,4},{6,5},{7,6},{8,7},{9,8},{10,9... | collective-permute-start | bytes 589832 | tf_op jit(solution)/shard_map/ppermute | solution.py:36
  10.1 0.1 pad_add_fusion.place_ref
  10.1 4.0 %shard_map.60 = (bf16[4,3,64,256]{3,2,1,0:T(8,128)(2,1)S(1)}, bf16[4,3,64,256]{3,2,1,0:T(8,128)(2,1)}, bf16[9,512,512]{2,1,0:T(8,128)(2,1)S(1)}) custom-call(s32[4]{0:T(128)S(1)} %pad_add_fusion.place_ref, bf16[4,3,64,512]{3,2,1,0:T(8,128)(2,1)} %bitcast.61, bf16[9,512,512]{2,1,0:T(8,128)(2,1)} %bitcast.52), custom_call_target="tpu_custom_call" | custom-call | flops 450000000 | bytes 12000000 | tf_op jit(solution)/shard_map/pallas_call | solution.py:243
  14.2 0.1 collective-permute-start.4
  14.3 1.1 %shard_map.61.refs_3_ = f32[1,3,72,512]{3,2,1,0:T(8,128)S(1)} custom-call(bf16[4,3,64,512]{3,2,1,0:T(8,128)(2,1)S(1)} %bitcast.62, bf16[24,8,512]{2,1,0:T(8,128)(2,1)S(1)} %collective-permute-done.low_ref.refs_1_.refs_2_, bf16[24,8,512]{2,1,0:T(8,128)(2,1)S(1)} %collective-permute-done.1.high_ref.refs_2_.refs_3_, ...), custom_call_target="tpu_custom_call" | custom-call | flops 1200000000 | bytes 5000000 | tf_op jit(solution)/shard_map/pallas_call | solution.py:132
  15.5 1.7 %shard_map.62 = (bf16[3,72,512]{2,1,0:T(8,128)(2,1)S(1)}, bf16[3,72,512]{2,1,0:T(8,128)(2,1)S(1)}) custom-call(bf16[3,64,512]{2,1,0:T(8,128)(2,1)S(1)} %bitcast.68, bf16[24,8,512]{2,1,0:T(8,128)(2,1)S(1)} %collective-permute-done.low_ref.refs_1_.refs_2_, bf16[24,8,512]{2,1,0:T(8,128)(2,1)S(1)} %collective-permute-done.1.high_ref.refs_2_.refs_3_, ...), custom_call_target="tpu_custom_call" | custom-call | flops 1100000000 | bytes 6000000 | tf_op jit(solution)/shard_map/pallas_call | solution.py:200
  17.1 0.9 %collective-permute-start.2 = (bf16[3,72,512]{2,1,0:T(8,128)(2,1)S(1)}, bf16[3,72,512]{2,1,0:T(8,128)(2,1)S(1)}, u32[]{:S(2)}, u32[]{:S(2)}) collective-permute-start(bf16[3,72,512]{2,1,0:T(8,128)(2,1)S(1)} %get-tuple-element.37), channel_id=1, source_target_pairs={{0,224},{32,0},{64,32},{96,64},{128,96},{160,128},{192,160},{224,1... | collective-permute-start | bytes 663560 | tf_op jit(solution)/shard_map/ppermute | solution.py:41
  18.0 2.3 %copy-done = bf16[1,3,3,512,512]{4,3,2,1,0:T(8,128)(2,1)S(1)} copy-done((bf16[1,3,3,512,512]{4,3,2,1,0:T(8,128)(2,1)S(1)}, bf16[1,3,3,512,512]{4,3,2,1,0:T(8,128)(2,1)}, u32[]{:S(2)}) %copy-start) | copy-done | bytes 4718616
  20.4 1.1 %shard_map.63.refs_5_ = f32[1,3,72,512]{3,2,1,0:T(8,128)S(1)} custom-call(bf16[4,3,64,512]{3,2,1,0:T(8,128)(2,1)S(1)} %bitcast.63, bf16[24,8,512]{2,1,0:T(8,128)(2,1)S(1)} %collective-permute-done.low_ref.refs_1_.refs_2_, bf16[24,8,512]{2,1,0:T(8,128)(2,1)S(1)} %collective-permute-done.1.high_ref.refs_2_.refs_3_, bf16[9,512,512]{2,1,0:T(8,128)(2,1)S(1)} %bitcast.53), custom_call_target="tpu_custom_call" | custom-call | flops 1200000000 | bytes 5000000 | tf_op jit(solution)/shard_map/pallas_call | solution.py:132
  21.5 3.7 %collective-permute-done.2.refs_4_ = bf16[3,72,512]{2,1,0:T(8,128)(2,1)S(1)} collective-permute-done((bf16[3,72,512]{2,1,0:T(8,128)(2,1)S(1)}, bf16[3,72,512]{2,1,0:T(8,128)(2,1)S(1)}, u32[]{:S(2)}, u32[]{:S(2)}) %collective-permute-start.2) | collective-permute-done | bytes 221216 | tf_op jit(solution)/shard_map/ppermute | solution.py:41
  25.3 1.7 %shard_map.64 = (bf16[3,72,512]{2,1,0:T(8,128)(2,1)S(1)}, bf16[3,72,512]{2,1,0:T(8,128)(2,1)S(1)}) custom-call(s32[1]{0:T(128)} %bitcast.8.refs_0_.flag_ref, bf16[3,3,64,512]{3,2,1,0:T(8,128)(2,1)S(1)} %copy-done.3, bf16[24,8,512]{2,1,0:T(8,128)(2,1)S(1)} %collective-permute-done.low_ref.refs_1_.refs_2_, ...), custom_call_target="tpu_custom_call" | custom-call | flops 1100000000 | bytes 6000000 | tf_op jit(solution)/shard_map/pallas_call | solution.py:200
  26.9 0.1 collective-permute-start.3
  27.0 1.1 %shard_map.65.refs_5_ = f32[1,3,72,512]{3,2,1,0:T(8,128)S(1)} custom-call(bf16[4,3,64,512]{3,2,1,0:T(8,128)(2,1)S(1)} %bitcast.64, bf16[24,8,512]{2,1,0:T(8,128)(2,1)S(1)} %collective-permute-done.low_ref.refs_1_.refs_2_, bf16[24,8,512]{2,1,0:T(8,128)(2,1)S(1)} %collective-permute-done.1.high_ref.refs_2_.refs_3_, bf16[9,512,512]{2,1,0:T(8,128)(2,1)S(1)} %bitcast.55), custom_call_target="tpu_custom_call" | custom-call | flops 1200000000 | bytes 5000000 | tf_op jit(solution)/shard_map/pallas_call | solution.py:132
  28.2 2.1 %collective-permute-start.7 = (bf16[2,3,72,512]{3,2,1,0:T(8,128)(2,1)S(1)}, bf16[2,3,72,512]{3,2,1,0:T(8,128)(2,1)S(1)}, u32[]{:S(2)}, u32[]{:S(2)}) collective-permute-start(bf16[2,3,72,512]{3,2,1,0:T(8,128)(2,1)S(1)} %pad_maximum_fusion.both0), channel_id=1, source_target_pairs={{0,2},{1,3},{2,0},{3,1},{4,6},{5,7},{6,4},{7,5},{8,10},{9,11},{10,... | collective-permute-start | bytes 1327112 | tf_op jit(solution)/shard_map/ppermute | solution.py:36
  30.3 4.9 %collective-permute-done.3.refs_4_ = bf16[3,72,512]{2,1,0:T(8,128)(2,1)S(1)} collective-permute-done((bf16[3,72,512]{2,1,0:T(8,128)(2,1)S(1)}, bf16[3,72,512]{2,1,0:T(8,128)(2,1)S(1)}, u32[]{:S(2)}, u32[]{:S(2)}) %collective-permute-start.3) | collective-permute-done | bytes 221216 | tf_op jit(solution)/shard_map/ppermute | solution.py:41
  35.2 1.7 %shard_map.66 = (bf16[3,72,512]{2,1,0:T(8,128)(2,1)S(1)}, bf16[3,72,512]{2,1,0:T(8,128)(2,1)S(1)}) custom-call(s32[1]{0:T(128)} %bitcast.8.refs_0_.flag_ref, bf16[3,3,64,512]{3,2,1,0:T(8,128)(2,1)S(1)} %copy-done.3, bf16[24,8,512]{2,1,0:T(8,128)(2,1)S(1)} %collective-permute-done.low_ref.refs_1_.refs_2_, ...), custom_call_target="tpu_custom_call" | custom-call | flops 1100000000 | bytes 6000000 | tf_op jit(solution)/shard_map/pallas_call | solution.py:200
  36.9 0.1 collective-permute-start.5
  37.0 1.1 %shard_map.67.factor_ref.refs_5_ = f32[1,3,72,512]{3,2,1,0:T(8,128)S(1)} custom-call(bf16[4,3,64,512]{3,2,1,0:T(8,128)(2,1)S(1)} %bitcast.65, bf16[24,8,512]{2,1,0:T(8,128)(2,1)S(1)} %collective-permute-done.low_ref.refs_1_.refs_2_, bf16[24,8,512]{2,1,0:T(8,128)(2,1)S(1)} %collective-permute-done.1.high_ref.refs_2_.refs_3_, bf16[9,512,512]{2,1,0:T(8,128)(2,1)S(1)} %bitcast.57), custom_call_target="tpu_custom_call" | custom-call | flops 1200000000 | bytes 5000000 | tf_op jit(solution)/shard_map/pallas_call | solution.py:132
  38.1 3.1 %collective-permute-start.8 = (bf16[3,72,512]{2,1,0:T(8,128)(2,1)S(1)}, bf16[3,72,512]{2,1,0:T(8,128)(2,1)S(1)}, u32[]{:S(2)}, u32[]{:S(2)}) collective-permute-start(bf16[3,72,512]{2,1,0:T(8,128)(2,1)S(1)} %get-tuple-element.50.third0), channel_id=1, source_target_pairs={{0,2},{1,3},{2,0},{3,1},{4,6},{5,7},{6,4},{7,5},{8,10},{9,11},{10,... | collective-permute-start | bytes 663560 | tf_op jit(solution)/shard_map/ppermute | solution.py:36
  41.2 3.8 %collective-permute-done.5.relay_ref.refs_4_ = bf16[3,72,512]{2,1,0:T(8,128)(2,1)S(1)} collective-permute-done((bf16[3,72,512]{2,1,0:T(8,128)(2,1)S(1)}, bf16[3,72,512]{2,1,0:T(8,128)(2,1)S(1)}, u32[]{:S(2)}, u32[]{:S(2)}) %collective-permute-start.5) | collective-permute-done | bytes 221216 | tf_op jit(solution)/shard_map/ppermute | solution.py:41
  45.0 0.1 shard_map.68.last0
  45.1 2.9 %collective-permute-start.6 = (bf16[3,72,512]{2,1,0:T(8,128)(2,1)S(1)}, bf16[3,72,512]{2,1,0:T(8,128)(2,1)S(1)}, u32[]{:S(2)}, u32[]{:S(2)}) collective-permute-start(bf16[3,72,512]{2,1,0:T(8,128)(2,1)S(1)} %shard_map.68.last0), channel_id=1, source_target_pairs={{0,2},{1,3},{2,0},{3,1},{4,6},{5,7},{6,4},{7,5},{8,10},{9,11},{10,... | collective-permute-start | bytes 663560 | tf_op jit(solution)/shard_map/ppermute | solution.py:36
  48.0 3.4 %shard_map.69.total_ref = f32[3,256,1536]{2,1,0:T(8,128)S(1)} custom-call(bf16[4,3,64,256]{3,2,1,0:T(8,128)(2,1)S(1)} %get-tuple-element.40.x0, bf16[4,3,64,256]{3,2,1,0:T(8,128)(2,1)S(1)} %collective-permute-done.4.x1.x_ref, bf16[2,3,72,512]{3,2,1,0:T(8,128)(2,1)S(1)} %pad_maximum_fusion.both0, bf16[2,3,72,512]{3,2,1,0:T(8,128)(2,1)S(1)} %collective-permute-done.7.both1, ...), custom_call_target="tpu_custom_call" | custom-call | flops 3000000000 | bytes 8000000 | tf_op jit(solution)/shard_map/pallas_call | solution.py:294
  51.5 0.5 collective-permute-done.6.g_ref
  51.9 0.8 shard_map.70
  52.8 0.1 collective-permute-start.9
  52.9 1.7 %collective-permute-done.9 = bf16[4,6,16,512]{3,2,1,0:T(8,128)(2,1)S(1)} collective-permute-done((bf16[4,6,16,512]{3,2,1,0:T(8,128)(2,1)S(1)}, bf16[4,6,16,512]{3,2,1,0:T(8,128)(2,1)S(1)}, u32[]{:S(2)}, u32[]{:S(2)}) %collective-permute-start.9) | collective-permute-done | bytes 393248 | tf_op jit(solution)/shard_map/ppermute | solution.py:36
  54.6 0.1 add_convert_fusion.2
  54.7 0.2 collective-permute-start.10
  55.0 0.1 collective-permute-start.12
  55.1 0.5 collective-permute-start.11
  55.5 1.0 %collective-permute-done.10 = bf16[4,2,3,16,512]{4,3,2,1,0:T(8,128)(2,1)S(1)} collective-permute-done((bf16[4,2,3,16,512]{4,3,2,1,0:T(8,128)(2,1)S(1)}, bf16[4,2,3,16,512]{4,3,2,1,0:T(8,128)(2,1)S(1)}, u32[]{:S(2)}, u32[]{:S(2)}) %collective-permute-start.10) | collective-permute-done | bytes 393248 | tf_op jit(solution)/shard_map/ppermute | solution.py:36
  56.5 0.1 fusion.8
  56.6 6.1 %collective-permute-start.18 = (bf16[2,3,16,512]{3,2,1,0:T(8,128)(2,1)S(1)}, bf16[2,3,16,512]{3,2,1,0:T(8,128)(2,1)S(1)}, u32[]{:S(2)}, u32[]{:S(2)}) collective-permute-start(bf16[2,3,16,512]{3,2,1,0:T(8,128)(2,1)S(1)} %get-tuple-element.66), channel_id=1, source_target_pairs={{0,12},{1,13},{2,14},{3,15},{4,0},{5,1},{6,2},{7,3},{8,4},{9,5},{1... | collective-permute-start | bytes 294920 | tf_op jit(solution)/shard_map/ppermute | solution.py:36
  62.7 1.6 %collective-permute-start.16 = (bf16[2,3,16,512]{3,2,1,0:T(8,128)(2,1)S(1)}, bf16[2,3,16,512]{3,2,1,0:T(8,128)(2,1)S(1)}, u32[]{:S(2)}, u32[]{:S(2)}) collective-permute-start(bf16[2,3,16,512]{3,2,1,0:T(8,128)(2,1)S(1)} %get-tuple-element.67), channel_id=1, source_target_pairs={{0,8},{1,9},{2,10},{3,11},{4,12},{5,13},{6,14},{7,15},{8,0},{9,1},... | collective-permute-start | bytes 294920 | tf_op jit(solution)/shard_map/ppermute | solution.py:36
  64.3 0.8 collective-permute-start.17
  65.1 1.7 %shard_map.71 = (bf16[3,72,512]{2,1,0:T(8,128)(2,1)S(1)}, bf16[3,72,512]{2,1,0:T(8,128)(2,1)}) custom-call(s32[1]{0:T(128)} %bitcast.8.refs_0_.flag_ref, bf16[3,3,64,512]{3,2,1,0:T(8,128)(2,1)S(1)} %copy-done.3, bf16[24,8,512]{2,1,0:T(8,128)(2,1)S(1)} %collective-permute-done.low_ref.refs_1_.refs_2_, ...), custom_call_target="tpu_custom_call" | custom-call | flops 1100000000 | bytes 6000000 | tf_op jit(solution)/shard_map/pallas_call | solution.py:200
  66.8 1.1 %collective-permute-done.12 = bf16[4,6,16,512]{3,2,1,0:T(8,128)(2,1)S(1)} collective-permute-done((bf16[4,6,16,512]{3,2,1,0:T(8,128)(2,1)S(1)}, bf16[4,6,16,512]{3,2,1,0:T(8,128)(2,1)S(1)}, u32[]{:S(2)}, u32[]{:S(2)}) %collective-permute-start.12) | collective-permute-done | bytes 393248 | tf_op jit(solution)/shard_map/ppermute | solution.py:36
  68.0 0.2 add_convert_fusion
  68.2 3.0 %collective-permute-start.13 = (bf16[6,16,512]{2,1,0:T(8,128)(2,1)S(1)}, bf16[6,16,512]{2,1,0:T(8,128)(2,1)S(1)}, u32[]{:S(2)}, u32[]{:S(2)}) collective-permute-start(bf16[6,16,512]{2,1,0:T(8,128)(2,1)S(1)} %get-tuple-element.69), channel_id=1, source_target_pairs={{0,4},{1,5},{2,6},{3,7},{4,8},{5,9},{6,10},{7,11},{8,12},{9,13},{1... | collective-permute-start | bytes 294920 | tf_op jit(solution)/shard_map/ppermute | solution.py:36
  71.2 1.7 %collective-permute-start.15 = (bf16[6,16,512]{2,1,0:T(8,128)(2,1)S(1)}, bf16[6,16,512]{2,1,0:T(8,128)(2,1)S(1)}, u32[]{:S(2)}, u32[]{:S(2)}) collective-permute-start(bf16[6,16,512]{2,1,0:T(8,128)(2,1)S(1)} %get-tuple-element.70), channel_id=1, source_target_pairs={{0,12},{1,13},{2,14},{3,15},{4,0},{5,1},{6,2},{7,3},{8,4},{9,5},{1... | collective-permute-start | bytes 294920 | tf_op jit(solution)/shard_map/ppermute | solution.py:36
  72.9 1.0 %maximum_bitcast_fusion = bf16[4,1,3,64,512]{4,3,2,1,0:T(8,128)(2,1)} fusion(bf16[1,3,64,512]{3,2,1,0:T(8,128)(2,1)S(1)} %slice_bitcast_fusion, bf16[1,3,64,512]{3,2,1,0:T(8,128)(2,1)S(1)} %slice_bitcast_fusion.1, bf16[1,3,64,512]{3,2,1,0:T(8,128)(2,1)S(1)} %slice_bitcast_fusion.2, bf16[1,3,64,512]{3,2,1,0:T(8,128)(2,1)S(1)} %slice_bitcast_fusion.3), kind=kLoop, calls=%fused_computation | loop fusion | flops 1179648 | bytes 1572864
  73.9 2.3 %collective-permute-start.14 = (bf16[6,16,512]{2,1,0:T(8,128)(2,1)S(1)}, bf16[6,16,512]{2,1,0:T(8,128)(2,1)S(1)}, u32[]{:S(2)}, u32[]{:S(2)}) collective-permute-start(bf16[6,16,512]{2,1,0:T(8,128)(2,1)S(1)} %get-tuple-element.71), channel_id=1, source_target_pairs={{0,8},{1,9},{2,10},{3,11},{4,12},{5,13},{6,14},{7,15},{8,0},{9,1},... | collective-permute-start | bytes 294920 | tf_op jit(solution)/shard_map/ppermute | solution.py:36
  76.2 2.9 %collective-permute-start.19 = (bf16[3,16,512]{2,1,0:T(8,128)(2,1)S(1)}, bf16[3,16,512]{2,1,0:T(8,128)(2,1)S(1)}, u32[]{:S(2)}, u32[]{:S(2)}) collective-permute-start(bf16[3,16,512]{2,1,0:T(8,128)(2,1)S(1)} %slice_bitcast_fusion.8), channel_id=1, source_target_pairs={{0,16},{1,17},{2,18},{3,19},{4,20},{5,21},{6,22},{7,23},{8,24},{9,... | collective-permute-start | bytes 147464 | tf_op jit(solution)/shard_map/ppermute | solution.py:36
  79.2 5.9 %collective-permute-done.14 = bf16[6,16,512]{2,1,0:T(8,128)(2,1)S(1)} collective-permute-done((bf16[6,16,512]{2,1,0:T(8,128)(2,1)S(1)}, bf16[6,16,512]{2,1,0:T(8,128)(2,1)S(1)}, u32[]{:S(2)}, u32[]{:S(2)}) %collective-permute-start.14) | collective-permute-done | bytes 98336 | tf_op jit(solution)/shard_map/ppermute | solution.py:36
  85.2 0.7 fusion
  (31 shorter events, 0.3 us)
Async XLA Ops:
  0.6 13.7 %copy-start.2 = (bf16[4,1,3,64,512]{4,3,2,1,0:T(8,128)(2,1)S(1)}, bf16[4,1,3,64,512]{4,3,2,1,0:T(8,128)(2,1)}, u32[]{:S(2)}) copy-start(bf16[4,1,3,64,512]{4,3,2,1,0:T(8,128)(2,1)} %param.4) | copy-start | bytes 2359300
  2.0 12.3 %collective-permute-start = (bf16[24,8,512]{2,1,0:T(8,128)(2,1)S(1)}, bf16[24,8,512]{2,1,0:T(8,128)(2,1)S(1)}, u32[]{:S(2)}, u32[]{:S(2)}) collective-permute-start(bf16[24,8,512]{2,1,0:T(8,128)(2,1)S(1)} %get-tuple-element.33), channel_id=1, source_target_pairs={{0,1},{1,2},{2,3},{3,4},{4,5},{5,6},{6,7},{7,8},{8,9},{9,10},{10,1... | collective-permute-start | bytes 589832 | tf_op jit(solution)/shard_map/ppermute | solution.py:36
  2.1 12.2 %collective-permute-start.1 = (bf16[24,8,512]{2,1,0:T(8,128)(2,1)S(1)}, bf16[24,8,512]{2,1,0:T(8,128)(2,1)S(1)}, u32[]{:S(2)}, u32[]{:S(2)}) collective-permute-start(bf16[24,8,512]{2,1,0:T(8,128)(2,1)S(1)} %get-tuple-element.34), channel_id=1, source_target_pairs={{0,31},{1,0},{2,1},{3,2},{4,3},{5,4},{6,5},{7,6},{8,7},{9,8},{10,9... | collective-permute-start | bytes 589832 | tf_op jit(solution)/shard_map/ppermute | solution.py:36
  10.1 5.3 %copy-start.4 = (bf16[1,3,64,512]{3,2,1,0:T(8,128)(2,1)S(1)}, bf16[1,3,64,512]{3,2,1,0:T(8,128)(2,1)}, u32[]{:S(2)}) copy-start(bf16[1,3,64,512]{3,2,1,0:T(8,128)(2,1)} %param.6) | copy-start | bytes 589828
  14.2 12.8 %collective-permute-start.4 = (bf16[4,3,64,256]{3,2,1,0:T(8,128)(2,1)}, bf16[4,3,64,256]{3,2,1,0:T(8,128)(2,1)S(1)}, u32[]{:S(2)}, u32[]{:S(2)}) collective-permute-start(bf16[4,3,64,256]{3,2,1,0:T(8,128)(2,1)} %get-tuple-element.41), channel_id=1, source_target_pairs={{0,2},{1,3},{2,0},{3,1},{4,6},{5,7},{6,4},{7,5},{8,10},{9,11},{10,... | collective-permute-start | bytes 1179656 | tf_op jit(solution)/shard_map/ppermute | solution.py:36
  15.5 9.8 %copy-start.3 = (bf16[3,3,64,512]{3,2,1,0:T(8,128)(2,1)S(1)}, bf16[3,3,64,512]{3,2,1,0:T(8,128)(2,1)}, u32[]{:S(2)}) copy-start(bf16[3,3,64,512]{3,2,1,0:T(8,128)(2,1)} %refs_1_.5) | copy-start | bytes 1769476
  17.1 8.1 %collective-permute-start.2 = (bf16[3,72,512]{2,1,0:T(8,128)(2,1)S(1)}, bf16[3,72,512]{2,1,0:T(8,128)(2,1)S(1)}, u32[]{:S(2)}, u32[]{:S(2)}) collective-permute-start(bf16[3,72,512]{2,1,0:T(8,128)(2,1)S(1)} %get-tuple-element.37), channel_id=1, source_target_pairs={{0,224},{32,0},{64,32},{96,64},{128,96},{160,128},{192,160},{224,1... | collective-permute-start | bytes 663560 | tf_op jit(solution)/shard_map/ppermute | solution.py:41
  18.0 2.3 %copy-start = (bf16[1,3,3,512,512]{4,3,2,1,0:T(8,128)(2,1)S(1)}, bf16[1,3,3,512,512]{4,3,2,1,0:T(8,128)(2,1)}, u32[]{:S(2)}) copy-start(bf16[1,3,3,512,512]{4,3,2,1,0:T(8,128)(2,1)} %param.5) | copy-start | bytes 14155780
  20.4 4.9 %copy-start.1 = (bf16[1,3,3,512,512]{4,3,2,1,0:T(8,128)(2,1)S(1)}, bf16[1,3,3,512,512]{4,3,2,1,0:T(8,128)(2,1)}, u32[]{:S(2)}) copy-start(bf16[1,3,3,512,512]{4,3,2,1,0:T(8,128)(2,1)} %param.5) | copy-start | bytes 14155780
  26.9 8.3 %collective-permute-start.3 = (bf16[3,72,512]{2,1,0:T(8,128)(2,1)S(1)}, bf16[3,72,512]{2,1,0:T(8,128)(2,1)S(1)}, u32[]{:S(2)}, u32[]{:S(2)}) collective-permute-start(bf16[3,72,512]{2,1,0:T(8,128)(2,1)S(1)} %get-tuple-element.39), channel_id=1, source_target_pairs={{0,224},{32,0},{64,32},{96,64},{128,96},{160,128},{192,160},{224,1... | collective-permute-start | bytes 663560 | tf_op jit(solution)/shard_map/ppermute | solution.py:41
  28.2 19.8 %collective-permute-start.7 = (bf16[2,3,72,512]{3,2,1,0:T(8,128)(2,1)S(1)}, bf16[2,3,72,512]{3,2,1,0:T(8,128)(2,1)S(1)}, u32[]{:S(2)}, u32[]{:S(2)}) collective-permute-start(bf16[2,3,72,512]{3,2,1,0:T(8,128)(2,1)S(1)} %pad_maximum_fusion.both0), channel_id=1, source_target_pairs={{0,2},{1,3},{2,0},{3,1},{4,6},{5,7},{6,4},{7,5},{8,10},{9,11},{10,... | collective-permute-start | bytes 1327112 | tf_op jit(solution)/shard_map/ppermute | solution.py:36
  36.9 8.1 %collective-permute-start.5 = (bf16[3,72,512]{2,1,0:T(8,128)(2,1)S(1)}, bf16[3,72,512]{2,1,0:T(8,128)(2,1)S(1)}, u32[]{:S(2)}, u32[]{:S(2)}) collective-permute-start(bf16[3,72,512]{2,1,0:T(8,128)(2,1)S(1)} %get-tuple-element.43), channel_id=1, source_target_pairs={{0,224},{32,0},{64,32},{96,64},{128,96},{160,128},{192,160},{224,1... | collective-permute-start | bytes 663560 | tf_op jit(solution)/shard_map/ppermute | solution.py:41
  38.1 9.9 %collective-permute-start.8 = (bf16[3,72,512]{2,1,0:T(8,128)(2,1)S(1)}, bf16[3,72,512]{2,1,0:T(8,128)(2,1)S(1)}, u32[]{:S(2)}, u32[]{:S(2)}) collective-permute-start(bf16[3,72,512]{2,1,0:T(8,128)(2,1)S(1)} %get-tuple-element.50.third0), channel_id=1, source_target_pairs={{0,2},{1,3},{2,0},{3,1},{4,6},{5,7},{6,4},{7,5},{8,10},{9,11},{10,... | collective-permute-start | bytes 663560 | tf_op jit(solution)/shard_map/ppermute | solution.py:36
  45.1 6.8 %collective-permute-start.6 = (bf16[3,72,512]{2,1,0:T(8,128)(2,1)S(1)}, bf16[3,72,512]{2,1,0:T(8,128)(2,1)S(1)}, u32[]{:S(2)}, u32[]{:S(2)}) collective-permute-start(bf16[3,72,512]{2,1,0:T(8,128)(2,1)S(1)} %shard_map.68.last0), channel_id=1, source_target_pairs={{0,2},{1,3},{2,0},{3,1},{4,6},{5,7},{6,4},{7,5},{8,10},{9,11},{10,... | collective-permute-start | bytes 663560 | tf_op jit(solution)/shard_map/ppermute | solution.py:36
  52.8 1.8 %collective-permute-start.9 = (bf16[4,6,16,512]{3,2,1,0:T(8,128)(2,1)S(1)}, bf16[4,6,16,512]{3,2,1,0:T(8,128)(2,1)S(1)}, u32[]{:S(2)}, u32[]{:S(2)}) collective-permute-start(bf16[4,6,16,512]{3,2,1,0:T(8,128)(2,1)S(1)} %get-tuple-element.55), channel_id=1, source_target_pairs={{0,1},{1,0},{2,3},{3,2},{4,5},{5,4},{6,7},{7,6},{8,9},{9,8},{10,11... | collective-permute-start | bytes 1179656 | tf_op jit(solution)/shard_map/ppermute | solution.py:36
  54.7 1.8 %collective-permute-start.10 = (bf16[4,2,3,16,512]{4,3,2,1,0:T(8,128)(2,1)S(1)}, bf16[4,2,3,16,512]{4,3,2,1,0:T(8,128)(2,1)S(1)}, u32[]{:S(2)}, u32[]{:S(2)}) collective-permute-start(bf16[4,2,3,16,512]{4,3,2,1,0:T(8,128)(2,1)S(1)} %get-tuple-element.56), channel_id=1, source_target_pairs={{0,1},{1,0},{2,3},{3,2},{4,5},{5,4},{6,7},{7,6},{8,9},{9,8},{10,11... | collective-permute-start | bytes 1179656 | tf_op jit(solution)/shard_map/ppermute | solution.py:36
  55.0 13.0 %collective-permute-start.12 = (bf16[4,6,16,512]{3,2,1,0:T(8,128)(2,1)S(1)}, bf16[4,6,16,512]{3,2,1,0:T(8,128)(2,1)S(1)}, u32[]{:S(2)}, u32[]{:S(2)}) collective-permute-start(bf16[4,6,16,512]{3,2,1,0:T(8,128)(2,1)S(1)} %add_convert_fusion.2), channel_id=1, source_target_pairs={{0,16},{1,17},{2,18},{3,19},{4,20},{5,21},{6,22},{7,23},{8,24},{9,... | collective-permute-start | bytes 1179656 | tf_op jit(solution)/shard_map/ppermute | solution.py:36
  55.1 11.8 %collective-permute-start.11 = (bf16[4,6,16,512]{3,2,1,0:T(8,128)(2,1)S(1)}, bf16[4,6,16,512]{3,2,1,0:T(8,128)(2,1)S(1)}, u32[]{:S(2)}, u32[]{:S(2)}) collective-permute-start(bf16[4,6,16,512]{3,2,1,0:T(8,128)(2,1)S(1)} %get-tuple-element.60), channel_id=1, source_target_pairs={{0,1},{1,0},{2,3},{3,2},{4,5},{5,4},{6,7},{7,6},{8,9},{9,8},{10,11... | collective-permute-start | bytes 1179656 | tf_op jit(solution)/shard_map/ppermute | solution.py:36
  56.6 17.2 %collective-permute-start.18 = (bf16[2,3,16,512]{3,2,1,0:T(8,128)(2,1)S(1)}, bf16[2,3,16,512]{3,2,1,0:T(8,128)(2,1)S(1)}, u32[]{:S(2)}, u32[]{:S(2)}) collective-permute-start(bf16[2,3,16,512]{3,2,1,0:T(8,128)(2,1)S(1)} %get-tuple-element.66), channel_id=1, source_target_pairs={{0,12},{1,13},{2,14},{3,15},{4,0},{5,1},{6,2},{7,3},{8,4},{9,5},{1... | collective-permute-start | bytes 294920 | tf_op jit(solution)/shard_map/ppermute | solution.py:36
  62.7 13.5 %collective-permute-start.16 = (bf16[2,3,16,512]{3,2,1,0:T(8,128)(2,1)S(1)}, bf16[2,3,16,512]{3,2,1,0:T(8,128)(2,1)S(1)}, u32[]{:S(2)}, u32[]{:S(2)}) collective-permute-start(bf16[2,3,16,512]{3,2,1,0:T(8,128)(2,1)S(1)} %get-tuple-element.67), channel_id=1, source_target_pairs={{0,8},{1,9},{2,10},{3,11},{4,12},{5,13},{6,14},{7,15},{8,0},{9,1},... | collective-permute-start | bytes 294920 | tf_op jit(solution)/shard_map/ppermute | solution.py:36
  64.3 11.8 %collective-permute-start.17 = (bf16[2,3,16,512]{3,2,1,0:T(8,128)(2,1)S(1)}, bf16[2,3,16,512]{3,2,1,0:T(8,128)(2,1)S(1)}, u32[]{:S(2)}, u32[]{:S(2)}) collective-permute-start(bf16[2,3,16,512]{3,2,1,0:T(8,128)(2,1)S(1)} %get-tuple-element.68), channel_id=1, source_target_pairs={{0,4},{1,5},{2,6},{3,7},{4,8},{5,9},{6,10},{7,11},{8,12},{9,13},{1... | collective-permute-start | bytes 294920 | tf_op jit(solution)/shard_map/ppermute | solution.py:36
  68.2 11.0 %collective-permute-start.13 = (bf16[6,16,512]{2,1,0:T(8,128)(2,1)S(1)}, bf16[6,16,512]{2,1,0:T(8,128)(2,1)S(1)}, u32[]{:S(2)}, u32[]{:S(2)}) collective-permute-start(bf16[6,16,512]{2,1,0:T(8,128)(2,1)S(1)} %get-tuple-element.69), channel_id=1, source_target_pairs={{0,4},{1,5},{2,6},{3,7},{4,8},{5,9},{6,10},{7,11},{8,12},{9,13},{1... | collective-permute-start | bytes 294920 | tf_op jit(solution)/shard_map/ppermute | solution.py:36
  71.2 7.9 %collective-permute-start.15 = (bf16[6,16,512]{2,1,0:T(8,128)(2,1)S(1)}, bf16[6,16,512]{2,1,0:T(8,128)(2,1)S(1)}, u32[]{:S(2)}, u32[]{:S(2)}) collective-permute-start(bf16[6,16,512]{2,1,0:T(8,128)(2,1)S(1)} %get-tuple-element.70), channel_id=1, source_target_pairs={{0,12},{1,13},{2,14},{3,15},{4,0},{5,1},{6,2},{7,3},{8,4},{9,5},{1... | collective-permute-start | bytes 294920 | tf_op jit(solution)/shard_map/ppermute | solution.py:36
  73.9 11.2 %collective-permute-start.14 = (bf16[6,16,512]{2,1,0:T(8,128)(2,1)S(1)}, bf16[6,16,512]{2,1,0:T(8,128)(2,1)S(1)}, u32[]{:S(2)}, u32[]{:S(2)}) collective-permute-start(bf16[6,16,512]{2,1,0:T(8,128)(2,1)S(1)} %get-tuple-element.71), channel_id=1, source_target_pairs={{0,8},{1,9},{2,10},{3,11},{4,12},{5,13},{6,14},{7,15},{8,0},{9,1},... | collective-permute-start | bytes 294920 | tf_op jit(solution)/shard_map/ppermute | solution.py:36
  76.2 8.9 %collective-permute-start.19 = (bf16[3,16,512]{2,1,0:T(8,128)(2,1)S(1)}, bf16[3,16,512]{2,1,0:T(8,128)(2,1)S(1)}, u32[]{:S(2)}, u32[]{:S(2)}) collective-permute-start(bf16[3,16,512]{2,1,0:T(8,128)(2,1)S(1)} %slice_bitcast_fusion.8), channel_id=1, source_target_pairs={{0,16},{1,17},{2,18},{3,19},{4,20},{5,21},{6,22},{7,23},{8,24},{9,... | collective-permute-start | bytes 147464 | tf_op jit(solution)/shard_map/ppermute | solution.py:36

commit v9 on v8

--- a/solution.py
+++ b/solution.py
@@ -213,7 +213,9 @@
 
 def spread_kernel(place_ref, x_ref, source_ref, out0, out1, w_ref, field_ref, done):
     copies = [pltpu.make_async_copy(x_ref.at[t], field_ref.at[t], done.at[t]) for t in range(STEPS)]
-    copies.append(pltpu.make_async_copy(source_ref, w_ref, done.at[STEPS]))
+    for n in range(3):
+        rows = slice(3 * n, 3 * n + 3)
+        copies.append(pltpu.make_async_copy(source_ref.at[rows], w_ref.at[rows], done.at[STEPS + n]))
     for copy in copies:
         copy.start()
     h, j, k, c = (place_ref[n] for n in range(4))
@@ -234,7 +236,8 @@
             for r in range(ROWS):
                 at = (t * ROWS + r) * WIDTH
                 out[t, r] = value[at : at + WIDTH, n * HALF : (n + 1) * HALF]
-    copies[STEPS].wait()
+    for copy in copies[STEPS:]:
+        copy.wait()
 
 
 def spread(place, x, weights):
@@ -247,7 +250,7 @@
         out_specs=(VMEM, VMEM, VMEM),
         scratch_shapes=[
             pltpu.VMEM((STEPS, ROWS, WIDTH, CH), BF),
-            pltpu.SemaphoreType.DMA((STEPS + 1,)),
+            pltpu.SemaphoreType.DMA((STEPS + 3,)),
         ],
         compiler_params=params(),
         cost_estimate=cost(4.5e8, 1.2e7),

time: 86.7 us -> 86.7 us (level)
  no operation moved by 1% of the time
where the time goes in v9:
time: 86.7 us; the launch traced here: 85.9 us
  starting transfers between devices  36.5 us (42%)
  waiting for transfers between devices  22.7 us (26%)
  Pallas kernels  20.9 us (24%)
  local copies, waits for them, and re-layouts  2.44 us (3%)
  other arithmetic  2.36 us (3%)
  between operations  0.94 us (1%)
    ppermute x17, starting transfers between devices, send(): return lax.ppermute(block, 'az', route)  35.5 us
    ppermute x3, waiting for transfers between devices, relay(): lax.ppermute(block, 'segment', [(i, (i - 1) % count) for i in range(count)])  12.4 us
    ppermute x17, waiting for transfers between devices, send(): return lax.ppermute(block, 'az', route)  10.3 us
    pallas_call x4, Pallas kernels, back_step(): pl.pallas_call(lambda *refs: back_kernel(first, *refs), grid=(1,), out_sh...  6.67 us
    pallas_call x4, Pallas kernels, slope_factors(): pl.pallas_call(factor_kernel, grid=(1,), out_shape=jax.ShapeDtypeStruct((...  4.5 us
    pallas_call x1, Pallas kernels, spread(): pl.pallas_call(spread_kernel, out_shape=(shape, shape, pltpu.VMEM(weights...  4.07 us
    pallas_call x1, Pallas kernels, early_products(): pl.pallas_call(early_kernel, out_shape=jax.ShapeDtypeStruct((3, HALF, 3 *...  3.45 us
    unnamed x10, local copies, waits for them, and re-layouts  2.36 us
  transfers between devices with their start and end apart: 20, of which 8 were waited for; matrix products, arithmetic and copies ran while one was open for 2% of the time, Pallas kernels for 22%

profile of v9, /device:TPU:6, one launch (start us, length us, event | category | flops | bytes accessed | tf_op | source)
XLA Modules:
  0.0 85.9 jit_solution(2913009344158707034)
XLA Ops:
  0.6 1.3 %shard_map.59 = (bf16[24,8,512]{2,1,0:T(8,128)(2,1)S(1)}, bf16[24,8,512]{2,1,0:T(8,128)(2,1)S(1)}) custom-call(bf16[4,3,64,512]{3,2,1,0:T(8,128)(2,1)} %bitcast.59, bf16[3,64,512]{2,1,0:T(8,128)(2,1)} %bitcast.66, bf16[3,3,64,512]{3,2,1,0:T(8,128)(2,1)} %refs_1_.5, bf16[4,3,64,512]{3,2,1,0:T(8,128)(2,1)} %bitcast.60, bf16[3,64,512]{2,1,0:T(8,128)(2,1)} %bitcast.67, ...), custom_call_target="tpu_custom_call" | custom-call | bytes 1048576 | tf_op jit(solution)/shard_map/pallas_call | solution.py:79
  2.0 0.1 collective-permute-start
  2.1 8.0 %collective-permute-start.1 = (bf16[24,8,512]{2,1,0:T(8,128)(2,1)S(1)}, bf16[24,8,512]{2,1,0:T(8,128)(2,1)S(1)}, u32[]{:S(2)}, u32[]{:S(2)}) collective-permute-start(bf16[24,8,512]{2,1,0:T(8,128)(2,1)S(1)} %get-tuple-element.34), channel_id=1, source_target_pairs={{0,31},{1,0},{2,1},{3,2},{4,3},{5,4},{6,5},{7,6},{8,7},{9,8},{10,9... | collective-permute-start | bytes 589832 | tf_op jit(solution)/shard_map/ppermute | solution.py:36
  10.1 0.1 pad_add_fusion.place_ref
  10.1 4.1 %shard_map.60 = (bf16[4,3,64,256]{3,2,1,0:T(8,128)(2,1)S(1)}, bf16[4,3,64,256]{3,2,1,0:T(8,128)(2,1)}, bf16[9,512,512]{2,1,0:T(8,128)(2,1)S(1)}) custom-call(s32[4]{0:T(128)S(1)} %pad_add_fusion.place_ref, bf16[4,3,64,512]{3,2,1,0:T(8,128)(2,1)} %bitcast.61, bf16[9,512,512]{2,1,0:T(8,128)(2,1)} %bitcast.52), custom_call_target="tpu_custom_call" | custom-call | flops 450000000 | bytes 12000000 | tf_op jit(solution)/shard_map/pallas_call | solution.py:246
  14.2 0.1 collective-permute-start.4
  14.3 1.1 %shard_map.61.refs_3_ = f32[1,3,72,512]{3,2,1,0:T(8,128)S(1)} custom-call(bf16[4,3,64,512]{3,2,1,0:T(8,128)(2,1)S(1)} %bitcast.62, bf16[24,8,512]{2,1,0:T(8,128)(2,1)S(1)} %collective-permute-done.low_ref.refs_1_.refs_2_, bf16[24,8,512]{2,1,0:T(8,128)(2,1)S(1)} %collective-permute-done.1.high_ref.refs_2_.refs_3_, ...), custom_call_target="tpu_custom_call" | custom-call | flops 1200000000 | bytes 5000000 | tf_op jit(solution)/shard_map/pallas_call | solution.py:132
  15.5 1.7 %shard_map.62 = (bf16[3,72,512]{2,1,0:T(8,128)(2,1)S(1)}, bf16[3,72,512]{2,1,0:T(8,128)(2,1)S(1)}) custom-call(bf16[3,64,512]{2,1,0:T(8,128)(2,1)S(1)} %bitcast.68, bf16[24,8,512]{2,1,0:T(8,128)(2,1)S(1)} %collective-permute-done.low_ref.refs_1_.refs_2_, bf16[24,8,512]{2,1,0:T(8,128)(2,1)S(1)} %collective-permute-done.1.high_ref.refs_2_.refs_3_, ...), custom_call_target="tpu_custom_call" | custom-call | flops 1100000000 | bytes 6000000 | tf_op jit(solution)/shard_map/pallas_call | solution.py:200
  17.2 0.9 %collective-permute-start.2 = (bf16[3,72,512]{2,1,0:T(8,128)(2,1)S(1)}, bf16[3,72,512]{2,1,0:T(8,128)(2,1)S(1)}, u32[]{:S(2)}, u32[]{:S(2)}) collective-permute-start(bf16[3,72,512]{2,1,0:T(8,128)(2,1)S(1)} %get-tuple-element.37), channel_id=1, source_target_pairs={{0,224},{32,0},{64,32},{96,64},{128,96},{160,128},{192,160},{224,1... | collective-permute-start | bytes 663560 | tf_op jit(solution)/shard_map/ppermute | solution.py:41
  18.1 2.3 %copy-done = bf16[1,3,3,512,512]{4,3,2,1,0:T(8,128)(2,1)S(1)} copy-done((bf16[1,3,3,512,512]{4,3,2,1,0:T(8,128)(2,1)S(1)}, bf16[1,3,3,512,512]{4,3,2,1,0:T(8,128)(2,1)}, u32[]{:S(2)}) %copy-start) | copy-done | bytes 4718616
  20.4 1.1 %shard_map.63.refs_5_ = f32[1,3,72,512]{3,2,1,0:T(8,128)S(1)} custom-call(bf16[4,3,64,512]{3,2,1,0:T(8,128)(2,1)S(1)} %bitcast.63, bf16[24,8,512]{2,1,0:T(8,128)(2,1)S(1)} %collective-permute-done.low_ref.refs_1_.refs_2_, bf16[24,8,512]{2,1,0:T(8,128)(2,1)S(1)} %collective-permute-done.1.high_ref.refs_2_.refs_3_, bf16[9,512,512]{2,1,0:T(8,128)(2,1)S(1)} %bitcast.53), custom_call_target="tpu_custom_call" | custom-call | flops 1200000000 | bytes 5000000 | tf_op jit(solution)/shard_map/pallas_call | solution.py:132
  21.5 3.7 %collective-permute-done.2.refs_4_ = bf16[3,72,512]{2,1,0:T(8,128)(2,1)S(1)} collective-permute-done((bf16[3,72,512]{2,1,0:T(8,128)(2,1)S(1)}, bf16[3,72,512]{2,1,0:T(8,128)(2,1)S(1)}, u32[]{:S(2)}, u32[]{:S(2)}) %collective-permute-start.2) | collective-permute-done | bytes 221216 | tf_op jit(solution)/shard_map/ppermute | solution.py:41
  25.3 1.7 %shard_map.64 = (bf16[3,72,512]{2,1,0:T(8,128)(2,1)S(1)}, bf16[3,72,512]{2,1,0:T(8,128)(2,1)S(1)}) custom-call(s32[1]{0:T(128)} %bitcast.8.refs_0_.flag_ref, bf16[3,3,64,512]{3,2,1,0:T(8,128)(2,1)S(1)} %copy-done.3, bf16[24,8,512]{2,1,0:T(8,128)(2,1)S(1)} %collective-permute-done.low_ref.refs_1_.refs_2_, ...), custom_call_target="tpu_custom_call" | custom-call | flops 1100000000 | bytes 6000000 | tf_op jit(solution)/shard_map/pallas_call | solution.py:200
  27.0 0.1 collective-permute-start.3
  27.1 1.1 %shard_map.65.refs_5_ = f32[1,3,72,512]{3,2,1,0:T(8,128)S(1)} custom-call(bf16[4,3,64,512]{3,2,1,0:T(8,128)(2,1)S(1)} %bitcast.64, bf16[24,8,512]{2,1,0:T(8,128)(2,1)S(1)} %collective-permute-done.low_ref.refs_1_.refs_2_, bf16[24,8,512]{2,1,0:T(8,128)(2,1)S(1)} %collective-permute-done.1.high_ref.refs_2_.refs_3_, bf16[9,512,512]{2,1,0:T(8,128)(2,1)S(1)} %bitcast.55), custom_call_target="tpu_custom_call" | custom-call | flops 1200000000 | bytes 5000000 | tf_op jit(solution)/shard_map/pallas_call | solution.py:132
  28.3 2.1 %collective-permute-start.7 = (bf16[2,3,72,512]{3,2,1,0:T(8,128)(2,1)S(1)}, bf16[2,3,72,512]{3,2,1,0:T(8,128)(2,1)S(1)}, u32[]{:S(2)}, u32[]{:S(2)}) collective-permute-start(bf16[2,3,72,512]{3,2,1,0:T(8,128)(2,1)S(1)} %pad_maximum_fusion.both0), channel_id=1, source_target_pairs={{0,2},{1,3},{2,0},{3,1},{4,6},{5,7},{6,4},{7,5},{8,10},{9,11},{10,... | collective-permute-start | bytes 1327112 | tf_op jit(solution)/shard_map/ppermute | solution.py:36
  30.3 4.9 %collective-permute-done.3.refs_4_ = bf16[3,72,512]{2,1,0:T(8,128)(2,1)S(1)} collective-permute-done((bf16[3,72,512]{2,1,0:T(8,128)(2,1)S(1)}, bf16[3,72,512]{2,1,0:T(8,128)(2,1)S(1)}, u32[]{:S(2)}, u32[]{:S(2)}) %collective-permute-start.3) | collective-permute-done | bytes 221216 | tf_op jit(solution)/shard_map/ppermute | solution.py:41
  35.2 1.7 %shard_map.66 = (bf16[3,72,512]{2,1,0:T(8,128)(2,1)S(1)}, bf16[3,72,512]{2,1,0:T(8,128)(2,1)S(1)}) custom-call(s32[1]{0:T(128)} %bitcast.8.refs_0_.flag_ref, bf16[3,3,64,512]{3,2,1,0:T(8,128)(2,1)S(1)} %copy-done.3, bf16[24,8,512]{2,1,0:T(8,128)(2,1)S(1)} %collective-permute-done.low_ref.refs_1_.refs_2_, ...), custom_call_target="tpu_custom_call" | custom-call | flops 1100000000 | bytes 6000000 | tf_op jit(solution)/shard_map/pallas_call | solution.py:200
  36.9 0.1 collective-permute-start.5
  37.0 1.1 %shard_map.67.factor_ref.refs_5_ = f32[1,3,72,512]{3,2,1,0:T(8,128)S(1)} custom-call(bf16[4,3,64,512]{3,2,1,0:T(8,128)(2,1)S(1)} %bitcast.65, bf16[24,8,512]{2,1,0:T(8,128)(2,1)S(1)} %collective-permute-done.low_ref.refs_1_.refs_2_, bf16[24,8,512]{2,1,0:T(8,128)(2,1)S(1)} %collective-permute-done.1.high_ref.refs_2_.refs_3_, bf16[9,512,512]{2,1,0:T(8,128)(2,1)S(1)} %bitcast.57), custom_call_target="tpu_custom_call" | custom-call | flops 1200000000 | bytes 5000000 | tf_op jit(solution)/shard_map/pallas_call | solution.py:132
  38.1 3.2 %collective-permute-start.8 = (bf16[3,72,512]{2,1,0:T(8,128)(2,1)S(1)}, bf16[3,72,512]{2,1,0:T(8,128)(2,1)S(1)}, u32[]{:S(2)}, u32[]{:S(2)}) collective-permute-start(bf16[3,72,512]{2,1,0:T(8,128)(2,1)S(1)} %get-tuple-element.50.third0), channel_id=1, source_target_pairs={{0,2},{1,3},{2,0},{3,1},{4,6},{5,7},{6,4},{7,5},{8,10},{9,11},{10,... | collective-permute-start | bytes 663560 | tf_op jit(solution)/shard_map/ppermute | solution.py:36
  41.3 3.7 %collective-permute-done.5.relay_ref.refs_4_ = bf16[3,72,512]{2,1,0:T(8,128)(2,1)S(1)} collective-permute-done((bf16[3,72,512]{2,1,0:T(8,128)(2,1)S(1)}, bf16[3,72,512]{2,1,0:T(8,128)(2,1)S(1)}, u32[]{:S(2)}, u32[]{:S(2)}) %collective-permute-start.5) | collective-permute-done | bytes 221216 | tf_op jit(solution)/shard_map/ppermute | solution.py:41
  45.0 0.1 shard_map.68.last0
  45.1 3.0 %collective-permute-start.6 = (bf16[3,72,512]{2,1,0:T(8,128)(2,1)S(1)}, bf16[3,72,512]{2,1,0:T(8,128)(2,1)S(1)}, u32[]{:S(2)}, u32[]{:S(2)}) collective-permute-start(bf16[3,72,512]{2,1,0:T(8,128)(2,1)S(1)} %shard_map.68.last0), channel_id=1, source_target_pairs={{0,2},{1,3},{2,0},{3,1},{4,6},{5,7},{6,4},{7,5},{8,10},{9,11},{10,... | collective-permute-start | bytes 663560 | tf_op jit(solution)/shard_map/ppermute | solution.py:36
  48.1 3.4 %shard_map.69.total_ref = f32[3,256,1536]{2,1,0:T(8,128)S(1)} custom-call(bf16[4,3,64,256]{3,2,1,0:T(8,128)(2,1)S(1)} %get-tuple-element.40.x0, bf16[4,3,64,256]{3,2,1,0:T(8,128)(2,1)S(1)} %collective-permute-done.4.x1.x_ref, bf16[2,3,72,512]{3,2,1,0:T(8,128)(2,1)S(1)} %pad_maximum_fusion.both0, bf16[2,3,72,512]{3,2,1,0:T(8,128)(2,1)S(1)} %collective-permute-done.7.both1, ...), custom_call_target="tpu_custom_call" | custom-call | flops 3000000000 | bytes 8000000 | tf_op jit(solution)/shard_map/pallas_call | solution.py:297
  51.6 0.5 collective-permute-done.6.g_ref
  52.0 0.8 shard_map.70
  52.8 0.1 collective-permute-start.9
  53.0 1.7 %collective-permute-done.9 = bf16[4,6,16,512]{3,2,1,0:T(8,128)(2,1)S(1)} collective-permute-done((bf16[4,6,16,512]{3,2,1,0:T(8,128)(2,1)S(1)}, bf16[4,6,16,512]{3,2,1,0:T(8,128)(2,1)S(1)}, u32[]{:S(2)}, u32[]{:S(2)}) %collective-permute-start.9) | collective-permute-done | bytes 393248 | tf_op jit(solution)/shard_map/ppermute | solution.py:36
  54.6 0.1 add_convert_fusion.2
  54.8 0.2 collective-permute-start.10
  55.0 0.1 collective-permute-start.12
  55.1 0.5 collective-permute-start.11
  55.6 1.0 %collective-permute-done.10 = bf16[4,2,3,16,512]{4,3,2,1,0:T(8,128)(2,1)S(1)} collective-permute-done((bf16[4,2,3,16,512]{4,3,2,1,0:T(8,128)(2,1)S(1)}, bf16[4,2,3,16,512]{4,3,2,1,0:T(8,128)(2,1)S(1)}, u32[]{:S(2)}, u32[]{:S(2)}) %collective-permute-start.10) | collective-permute-done | bytes 393248 | tf_op jit(solution)/shard_map/ppermute | solution.py:36
  56.6 0.1 fusion.8
  56.7 6.0 %collective-permute-start.18 = (bf16[2,3,16,512]{3,2,1,0:T(8,128)(2,1)S(1)}, bf16[2,3,16,512]{3,2,1,0:T(8,128)(2,1)S(1)}, u32[]{:S(2)}, u32[]{:S(2)}) collective-permute-start(bf16[2,3,16,512]{3,2,1,0:T(8,128)(2,1)S(1)} %get-tuple-element.66), channel_id=1, source_target_pairs={{0,12},{1,13},{2,14},{3,15},{4,0},{5,1},{6,2},{7,3},{8,4},{9,5},{1... | collective-permute-start | bytes 294920 | tf_op jit(solution)/shard_map/ppermute | solution.py:36
  62.7 1.7 %collective-permute-start.16 = (bf16[2,3,16,512]{3,2,1,0:T(8,128)(2,1)S(1)}, bf16[2,3,16,512]{3,2,1,0:T(8,128)(2,1)S(1)}, u32[]{:S(2)}, u32[]{:S(2)}) collective-permute-start(bf16[2,3,16,512]{3,2,1,0:T(8,128)(2,1)S(1)} %get-tuple-element.67), channel_id=1, source_target_pairs={{0,8},{1,9},{2,10},{3,11},{4,12},{5,13},{6,14},{7,15},{8,0},{9,1},... | collective-permute-start | bytes 294920 | tf_op jit(solution)/shard_map/ppermute | solution.py:36
  64.4 0.8 collective-permute-start.17
  65.1 1.7 %shard_map.71 = (bf16[3,72,512]{2,1,0:T(8,128)(2,1)S(1)}, bf16[3,72,512]{2,1,0:T(8,128)(2,1)}) custom-call(s32[1]{0:T(128)} %bitcast.8.refs_0_.flag_ref, bf16[3,3,64,512]{3,2,1,0:T(8,128)(2,1)S(1)} %copy-done.3, bf16[24,8,512]{2,1,0:T(8,128)(2,1)S(1)} %collective-permute-done.low_ref.refs_1_.refs_2_, ...), custom_call_target="tpu_custom_call" | custom-call | flops 1100000000 | bytes 6000000 | tf_op jit(solution)/shard_map/pallas_call | solution.py:200
  66.8 1.2 %collective-permute-done.12 = bf16[4,6,16,512]{3,2,1,0:T(8,128)(2,1)S(1)} collective-permute-done((bf16[4,6,16,512]{3,2,1,0:T(8,128)(2,1)S(1)}, bf16[4,6,16,512]{3,2,1,0:T(8,128)(2,1)S(1)}, u32[]{:S(2)}, u32[]{:S(2)}) %collective-permute-start.12) | collective-permute-done | bytes 393248 | tf_op jit(solution)/shard_map/ppermute | solution.py:36
  68.0 0.2 add_convert_fusion
  68.3 2.9 %collective-permute-start.13 = (bf16[6,16,512]{2,1,0:T(8,128)(2,1)S(1)}, bf16[6,16,512]{2,1,0:T(8,128)(2,1)S(1)}, u32[]{:S(2)}, u32[]{:S(2)}) collective-permute-start(bf16[6,16,512]{2,1,0:T(8,128)(2,1)S(1)} %get-tuple-element.69), channel_id=1, source_target_pairs={{0,4},{1,5},{2,6},{3,7},{4,8},{5,9},{6,10},{7,11},{8,12},{9,13},{1... | collective-permute-start | bytes 294920 | tf_op jit(solution)/shard_map/ppermute | solution.py:36
  71.2 1.6 %collective-permute-start.15 = (bf16[6,16,512]{2,1,0:T(8,128)(2,1)S(1)}, bf16[6,16,512]{2,1,0:T(8,128)(2,1)S(1)}, u32[]{:S(2)}, u32[]{:S(2)}) collective-permute-start(bf16[6,16,512]{2,1,0:T(8,128)(2,1)S(1)} %get-tuple-element.70), channel_id=1, source_target_pairs={{0,12},{1,13},{2,14},{3,15},{4,0},{5,1},{6,2},{7,3},{8,4},{9,5},{1... | collective-permute-start | bytes 294920 | tf_op jit(solution)/shard_map/ppermute | solution.py:36
  72.8 1.0 %maximum_bitcast_fusion = bf16[4,1,3,64,512]{4,3,2,1,0:T(8,128)(2,1)} fusion(bf16[1,3,64,512]{3,2,1,0:T(8,128)(2,1)S(1)} %slice_bitcast_fusion, bf16[1,3,64,512]{3,2,1,0:T(8,128)(2,1)S(1)} %slice_bitcast_fusion.1, bf16[1,3,64,512]{3,2,1,0:T(8,128)(2,1)S(1)} %slice_bitcast_fusion.2, bf16[1,3,64,512]{3,2,1,0:T(8,128)(2,1)S(1)} %slice_bitcast_fusion.3), kind=kLoop, calls=%fused_computation | loop fusion | flops 1179648 | bytes 1572864
  73.8 2.3 %collective-permute-start.14 = (bf16[6,16,512]{2,1,0:T(8,128)(2,1)S(1)}, bf16[6,16,512]{2,1,0:T(8,128)(2,1)S(1)}, u32[]{:S(2)}, u32[]{:S(2)}) collective-permute-start(bf16[6,16,512]{2,1,0:T(8,128)(2,1)S(1)} %get-tuple-element.71), channel_id=1, source_target_pairs={{0,8},{1,9},{2,10},{3,11},{4,12},{5,13},{6,14},{7,15},{8,0},{9,1},... | collective-permute-start | bytes 294920 | tf_op jit(solution)/shard_map/ppermute | solution.py:36
  76.2 3.0 %collective-permute-start.19 = (bf16[3,16,512]{2,1,0:T(8,128)(2,1)S(1)}, bf16[3,16,512]{2,1,0:T(8,128)(2,1)S(1)}, u32[]{:S(2)}, u32[]{:S(2)}) collective-permute-start(bf16[3,16,512]{2,1,0:T(8,128)(2,1)S(1)} %slice_bitcast_fusion.8), channel_id=1, source_target_pairs={{0,16},{1,17},{2,18},{3,19},{4,20},{5,21},{6,22},{7,23},{8,24},{9,... | collective-permute-start | bytes 147464 | tf_op jit(solution)/shard_map/ppermute | solution.py:36
  79.1 6.0 %collective-permute-done.14 = bf16[6,16,512]{2,1,0:T(8,128)(2,1)S(1)} collective-permute-done((bf16[6,16,512]{2,1,0:T(8,128)(2,1)S(1)}, bf16[6,16,512]{2,1,0:T(8,128)(2,1)S(1)}, u32[]{:S(2)}, u32[]{:S(2)}) %collective-permute-start.14) | collective-permute-done | bytes 98336 | tf_op jit(solution)/shard_map/ppermute | solution.py:36
  85.2 0.7 fusion
  (31 shorter events, 0.3 us)
Async XLA Ops:
  0.6 13.7 %copy-start.2 = (bf16[4,1,3,64,512]{4,3,2,1,0:T(8,128)(2,1)S(1)}, bf16[4,1,3,64,512]{4,3,2,1,0:T(8,128)(2,1)}, u32[]{:S(2)}) copy-start(bf16[4,1,3,64,512]{4,3,2,1,0:T(8,128)(2,1)} %param.4) | copy-start | bytes 2359300
  2.0 12.4 %collective-permute-start = (bf16[24,8,512]{2,1,0:T(8,128)(2,1)S(1)}, bf16[24,8,512]{2,1,0:T(8,128)(2,1)S(1)}, u32[]{:S(2)}, u32[]{:S(2)}) collective-permute-start(bf16[24,8,512]{2,1,0:T(8,128)(2,1)S(1)} %get-tuple-element.33), channel_id=1, source_target_pairs={{0,1},{1,2},{2,3},{3,4},{4,5},{5,6},{6,7},{7,8},{8,9},{9,10},{10,1... | collective-permute-start | bytes 589832 | tf_op jit(solution)/shard_map/ppermute | solution.py:36
  2.1 12.3 %collective-permute-start.1 = (bf16[24,8,512]{2,1,0:T(8,128)(2,1)S(1)}, bf16[24,8,512]{2,1,0:T(8,128)(2,1)S(1)}, u32[]{:S(2)}, u32[]{:S(2)}) collective-permute-start(bf16[24,8,512]{2,1,0:T(8,128)(2,1)S(1)} %get-tuple-element.34), channel_id=1, source_target_pairs={{0,31},{1,0},{2,1},{3,2},{4,3},{5,4},{6,5},{7,6},{8,7},{9,8},{10,9... | collective-permute-start | bytes 589832 | tf_op jit(solution)/shard_map/ppermute | solution.py:36
  10.1 5.3 %copy-start.4 = (bf16[1,3,64,512]{3,2,1,0:T(8,128)(2,1)S(1)}, bf16[1,3,64,512]{3,2,1,0:T(8,128)(2,1)}, u32[]{:S(2)}) copy-start(bf16[1,3,64,512]{3,2,1,0:T(8,128)(2,1)} %param.6) | copy-start | bytes 589828
  14.2 12.8 %collective-permute-start.4 = (bf16[4,3,64,256]{3,2,1,0:T(8,128)(2,1)}, bf16[4,3,64,256]{3,2,1,0:T(8,128)(2,1)S(1)}, u32[]{:S(2)}, u32[]{:S(2)}) collective-permute-start(bf16[4,3,64,256]{3,2,1,0:T(8,128)(2,1)} %get-tuple-element.41), channel_id=1, source_target_pairs={{0,2},{1,3},{2,0},{3,1},{4,6},{5,7},{6,4},{7,5},{8,10},{9,11},{10,... | collective-permute-start | bytes 1179656 | tf_op jit(solution)/shard_map/ppermute | solution.py:36
  15.5 9.8 %copy-start.3 = (bf16[3,3,64,512]{3,2,1,0:T(8,128)(2,1)S(1)}, bf16[3,3,64,512]{3,2,1,0:T(8,128)(2,1)}, u32[]{:S(2)}) copy-start(bf16[3,3,64,512]{3,2,1,0:T(8,128)(2,1)} %refs_1_.5) | copy-start | bytes 1769476
  17.2 8.1 %collective-permute-start.2 = (bf16[3,72,512]{2,1,0:T(8,128)(2,1)S(1)}, bf16[3,72,512]{2,1,0:T(8,128)(2,1)S(1)}, u32[]{:S(2)}, u32[]{:S(2)}) collective-permute-start(bf16[3,72,512]{2,1,0:T(8,128)(2,1)S(1)} %get-tuple-element.37), channel_id=1, source_target_pairs={{0,224},{32,0},{64,32},{96,64},{128,96},{160,128},{192,160},{224,1... | collective-permute-start | bytes 663560 | tf_op jit(solution)/shard_map/ppermute | solution.py:41
  18.1 2.3 %copy-start = (bf16[1,3,3,512,512]{4,3,2,1,0:T(8,128)(2,1)S(1)}, bf16[1,3,3,512,512]{4,3,2,1,0:T(8,128)(2,1)}, u32[]{:S(2)}) copy-start(bf16[1,3,3,512,512]{4,3,2,1,0:T(8,128)(2,1)} %param.5) | copy-start | bytes 14155780
  20.4 4.9 %copy-start.1 = (bf16[1,3,3,512,512]{4,3,2,1,0:T(8,128)(2,1)S(1)}, bf16[1,3,3,512,512]{4,3,2,1,0:T(8,128)(2,1)}, u32[]{:S(2)}) copy-start(bf16[1,3,3,512,512]{4,3,2,1,0:T(8,128)(2,1)} %param.5) | copy-start | bytes 14155780
  27.0 8.3 %collective-permute-start.3 = (bf16[3,72,512]{2,1,0:T(8,128)(2,1)S(1)}, bf16[3,72,512]{2,1,0:T(8,128)(2,1)S(1)}, u32[]{:S(2)}, u32[]{:S(2)}) collective-permute-start(bf16[3,72,512]{2,1,0:T(8,128)(2,1)S(1)} %get-tuple-element.39), channel_id=1, source_target_pairs={{0,224},{32,0},{64,32},{96,64},{128,96},{160,128},{192,160},{224,1... | collective-permute-start | bytes 663560 | tf_op jit(solution)/shard_map/ppermute | solution.py:41
  28.3 19.8 %collective-permute-start.7 = (bf16[2,3,72,512]{3,2,1,0:T(8,128)(2,1)S(1)}, bf16[2,3,72,512]{3,2,1,0:T(8,128)(2,1)S(1)}, u32[]{:S(2)}, u32[]{:S(2)}) collective-permute-start(bf16[2,3,72,512]{3,2,1,0:T(8,128)(2,1)S(1)} %pad_maximum_fusion.both0), channel_id=1, source_target_pairs={{0,2},{1,3},{2,0},{3,1},{4,6},{5,7},{6,4},{7,5},{8,10},{9,11},{10,... | collective-permute-start | bytes 1327112 | tf_op jit(solution)/shard_map/ppermute | solution.py:36
  36.9 8.1 %collective-permute-start.5 = (bf16[3,72,512]{2,1,0:T(8,128)(2,1)S(1)}, bf16[3,72,512]{2,1,0:T(8,128)(2,1)S(1)}, u32[]{:S(2)}, u32[]{:S(2)}) collective-permute-start(bf16[3,72,512]{2,1,0:T(8,128)(2,1)S(1)} %get-tuple-element.43), channel_id=1, source_target_pairs={{0,224},{32,0},{64,32},{96,64},{128,96},{160,128},{192,160},{224,1... | collective-permute-start | bytes 663560 | tf_op jit(solution)/shard_map/ppermute | solution.py:41
  38.1 10.0 %collective-permute-start.8 = (bf16[3,72,512]{2,1,0:T(8,128)(2,1)S(1)}, bf16[3,72,512]{2,1,0:T(8,128)(2,1)S(1)}, u32[]{:S(2)}, u32[]{:S(2)}) collective-permute-start(bf16[3,72,512]{2,1,0:T(8,128)(2,1)S(1)} %get-tuple-element.50.third0), channel_id=1, source_target_pairs={{0,2},{1,3},{2,0},{3,1},{4,6},{5,7},{6,4},{7,5},{8,10},{9,11},{10,... | collective-permute-start | bytes 663560 | tf_op jit(solution)/shard_map/ppermute | solution.py:36
  45.1 6.9 %collective-permute-start.6 = (bf16[3,72,512]{2,1,0:T(8,128)(2,1)S(1)}, bf16[3,72,512]{2,1,0:T(8,128)(2,1)S(1)}, u32[]{:S(2)}, u32[]{:S(2)}) collective-permute-start(bf16[3,72,512]{2,1,0:T(8,128)(2,1)S(1)} %shard_map.68.last0), channel_id=1, source_target_pairs={{0,2},{1,3},{2,0},{3,1},{4,6},{5,7},{6,4},{7,5},{8,10},{9,11},{10,... | collective-permute-start | bytes 663560 | tf_op jit(solution)/shard_map/ppermute | solution.py:36
  52.8 1.8 %collective-permute-start.9 = (bf16[4,6,16,512]{3,2,1,0:T(8,128)(2,1)S(1)}, bf16[4,6,16,512]{3,2,1,0:T(8,128)(2,1)S(1)}, u32[]{:S(2)}, u32[]{:S(2)}) collective-permute-start(bf16[4,6,16,512]{3,2,1,0:T(8,128)(2,1)S(1)} %get-tuple-element.55), channel_id=1, source_target_pairs={{0,1},{1,0},{2,3},{3,2},{4,5},{5,4},{6,7},{7,6},{8,9},{9,8},{10,11... | collective-permute-start | bytes 1179656 | tf_op jit(solution)/shard_map/ppermute | solution.py:36
  54.8 1.8 %collective-permute-start.10 = (bf16[4,2,3,16,512]{4,3,2,1,0:T(8,128)(2,1)S(1)}, bf16[4,2,3,16,512]{4,3,2,1,0:T(8,128)(2,1)S(1)}, u32[]{:S(2)}, u32[]{:S(2)}) collective-permute-start(bf16[4,2,3,16,512]{4,3,2,1,0:T(8,128)(2,1)S(1)} %get-tuple-element.56), channel_id=1, source_target_pairs={{0,1},{1,0},{2,3},{3,2},{4,5},{5,4},{6,7},{7,6},{8,9},{9,8},{10,11... | collective-permute-start | bytes 1179656 | tf_op jit(solution)/shard_map/ppermute | solution.py:36
  55.0 13.0 %collective-permute-start.12 = (bf16[4,6,16,512]{3,2,1,0:T(8,128)(2,1)S(1)}, bf16[4,6,16,512]{3,2,1,0:T(8,128)(2,1)S(1)}, u32[]{:S(2)}, u32[]{:S(2)}) collective-permute-start(bf16[4,6,16,512]{3,2,1,0:T(8,128)(2,1)S(1)} %add_convert_fusion.2), channel_id=1, source_target_pairs={{0,16},{1,17},{2,18},{3,19},{4,20},{5,21},{6,22},{7,23},{8,24},{9,... | collective-permute-start | bytes 1179656 | tf_op jit(solution)/shard_map/ppermute | solution.py:36
  55.1 11.7 %collective-permute-start.11 = (bf16[4,6,16,512]{3,2,1,0:T(8,128)(2,1)S(1)}, bf16[4,6,16,512]{3,2,1,0:T(8,128)(2,1)S(1)}, u32[]{:S(2)}, u32[]{:S(2)}) collective-permute-start(bf16[4,6,16,512]{3,2,1,0:T(8,128)(2,1)S(1)} %get-tuple-element.60), channel_id=1, source_target_pairs={{0,1},{1,0},{2,3},{3,2},{4,5},{5,4},{6,7},{7,6},{8,9},{9,8},{10,11... | collective-permute-start | bytes 1179656 | tf_op jit(solution)/shard_map/ppermute | solution.py:36
  56.7 17.1 %collective-permute-start.18 = (bf16[2,3,16,512]{3,2,1,0:T(8,128)(2,1)S(1)}, bf16[2,3,16,512]{3,2,1,0:T(8,128)(2,1)S(1)}, u32[]{:S(2)}, u32[]{:S(2)}) collective-permute-start(bf16[2,3,16,512]{3,2,1,0:T(8,128)(2,1)S(1)} %get-tuple-element.66), channel_id=1, source_target_pairs={{0,12},{1,13},{2,14},{3,15},{4,0},{5,1},{6,2},{7,3},{8,4},{9,5},{1... | collective-permute-start | bytes 294920 | tf_op jit(solution)/shard_map/ppermute | solution.py:36
  62.7 13.4 %collective-permute-start.16 = (bf16[2,3,16,512]{3,2,1,0:T(8,128)(2,1)S(1)}, bf16[2,3,16,512]{3,2,1,0:T(8,128)(2,1)S(1)}, u32[]{:S(2)}, u32[]{:S(2)}) collective-permute-start(bf16[2,3,16,512]{3,2,1,0:T(8,128)(2,1)S(1)} %get-tuple-element.67), channel_id=1, source_target_pairs={{0,8},{1,9},{2,10},{3,11},{4,12},{5,13},{6,14},{7,15},{8,0},{9,1},... | collective-permute-start | bytes 294920 | tf_op jit(solution)/shard_map/ppermute | solution.py:36
  64.4 11.7 %collective-permute-start.17 = (bf16[2,3,16,512]{3,2,1,0:T(8,128)(2,1)S(1)}, bf16[2,3,16,512]{3,2,1,0:T(8,128)(2,1)S(1)}, u32[]{:S(2)}, u32[]{:S(2)}) collective-permute-start(bf16[2,3,16,512]{3,2,1,0:T(8,128)(2,1)S(1)} %get-tuple-element.68), channel_id=1, source_target_pairs={{0,4},{1,5},{2,6},{3,7},{4,8},{5,9},{6,10},{7,11},{8,12},{9,13},{1... | collective-permute-start | bytes 294920 | tf_op jit(solution)/shard_map/ppermute | solution.py:36
  68.3 10.9 %collective-permute-start.13 = (bf16[6,16,512]{2,1,0:T(8,128)(2,1)S(1)}, bf16[6,16,512]{2,1,0:T(8,128)(2,1)S(1)}, u32[]{:S(2)}, u32[]{:S(2)}) collective-permute-start(bf16[6,16,512]{2,1,0:T(8,128)(2,1)S(1)} %get-tuple-element.69), channel_id=1, source_target_pairs={{0,4},{1,5},{2,6},{3,7},{4,8},{5,9},{6,10},{7,11},{8,12},{9,13},{1... | collective-permute-start | bytes 294920 | tf_op jit(solution)/shard_map/ppermute | solution.py:36
  71.2 7.9 %collective-permute-start.15 = (bf16[6,16,512]{2,1,0:T(8,128)(2,1)S(1)}, bf16[6,16,512]{2,1,0:T(8,128)(2,1)S(1)}, u32[]{:S(2)}, u32[]{:S(2)}) collective-permute-start(bf16[6,16,512]{2,1,0:T(8,128)(2,1)S(1)} %get-tuple-element.70), channel_id=1, source_target_pairs={{0,12},{1,13},{2,14},{3,15},{4,0},{5,1},{6,2},{7,3},{8,4},{9,5},{1... | collective-permute-start | bytes 294920 | tf_op jit(solution)/shard_map/ppermute | solution.py:36
  73.8 11.3 %collective-permute-start.14 = (bf16[6,16,512]{2,1,0:T(8,128)(2,1)S(1)}, bf16[6,16,512]{2,1,0:T(8,128)(2,1)S(1)}, u32[]{:S(2)}, u32[]{:S(2)}) collective-permute-start(bf16[6,16,512]{2,1,0:T(8,128)(2,1)S(1)} %get-tuple-element.71), channel_id=1, source_target_pairs={{0,8},{1,9},{2,10},{3,11},{4,12},{5,13},{6,14},{7,15},{8,0},{9,1},... | collective-permute-start | bytes 294920 | tf_op jit(solution)/shard_map/ppermute | solution.py:36
  76.2 9.0 %collective-permute-start.19 = (bf16[3,16,512]{2,1,0:T(8,128)(2,1)S(1)}, bf16[3,16,512]{2,1,0:T(8,128)(2,1)S(1)}, u32[]{:S(2)}, u32[]{:S(2)}) collective-permute-start(bf16[3,16,512]{2,1,0:T(8,128)(2,1)S(1)} %slice_bitcast_fusion.8), channel_id=1, source_target_pairs={{0,16},{1,17},{2,18},{3,19},{4,20},{5,21},{6,22},{7,23},{8,24},{9,... | collective-permute-start | bytes 147464 | tf_op jit(solution)/shard_map/ppermute | solution.py:36
